TPU v7x, 32 devices: a whole 2x2x4 slice. The times are simulated.
32 devices in a mesh: groups: 2 (over y), ctx: 4 (over z), exp: 2 (over x), tp: 2 (over core).
Axes of the slice: x: 2, y: 2, z: 4, core: 2. Of those that a mesh axis runs over, the one named last changes fastest.
Arguments:
- queries: bfloat16 [4, 512, 20, 128], P(('groups', 'exp'), 'ctx', 'tp'), parts along dimension 0, may hold values from -9 to 9
- key_states: bfloat16 [4, 512, 4, 128], P(('groups', 'exp'), 'ctx', 'tp'), parts along dimension 0, may hold values from -9 to 9
- values: bfloat16 [4, 512, 4, 128], P(('groups', 'exp'), 'ctx', 'tp'), parts along dimension 0, may hold values from -6 to 6
- doc_ids: int32 [4, 512], P(('groups', 'exp'), 'ctx'), parts along dimension 0, may hold values from 0 to 3, never falling along the last dimension, each value on 1 to 256 neighbouring positions
- residual: bfloat16 [4, 512, 5120], P(('groups', 'exp'), ('ctx', 'tp')), parts along dimension 0, may hold values from -6 to 6
- out_proj: bfloat16 [2560, 5120], P('tp', 'ctx'), may hold values from -0.125 to 0.125
- norm_gain: bfloat16 [5120], replicated, may hold values from 0.5 to 1.5
- router: bfloat16 [5120, 64], P(None, 'exp'), may hold values from -0.078125 to 0.078125
- expert_ids: int32 [4, 512, 1], P(('groups', 'exp'), ('ctx', 'tp')), parts along dimension 0, may hold values from 0 to 63; in each aligned block of 64 rows (0 to 63, 64 to 127, ..., all dimensions but the last counted through in order) at most 2 rows name the same one
- keep_counts: int32 [128], P('groups'), parts along dimension 0, may hold values from 1 to 2
Outputs:
- expert_inputs: bfloat16 [32, 64, 2, 5120], P(('groups', 'ctx', 'tp'), 'exp'), parts along dimension 0
There are 2 independent parts, one for each index of `groups`. A program takes and returns all parts, laid end to end along the dimension named above; an argument that names none is the same for every part. Nothing has to cross between parts.
Inputs may be any that keep to these rules, and one draw needn't show every extreme that they name: `doc_ids`: doc ids never fall along a request; a document holds at most 256 tokens, and some document holds exactly that many. `expert_ids`: in each aligned block of 64 tokens (the rows of one device) no expert is named more than 2 times, and in some blocks one expert is named exactly 2 times.
All inputs are finite; a program needn't handle non-finite values.
Results may differ from a plain program's by a relative error of at most 0.013.
Values may be sent and summed in bfloat16 or wider, within the bound.
No kernel may reach another device: no remote copies, remote signals or barrier semaphores. Data moves between devices by JAX's collectives and lax.ppermute only.
A program may use at most 64 MiB of HBM per device.

v0:
```python
import functools
import math

import jax
import jax.numpy as jnp
from jax import lax
from jax.experimental import pallas as pl
from jax.experimental.pallas import tpu as pltpu
from jax.sharding import PartitionSpec as P

CAP = 2
EPSILON = 1e-05
DOC_ROWS = 16
VMEM_LIMIT = 16 * 1024 * 1024
VMEM_MOST = 61 * 1024 * 1024
VMEM_MUCH = 52 * 1024 * 1024
PIECE = 256


def fetch(refs, buffers, sems):
    copies = [
        pltpu.make_async_copy(ref, buffer, sems.at[number])
        for number, (ref, buffer) in enumerate(zip(refs, buffers))
    ]
    for copy in copies:
        copy.start()
    return [copy.wait for copy in copies]


def pack_kernel(groups, key_ref, value_ref, doc_ref, out_ref, *scratch):
    buffers, sems = scratch[:-1], scratch[-1]
    for wait in fetch((key_ref, value_ref, doc_ref), buffers, sems):
        wait()
    key_ref, value_ref, doc_ref = buffers
    rows, head_size = key_ref.shape
    tokens = rows // groups
    token = lax.broadcasted_iota(jnp.int32, (tokens, rows), 0)
    row = lax.broadcasted_iota(jnp.int32, (tokens, rows), 1)
    for group in range(groups):
        pick = (row == token * groups + group).astype(jnp.bfloat16)
        for place, ref in enumerate((key_ref, value_ref)):
            first = (place * groups + group) * tokens
            out_ref[first : first + tokens, :] = jnp.dot(
                pick, ref[...], preferred_element_type=jnp.float32
            ).astype(jnp.bfloat16)
    out_ref[2 * rows :, :] = jnp.broadcast_to(
        (doc_ref[...] + 1).astype(jnp.float32), (DOC_ROWS, tokens)
    ).astype(jnp.bfloat16)


def stage_kernel(count, *refs):
    for wait in fetch(refs[:count], refs[count:-1], refs[-1]):
        wait()


def attention_kernel(ratio, groups, pair, place_ref, query_ref, *refs):
    pack_refs, out_refs = refs[:-pair], refs[-pair:]
    heads, tokens, head_size = query_ref.shape
    scale = 1.0 / math.sqrt(head_size)
    core = place_ref[0]
    part_rows = tokens // pair
    held_rows = groups * tokens
    rows = lax.broadcasted_iota(jnp.int32, (tokens, tokens), 0)
    columns = lax.broadcasted_iota(jnp.int32, (tokens, tokens), 1)
    docs = [ref[2 * held_rows : 2 * held_rows + 1, :].astype(jnp.float32) for ref in pack_refs]
    own_doc = jnp.sum(jnp.where(rows == columns, docs[0], 0.0), axis=1, keepdims=True)
    allowed = [(own_doc == docs[0]) & (columns <= rows)] + [own_doc == doc for doc in docs[1:]]
    allowed = jnp.concatenate(allowed, axis=1)
    for group in range(groups):
        first = group * tokens
        keys = jnp.concatenate([ref[first : first + tokens, :] for ref in pack_refs], axis=0)
        first = held_rows + group * tokens
        held = jnp.concatenate([ref[first : first + tokens, :] for ref in pack_refs], axis=0)
        for head in range(group * ratio, (group + 1) * ratio):
            scores = lax.dot_general(
                query_ref[head], keys, (((1,), (1,)), ((), ())), preferred_element_type=jnp.float32
            )
            scores = jnp.where(allowed, scores * scale, -1e30)
            weights = jnp.exp(scores - jnp.max(scores, axis=1, keepdims=True))
            totals = jnp.sum(weights, axis=1, keepdims=True)
            mixed = jnp.dot(
                weights.astype(jnp.bfloat16), held, preferred_element_type=jnp.float32
            )
            mixed = (mixed / totals).astype(jnp.bfloat16)
            parts = [mixed[i * part_rows : (i + 1) * part_rows] for i in range(pair)]
            for turn in range(pair):
                piece = parts[turn]
                for own in range(1, pair):
                    piece = jnp.where(core == own, parts[(own + turn) % pair], piece)
                out_refs[turn][:, head * head_size : (head + 1) * head_size] = piece


def project_kernel(pair, *refs):
    block_refs, weight_refs, out_ref = refs[:pair], refs[pair : 2 * pair], refs[2 * pair]
    buffers, sems = refs[2 * pair + 1 : 3 * pair + 1], refs[3 * pair + 1]
    columns = out_ref.shape[1]
    piece = PIECE if columns % PIECE == 0 else columns
    parts = [pl.ds(first, piece) for first in range(0, columns, piece)]
    copies = [
        [
            pltpu.make_async_copy(
                weight_refs[turn].at[:, part], buffers[turn].at[:, part], sems.at[turn, number]
            )
            for turn in range(pair)
        ]
        for number, part in enumerate(parts)
    ]
    for group in copies:
        for copy in group:
            copy.start()
    for group, part in zip(copies, parts):
        total = None
        for turn in range(pair):
            group[turn].wait()
            product = jnp.dot(
                block_refs[turn][...],
                buffers[turn][:, part],
                preferred_element_type=jnp.float32,
            )
            total = product if total is None else total + product
        out_ref[:, part] = total.astype(out_ref.dtype)


def columns_of(chunk_ref, step, spots, ctx_index):
    columns = chunk_ref.shape[1]
    first = 0 if spots == 1 else lax.rem(ctx_index + step, spots) * columns
    return pl.ds(pl.multiple_of(first, 128), columns)


def hidden_kernel(step, spots, place_ref, residual_ref, chunk_ref, out_ref):
    part = columns_of(chunk_ref, step, spots, place_ref[0])
    out_ref[...] = (
        residual_ref[:, part].astype(jnp.float32) + chunk_ref[...].astype(jnp.float32)
    ).astype(out_ref.dtype)


def collect_kernel(steps, spots, exp_count, place_ref, *refs):
    count = len(steps)
    chunk_refs, out_refs = refs[:-exp_count], refs[-exp_count:]
    for back, out_ref in enumerate(out_refs):
        for step, chunk_ref in zip(steps, chunk_refs[back * count : (back + 1) * count]):
            out_ref[:, columns_of(chunk_ref, step, spots, place_ref[0])] = chunk_ref[...]


def finish_kernel(steps, spots, back, exp_count, place_ref, *refs):
    count = len(steps)
    chunk_refs = refs[:count]
    hidden_ref, id_ref, keep_ref, gain_ref, router_ref = refs[count : count + 5]
    out_ref, total_ref, normed_ref, result_ref, out_sem = refs[-5:]
    rows, width = hidden_ref.shape
    experts = keep_ref.shape[1]
    here = router_ref.shape[0]
    ctx_index, exp_index = place_ref[0], place_ref[1]
    keep = keep_ref[...].astype(jnp.float32)
    upper = (
        lax.broadcasted_iota(jnp.int32, (rows, rows), 0)
        < lax.broadcasted_iota(jnp.int32, (rows, rows), 1)
    ).astype(jnp.bfloat16)
    total_ref[...] = hidden_ref[...].astype(jnp.float32)
    for step, chunk_ref in zip(steps, chunk_refs):
        part = columns_of(chunk_ref, step, spots, ctx_index)
        total_ref[:, part] = chunk_ref[...].astype(jnp.float32)
    hidden = total_ref[...]
    power = jnp.sum(hidden * hidden, axis=1, keepdims=True)
    factor = lax.rsqrt(power / width + EPSILON)
    normed_ref[...] = (hidden * factor * gain_ref[...].astype(jnp.float32)).astype(jnp.bfloat16)
    ids = id_ref[...]
    onehot = (ids == lax.broadcasted_iota(jnp.int32, (experts, rows), 0)).astype(jnp.float32)
    earlier = jnp.dot(onehot.astype(jnp.bfloat16), upper, preferred_element_type=jnp.float32)
    ranking = jnp.sum(onehot * earlier, axis=0, keepdims=True)
    limits = jnp.dot(
        keep.astype(jnp.bfloat16),
        onehot.astype(jnp.bfloat16),
        preferred_element_type=jnp.float32,
    )
    local = ids - exp_index * here
    logits = lax.dot_general(
        router_ref[...],
        normed_ref[...],
        (((1,), (1,)), ((), ())),
        preferred_element_type=jnp.float32,
    )
    chosen = local == lax.broadcasted_iota(jnp.int32, (here, rows), 0)
    gates = jax.nn.sigmoid(jnp.sum(jnp.where(chosen, logits, 0.0), axis=0, keepdims=True))
    target = local * CAP + ranking.astype(jnp.int32)
    target = jnp.where((ranking < limits) & (local >= 0) & (local < here), target, -1)
    table = lax.broadcasted_iota(jnp.int32, (here * CAP, rows), 0) == target
    slot_gates = jnp.sum(jnp.where(table, gates, 0.0), axis=1, keepdims=True)
    slots = jnp.dot(
        table.astype(jnp.bfloat16), normed_ref[...], preferred_element_type=jnp.float32
    )
    result_ref[...] = (slots * slot_gates).astype(jnp.bfloat16).reshape(result_ref.shape)
    source = lax.rem(exp_index - back + exp_count, exp_count)
    copy = pltpu.make_async_copy(result_ref, out_ref.at[source], out_sem)
    copy.start()
    copy.wait()


def on_device(
    queries,
    key_states,
    values,
    doc_ids,
    residual,
    out_proj,
    norm_gain,
    router,
    expert_ids,
    keep_counts,
):
    _, tokens, heads, head_size = queries.shape
    groups = key_states.shape[2]
    ctx_count = lax.axis_size("ctx")
    pair = lax.axis_size("tp")
    exp_count = lax.axis_size("exp")
    part_rows = tokens // pair
    width = residual.shape[2]
    columns = out_proj.shape[1]
    experts_here = router.shape[1]
    ctx_index = lax.axis_index("ctx")
    core = lax.axis_index("tp")
    exp_index = lax.axis_index("exp")
    reach = -(-(ctx_count * tokens // 2 - 1) // tokens)
    vmem = pl.BlockSpec(memory_space=pltpu.VMEM)
    smem = pl.BlockSpec(memory_space=pltpu.SMEM)
    anywhere = pl.BlockSpec(memory_space=pl.ANY)
    params = pltpu.CompilerParams(vmem_limit_bytes=VMEM_LIMIT)
    most = pltpu.CompilerParams(vmem_limit_bytes=VMEM_MOST)
    much = pltpu.CompilerParams(vmem_limit_bytes=VMEM_MUCH)
    bf16, f32 = jnp.bfloat16, jnp.float32

    def over(array, axis, step):
        count = lax.axis_size(axis)
        if step % count == 0:
            return array
        return lax.ppermute(array, axis, [(i, (i + step) % count) for i in range(count)])

    def along(array, moves):
        return lax.ppermute(array, "ctx", moves)

    pack = pl.pallas_call(
        functools.partial(pack_kernel, groups),
        out_shape=jax.ShapeDtypeStruct((2 * groups * tokens + DOC_ROWS, head_size), bf16),
        in_specs=[anywhere] * 3,
        out_specs=vmem,
        scratch_shapes=[pltpu.VMEM((groups * tokens, head_size), bf16)] * 2
        + [pltpu.VMEM(doc_ids.shape, doc_ids.dtype), pltpu.SemaphoreType.DMA((3,))],
        compiler_params=most,
    )(
        key_states.reshape(groups * tokens, head_size),
        values.reshape(groups * tokens, head_size),
        doc_ids,
    )
    packs = [pack] + [
        lax.ppermute(pack, "ctx", [(i, i + step) for i in range(ctx_count - step)])
        for step in range(1, reach + 1)
    ]
    ids, own_residual = expert_ids[:, :, 0], residual[0]
    pack, own_queries, early_weights = lax.optimization_barrier(
        (pack, queries[0].transpose(1, 0, 2), out_proj)
    )
    weights = [out_proj] + [over(early_weights, "tp", turn) for turn in range(1, pair)]
    staged_queries, packs[0] = pl.pallas_call(
        functools.partial(stage_kernel, 2),
        out_shape=[
            jax.ShapeDtypeStruct(own_queries.shape, bf16),
            jax.ShapeDtypeStruct(pack.shape, bf16),
        ],
        in_specs=[anywhere] * 2,
        out_specs=[vmem] * 2,
        scratch_shapes=[pltpu.SemaphoreType.DMA((2,))],
        compiler_params=much,
    )(own_queries, pack)
    all_ids = [ids] + [over(ids, "exp", back) for back in range(1, exp_count)]
    pieces = pl.pallas_call(
        functools.partial(attention_kernel, heads // groups, groups, pair),
        out_shape=[jax.ShapeDtypeStruct((part_rows, heads * head_size), bf16)] * pair,
        in_specs=[smem] + [vmem] * (1 + len(packs)),
        out_specs=[vmem] * pair,
        compiler_params=params,
    )(core.reshape(1), staged_queries, *packs)

    project = pl.pallas_call(
        functools.partial(project_kernel, pair),
        out_shape=jax.ShapeDtypeStruct((part_rows, columns), bf16),
        in_specs=[vmem] * pair + [anywhere] * pair,
        out_specs=vmem,
        scratch_shapes=[pltpu.VMEM(out_proj.shape, bf16)] * pair
        + [pltpu.SemaphoreType.DMA((pair, max(1, columns // PIECE)))],
        compiler_params=much,
        cost_estimate=pl.CostEstimate(
            flops=2 * pair * part_rows * out_proj.size,
            bytes_accessed=2 * pair * out_proj.size,
            transcendentals=0,
        ),
    )
    block = [over(pieces[turn], "tp", turn) for turn in range(pair)]

    aligned = columns % 128 == 0
    hidden = None

    def forward(chunk, step, spots):
        hidden = pl.pallas_call(
            functools.partial(hidden_kernel, step, spots),
            out_shape=jax.ShapeDtypeStruct(chunk.shape, bf16),
            in_specs=[smem] + [vmem] * 2,
            out_specs=vmem,
            compiler_params=params,
        )(ctx_index.reshape(1), own_residual, chunk)
        return [over(hidden, "exp", back) for back in range(exp_count)]

    def collect(steps, spots):
        arrays = [flat[step][back] for back in range(exp_count) for step in steps]
        return pl.pallas_call(
            functools.partial(collect_kernel, steps, spots, exp_count),
            out_shape=[jax.ShapeDtypeStruct((part_rows, width), bf16)] * exp_count,
            in_specs=[smem] + [vmem] * len(arrays),
            out_specs=[vmem] * exp_count,
            compiler_params=params,
        )(ctx_index.reshape(1), *arrays)

    chunks, flat = [], []
    late_from = max(1, ctx_count - 2)
    for step in range(ctx_count):
        last = step == ctx_count - 1
        following = None if last else [over(array, "ctx", 1) for array in block]
        if step == 1:
            block, all_ids = lax.optimization_barrier((block, all_ids))
        if step == 2:
            block, chunks[1] = lax.optimization_barrier((block, chunks[1]))
        if last and aligned:
            hidden = collect(list(range(late_from)), ctx_count)
            block, hidden = lax.optimization_barrier((block, hidden))
        total = project(*block, *weights)
        chunk = over(total, "ctx", ctx_count - step)
        if not last:
            block = [lax.optimization_barrier((array, total))[0] for array in following]
        chunks.append(chunk)
        if aligned:
            flat.append(forward(chunk, step, ctx_count))
    if aligned:
        late_steps, spots = list(range(late_from, ctx_count)), ctx_count
    else:
        whole = jnp.roll(jnp.stack(chunks), ctx_index, axis=0)
        whole = whole.transpose(1, 0, 2).reshape(part_rows, width)
        flat.append(forward(whole, 0, 1))
        hidden = collect([0], 1)
        late_steps, spots = [], 1
    places = jnp.stack([ctx_index, exp_index])
    out = None
    for back in range(exp_count):
        operands = (
            [places]
            + [flat[step][back] for step in late_steps]
            + [hidden[back], all_ids[back], keep_counts.reshape(1, -1)]
            + [norm_gain.reshape(1, -1), router.T]
        )
        kept = [] if out is None else [out]
        out = pl.pallas_call(
            functools.partial(finish_kernel, late_steps, spots, back, exp_count),
            out_shape=jax.ShapeDtypeStruct((exp_count, experts_here, CAP, width), bf16),
            in_specs=[smem] + [vmem] * (len(operands) - 1) + [anywhere] * len(kept),
            out_specs=anywhere,
            scratch_shapes=[
                pltpu.VMEM((part_rows, width), f32),
                pltpu.VMEM((part_rows, width), bf16),
                pltpu.VMEM((experts_here, CAP, width), bf16),
                pltpu.SemaphoreType.DMA,
            ],
            input_output_aliases={len(operands): 0} if kept else {},
            compiler_params=params,
        )(*operands, *kept)
    return out


def solution(mesh):
    placed = (
        P(("groups", "exp"), "ctx", "tp", None),
        P(("groups", "exp"), "ctx", "tp", None),
        P(("groups", "exp"), "ctx", "tp", None),
        P(("groups", "exp"), "ctx"),
        P(("groups", "exp"), ("ctx", "tp"), None),
        P("tp", "ctx"),
        P(),
        P(None, "exp"),
        P(("groups", "exp"), ("ctx", "tp"), None),
        P("groups"),
    )
    return jax.shard_map(
        on_device,
        mesh=mesh,
        in_specs=placed,
        out_specs=P(("groups", "ctx", "tp"), "exp", None, None),
        check_vma=False,
    )
```

profile of v0, /device:TPU:0, one launch (start us, length us, event | category | flops | bytes accessed | tf_op | source)
XLA Modules:
  0.0 80.1 jit_solution(9864695448052991204)
XLA Ops:
  0.0 1.8 %shard_map.100.refs_1_ = bf16[528,128]{1,0:T(8,128)(2,1)} custom-call(bf16[256,128]{1,0:T(8,128)(2,1)} %bitcast.23, bf16[256,128]{1,0:T(8,128)(2,1)} %bitcast.24, s32[1,128]{1,0:T(1,128)} %doc_ref.1), custom_call_target="tpu_custom_call" | custom-call | tf_op jit(solution)/shard_map/pallas_call | solution.py:241
  2.3 4.5 %collective-permute-start = (bf16[528,128]{1,0:T(8,128)(2,1)}, bf16[528,128]{1,0:T(8,128)(2,1)S(1)}, u32[]{:S(2)}, u32[]{:S(2)}) collective-permute-start(bf16[528,128]{1,0:T(8,128)(2,1)} %shard_map.100.refs_1_), channel_id=1, source_target_pairs={{0,4},{4,8},{8,12},{1,5},{5,9},{9,13},{2,6},{6,10},{10,14},{3,7},{... | collective-permute-start | bytes 405512 | tf_op jit(solution)/shard_map/ppermute | solution.py:255
  6.8 4.5 %collective-permute-start.1 = (bf16[528,128]{1,0:T(8,128)(2,1)}, bf16[528,128]{1,0:T(8,128)(2,1)S(1)}, u32[]{:S(2)}, u32[]{:S(2)}) collective-permute-start(bf16[528,128]{1,0:T(8,128)(2,1)} %shard_map.100.refs_1_), channel_id=1, source_target_pairs={{0,8},{4,12},{1,9},{5,13},{2,10},{6,14},{3,11},{7,15},{16,24},{20,... | collective-permute-start | bytes 405512 | tf_op jit(solution)/shard_map/ppermute | solution.py:255
  11.3 0.9 %copy-done.2 = bf16[528,128]{1,0:T(8,128)(2,1)S(1)} copy-done((bf16[528,128]{1,0:T(8,128)(2,1)S(1)}, bf16[528,128]{1,0:T(8,128)(2,1)}, u32[]{:S(2)}) %copy-start.2) | copy-done | bytes 135192
  12.2 1.0 %copy-done.3 = bf16[1,128,10,128]{3,1,2,0:T(8,128)(2,1)S(1)} copy-done((bf16[1,128,10,128]{3,1,2,0:T(8,128)(2,1)S(1)}, bf16[1,128,10,128]{3,1,2,0:T(8,128)(2,1)}, u32[]{:S(2)}) %copy-start.3) | copy-done | bytes 327704
  13.5 1.3 %collective-permute-done.1.refs_2_ = bf16[528,128]{1,0:T(8,128)(2,1)S(1)} collective-permute-done((bf16[528,128]{1,0:T(8,128)(2,1)}, bf16[528,128]{1,0:T(8,128)(2,1)S(1)}, u32[]{:S(2)}, u32[]{:S(2)}) %collective-permute-start.1) | collective-permute-done | bytes 135200 | tf_op jit(solution)/shard_map/ppermute | solution.py:255
  14.9 2.7 %shard_map.102 = (bf16[64,1280]{1,0:T(8,128)(2,1)S(1)}, bf16[64,1280]{1,0:T(8,128)(2,1)S(1)}) custom-call(s32[1]{0:T(128)} %bitcast.3.place_ref, bf16[10,128,128]{2,1,0:T(8,128)(2,1)S(1)} %get-tuple-element.32.query_ref, bf16[528,128]{1,0:T(8,128)(2,1)S(1)} %get-tuple-element.33.refs_0_, bf16[528,128]{1,0:T(8,128)(2,1)S(1)} %collective-permute-done.refs_1_, ...), custom_call_target="tpu_custom_call" | custom-call | tf_op jit(solution)/shard_map/pallas_call | solution.py:275
  17.7 1.4 %collective-permute-done.3.refs_1_ = bf16[64,1280]{1,0:T(8,128)(2,1)S(1)} collective-permute-done((bf16[64,1280]{1,0:T(8,128)(2,1)S(1)}, bf16[64,1280]{1,0:T(8,128)(2,1)S(1)}, u32[]{:S(2)}, u32[]{:S(2)}) %collective-permute-start.3) | collective-permute-done | bytes 163872 | tf_op jit(solution)/shard_map/ppermute | solution.py:236
  19.1 3.1 %collective-permute-start.6 = (bf16[64,1280]{1,0:T(8,128)(2,1)S(1)}, bf16[64,1280]{1,0:T(8,128)(2,1)S(1)}, u32[]{:S(2)}, u32[]{:S(2)}) collective-permute-start(bf16[64,1280]{1,0:T(8,128)(2,1)S(1)} %collective-permute-done.3.refs_1_), channel_id=1, source_target_pairs={{0,4},{4,8},{8,12},{12,0},{1,5},{5,9},{9,13},{13,1},{2,6},{6,10},{... | collective-permute-start | bytes 491528 | tf_op jit(solution)/shard_map/ppermute | solution.py:236
  22.2 0.8 collective-permute-start.2
  22.9 1.5 %collective-permute-start.7 = (s32[1,64]{1,0:T(1,128)}, s32[1,64]{1,0:T(1,128)S(1)}, u32[]{:S(2)}, u32[]{:S(2)}) collective-permute-start(s32[1,64]{1,0:T(1,128)} %bitcast.21), channel_id=1, source_target_pairs={{0,2},{2,0},{1,3},{3,1},{4,6},{6,4},{5,7},{7,5},{8,10},{10,8},{9,1... | collective-permute-start | bytes 776 | tf_op jit(solution)/shard_map/ppermute | solution.py:236
  24.4 3.9 %shard_map.103.chunk_ref = bf16[64,1280]{1,0:T(8,128)(2,1)S(1)} custom-call(bf16[64,1280]{1,0:T(8,128)(2,1)S(1)} %get-tuple-element.34.refs_0_, bf16[64,1280]{1,0:T(8,128)(2,1)S(1)} %collective-permute-done.3.refs_1_, bf16[1280,1280]{1,0:T(8,128)(2,1)} %refs_2_.7, bf16[1280,1280]{1,0:T(8,128)(2,1)} %collective-permute-done.4.refs_3_), custom_call_target="tpu_custom_call" | custom-call | flops 419430400 | bytes 6553600 | tf_op jit(solution)/shard_map/pallas_call | solution.py:334
  28.4 1.4 %collective-permute-done.6.refs_1_ = bf16[64,1280]{1,0:T(8,128)(2,1)S(1)} collective-permute-done((bf16[64,1280]{1,0:T(8,128)(2,1)S(1)}, bf16[64,1280]{1,0:T(8,128)(2,1)S(1)}, u32[]{:S(2)}, u32[]{:S(2)}) %collective-permute-start.6) | collective-permute-done | bytes 163872 | tf_op jit(solution)/shard_map/ppermute | solution.py:236
  29.8 3.0 %collective-permute-done.2.refs_0_ = bf16[64,1280]{1,0:T(8,128)(2,1)S(1)} collective-permute-done((bf16[64,1280]{1,0:T(8,128)(2,1)S(1)}, bf16[64,1280]{1,0:T(8,128)(2,1)S(1)}, u32[]{:S(2)}, u32[]{:S(2)}) %collective-permute-start.2) | collective-permute-done | bytes 163872 | tf_op jit(solution)/shard_map/ppermute | solution.py:236
  33.3 3.9 %shard_map.104 = bf16[64,1280]{1,0:T(8,128)(2,1)S(1)} custom-call(bf16[64,1280]{1,0:T(8,128)(2,1)S(1)} %collective-permute-done.2.refs_0_, bf16[64,1280]{1,0:T(8,128)(2,1)S(1)} %collective-permute-done.6.refs_1_, bf16[1280,1280]{1,0:T(8,128)(2,1)} %refs_2_.7, bf16[1280,1280]{1,0:T(8,128)(2,1)} %collective-permute-done.4.refs_3_), custom_call_target="tpu_custom_call" | custom-call | flops 419430400 | bytes 6553600 | tf_op jit(solution)/shard_map/pallas_call | solution.py:334
  37.2 3.5 %collective-permute-start.9 = (bf16[64,1280]{1,0:T(8,128)(2,1)S(1)}, bf16[64,1280]{1,0:T(8,128)(2,1)S(1)}, u32[]{:S(2)}, u32[]{:S(2)}) collective-permute-start(bf16[64,1280]{1,0:T(8,128)(2,1)S(1)} %shard_map.104), channel_id=1, source_target_pairs={{0,12},{4,0},{8,4},{12,8},{1,13},{5,1},{9,5},{13,9},{2,14},{6,2},{... | collective-permute-start | bytes 491528 | tf_op jit(solution)/shard_map/ppermute | solution.py:236
  40.8 1.2 %collective-permute-done.8.refs_1_ = bf16[64,1280]{1,0:T(8,128)(2,1)S(1)} collective-permute-done((bf16[64,1280]{1,0:T(8,128)(2,1)S(1)}, bf16[64,1280]{1,0:T(8,128)(2,1)S(1)}, u32[]{:S(2)}, u32[]{:S(2)}) %collective-permute-start.8) | collective-permute-done | bytes 163872 | tf_op jit(solution)/shard_map/ppermute | solution.py:236
  42.0 3.4 %collective-permute-done.5.refs_0_ = bf16[64,1280]{1,0:T(8,128)(2,1)S(1)} collective-permute-done((bf16[64,1280]{1,0:T(8,128)(2,1)S(1)}, bf16[64,1280]{1,0:T(8,128)(2,1)S(1)}, u32[]{:S(2)}, u32[]{:S(2)}) %collective-permute-start.5) | collective-permute-done | bytes 163872 | tf_op jit(solution)/shard_map/ppermute | solution.py:236
  45.4 1.5 %collective-permute-start.14 = (bf16[64,1280]{1,0:T(8,128)(2,1)S(1)}, bf16[64,1280]{1,0:T(8,128)(2,1)S(1)}, u32[]{:S(2)}, u32[]{:S(2)}) collective-permute-start(bf16[64,1280]{1,0:T(8,128)(2,1)S(1)} %shard_map.107.refs_0_), channel_id=1, source_target_pairs={{0,2},{2,0},{1,3},{3,1},{4,6},{6,4},{5,7},{7,5},{8,10},{10,8},{9,1... | collective-permute-start | bytes 491528 | tf_op jit(solution)/shard_map/ppermute | solution.py:236
  46.9 1.8 %collective-permute-done.9.chunk_ref = bf16[64,1280]{1,0:T(8,128)(2,1)S(1)} collective-permute-done((bf16[64,1280]{1,0:T(8,128)(2,1)S(1)}, bf16[64,1280]{1,0:T(8,128)(2,1)S(1)}, u32[]{:S(2)}, u32[]{:S(2)}) %collective-permute-start.9) | collective-permute-done | bytes 163872 | tf_op jit(solution)/shard_map/ppermute | solution.py:236
  48.8 1.6 %collective-permute-start.15 = (bf16[64,1280]{1,0:T(8,128)(2,1)S(1)}, bf16[64,1280]{1,0:T(8,128)(2,1)S(1)}, u32[]{:S(2)}, u32[]{:S(2)}) collective-permute-start(bf16[64,1280]{1,0:T(8,128)(2,1)S(1)} %shard_map.108.refs_1_), channel_id=1, source_target_pairs={{0,2},{2,0},{1,3},{3,1},{4,6},{6,4},{5,7},{7,5},{8,10},{10,8},{9,1... | collective-permute-start | bytes 491528 | tf_op jit(solution)/shard_map/ppermute | solution.py:236
  50.3 3.9 %shard_map.105 = bf16[64,1280]{1,0:T(8,128)(2,1)S(1)} custom-call(bf16[64,1280]{1,0:T(8,128)(2,1)S(1)} %collective-permute-done.5.refs_0_, bf16[64,1280]{1,0:T(8,128)(2,1)S(1)} %collective-permute-done.8.refs_1_, bf16[1280,1280]{1,0:T(8,128)(2,1)} %refs_2_.7, bf16[1280,1280]{1,0:T(8,128)(2,1)} %collective-permute-done.4.refs_3_), custom_call_target="tpu_custom_call" | custom-call | flops 419430400 | bytes 6553600 | tf_op jit(solution)/shard_map/pallas_call | solution.py:334
  54.3 0.8 %collective-permute-start.10 = (bf16[64,1280]{1,0:T(8,128)(2,1)S(1)}, bf16[64,1280]{1,0:T(8,128)(2,1)S(1)}, u32[]{:S(2)}, u32[]{:S(2)}) collective-permute-start(bf16[64,1280]{1,0:T(8,128)(2,1)S(1)} %shard_map.105), channel_id=1, source_target_pairs={{0,8},{4,12},{8,0},{12,4},{1,9},{5,13},{9,1},{13,5},{2,10},{6,14},... | collective-permute-start | bytes 491528 | tf_op jit(solution)/shard_map/ppermute | solution.py:236
  55.2 4.0 %shard_map.110 = bf16[64,1280]{1,0:T(8,128)(2,1)S(1)} custom-call(bf16[64,1280]{1,0:T(8,128)(2,1)S(1)} %collective-permute-done.12.refs_0_, bf16[64,1280]{1,0:T(8,128)(2,1)S(1)} %collective-permute-done.13.refs_1_, bf16[1280,1280]{1,0:T(8,128)(2,1)} %refs_2_.7, bf16[1280,1280]{1,0:T(8,128)(2,1)} %collective-permute-done.4.refs_3_), custom_call_target="tpu_custom_call" | custom-call | flops 419430400 | bytes 6553600 | tf_op jit(solution)/shard_map/pallas_call | solution.py:334
  59.2 0.9 %collective-permute-start.16 = (bf16[64,1280]{1,0:T(8,128)(2,1)S(1)}, bf16[64,1280]{1,0:T(8,128)(2,1)S(1)}, u32[]{:S(2)}, u32[]{:S(2)}) collective-permute-start(bf16[64,1280]{1,0:T(8,128)(2,1)S(1)} %shard_map.110), channel_id=1, source_target_pairs={{0,4},{4,8},{8,12},{12,0},{1,5},{5,9},{9,13},{13,1},{2,6},{6,10},{... | collective-permute-start | bytes 491528 | tf_op jit(solution)/shard_map/ppermute | solution.py:236
  60.1 7.8 %collective-permute-done.10.chunk_ref = bf16[64,1280]{1,0:T(8,128)(2,1)S(1)} collective-permute-done((bf16[64,1280]{1,0:T(8,128)(2,1)S(1)}, bf16[64,1280]{1,0:T(8,128)(2,1)S(1)}, u32[]{:S(2)}, u32[]{:S(2)}) %collective-permute-start.10) | collective-permute-done | bytes 163872 | tf_op jit(solution)/shard_map/ppermute | solution.py:236
  68.0 0.6 collective-permute-start.11
  68.6 1.6 %collective-permute-start.17 = (bf16[64,1280]{1,0:T(8,128)(2,1)S(1)}, bf16[64,1280]{1,0:T(8,128)(2,1)S(1)}, u32[]{:S(2)}, u32[]{:S(2)}) collective-permute-start(bf16[64,1280]{1,0:T(8,128)(2,1)S(1)} %shard_map.111.refs_1_), channel_id=1, source_target_pairs={{0,2},{2,0},{1,3},{3,1},{4,6},{6,4},{5,7},{7,5},{8,10},{10,8},{9,1... | collective-permute-start | bytes 491528 | tf_op jit(solution)/shard_map/ppermute | solution.py:236
  70.3 2.5 %shard_map.112.refs_7_ = bf16[2,32,2,5120]{3,2,1,0:T(2,128)(2,1)} custom-call(s32[2]{0:T(128)S(1)} %pad_add_fusion.place_ref, bf16[64,1280]{1,0:T(8,128)(2,1)S(1)} %shard_map.106.refs_0_, bf16[64,1280]{1,0:T(8,128)(2,1)S(1)} %shard_map.111.refs_1_, bf16[64,5120]{1,0:T(8,128)(2,1)S(1)} %get-tuple-element.53.refs_2_, s32[1,64]{1,0:T(1,128)S(1)} %bitcast.22, ...), custom_call_target="tpu_custom_call" | custom-call | tf_op jit(solution)/shard_map/pallas_call | solution.py:359
  72.8 2.4 %collective-permute-done.11.refs_0_ = bf16[64,1280]{1,0:T(8,128)(2,1)S(1)} collective-permute-done((bf16[64,1280]{1,0:T(8,128)(2,1)S(1)}, bf16[64,1280]{1,0:T(8,128)(2,1)S(1)}, u32[]{:S(2)}, u32[]{:S(2)}) %collective-permute-start.11) | collective-permute-done | bytes 163872 | tf_op jit(solution)/shard_map/ppermute | solution.py:236
  75.1 2.5 %collective-permute-done.17.refs_1_ = bf16[64,1280]{1,0:T(8,128)(2,1)S(1)} collective-permute-done((bf16[64,1280]{1,0:T(8,128)(2,1)S(1)}, bf16[64,1280]{1,0:T(8,128)(2,1)S(1)}, u32[]{:S(2)}, u32[]{:S(2)}) %collective-permute-start.17) | collective-permute-done | bytes 163872 | tf_op jit(solution)/shard_map/ppermute | solution.py:236
  77.6 2.5 %shard_map.113 = bf16[2,32,2,5120]{3,2,1,0:T(2,128)(2,1)} custom-call(s32[2]{0:T(128)S(1)} %pad_add_fusion.place_ref, bf16[64,1280]{1,0:T(8,128)(2,1)S(1)} %collective-permute-done.11.refs_0_, bf16[64,1280]{1,0:T(8,128)(2,1)S(1)} %collective-permute-done.17.refs_1_, bf16[64,5120]{1,0:T(8,128)(2,1)S(1)} %get-tuple-element.51.refs_2_, ...), custom_call_target="tpu_custom_call", output_to_operand_aliasing={{}: (8, {})} | custom-call | tf_op jit(solution)/shard_map/pallas_call | solution.py:359
  (34 shorter events, 1.6 us)
Async XLA Ops:
  1.8 22.7 %collective-permute-start.4 = (bf16[1280,1280]{1,0:T(8,128)(2,1)}, bf16[1280,1280]{1,0:T(8,128)(2,1)}, u32[]{:S(2)}, u32[]{:S(2)}) collective-permute-start(bf16[1280,1280]{1,0:T(8,128)(2,1)} %refs_2_.7), channel_id=1, source_target_pairs={{0,1},{1,0},{2,3},{3,2},{4,5},{5,4},{6,7},{7,6},{8,9},{9,8},{10,11... | collective-permute-start | bytes 9830408 | tf_op jit(solution)/shard_map/ppermute | solution.py:236
  2.3 11.2 %collective-permute-start = (bf16[528,128]{1,0:T(8,128)(2,1)}, bf16[528,128]{1,0:T(8,128)(2,1)S(1)}, u32[]{:S(2)}, u32[]{:S(2)}) collective-permute-start(bf16[528,128]{1,0:T(8,128)(2,1)} %shard_map.100.refs_1_), channel_id=1, source_target_pairs={{0,4},{4,8},{8,12},{1,5},{5,9},{9,13},{2,6},{6,10},{10,14},{3,7},{... | collective-permute-start | bytes 405512 | tf_op jit(solution)/shard_map/ppermute | solution.py:255
  6.8 8.1 %collective-permute-start.1 = (bf16[528,128]{1,0:T(8,128)(2,1)}, bf16[528,128]{1,0:T(8,128)(2,1)S(1)}, u32[]{:S(2)}, u32[]{:S(2)}) collective-permute-start(bf16[528,128]{1,0:T(8,128)(2,1)} %shard_map.100.refs_1_), channel_id=1, source_target_pairs={{0,8},{4,12},{1,9},{5,13},{2,10},{6,14},{3,11},{7,15},{16,24},{20,... | collective-permute-start | bytes 405512 | tf_op jit(solution)/shard_map/ppermute | solution.py:255
  11.3 0.9 %copy-start.2 = (bf16[528,128]{1,0:T(8,128)(2,1)S(1)}, bf16[528,128]{1,0:T(8,128)(2,1)}, u32[]{:S(2)}) copy-start(bf16[528,128]{1,0:T(8,128)(2,1)} %shard_map.100.refs_1_) | copy-start | bytes 405508
  12.2 1.0 %copy-start.3 = (bf16[1,128,10,128]{3,1,2,0:T(8,128)(2,1)S(1)}, bf16[1,128,10,128]{3,1,2,0:T(8,128)(2,1)}, u32[]{:S(2)}) copy-start(bf16[1,128,10,128]{3,1,2,0:T(8,128)(2,1)} %param.10) | copy-start | bytes 983044
  17.6 1.5 %collective-permute-start.3 = (bf16[64,1280]{1,0:T(8,128)(2,1)S(1)}, bf16[64,1280]{1,0:T(8,128)(2,1)S(1)}, u32[]{:S(2)}, u32[]{:S(2)}) collective-permute-start(bf16[64,1280]{1,0:T(8,128)(2,1)S(1)} %get-tuple-element.35), channel_id=1, source_target_pairs={{0,1},{1,0},{2,3},{3,2},{4,5},{5,4},{6,7},{7,6},{8,9},{9,8},{10,11... | collective-permute-start | bytes 491528 | tf_op jit(solution)/shard_map/ppermute | solution.py:236
  19.1 10.8 %collective-permute-start.6 = (bf16[64,1280]{1,0:T(8,128)(2,1)S(1)}, bf16[64,1280]{1,0:T(8,128)(2,1)S(1)}, u32[]{:S(2)}, u32[]{:S(2)}) collective-permute-start(bf16[64,1280]{1,0:T(8,128)(2,1)S(1)} %collective-permute-done.3.refs_1_), channel_id=1, source_target_pairs={{0,4},{4,8},{8,12},{12,0},{1,5},{5,9},{9,13},{13,1},{2,6},{6,10},{... | collective-permute-start | bytes 491528 | tf_op jit(solution)/shard_map/ppermute | solution.py:236
  22.2 10.7 %collective-permute-start.2 = (bf16[64,1280]{1,0:T(8,128)(2,1)S(1)}, bf16[64,1280]{1,0:T(8,128)(2,1)S(1)}, u32[]{:S(2)}, u32[]{:S(2)}) collective-permute-start(bf16[64,1280]{1,0:T(8,128)(2,1)S(1)} %get-tuple-element.34.refs_0_), channel_id=1, source_target_pairs={{0,4},{4,8},{8,12},{12,0},{1,5},{5,9},{9,13},{13,1},{2,6},{6,10},{... | collective-permute-start | bytes 491528 | tf_op jit(solution)/shard_map/ppermute | solution.py:236
  22.9 10.3 %collective-permute-start.7 = (s32[1,64]{1,0:T(1,128)}, s32[1,64]{1,0:T(1,128)S(1)}, u32[]{:S(2)}, u32[]{:S(2)}) collective-permute-start(s32[1,64]{1,0:T(1,128)} %bitcast.21), channel_id=1, source_target_pairs={{0,2},{2,0},{1,3},{3,1},{4,6},{6,4},{5,7},{7,5},{8,10},{10,8},{9,1... | collective-permute-start | bytes 776 | tf_op jit(solution)/shard_map/ppermute | solution.py:236
  28.4 12.4 %copy-start = (bf16[1,64,5120]{2,1,0:T(8,128)(2,1)S(1)}, bf16[1,64,5120]{2,1,0:T(8,128)(2,1)}, u32[]{:S(2)}) copy-start(bf16[1,64,5120]{2,1,0:T(8,128)(2,1)} %param.14) | copy-start | bytes 1966084
  32.9 9.1 %collective-permute-start.8 = (bf16[64,1280]{1,0:T(8,128)(2,1)S(1)}, bf16[64,1280]{1,0:T(8,128)(2,1)S(1)}, u32[]{:S(2)}, u32[]{:S(2)}) collective-permute-start(bf16[64,1280]{1,0:T(8,128)(2,1)S(1)} %collective-permute-done.6.refs_1_), channel_id=1, source_target_pairs={{0,4},{4,8},{8,12},{12,0},{1,5},{5,9},{9,13},{13,1},{2,6},{6,10},{... | collective-permute-start | bytes 491528 | tf_op jit(solution)/shard_map/ppermute | solution.py:236
  32.9 12.5 %collective-permute-start.5 = (bf16[64,1280]{1,0:T(8,128)(2,1)S(1)}, bf16[64,1280]{1,0:T(8,128)(2,1)S(1)}, u32[]{:S(2)}, u32[]{:S(2)}) collective-permute-start(bf16[64,1280]{1,0:T(8,128)(2,1)S(1)} %collective-permute-done.2.refs_0_), channel_id=1, source_target_pairs={{0,4},{4,8},{8,12},{12,0},{1,5},{5,9},{9,13},{13,1},{2,6},{6,10},{... | collective-permute-start | bytes 491528 | tf_op jit(solution)/shard_map/ppermute | solution.py:236
  37.2 11.5 %collective-permute-start.9 = (bf16[64,1280]{1,0:T(8,128)(2,1)S(1)}, bf16[64,1280]{1,0:T(8,128)(2,1)S(1)}, u32[]{:S(2)}, u32[]{:S(2)}) collective-permute-start(bf16[64,1280]{1,0:T(8,128)(2,1)S(1)} %shard_map.104), channel_id=1, source_target_pairs={{0,12},{4,0},{8,4},{12,8},{1,13},{5,1},{9,5},{13,9},{2,14},{6,2},{... | collective-permute-start | bytes 491528 | tf_op jit(solution)/shard_map/ppermute | solution.py:236
  42.0 13.1 %collective-permute-start.13 = (bf16[64,1280]{1,0:T(8,128)(2,1)S(1)}, bf16[64,1280]{1,0:T(8,128)(2,1)S(1)}, u32[]{:S(2)}, u32[]{:S(2)}) collective-permute-start(bf16[64,1280]{1,0:T(8,128)(2,1)S(1)} %collective-permute-done.8.refs_1_), channel_id=1, source_target_pairs={{0,4},{4,8},{8,12},{12,0},{1,5},{5,9},{9,13},{13,1},{2,6},{6,10},{... | collective-permute-start | bytes 491528 | tf_op jit(solution)/shard_map/ppermute | solution.py:236
  45.4 9.7 %collective-permute-start.12 = (bf16[64,1280]{1,0:T(8,128)(2,1)S(1)}, bf16[64,1280]{1,0:T(8,128)(2,1)S(1)}, u32[]{:S(2)}, u32[]{:S(2)}) collective-permute-start(bf16[64,1280]{1,0:T(8,128)(2,1)S(1)} %collective-permute-done.5.refs_0_), channel_id=1, source_target_pairs={{0,4},{4,8},{8,12},{12,0},{1,5},{5,9},{9,13},{13,1},{2,6},{6,10},{... | collective-permute-start | bytes 491528 | tf_op jit(solution)/shard_map/ppermute | solution.py:236
  45.4 9.7 %collective-permute-start.14 = (bf16[64,1280]{1,0:T(8,128)(2,1)S(1)}, bf16[64,1280]{1,0:T(8,128)(2,1)S(1)}, u32[]{:S(2)}, u32[]{:S(2)}) collective-permute-start(bf16[64,1280]{1,0:T(8,128)(2,1)S(1)} %shard_map.107.refs_0_), channel_id=1, source_target_pairs={{0,2},{2,0},{1,3},{3,1},{4,6},{6,4},{5,7},{7,5},{8,10},{10,8},{9,1... | collective-permute-start | bytes 491528 | tf_op jit(solution)/shard_map/ppermute | solution.py:236
  48.8 6.3 %collective-permute-start.15 = (bf16[64,1280]{1,0:T(8,128)(2,1)S(1)}, bf16[64,1280]{1,0:T(8,128)(2,1)S(1)}, u32[]{:S(2)}, u32[]{:S(2)}) collective-permute-start(bf16[64,1280]{1,0:T(8,128)(2,1)S(1)} %shard_map.108.refs_1_), channel_id=1, source_target_pairs={{0,2},{2,0},{1,3},{3,1},{4,6},{6,4},{5,7},{7,5},{8,10},{10,8},{9,1... | collective-permute-start | bytes 491528 | tf_op jit(solution)/shard_map/ppermute | solution.py:236
  54.3 13.7 %collective-permute-start.10 = (bf16[64,1280]{1,0:T(8,128)(2,1)S(1)}, bf16[64,1280]{1,0:T(8,128)(2,1)S(1)}, u32[]{:S(2)}, u32[]{:S(2)}) collective-permute-start(bf16[64,1280]{1,0:T(8,128)(2,1)S(1)} %shard_map.105), channel_id=1, source_target_pairs={{0,8},{4,12},{8,0},{12,4},{1,9},{5,13},{9,1},{13,5},{2,10},{6,14},... | collective-permute-start | bytes 491528 | tf_op jit(solution)/shard_map/ppermute | solution.py:236
  55.2 15.0 %copy-start.6 = (bf16[5120]{0:T(1024)(128)(2,1)S(1)}, bf16[5120]{0:T(1024)(128)(2,1)}, u32[]{:S(2)}) copy-start(bf16[5120]{0:T(1024)(128)(2,1)} %param.16) | copy-start | bytes 30724
  55.2 15.1 %copy-start.1 = (bf16[5120,32]{0,1:T(8,128)(2,1)S(1)}, bf16[5120,32]{0,1:T(8,128)(2,1)}, u32[]{:S(2)}) copy-start(bf16[5120,32]{0,1:T(8,128)(2,1)} %param.17) | copy-start | bytes 983044
  55.2 15.1 %copy-start.4 = (s32[64]{0:T(128)S(1)}, s32[64]{0:T(128)}, u32[]{:S(2)}) copy-start(s32[64]{0:T(128)} %param.19) | copy-start | bytes 772
  55.2 15.1 %copy-start.5 = (s32[1,64,1]{1,2,0:T(1,128)S(1)}, s32[1,64,1]{1,2,0:T(1,128)}, u32[]{:S(2)}) copy-start(s32[1,64,1]{1,2,0:T(1,128)} %param.18) | copy-start | bytes 772
  59.2 9.4 %collective-permute-start.16 = (bf16[64,1280]{1,0:T(8,128)(2,1)S(1)}, bf16[64,1280]{1,0:T(8,128)(2,1)S(1)}, u32[]{:S(2)}, u32[]{:S(2)}) collective-permute-start(bf16[64,1280]{1,0:T(8,128)(2,1)S(1)} %shard_map.110), channel_id=1, source_target_pairs={{0,4},{4,8},{8,12},{12,0},{1,5},{5,9},{9,13},{13,1},{2,6},{6,10},{... | collective-permute-start | bytes 491528 | tf_op jit(solution)/shard_map/ppermute | solution.py:236
  68.0 7.2 %collective-permute-start.11 = (bf16[64,1280]{1,0:T(8,128)(2,1)S(1)}, bf16[64,1280]{1,0:T(8,128)(2,1)S(1)}, u32[]{:S(2)}, u32[]{:S(2)}) collective-permute-start(bf16[64,1280]{1,0:T(8,128)(2,1)S(1)} %shard_map.106.refs_0_), channel_id=1, source_target_pairs={{0,2},{2,0},{1,3},{3,1},{4,6},{6,4},{5,7},{7,5},{8,10},{10,8},{9,1... | collective-permute-start | bytes 491528 | tf_op jit(solution)/shard_map/ppermute | solution.py:236
  68.6 9.0 %collective-permute-start.17 = (bf16[64,1280]{1,0:T(8,128)(2,1)S(1)}, bf16[64,1280]{1,0:T(8,128)(2,1)S(1)}, u32[]{:S(2)}, u32[]{:S(2)}) collective-permute-start(bf16[64,1280]{1,0:T(8,128)(2,1)S(1)} %shard_map.111.refs_1_), channel_id=1, source_target_pairs={{0,2},{2,0},{1,3},{3,1},{4,6},{6,4},{5,7},{7,5},{8,10},{10,8},{9,1... | collective-permute-start | bytes 491528 | tf_op jit(solution)/shard_map/ppermute | solution.py:236
where the time goes:
time: 80.3 us; the launch traced here: 80.1 us
  waiting for transfers between devices  26.3 us (33%)
  starting transfers between devices  25.8 us (32%)
  Pallas kernels  25.7 us (32%)
  local copies, waits for them, and re-layouts  1.92 us (2%)
    ppermute x16, waiting for transfers between devices, over(): lax.ppermute(array, axis, [(i, (i + step) % count) for i in range(count)])  25 us
    ppermute x16, starting transfers between devices, over(): lax.ppermute(array, axis, [(i, (i + step) % count) for i in range(count)])  16.8 us
    pallas_call x4, Pallas kernels, on_device(): total = project(*block, *weights)  15.8 us
    ppermute x2, starting transfers between devices, on_device(): lax.ppermute(pack, 'ctx', [(i, i + step) for i in range(ctx_count - step)])  9 us
    pallas_call x2, Pallas kernels, on_device(): pl.pallas_call(functools.partial(finish_kernel, late_steps, spots, back,...  4.91 us
    pallas_call x1, Pallas kernels, on_device(): pl.pallas_call(functools.partial(attention_kernel, heads // groups, group...  2.73 us
    unnamed x14, local copies, waits for them, and re-layouts  1.91 us
    pallas_call x1, Pallas kernels, on_device(): pl.pallas_call(functools.partial(pack_kernel, groups), out_shape=jax.Shap...  1.77 us
  transfers between devices with their start and end apart: 18, of which 10 were waited for; matrix products, arithmetic and copies ran while one was open for 0% of the time, Pallas kernels for 27%

commit v1 on v0

--- a/solution.py
+++ b/solution.py
@@ -11,10 +11,9 @@
 CAP = 2
 EPSILON = 1e-05
 DOC_ROWS = 16
-VMEM_LIMIT = 16 * 1024 * 1024
+VMEM_LIMIT = 12 * 1024 * 1024
 VMEM_MOST = 61 * 1024 * 1024
 VMEM_MUCH = 52 * 1024 * 1024
-PIECE = 256
 
 
 def fetch(refs, buffers, sems):
@@ -92,33 +91,11 @@
 
 def project_kernel(pair, *refs):
     block_refs, weight_refs, out_ref = refs[:pair], refs[pair : 2 * pair], refs[2 * pair]
-    buffers, sems = refs[2 * pair + 1 : 3 * pair + 1], refs[3 * pair + 1]
-    columns = out_ref.shape[1]
-    piece = PIECE if columns % PIECE == 0 else columns
-    parts = [pl.ds(first, piece) for first in range(0, columns, piece)]
-    copies = [
-        [
-            pltpu.make_async_copy(
-                weight_refs[turn].at[:, part], buffers[turn].at[:, part], sems.at[turn, number]
-            )
-            for turn in range(pair)
-        ]
-        for number, part in enumerate(parts)
-    ]
-    for group in copies:
-        for copy in group:
-            copy.start()
-    for group, part in zip(copies, parts):
-        total = None
-        for turn in range(pair):
-            group[turn].wait()
-            product = jnp.dot(
-                block_refs[turn][...],
-                buffers[turn][:, part],
-                preferred_element_type=jnp.float32,
-            )
-            total = product if total is None else total + product
-        out_ref[:, part] = total.astype(out_ref.dtype)
+    total = None
+    for block_ref, weight_ref in zip(block_refs, weight_refs):
+        product = jnp.dot(block_ref[...], weight_ref[...], preferred_element_type=jnp.float32)
+        total = product if total is None else total + product
+    out_ref[...] = total.astype(out_ref.dtype)
 
 
 def columns_of(chunk_ref, step, spots, ctx_index):
@@ -283,11 +260,9 @@
     project = pl.pallas_call(
         functools.partial(project_kernel, pair),
         out_shape=jax.ShapeDtypeStruct((part_rows, columns), bf16),
-        in_specs=[vmem] * pair + [anywhere] * pair,
+        in_specs=[vmem] * (2 * pair),
         out_specs=vmem,
-        scratch_shapes=[pltpu.VMEM(out_proj.shape, bf16)] * pair
-        + [pltpu.SemaphoreType.DMA((pair, max(1, columns // PIECE)))],
-        compiler_params=much,
+        compiler_params=params,
         cost_estimate=pl.CostEstimate(
             flops=2 * pair * part_rows * out_proj.size,
             bytes_accessed=2 * pair * out_proj.size,
@@ -295,6 +270,15 @@
         ),
     )
     block = [over(pieces[turn], "tp", turn) for turn in range(pair)]
+    block[-1], swapped = lax.optimization_barrier((block[-1], weights[1:]))
+    weights = weights[:1] + [*pl.pallas_call(
+        functools.partial(stage_kernel, pair - 1),
+        out_shape=[jax.ShapeDtypeStruct(out_proj.shape, bf16)] * (pair - 1),
+        in_specs=[anywhere] * (pair - 1),
+        out_specs=[vmem] * (pair - 1),
+        scratch_shapes=[pltpu.SemaphoreType.DMA((pair - 1,))],
+        compiler_params=params,
+    )(*swapped)]
 
     aligned = columns % 128 == 0
     hidden = None
@@ -327,7 +311,7 @@
         if step == 1:
             block, all_ids = lax.optimization_barrier((block, all_ids))
         if step == 2:
-            block, chunks[1] = lax.optimization_barrier((block, chunks[1]))
+            block, chunks[1], flat[:1] = lax.optimization_barrier((block, chunks[1], flat[:1]))
         if last and aligned:
             hidden = collect(list(range(late_from)), ctx_count)
             block, hidden = lax.optimization_barrier((block, hidden))
@@ -337,7 +321,10 @@
             block = [lax.optimization_barrier((array, total))[0] for array in following]
         chunks.append(chunk)
         if aligned:
-            flat.append(forward(chunk, step, ctx_count))
+            if step == 2:
+                first, _ = lax.optimization_barrier((chunks[1], total))
+                flat[1] = forward(first, 1, ctx_count)
+            flat.append(forward(chunk, step, ctx_count) if step != 1 else None)
     if aligned:
         late_steps, spots = list(range(late_from, ctx_count)), ctx_count
     else:

time: 80.3 us -> 74.4 us (0.927)
  Pallas kernels: 25.7 us -> 17.9 us
  starting transfers between devices: 25.8 us -> 28 us
  waiting for transfers between devices: 26.3 us -> 24.5 us
  local copies, waits for them, and re-layouts: 1.92 us -> 3.45 us
    pallas_call x4, Pallas kernels: 15.8 us -> 6.96 us  [on_device(): total = project(*block, *weights)]
    ppermute x16, starting transfers between devices: 16.8 us -> 19 us  [over(): lax.ppermute(array, axis, [(i, (i + step) % count) for i in range(count)])]
    ppermute x16, waiting for transfers between devices: 25 us -> 23.1 us  [over(): lax.ppermute(array, axis, [(i, (i + step) % count) for i in range(count)])]
    unnamed x14 -> x16, local copies, waits for them, and re-layouts: 1.91 us -> 3.43 us
  transfers between devices with their start and end apart: 18 -> 18, of which waited for: 10 -> 11; matrix products, arithmetic and copies ran while one was open for 0% -> 0% of each run, Pallas kernels for 27% -> 18%
where the time goes in v1:
time: 74.4 us; the launch traced here: 74.1 us
  starting transfers between devices  28 us (38%)
  waiting for transfers between devices  24.5 us (33%)
  Pallas kernels  17.9 us (24%)
  local copies, waits for them, and re-layouts  3.45 us (5%)
    ppermute x16, waiting for transfers between devices, over(): lax.ppermute(array, axis, [(i, (i + step) % count) for i in range(count)])  23.1 us
    ppermute x16, starting transfers between devices, over(): lax.ppermute(array, axis, [(i, (i + step) % count) for i in range(count)])  19 us
    ppermute x2, starting transfers between devices, on_device(): lax.ppermute(pack, 'ctx', [(i, i + step) for i in range(ctx_count - step)])  9 us
    pallas_call x4, Pallas kernels, on_device(): total = project(*block, *weights)  6.96 us
    pallas_call x2, Pallas kernels, on_device(): pl.pallas_call(functools.partial(finish_kernel, late_steps, spots, back,...  4.91 us
    unnamed x16, local copies, waits for them, and re-layouts  3.43 us
    pallas_call x1, Pallas kernels, on_device(): pl.pallas_call(functools.partial(attention_kernel, heads // groups, group...  3.39 us
    pallas_call x1, Pallas kernels, on_device(): pl.pallas_call(functools.partial(pack_kernel, groups), out_shape=jax.Shap...  1.77 us
  transfers between devices with their start and end apart: 18, of which 11 were waited for; matrix products, arithmetic and copies ran while one was open for 0% of the time, Pallas kernels for 18%

profile of v1, /device:TPU:0, one launch (start us, length us, event | category | flops | bytes accessed | tf_op | source)
XLA Modules:
  0.0 74.1 jit_solution(13784544938002191542)
XLA Ops:
  0.0 1.8 %shard_map.100.refs_1_ = bf16[528,128]{1,0:T(8,128)(2,1)} custom-call(bf16[256,128]{1,0:T(8,128)(2,1)} %bitcast.23, bf16[256,128]{1,0:T(8,128)(2,1)} %bitcast.24, s32[1,128]{1,0:T(1,128)} %doc_ref.1), custom_call_target="tpu_custom_call" | custom-call | tf_op jit(solution)/shard_map/pallas_call | solution.py:218
  2.3 4.5 %collective-permute-start = (bf16[528,128]{1,0:T(8,128)(2,1)}, bf16[528,128]{1,0:T(8,128)(2,1)S(1)}, u32[]{:S(2)}, u32[]{:S(2)}) collective-permute-start(bf16[528,128]{1,0:T(8,128)(2,1)} %shard_map.100.refs_1_), channel_id=1, source_target_pairs={{0,4},{4,8},{8,12},{1,5},{5,9},{9,13},{2,6},{6,10},{10,14},{3,7},{... | collective-permute-start | bytes 405512 | tf_op jit(solution)/shard_map/ppermute | solution.py:232
  6.8 4.5 %collective-permute-start.1 = (bf16[528,128]{1,0:T(8,128)(2,1)}, bf16[528,128]{1,0:T(8,128)(2,1)S(1)}, u32[]{:S(2)}, u32[]{:S(2)}) collective-permute-start(bf16[528,128]{1,0:T(8,128)(2,1)} %shard_map.100.refs_1_), channel_id=1, source_target_pairs={{0,8},{4,12},{1,9},{5,13},{2,10},{6,14},{3,11},{7,15},{16,24},{20,... | collective-permute-start | bytes 405512 | tf_op jit(solution)/shard_map/ppermute | solution.py:232
  11.3 0.9 %copy-done.3 = bf16[528,128]{1,0:T(8,128)(2,1)S(1)} copy-done((bf16[528,128]{1,0:T(8,128)(2,1)S(1)}, bf16[528,128]{1,0:T(8,128)(2,1)}, u32[]{:S(2)}) %copy-start.3) | copy-done | bytes 135192
  12.2 1.0 %copy-done.4 = bf16[1,128,10,128]{3,1,2,0:T(8,128)(2,1)S(1)} copy-done((bf16[1,128,10,128]{3,1,2,0:T(8,128)(2,1)S(1)}, bf16[1,128,10,128]{3,1,2,0:T(8,128)(2,1)}, u32[]{:S(2)}) %copy-start.4) | copy-done | bytes 327704
  13.5 1.4 %collective-permute-done.1.refs_2_ = bf16[528,128]{1,0:T(8,128)(2,1)S(1)} collective-permute-done((bf16[528,128]{1,0:T(8,128)(2,1)}, bf16[528,128]{1,0:T(8,128)(2,1)S(1)}, u32[]{:S(2)}, u32[]{:S(2)}) %collective-permute-start.1) | collective-permute-done | bytes 135200 | tf_op jit(solution)/shard_map/ppermute | solution.py:232
  14.9 3.4 %shard_map.102 = (bf16[64,1280]{1,0:T(8,128)(2,1)}, bf16[64,1280]{1,0:T(8,128)(2,1)S(1)}) custom-call(s32[1]{0:T(128)} %bitcast.3.place_ref, bf16[10,128,128]{2,1,0:T(8,128)(2,1)S(1)} %get-tuple-element.38.query_ref, bf16[528,128]{1,0:T(8,128)(2,1)S(1)} %get-tuple-element.39.refs_0_, bf16[528,128]{1,0:T(8,128)(2,1)S(1)} %collective-permute-done.refs_1_, ...), custom_call_target="tpu_custom_call" | custom-call | tf_op jit(solution)/shard_map/pallas_call | solution.py:252
  18.3 3.1 %collective-permute-start.2 = (bf16[64,1280]{1,0:T(8,128)(2,1)}, bf16[64,1280]{1,0:T(8,128)(2,1)S(1)}, u32[]{:S(2)}, u32[]{:S(2)}) collective-permute-start(bf16[64,1280]{1,0:T(8,128)(2,1)} %get-tuple-element.40.refs_0_), channel_id=1, source_target_pairs={{0,4},{4,8},{8,12},{12,0},{1,5},{5,9},{9,13},{13,1},{2,6},{6,10},{... | collective-permute-start | bytes 491528 | tf_op jit(solution)/shard_map/ppermute | solution.py:213
  21.4 1.5 %collective-permute-start.6 = (bf16[64,1280]{1,0:T(8,128)(2,1)}, bf16[64,1280]{1,0:T(8,128)(2,1)}, u32[]{:S(2)}, u32[]{:S(2)}) collective-permute-start(bf16[64,1280]{1,0:T(8,128)(2,1)} %collective-permute-done.3.refs_1_), channel_id=1, source_target_pairs={{0,4},{4,8},{8,12},{12,0},{1,5},{5,9},{9,13},{13,1},{2,6},{6,10},{... | collective-permute-start | bytes 491528 | tf_op jit(solution)/shard_map/ppermute | solution.py:213
  22.9 1.5 %collective-permute-start.7 = (s32[1,64]{1,0:T(1,128)}, s32[1,64]{1,0:T(1,128)S(1)}, u32[]{:S(2)}, u32[]{:S(2)}) collective-permute-start(s32[1,64]{1,0:T(1,128)} %bitcast.21), channel_id=1, source_target_pairs={{0,2},{2,0},{1,3},{3,1},{4,6},{6,4},{5,7},{7,5},{8,10},{10,8},{9,1... | collective-permute-start | bytes 776 | tf_op jit(solution)/shard_map/ppermute | solution.py:213
  24.8 1.5 %copy-done = bf16[1280,1280]{1,0:T(8,128)(2,1)S(1)} copy-done((bf16[1280,1280]{1,0:T(8,128)(2,1)S(1)}, bf16[1280,1280]{1,0:T(8,128)(2,1)}, u32[]{:S(2)}) %copy-start) | copy-done | bytes 3276824
  26.3 2.3 %shard_map.104.chunk_ref = bf16[64,1280]{1,0:T(8,128)(2,1)S(1)} custom-call(bf16[64,1280]{1,0:T(8,128)(2,1)} %get-tuple-element.40.refs_0_, bf16[64,1280]{1,0:T(8,128)(2,1)} %collective-permute-done.3.refs_1_, bf16[1280,1280]{1,0:T(8,128)(2,1)S(1)} %copy-done, bf16[1280,1280]{1,0:T(8,128)(2,1)S(1)} %shard_map.103.refs_3_), custom_call_target="tpu_custom_call" | custom-call | flops 419430400 | bytes 6553600 | tf_op jit(solution)/shard_map/pallas_call | solution.py:318
  28.6 0.7 collective-permute-done.2.refs_0_
  29.3 1.7 %collective-permute-start.5 = (bf16[64,1280]{1,0:T(8,128)(2,1)S(1)}, bf16[64,1280]{1,0:T(8,128)(2,1)S(1)}, u32[]{:S(2)}, u32[]{:S(2)}) collective-permute-start(bf16[64,1280]{1,0:T(8,128)(2,1)S(1)} %collective-permute-done.2.refs_0_), channel_id=1, source_target_pairs={{0,4},{4,8},{8,12},{12,0},{1,5},{5,9},{9,13},{13,1},{2,6},{6,10},{... | collective-permute-start | bytes 491528 | tf_op jit(solution)/shard_map/ppermute | solution.py:213
  31.6 1.1 %collective-permute-done.6.refs_1_ = bf16[64,1280]{1,0:T(8,128)(2,1)} collective-permute-done((bf16[64,1280]{1,0:T(8,128)(2,1)}, bf16[64,1280]{1,0:T(8,128)(2,1)}, u32[]{:S(2)}, u32[]{:S(2)}) %collective-permute-start.6) | collective-permute-done | bytes 163872 | tf_op jit(solution)/shard_map/ppermute | solution.py:213
  33.2 2.2 %shard_map.105 = bf16[64,1280]{1,0:T(8,128)(2,1)S(1)} custom-call(bf16[64,1280]{1,0:T(8,128)(2,1)S(1)} %collective-permute-done.2.refs_0_, bf16[64,1280]{1,0:T(8,128)(2,1)} %collective-permute-done.6.refs_1_, bf16[1280,1280]{1,0:T(8,128)(2,1)S(1)} %copy-done, bf16[1280,1280]{1,0:T(8,128)(2,1)S(1)} %shard_map.103.refs_3_), custom_call_target="tpu_custom_call" | custom-call | flops 419430400 | bytes 6553600 | tf_op jit(solution)/shard_map/pallas_call | solution.py:318
  35.4 3.5 %collective-permute-start.9 = (bf16[64,1280]{1,0:T(8,128)(2,1)S(1)}, bf16[64,1280]{1,0:T(8,128)(2,1)S(1)}, u32[]{:S(2)}, u32[]{:S(2)}) collective-permute-start(bf16[64,1280]{1,0:T(8,128)(2,1)S(1)} %shard_map.105), channel_id=1, source_target_pairs={{0,12},{4,0},{8,4},{12,8},{1,13},{5,1},{9,5},{13,9},{2,14},{6,2},{... | collective-permute-start | bytes 491528 | tf_op jit(solution)/shard_map/ppermute | solution.py:213
  38.8 3.1 %collective-permute-done.8.refs_1_ = bf16[64,1280]{1,0:T(8,128)(2,1)S(1)} collective-permute-done((bf16[64,1280]{1,0:T(8,128)(2,1)}, bf16[64,1280]{1,0:T(8,128)(2,1)S(1)}, u32[]{:S(2)}, u32[]{:S(2)}) %collective-permute-start.8) | collective-permute-done | bytes 163872 | tf_op jit(solution)/shard_map/ppermute | solution.py:213
  41.9 1.2 %collective-permute-start.14 = (bf16[64,1280]{1,0:T(8,128)(2,1)S(1)}, bf16[64,1280]{1,0:T(8,128)(2,1)S(1)}, u32[]{:S(2)}, u32[]{:S(2)}) collective-permute-start(bf16[64,1280]{1,0:T(8,128)(2,1)S(1)} %collective-permute-done.8.refs_1_), channel_id=1, source_target_pairs={{0,4},{4,8},{8,12},{12,0},{1,5},{5,9},{9,13},{13,1},{2,6},{6,10},{... | collective-permute-start | bytes 491528 | tf_op jit(solution)/shard_map/ppermute | solution.py:213
  43.1 2.3 %collective-permute-done.9.chunk_ref = bf16[64,1280]{1,0:T(8,128)(2,1)S(1)} collective-permute-done((bf16[64,1280]{1,0:T(8,128)(2,1)S(1)}, bf16[64,1280]{1,0:T(8,128)(2,1)S(1)}, u32[]{:S(2)}, u32[]{:S(2)}) %collective-permute-start.9) | collective-permute-done | bytes 163872 | tf_op jit(solution)/shard_map/ppermute | solution.py:213
  45.3 1.2 %shard_map.107 = bf16[64,1280]{1,0:T(8,128)(2,1)S(1)} custom-call(bf16[64,1280]{1,0:T(8,128)(2,1)S(1)} %collective-permute-done.5.refs_0_, bf16[64,1280]{1,0:T(8,128)(2,1)S(1)} %collective-permute-done.8.refs_1_, bf16[1280,1280]{1,0:T(8,128)(2,1)S(1)} %copy-done, bf16[1280,1280]{1,0:T(8,128)(2,1)S(1)} %shard_map.103.refs_3_), custom_call_target="tpu_custom_call" | custom-call | flops 419430400 | bytes 6553600 | tf_op jit(solution)/shard_map/pallas_call | solution.py:318
  46.6 1.6 %collective-permute-start.15 = (bf16[64,1280]{1,0:T(8,128)(2,1)S(1)}, bf16[64,1280]{1,0:T(8,128)(2,1)S(1)}, u32[]{:S(2)}, u32[]{:S(2)}) collective-permute-start(bf16[64,1280]{1,0:T(8,128)(2,1)S(1)} %shard_map.109.refs_1_), channel_id=1, source_target_pairs={{0,2},{2,0},{1,3},{3,1},{4,6},{6,4},{5,7},{7,5},{8,10},{10,8},{9,1... | collective-permute-start | bytes 491528 | tf_op jit(solution)/shard_map/ppermute | solution.py:213
  48.9 2.5 %collective-permute-done.14.refs_1_ = bf16[64,1280]{1,0:T(8,128)(2,1)S(1)} collective-permute-done((bf16[64,1280]{1,0:T(8,128)(2,1)S(1)}, bf16[64,1280]{1,0:T(8,128)(2,1)S(1)}, u32[]{:S(2)}, u32[]{:S(2)}) %collective-permute-start.14) | collective-permute-done | bytes 163872 | tf_op jit(solution)/shard_map/ppermute | solution.py:213
  51.4 1.2 %collective-permute-done.15.refs_3_ = bf16[64,1280]{1,0:T(8,128)(2,1)S(1)} collective-permute-done((bf16[64,1280]{1,0:T(8,128)(2,1)S(1)}, bf16[64,1280]{1,0:T(8,128)(2,1)S(1)}, u32[]{:S(2)}, u32[]{:S(2)}) %collective-permute-start.15) | collective-permute-done | bytes 163872 | tf_op jit(solution)/shard_map/ppermute | solution.py:213
  52.7 1.2 %shard_map.111 = bf16[64,1280]{1,0:T(8,128)(2,1)S(1)} custom-call(bf16[64,1280]{1,0:T(8,128)(2,1)S(1)} %collective-permute-done.13.refs_0_, bf16[64,1280]{1,0:T(8,128)(2,1)S(1)} %collective-permute-done.14.refs_1_, bf16[1280,1280]{1,0:T(8,128)(2,1)S(1)} %copy-done, bf16[1280,1280]{1,0:T(8,128)(2,1)S(1)} %shard_map.103.refs_3_), custom_call_target="tpu_custom_call" | custom-call | flops 419430400 | bytes 6553600 | tf_op jit(solution)/shard_map/pallas_call | solution.py:318
  54.0 0.7 collective-permute-start.16
  54.7 7.2 %collective-permute-done.11.chunk_ref = bf16[64,1280]{1,0:T(8,128)(2,1)S(1)} collective-permute-done((bf16[64,1280]{1,0:T(8,128)(2,1)S(1)}, bf16[64,1280]{1,0:T(8,128)(2,1)S(1)}, u32[]{:S(2)}, u32[]{:S(2)}) %collective-permute-start.11) | collective-permute-done | bytes 163872 | tf_op jit(solution)/shard_map/ppermute | solution.py:213
  62.0 1.6 %collective-permute-start.12 = (bf16[64,1280]{1,0:T(8,128)(2,1)S(1)}, bf16[64,1280]{1,0:T(8,128)(2,1)S(1)}, u32[]{:S(2)}, u32[]{:S(2)}) collective-permute-start(bf16[64,1280]{1,0:T(8,128)(2,1)S(1)} %shard_map.108.refs_0_), channel_id=1, source_target_pairs={{0,2},{2,0},{1,3},{3,1},{4,6},{6,4},{5,7},{7,5},{8,10},{10,8},{9,1... | collective-permute-start | bytes 491528 | tf_op jit(solution)/shard_map/ppermute | solution.py:213
  64.3 2.5 %shard_map.113.refs_7_ = bf16[2,32,2,5120]{3,2,1,0:T(2,128)(2,1)} custom-call(s32[2]{0:T(128)S(1)} %pad_add_fusion.place_ref, bf16[64,1280]{1,0:T(8,128)(2,1)S(1)} %shard_map.108.refs_0_, bf16[64,1280]{1,0:T(8,128)(2,1)S(1)} %shard_map.112.refs_1_, bf16[64,5120]{1,0:T(8,128)(2,1)S(1)} %get-tuple-element.65.refs_2_, s32[1,64]{1,0:T(1,128)S(1)} %bitcast.22, ...), custom_call_target="tpu_custom_call" | custom-call | tf_op jit(solution)/shard_map/pallas_call | solution.py:346
  66.7 2.4 %collective-permute-done.12.refs_0_ = bf16[64,1280]{1,0:T(8,128)(2,1)S(1)} collective-permute-done((bf16[64,1280]{1,0:T(8,128)(2,1)S(1)}, bf16[64,1280]{1,0:T(8,128)(2,1)S(1)}, u32[]{:S(2)}, u32[]{:S(2)}) %collective-permute-start.12) | collective-permute-done | bytes 163872 | tf_op jit(solution)/shard_map/ppermute | solution.py:213
  69.1 2.6 %collective-permute-done.17.refs_1_ = bf16[64,1280]{1,0:T(8,128)(2,1)S(1)} collective-permute-done((bf16[64,1280]{1,0:T(8,128)(2,1)S(1)}, bf16[64,1280]{1,0:T(8,128)(2,1)S(1)}, u32[]{:S(2)}, u32[]{:S(2)}) %collective-permute-start.17) | collective-permute-done | bytes 163872 | tf_op jit(solution)/shard_map/ppermute | solution.py:213
  71.7 2.5 %shard_map.114 = bf16[2,32,2,5120]{3,2,1,0:T(2,128)(2,1)} custom-call(s32[2]{0:T(128)S(1)} %pad_add_fusion.place_ref, bf16[64,1280]{1,0:T(8,128)(2,1)S(1)} %collective-permute-done.12.refs_0_, bf16[64,1280]{1,0:T(8,128)(2,1)S(1)} %collective-permute-done.17.refs_1_, bf16[64,5120]{1,0:T(8,128)(2,1)S(1)} %get-tuple-element.63.refs_2_, ...), custom_call_target="tpu_custom_call", output_to_operand_aliasing={{}: (8, {})} | custom-call | tf_op jit(solution)/shard_map/pallas_call | solution.py:346
  (37 shorter events, 3.9 us)
Async XLA Ops:
  1.8 19.6 %collective-permute-start.4 = (bf16[1280,1280]{1,0:T(8,128)(2,1)}, bf16[1280,1280]{1,0:T(8,128)(2,1)S(1)}, u32[]{:S(2)}, u32[]{:S(2)}) collective-permute-start(bf16[1280,1280]{1,0:T(8,128)(2,1)} %refs_2_.7), channel_id=1, source_target_pairs={{0,1},{1,0},{2,3},{3,2},{4,5},{5,4},{6,7},{7,6},{8,9},{9,8},{10,11... | collective-permute-start | bytes 9830408 | tf_op jit(solution)/shard_map/ppermute | solution.py:213
  2.3 11.2 %collective-permute-start = (bf16[528,128]{1,0:T(8,128)(2,1)}, bf16[528,128]{1,0:T(8,128)(2,1)S(1)}, u32[]{:S(2)}, u32[]{:S(2)}) collective-permute-start(bf16[528,128]{1,0:T(8,128)(2,1)} %shard_map.100.refs_1_), channel_id=1, source_target_pairs={{0,4},{4,8},{8,12},{1,5},{5,9},{9,13},{2,6},{6,10},{10,14},{3,7},{... | collective-permute-start | bytes 405512 | tf_op jit(solution)/shard_map/ppermute | solution.py:232
  6.8 8.1 %collective-permute-start.1 = (bf16[528,128]{1,0:T(8,128)(2,1)}, bf16[528,128]{1,0:T(8,128)(2,1)S(1)}, u32[]{:S(2)}, u32[]{:S(2)}) collective-permute-start(bf16[528,128]{1,0:T(8,128)(2,1)} %shard_map.100.refs_1_), channel_id=1, source_target_pairs={{0,8},{4,12},{1,9},{5,13},{2,10},{6,14},{3,11},{7,15},{16,24},{20,... | collective-permute-start | bytes 405512 | tf_op jit(solution)/shard_map/ppermute | solution.py:232
  11.3 0.9 %copy-start.3 = (bf16[528,128]{1,0:T(8,128)(2,1)S(1)}, bf16[528,128]{1,0:T(8,128)(2,1)}, u32[]{:S(2)}) copy-start(bf16[528,128]{1,0:T(8,128)(2,1)} %shard_map.100.refs_1_) | copy-start | bytes 405508
  12.2 1.0 %copy-start.4 = (bf16[1,128,10,128]{3,1,2,0:T(8,128)(2,1)S(1)}, bf16[1,128,10,128]{3,1,2,0:T(8,128)(2,1)}, u32[]{:S(2)}) copy-start(bf16[1,128,10,128]{3,1,2,0:T(8,128)(2,1)} %param.10) | copy-start | bytes 983044
  18.2 3.1 %collective-permute-start.3 = (bf16[64,1280]{1,0:T(8,128)(2,1)S(1)}, bf16[64,1280]{1,0:T(8,128)(2,1)}, u32[]{:S(2)}, u32[]{:S(2)}) collective-permute-start(bf16[64,1280]{1,0:T(8,128)(2,1)S(1)} %get-tuple-element.41), channel_id=1, source_target_pairs={{0,1},{1,0},{2,3},{3,2},{4,5},{5,4},{6,7},{7,6},{8,9},{9,8},{10,11... | collective-permute-start | bytes 491528 | tf_op jit(solution)/shard_map/ppermute | solution.py:213
  18.3 11.1 %collective-permute-start.2 = (bf16[64,1280]{1,0:T(8,128)(2,1)}, bf16[64,1280]{1,0:T(8,128)(2,1)S(1)}, u32[]{:S(2)}, u32[]{:S(2)}) collective-permute-start(bf16[64,1280]{1,0:T(8,128)(2,1)} %get-tuple-element.40.refs_0_), channel_id=1, source_target_pairs={{0,4},{4,8},{8,12},{12,0},{1,5},{5,9},{9,13},{13,1},{2,6},{6,10},{... | collective-permute-start | bytes 491528 | tf_op jit(solution)/shard_map/ppermute | solution.py:213
  21.4 11.4 %collective-permute-start.6 = (bf16[64,1280]{1,0:T(8,128)(2,1)}, bf16[64,1280]{1,0:T(8,128)(2,1)}, u32[]{:S(2)}, u32[]{:S(2)}) collective-permute-start(bf16[64,1280]{1,0:T(8,128)(2,1)} %collective-permute-done.3.refs_1_), channel_id=1, source_target_pairs={{0,4},{4,8},{8,12},{12,0},{1,5},{5,9},{9,13},{13,1},{2,6},{6,10},{... | collective-permute-start | bytes 491528 | tf_op jit(solution)/shard_map/ppermute | solution.py:213
  22.9 10.3 %collective-permute-start.7 = (s32[1,64]{1,0:T(1,128)}, s32[1,64]{1,0:T(1,128)S(1)}, u32[]{:S(2)}, u32[]{:S(2)}) collective-permute-start(s32[1,64]{1,0:T(1,128)} %bitcast.21), channel_id=1, source_target_pairs={{0,2},{2,0},{1,3},{3,1},{4,6},{6,4},{5,7},{7,5},{8,10},{10,8},{9,1... | collective-permute-start | bytes 776 | tf_op jit(solution)/shard_map/ppermute | solution.py:213
  24.4 1.9 %copy-start = (bf16[1280,1280]{1,0:T(8,128)(2,1)S(1)}, bf16[1280,1280]{1,0:T(8,128)(2,1)}, u32[]{:S(2)}) copy-start(bf16[1280,1280]{1,0:T(8,128)(2,1)} %refs_2_.7) | copy-start | bytes 9830404
  26.3 4.7 %copy-start.1 = (bf16[1,64,5120]{2,1,0:T(8,128)(2,1)S(1)}, bf16[1,64,5120]{2,1,0:T(8,128)(2,1)}, u32[]{:S(2)}) copy-start(bf16[1,64,5120]{2,1,0:T(8,128)(2,1)} %param.14) | copy-start | bytes 1966084
  29.3 9.5 %collective-permute-start.5 = (bf16[64,1280]{1,0:T(8,128)(2,1)S(1)}, bf16[64,1280]{1,0:T(8,128)(2,1)S(1)}, u32[]{:S(2)}, u32[]{:S(2)}) collective-permute-start(bf16[64,1280]{1,0:T(8,128)(2,1)S(1)} %collective-permute-done.2.refs_0_), channel_id=1, source_target_pairs={{0,4},{4,8},{8,12},{12,0},{1,5},{5,9},{9,13},{13,1},{2,6},{6,10},{... | collective-permute-start | bytes 491528 | tf_op jit(solution)/shard_map/ppermute | solution.py:213
  31.0 12.0 %collective-permute-start.10 = (bf16[64,1280]{1,0:T(8,128)(2,1)S(1)}, bf16[64,1280]{1,0:T(8,128)(2,1)S(1)}, u32[]{:S(2)}, u32[]{:S(2)}) collective-permute-start(bf16[64,1280]{1,0:T(8,128)(2,1)S(1)} %shard_map.106.refs_0_), channel_id=1, source_target_pairs={{0,2},{2,0},{1,3},{3,1},{4,6},{6,4},{5,7},{7,5},{8,10},{10,8},{9,1... | collective-permute-start | bytes 491528 | tf_op jit(solution)/shard_map/ppermute | solution.py:213
  32.8 9.1 %collective-permute-start.8 = (bf16[64,1280]{1,0:T(8,128)(2,1)}, bf16[64,1280]{1,0:T(8,128)(2,1)S(1)}, u32[]{:S(2)}, u32[]{:S(2)}) collective-permute-start(bf16[64,1280]{1,0:T(8,128)(2,1)} %collective-permute-done.6.refs_1_), channel_id=1, source_target_pairs={{0,4},{4,8},{8,12},{12,0},{1,5},{5,9},{9,13},{13,1},{2,6},{6,10},{... | collective-permute-start | bytes 491528 | tf_op jit(solution)/shard_map/ppermute | solution.py:213
  35.4 10.0 %collective-permute-start.9 = (bf16[64,1280]{1,0:T(8,128)(2,1)S(1)}, bf16[64,1280]{1,0:T(8,128)(2,1)S(1)}, u32[]{:S(2)}, u32[]{:S(2)}) collective-permute-start(bf16[64,1280]{1,0:T(8,128)(2,1)S(1)} %shard_map.105), channel_id=1, source_target_pairs={{0,12},{4,0},{8,4},{12,8},{1,13},{5,1},{9,5},{13,9},{2,14},{6,2},{... | collective-permute-start | bytes 491528 | tf_op jit(solution)/shard_map/ppermute | solution.py:213
  38.8 10.1 %collective-permute-start.13 = (bf16[64,1280]{1,0:T(8,128)(2,1)S(1)}, bf16[64,1280]{1,0:T(8,128)(2,1)S(1)}, u32[]{:S(2)}, u32[]{:S(2)}) collective-permute-start(bf16[64,1280]{1,0:T(8,128)(2,1)S(1)} %collective-permute-done.5.refs_0_), channel_id=1, source_target_pairs={{0,4},{4,8},{8,12},{12,0},{1,5},{5,9},{9,13},{13,1},{2,6},{6,10},{... | collective-permute-start | bytes 491528 | tf_op jit(solution)/shard_map/ppermute | solution.py:213
  41.9 9.5 %collective-permute-start.14 = (bf16[64,1280]{1,0:T(8,128)(2,1)S(1)}, bf16[64,1280]{1,0:T(8,128)(2,1)S(1)}, u32[]{:S(2)}, u32[]{:S(2)}) collective-permute-start(bf16[64,1280]{1,0:T(8,128)(2,1)S(1)} %collective-permute-done.8.refs_1_), channel_id=1, source_target_pairs={{0,4},{4,8},{8,12},{12,0},{1,5},{5,9},{9,13},{13,1},{2,6},{6,10},{... | collective-permute-start | bytes 491528 | tf_op jit(solution)/shard_map/ppermute | solution.py:213
  46.6 6.0 %collective-permute-start.15 = (bf16[64,1280]{1,0:T(8,128)(2,1)S(1)}, bf16[64,1280]{1,0:T(8,128)(2,1)S(1)}, u32[]{:S(2)}, u32[]{:S(2)}) collective-permute-start(bf16[64,1280]{1,0:T(8,128)(2,1)S(1)} %shard_map.109.refs_1_), channel_id=1, source_target_pairs={{0,2},{2,0},{1,3},{3,1},{4,6},{6,4},{5,7},{7,5},{8,10},{10,8},{9,1... | collective-permute-start | bytes 491528 | tf_op jit(solution)/shard_map/ppermute | solution.py:213
  48.2 13.7 %collective-permute-start.11 = (bf16[64,1280]{1,0:T(8,128)(2,1)S(1)}, bf16[64,1280]{1,0:T(8,128)(2,1)S(1)}, u32[]{:S(2)}, u32[]{:S(2)}) collective-permute-start(bf16[64,1280]{1,0:T(8,128)(2,1)S(1)} %shard_map.107), channel_id=1, source_target_pairs={{0,8},{4,12},{8,0},{12,4},{1,9},{5,13},{9,1},{13,5},{2,10},{6,14},... | collective-permute-start | bytes 491528 | tf_op jit(solution)/shard_map/ppermute | solution.py:213
  52.7 11.5 %copy-start.7 = (bf16[5120]{0:T(1024)(128)(2,1)S(1)}, bf16[5120]{0:T(1024)(128)(2,1)}, u32[]{:S(2)}) copy-start(bf16[5120]{0:T(1024)(128)(2,1)} %param.16) | copy-start | bytes 30724
  52.7 11.6 %copy-start.2 = (bf16[5120,32]{0,1:T(8,128)(2,1)S(1)}, bf16[5120,32]{0,1:T(8,128)(2,1)}, u32[]{:S(2)}) copy-start(bf16[5120,32]{0,1:T(8,128)(2,1)} %param.17) | copy-start | bytes 983044
  52.7 11.6 %copy-start.5 = (s32[64]{0:T(128)S(1)}, s32[64]{0:T(128)}, u32[]{:S(2)}) copy-start(s32[64]{0:T(128)} %param.19) | copy-start | bytes 772
  52.7 11.6 %copy-start.6 = (s32[1,64,1]{1,2,0:T(1,128)S(1)}, s32[1,64,1]{1,2,0:T(1,128)}, u32[]{:S(2)}) copy-start(s32[1,64,1]{1,2,0:T(1,128)} %param.18) | copy-start | bytes 772
  54.0 9.6 %collective-permute-start.16 = (bf16[64,1280]{1,0:T(8,128)(2,1)S(1)}, bf16[64,1280]{1,0:T(8,128)(2,1)S(1)}, u32[]{:S(2)}, u32[]{:S(2)}) collective-permute-start(bf16[64,1280]{1,0:T(8,128)(2,1)S(1)} %shard_map.111), channel_id=1, source_target_pairs={{0,4},{4,8},{8,12},{12,0},{1,5},{5,9},{9,13},{13,1},{2,6},{6,10},{... | collective-permute-start | bytes 491528 | tf_op jit(solution)/shard_map/ppermute | solution.py:213
  62.0 7.1 %collective-permute-start.12 = (bf16[64,1280]{1,0:T(8,128)(2,1)S(1)}, bf16[64,1280]{1,0:T(8,128)(2,1)S(1)}, u32[]{:S(2)}, u32[]{:S(2)}) collective-permute-start(bf16[64,1280]{1,0:T(8,128)(2,1)S(1)} %shard_map.108.refs_0_), channel_id=1, source_target_pairs={{0,2},{2,0},{1,3},{3,1},{4,6},{6,4},{5,7},{7,5},{8,10},{10,8},{9,1... | collective-permute-start | bytes 491528 | tf_op jit(solution)/shard_map/ppermute | solution.py:213
  63.6 8.1 %collective-permute-start.17 = (bf16[64,1280]{1,0:T(8,128)(2,1)S(1)}, bf16[64,1280]{1,0:T(8,128)(2,1)S(1)}, u32[]{:S(2)}, u32[]{:S(2)}) collective-permute-start(bf16[64,1280]{1,0:T(8,128)(2,1)S(1)} %shard_map.112.refs_1_), channel_id=1, source_target_pairs={{0,2},{2,0},{1,3},{3,1},{4,6},{6,4},{5,7},{7,5},{8,10},{10,8},{9,1... | collective-permute-start | bytes 491528 | tf_op jit(solution)/shard_map/ppermute | solution.py:213

commit v2 on v1

--- a/solution.py
+++ b/solution.py
@@ -12,6 +12,7 @@
 EPSILON = 1e-05
 DOC_ROWS = 16
 VMEM_LIMIT = 12 * 1024 * 1024
+VMEM_MORE = 16 * 1024 * 1024
 VMEM_MOST = 61 * 1024 * 1024
 VMEM_MUCH = 52 * 1024 * 1024
 
@@ -202,6 +203,7 @@
     smem = pl.BlockSpec(memory_space=pltpu.SMEM)
     anywhere = pl.BlockSpec(memory_space=pl.ANY)
     params = pltpu.CompilerParams(vmem_limit_bytes=VMEM_LIMIT)
+    more = pltpu.CompilerParams(vmem_limit_bytes=VMEM_MORE)
     most = pltpu.CompilerParams(vmem_limit_bytes=VMEM_MOST)
     much = pltpu.CompilerParams(vmem_limit_bytes=VMEM_MUCH)
     bf16, f32 = jnp.bfloat16, jnp.float32
@@ -254,7 +256,7 @@
         out_shape=[jax.ShapeDtypeStruct((part_rows, heads * head_size), bf16)] * pair,
         in_specs=[smem] + [vmem] * (1 + len(packs)),
         out_specs=[vmem] * pair,
-        compiler_params=params,
+        compiler_params=more,
     )(core.reshape(1), staged_queries, *packs)
 
     project = pl.pallas_call(
@@ -311,18 +313,19 @@
         if step == 1:
             block, all_ids = lax.optimization_barrier((block, all_ids))
         if step == 2:
-            block, chunks[1], flat[:1] = lax.optimization_barrier((block, chunks[1], flat[:1]))
+            block, flat[:1] = lax.optimization_barrier((block, flat[:1]))
         if last and aligned:
             hidden = collect(list(range(late_from)), ctx_count)
-            block, hidden = lax.optimization_barrier((block, hidden))
         total = project(*block, *weights)
         chunk = over(total, "ctx", ctx_count - step)
         if not last:
             block = [lax.optimization_barrier((array, total))[0] for array in following]
+        if last and aligned:
+            chunk, hidden = lax.optimization_barrier((chunk, hidden))
         chunks.append(chunk)
         if aligned:
             if step == 2:
-                first, _ = lax.optimization_barrier((chunks[1], total))
+                first, _ = lax.optimization_barrier((chunks[1], [total] + following[:1]))
                 flat[1] = forward(first, 1, ctx_count)
             flat.append(forward(chunk, step, ctx_count) if step != 1 else None)
     if aligned:

time: 74.4 us -> 74.9 us (level)
  waiting for transfers between devices: 24.5 us -> 13.4 us
  local copies, waits for them, and re-layouts: 3.45 us -> 9.51 us
  starting transfers between devices: 28 us -> 34 us
    ppermute x16, waiting for transfers between devices: 23.1 us -> 12 us  [over(): lax.ppermute(array, axis, [(i, (i + step) % count) for i in range(count)])]
    unnamed x16 -> x26, local copies, waits for them, and re-layouts: 3.43 us -> 9.5 us
    ppermute x16, starting transfers between devices: 19 us -> 25 us  [over(): lax.ppermute(array, axis, [(i, (i + step) % count) for i in range(count)])]
  transfers between devices with their start and end apart: 18 -> 18, of which waited for: 11 -> 9; matrix products, arithmetic and copies ran while one was open for 0% -> 0% of each run, Pallas kernels for 18% -> 17%
where the time goes in v2:
time: 74.9 us; the launch traced here: 74.5 us
  starting transfers between devices  34 us (45%)
  Pallas kernels  17.2 us (23%)
  waiting for transfers between devices  13.4 us (18%)
  local copies, waits for them, and re-layouts  9.51 us (13%)
    ppermute x16, starting transfers between devices, over(): lax.ppermute(array, axis, [(i, (i + step) % count) for i in range(count)])  25 us
    ppermute x16, waiting for transfers between devices, over(): lax.ppermute(array, axis, [(i, (i + step) % count) for i in range(count)])  12 us
    unnamed x26, local copies, waits for them, and re-layouts  9.5 us
    ppermute x2, starting transfers between devices, on_device(): lax.ppermute(pack, 'ctx', [(i, i + step) for i in range(ctx_count - step)])  9 us
    pallas_call x4, Pallas kernels, on_device(): total = project(*block, *weights)  6.94 us
    pallas_call x2, Pallas kernels, on_device(): pl.pallas_call(functools.partial(finish_kernel, late_steps, spots, back,...  4.9 us
    pallas_call x1, Pallas kernels, on_device(): pl.pallas_call(functools.partial(attention_kernel, heads // groups, group...  2.72 us
    pallas_call x1, Pallas kernels, on_device(): pl.pallas_call(functools.partial(pack_kernel, groups), out_shape=jax.Shap...  1.77 us
  transfers between devices with their start and end apart: 18, of which 9 were waited for; matrix products, arithmetic and copies ran while one was open for 0% of the time, Pallas kernels for 17%

profile of v2, /device:TPU:0, one launch (start us, length us, event | category | flops | bytes accessed | tf_op | source)
XLA Modules:
  0.0 74.5 jit_solution(12913773598338403907)
XLA Ops:
  0.0 1.8 %shard_map.100.refs_1_ = bf16[528,128]{1,0:T(8,128)(2,1)} custom-call(bf16[256,128]{1,0:T(8,128)(2,1)} %bitcast.23, bf16[256,128]{1,0:T(8,128)(2,1)} %bitcast.24, s32[1,128]{1,0:T(1,128)} %doc_ref.1), custom_call_target="tpu_custom_call" | custom-call | tf_op jit(solution)/shard_map/pallas_call | solution.py:220
  2.3 4.5 %collective-permute-start = (bf16[528,128]{1,0:T(8,128)(2,1)}, bf16[528,128]{1,0:T(8,128)(2,1)S(1)}, u32[]{:S(2)}, u32[]{:S(2)}) collective-permute-start(bf16[528,128]{1,0:T(8,128)(2,1)} %shard_map.100.refs_1_), channel_id=1, source_target_pairs={{0,4},{4,8},{8,12},{1,5},{5,9},{9,13},{2,6},{6,10},{10,14},{3,7},{... | collective-permute-start | bytes 405512 | tf_op jit(solution)/shard_map/ppermute | solution.py:234
  6.8 4.5 %collective-permute-start.1 = (bf16[528,128]{1,0:T(8,128)(2,1)}, bf16[528,128]{1,0:T(8,128)(2,1)S(1)}, u32[]{:S(2)}, u32[]{:S(2)}) collective-permute-start(bf16[528,128]{1,0:T(8,128)(2,1)} %shard_map.100.refs_1_), channel_id=1, source_target_pairs={{0,8},{4,12},{1,9},{5,13},{2,10},{6,14},{3,11},{7,15},{16,24},{20,... | collective-permute-start | bytes 405512 | tf_op jit(solution)/shard_map/ppermute | solution.py:234
  11.3 0.9 %copy-done.8 = bf16[528,128]{1,0:T(8,128)(2,1)S(1)} copy-done((bf16[528,128]{1,0:T(8,128)(2,1)S(1)}, bf16[528,128]{1,0:T(8,128)(2,1)}, u32[]{:S(2)}) %copy-start.8) | copy-done | bytes 135192
  12.2 1.0 %copy-done.9 = bf16[1,128,10,128]{3,1,2,0:T(8,128)(2,1)S(1)} copy-done((bf16[1,128,10,128]{3,1,2,0:T(8,128)(2,1)S(1)}, bf16[1,128,10,128]{3,1,2,0:T(8,128)(2,1)}, u32[]{:S(2)}) %copy-start.9) | copy-done | bytes 327704
  13.5 1.4 %collective-permute-done.1.refs_2_ = bf16[528,128]{1,0:T(8,128)(2,1)S(1)} collective-permute-done((bf16[528,128]{1,0:T(8,128)(2,1)}, bf16[528,128]{1,0:T(8,128)(2,1)S(1)}, u32[]{:S(2)}, u32[]{:S(2)}) %collective-permute-start.1) | collective-permute-done | bytes 135200 | tf_op jit(solution)/shard_map/ppermute | solution.py:234
  14.9 2.7 %shard_map.102 = (bf16[64,1280]{1,0:T(8,128)(2,1)S(1)}, bf16[64,1280]{1,0:T(8,128)(2,1)S(1)}) custom-call(s32[1]{0:T(128)} %bitcast.3.place_ref, bf16[10,128,128]{2,1,0:T(8,128)(2,1)S(1)} %get-tuple-element.36.query_ref, bf16[528,128]{1,0:T(8,128)(2,1)S(1)} %get-tuple-element.37.refs_0_, bf16[528,128]{1,0:T(8,128)(2,1)S(1)} %collective-permute-done.refs_1_, ...), custom_call_target="tpu_custom_call" | custom-call | tf_op jit(solution)/shard_map/pallas_call | solution.py:254
  17.7 3.1 %collective-permute-start.2 = (bf16[64,1280]{1,0:T(8,128)(2,1)S(1)}, bf16[64,1280]{1,0:T(8,128)(2,1)}, u32[]{:S(2)}, u32[]{:S(2)}) collective-permute-start(bf16[64,1280]{1,0:T(8,128)(2,1)S(1)} %get-tuple-element.38.refs_0_), channel_id=1, source_target_pairs={{0,4},{4,8},{8,12},{12,0},{1,5},{5,9},{9,13},{13,1},{2,6},{6,10},{... | collective-permute-start | bytes 491528 | tf_op jit(solution)/shard_map/ppermute | solution.py:215
  20.8 1.7 %copy-done.5 = bf16[1280,1280]{1,0:T(8,128)(2,1)} copy-done((bf16[1280,1280]{1,0:T(8,128)(2,1)}, bf16[1280,1280]{1,0:T(8,128)(2,1)S(1)}, u32[]{:S(2)}) %copy-start.5) | copy-done | bytes 3276824
  22.5 1.3 %collective-permute-start.6 = (bf16[64,1280]{1,0:T(8,128)(2,1)S(1)}, bf16[64,1280]{1,0:T(8,128)(2,1)}, u32[]{:S(2)}, u32[]{:S(2)}) collective-permute-start(bf16[64,1280]{1,0:T(8,128)(2,1)S(1)} %collective-permute-done.3.refs_1_), channel_id=1, source_target_pairs={{0,4},{4,8},{8,12},{12,0},{1,5},{5,9},{9,13},{13,1},{2,6},{6,10},{... | collective-permute-start | bytes 491528 | tf_op jit(solution)/shard_map/ppermute | solution.py:215
  23.8 1.9 %copy-done.6 = bf16[1280,1280]{1,0:T(8,128)(2,1)S(1)} copy-done((bf16[1280,1280]{1,0:T(8,128)(2,1)S(1)}, bf16[1280,1280]{1,0:T(8,128)(2,1)}, u32[]{:S(2)}) %copy-start.6) | copy-done | bytes 3276824
  26.2 1.2 %shard_map.104.chunk_ref = bf16[64,1280]{1,0:T(8,128)(2,1)S(1)} custom-call(bf16[64,1280]{1,0:T(8,128)(2,1)S(1)} %get-tuple-element.38.refs_0_, bf16[64,1280]{1,0:T(8,128)(2,1)S(1)} %collective-permute-done.3.refs_1_, bf16[1280,1280]{1,0:T(8,128)(2,1)S(1)} %copy-done, bf16[1280,1280]{1,0:T(8,128)(2,1)S(1)} %shard_map.103.refs_3_), custom_call_target="tpu_custom_call" | custom-call | flops 419430400 | bytes 6553600 | tf_op jit(solution)/shard_map/pallas_call | solution.py:319
  27.4 1.3 %collective-permute-done.2.refs_0_ = bf16[64,1280]{1,0:T(8,128)(2,1)} collective-permute-done((bf16[64,1280]{1,0:T(8,128)(2,1)S(1)}, bf16[64,1280]{1,0:T(8,128)(2,1)}, u32[]{:S(2)}, u32[]{:S(2)}) %collective-permute-start.2) | collective-permute-done | bytes 163872 | tf_op jit(solution)/shard_map/ppermute | solution.py:215
  28.7 1.3 %collective-permute-start.5 = (bf16[64,1280]{1,0:T(8,128)(2,1)}, bf16[64,1280]{1,0:T(8,128)(2,1)}, u32[]{:S(2)}, u32[]{:S(2)}) collective-permute-start(bf16[64,1280]{1,0:T(8,128)(2,1)} %collective-permute-done.2.refs_0_), channel_id=1, source_target_pairs={{0,4},{4,8},{8,12},{12,0},{1,5},{5,9},{9,13},{13,1},{2,6},{6,10},{... | collective-permute-start | bytes 491528 | tf_op jit(solution)/shard_map/ppermute | solution.py:215
  30.0 1.9 %collective-permute-done.6.refs_1_ = bf16[64,1280]{1,0:T(8,128)(2,1)} collective-permute-done((bf16[64,1280]{1,0:T(8,128)(2,1)S(1)}, bf16[64,1280]{1,0:T(8,128)(2,1)}, u32[]{:S(2)}, u32[]{:S(2)}) %collective-permute-start.6) | collective-permute-done | bytes 163872 | tf_op jit(solution)/shard_map/ppermute | solution.py:215
  32.0 1.5 %collective-permute-start.7 = (s32[1,64]{1,0:T(1,128)S(1)}, s32[1,64]{1,0:T(1,128)S(1)}, u32[]{:S(2)}, u32[]{:S(2)}) collective-permute-start(s32[1,64]{1,0:T(1,128)S(1)} %bitcast.21), channel_id=1, source_target_pairs={{0,2},{2,0},{1,3},{3,1},{4,6},{6,4},{5,7},{7,5},{8,10},{10,8},{9,1... | collective-permute-start | bytes 776 | tf_op jit(solution)/shard_map/ppermute | solution.py:215
  33.5 1.1 %copy-done.3 = bf16[1,64,5120]{2,1,0:T(8,128)(2,1)S(1)} copy-done((bf16[1,64,5120]{2,1,0:T(8,128)(2,1)S(1)}, bf16[1,64,5120]{2,1,0:T(8,128)(2,1)}, u32[]{:S(2)}) %copy-start.3) | copy-done | bytes 655384
  35.5 1.9 %copy-done.1 = bf16[1280,1280]{1,0:T(8,128)(2,1)S(1)} copy-done((bf16[1280,1280]{1,0:T(8,128)(2,1)S(1)}, bf16[1280,1280]{1,0:T(8,128)(2,1)}, u32[]{:S(2)}) %copy-start.1) | copy-done | bytes 3276824
  37.4 2.2 %shard_map.105 = bf16[64,1280]{1,0:T(8,128)(2,1)S(1)} custom-call(bf16[64,1280]{1,0:T(8,128)(2,1)} %collective-permute-done.2.refs_0_, bf16[64,1280]{1,0:T(8,128)(2,1)} %collective-permute-done.6.refs_1_, bf16[1280,1280]{1,0:T(8,128)(2,1)S(1)} %copy-done.1, bf16[1280,1280]{1,0:T(8,128)(2,1)S(1)} %shard_map.103.refs_3_), custom_call_target="tpu_custom_call" | custom-call | flops 419430400 | bytes 6553600 | tf_op jit(solution)/shard_map/pallas_call | solution.py:319
  40.5 3.1 %collective-permute-start.15 = (bf16[64,1280]{1,0:T(8,128)(2,1)S(1)}, bf16[64,1280]{1,0:T(8,128)(2,1)S(1)}, u32[]{:S(2)}, u32[]{:S(2)}) collective-permute-start(bf16[64,1280]{1,0:T(8,128)(2,1)S(1)} %shard_map.105), channel_id=1, source_target_pairs={{0,12},{4,0},{8,4},{12,8},{1,13},{5,1},{9,5},{13,9},{2,14},{6,2},{... | collective-permute-start | bytes 491528 | tf_op jit(solution)/shard_map/ppermute | solution.py:215
  43.7 2.2 %shard_map.107 = bf16[64,1280]{1,0:T(8,128)(2,1)S(1)} custom-call(bf16[64,1280]{1,0:T(8,128)(2,1)} %collective-permute-done.5.refs_0_, bf16[64,1280]{1,0:T(8,128)(2,1)} %collective-permute-done.8.refs_1_, bf16[1280,1280]{1,0:T(8,128)(2,1)S(1)} %copy-done.1, bf16[1280,1280]{1,0:T(8,128)(2,1)S(1)} %shard_map.103.refs_3_), custom_call_target="tpu_custom_call" | custom-call | flops 419430400 | bytes 6553600 | tf_op jit(solution)/shard_map/pallas_call | solution.py:319
  45.9 2.6 %collective-permute-start.10 = (bf16[64,1280]{1,0:T(8,128)(2,1)S(1)}, bf16[64,1280]{1,0:T(8,128)(2,1)S(1)}, u32[]{:S(2)}, u32[]{:S(2)}) collective-permute-start(bf16[64,1280]{1,0:T(8,128)(2,1)S(1)} %shard_map.107), channel_id=1, source_target_pairs={{0,8},{4,12},{8,0},{12,4},{1,9},{5,13},{9,1},{13,5},{2,10},{6,14},... | collective-permute-start | bytes 491528 | tf_op jit(solution)/shard_map/ppermute | solution.py:215
  49.2 1.6 %collective-permute-start.16 = (bf16[64,1280]{1,0:T(8,128)(2,1)S(1)}, bf16[64,1280]{1,0:T(8,128)(2,1)S(1)}, u32[]{:S(2)}, u32[]{:S(2)}) collective-permute-start(bf16[64,1280]{1,0:T(8,128)(2,1)S(1)} %shard_map.110.refs_1_), channel_id=1, source_target_pairs={{0,2},{2,0},{1,3},{3,1},{4,6},{6,4},{5,7},{7,5},{8,10},{10,8},{9,1... | collective-permute-start | bytes 491528 | tf_op jit(solution)/shard_map/ppermute | solution.py:215
  50.8 5.0 %collective-permute-done.13.refs_1_ = bf16[64,1280]{1,0:T(8,128)(2,1)S(1)} collective-permute-done((bf16[64,1280]{1,0:T(8,128)(2,1)}, bf16[64,1280]{1,0:T(8,128)(2,1)S(1)}, u32[]{:S(2)}, u32[]{:S(2)}) %collective-permute-start.13) | collective-permute-done | bytes 163872 | tf_op jit(solution)/shard_map/ppermute | solution.py:215
  55.8 1.2 %shard_map.109 = bf16[64,1280]{1,0:T(8,128)(2,1)S(1)} custom-call(bf16[64,1280]{1,0:T(8,128)(2,1)S(1)} %collective-permute-done.12.refs_0_, bf16[64,1280]{1,0:T(8,128)(2,1)S(1)} %collective-permute-done.13.refs_1_, bf16[1280,1280]{1,0:T(8,128)(2,1)S(1)} %copy-done.2, bf16[1280,1280]{1,0:T(8,128)(2,1)S(1)} %shard_map.103.refs_3_), custom_call_target="tpu_custom_call" | custom-call | flops 419430400 | bytes 6553600 | tf_op jit(solution)/shard_map/pallas_call | solution.py:319
  57.0 6.3 %collective-permute-start.14 = (bf16[64,1280]{1,0:T(8,128)(2,1)S(1)}, bf16[64,1280]{1,0:T(8,128)(2,1)S(1)}, u32[]{:S(2)}, u32[]{:S(2)}) collective-permute-start(bf16[64,1280]{1,0:T(8,128)(2,1)S(1)} %shard_map.109), channel_id=1, source_target_pairs={{0,4},{4,8},{8,12},{12,0},{1,5},{5,9},{9,13},{13,1},{2,6},{6,10},{... | collective-permute-start | bytes 491528 | tf_op jit(solution)/shard_map/ppermute | solution.py:215
  63.4 1.2 %collective-permute-done.10.chunk_ref = bf16[64,1280]{1,0:T(8,128)(2,1)S(1)} collective-permute-done((bf16[64,1280]{1,0:T(8,128)(2,1)S(1)}, bf16[64,1280]{1,0:T(8,128)(2,1)S(1)}, u32[]{:S(2)}, u32[]{:S(2)}) %collective-permute-start.10) | collective-permute-done | bytes 163872 | tf_op jit(solution)/shard_map/ppermute | solution.py:215
  64.6 1.6 %collective-permute-start.11 = (bf16[64,1280]{1,0:T(8,128)(2,1)S(1)}, bf16[64,1280]{1,0:T(8,128)(2,1)S(1)}, u32[]{:S(2)}, u32[]{:S(2)}) collective-permute-start(bf16[64,1280]{1,0:T(8,128)(2,1)S(1)} %shard_map.108.refs_0_), channel_id=1, source_target_pairs={{0,2},{2,0},{1,3},{3,1},{4,6},{6,4},{5,7},{7,5},{8,10},{10,8},{9,1... | collective-permute-start | bytes 491528 | tf_op jit(solution)/shard_map/ppermute | solution.py:215
  67.0 1.0 %copy-done.7 = bf16[5120,32]{0,1:T(8,128)(2,1)S(1)} copy-done((bf16[5120,32]{0,1:T(8,128)(2,1)S(1)}, bf16[5120,32]{0,1:T(8,128)(2,1)}, u32[]{:S(2)}) %copy-start.7) | copy-done | bytes 327704
  67.9 2.5 %shard_map.113.refs_7_ = bf16[2,32,2,5120]{3,2,1,0:T(2,128)(2,1)} custom-call(s32[2]{0:T(128)S(1)} %pad_add_fusion.place_ref, bf16[64,1280]{1,0:T(8,128)(2,1)S(1)} %shard_map.108.refs_0_, bf16[64,1280]{1,0:T(8,128)(2,1)S(1)} %shard_map.112.refs_1_, bf16[64,5120]{1,0:T(8,128)(2,1)S(1)} %get-tuple-element.61.refs_2_, s32[1,64]{1,0:T(1,128)S(1)} %bitcast.22, ...), custom_call_target="tpu_custom_call" | custom-call | tf_op jit(solution)/shard_map/pallas_call | solution.py:349
  70.4 1.6 %collective-permute-done.17.refs_1_ = bf16[64,1280]{1,0:T(8,128)(2,1)S(1)} collective-permute-done((bf16[64,1280]{1,0:T(8,128)(2,1)S(1)}, bf16[64,1280]{1,0:T(8,128)(2,1)S(1)}, u32[]{:S(2)}, u32[]{:S(2)}) %collective-permute-start.17) | collective-permute-done | bytes 163872 | tf_op jit(solution)/shard_map/ppermute | solution.py:215
  72.0 2.5 %shard_map.114 = bf16[2,32,2,5120]{3,2,1,0:T(2,128)(2,1)} custom-call(s32[2]{0:T(128)S(1)} %pad_add_fusion.place_ref, bf16[64,1280]{1,0:T(8,128)(2,1)S(1)} %collective-permute-done.11.refs_0_, bf16[64,1280]{1,0:T(8,128)(2,1)S(1)} %collective-permute-done.17.refs_1_, bf16[64,5120]{1,0:T(8,128)(2,1)S(1)} %get-tuple-element.59.refs_2_, ...), custom_call_target="tpu_custom_call", output_to_operand_aliasing={{}: (8, {})} | custom-call | tf_op jit(solution)/shard_map/pallas_call | solution.py:349
  (47 shorter events, 4.7 us)
Async XLA Ops:
  1.8 19.1 %collective-permute-start.4 = (bf16[1280,1280]{1,0:T(8,128)(2,1)}, bf16[1280,1280]{1,0:T(8,128)(2,1)S(1)}, u32[]{:S(2)}, u32[]{:S(2)}) collective-permute-start(bf16[1280,1280]{1,0:T(8,128)(2,1)} %refs_2_.7), channel_id=1, source_target_pairs={{0,1},{1,0},{2,3},{3,2},{4,5},{5,4},{6,7},{7,6},{8,9},{9,8},{10,11... | collective-permute-start | bytes 9830408 | tf_op jit(solution)/shard_map/ppermute | solution.py:215
  2.3 11.2 %collective-permute-start = (bf16[528,128]{1,0:T(8,128)(2,1)}, bf16[528,128]{1,0:T(8,128)(2,1)S(1)}, u32[]{:S(2)}, u32[]{:S(2)}) collective-permute-start(bf16[528,128]{1,0:T(8,128)(2,1)} %shard_map.100.refs_1_), channel_id=1, source_target_pairs={{0,4},{4,8},{8,12},{1,5},{5,9},{9,13},{2,6},{6,10},{10,14},{3,7},{... | collective-permute-start | bytes 405512 | tf_op jit(solution)/shard_map/ppermute | solution.py:234
  6.8 8.1 %collective-permute-start.1 = (bf16[528,128]{1,0:T(8,128)(2,1)}, bf16[528,128]{1,0:T(8,128)(2,1)S(1)}, u32[]{:S(2)}, u32[]{:S(2)}) collective-permute-start(bf16[528,128]{1,0:T(8,128)(2,1)} %shard_map.100.refs_1_), channel_id=1, source_target_pairs={{0,8},{4,12},{1,9},{5,13},{2,10},{6,14},{3,11},{7,15},{16,24},{20,... | collective-permute-start | bytes 405512 | tf_op jit(solution)/shard_map/ppermute | solution.py:234
  11.3 0.9 %copy-start.8 = (bf16[528,128]{1,0:T(8,128)(2,1)S(1)}, bf16[528,128]{1,0:T(8,128)(2,1)}, u32[]{:S(2)}) copy-start(bf16[528,128]{1,0:T(8,128)(2,1)} %shard_map.100.refs_1_) | copy-start | bytes 405508
  12.2 1.0 %copy-start.9 = (bf16[1,128,10,128]{3,1,2,0:T(8,128)(2,1)S(1)}, bf16[1,128,10,128]{3,1,2,0:T(8,128)(2,1)}, u32[]{:S(2)}) copy-start(bf16[1,128,10,128]{3,1,2,0:T(8,128)(2,1)} %param.10) | copy-start | bytes 983044
  17.6 3.2 %collective-permute-start.3 = (bf16[64,1280]{1,0:T(8,128)(2,1)S(1)}, bf16[64,1280]{1,0:T(8,128)(2,1)S(1)}, u32[]{:S(2)}, u32[]{:S(2)}) collective-permute-start(bf16[64,1280]{1,0:T(8,128)(2,1)S(1)} %get-tuple-element.39), channel_id=1, source_target_pairs={{0,1},{1,0},{2,3},{3,2},{4,5},{5,4},{6,7},{7,6},{8,9},{9,8},{10,11... | collective-permute-start | bytes 491528 | tf_op jit(solution)/shard_map/ppermute | solution.py:215
  17.7 8.5 %copy-start = (bf16[1280,1280]{1,0:T(8,128)(2,1)S(1)}, bf16[1280,1280]{1,0:T(8,128)(2,1)}, u32[]{:S(2)}) copy-start(bf16[1280,1280]{1,0:T(8,128)(2,1)} %refs_2_.7) | copy-start | bytes 9830404
  17.7 11.0 %collective-permute-start.2 = (bf16[64,1280]{1,0:T(8,128)(2,1)S(1)}, bf16[64,1280]{1,0:T(8,128)(2,1)}, u32[]{:S(2)}, u32[]{:S(2)}) collective-permute-start(bf16[64,1280]{1,0:T(8,128)(2,1)S(1)} %get-tuple-element.38.refs_0_), channel_id=1, source_target_pairs={{0,4},{4,8},{8,12},{12,0},{1,5},{5,9},{9,13},{13,1},{2,6},{6,10},{... | collective-permute-start | bytes 491528 | tf_op jit(solution)/shard_map/ppermute | solution.py:215
  20.8 1.7 %copy-start.5 = (bf16[1280,1280]{1,0:T(8,128)(2,1)}, bf16[1280,1280]{1,0:T(8,128)(2,1)S(1)}, u32[]{:S(2)}) copy-start(bf16[1280,1280]{1,0:T(8,128)(2,1)S(1)} %collective-permute-done.4.refs_0_) | copy-start | bytes 9830404
  22.5 9.4 %collective-permute-start.6 = (bf16[64,1280]{1,0:T(8,128)(2,1)S(1)}, bf16[64,1280]{1,0:T(8,128)(2,1)}, u32[]{:S(2)}, u32[]{:S(2)}) collective-permute-start(bf16[64,1280]{1,0:T(8,128)(2,1)S(1)} %collective-permute-done.3.refs_1_), channel_id=1, source_target_pairs={{0,4},{4,8},{8,12},{12,0},{1,5},{5,9},{9,13},{13,1},{2,6},{6,10},{... | collective-permute-start | bytes 491528 | tf_op jit(solution)/shard_map/ppermute | solution.py:215
  23.8 1.9 %copy-start.6 = (bf16[1280,1280]{1,0:T(8,128)(2,1)S(1)}, bf16[1280,1280]{1,0:T(8,128)(2,1)}, u32[]{:S(2)}) copy-start(bf16[1280,1280]{1,0:T(8,128)(2,1)} %copy-done.5) | copy-start | bytes 9830404
  26.2 5.8 %copy-start.11 = (s32[1,64,1]{1,2,0:T(1,128)S(1)}, s32[1,64,1]{1,2,0:T(1,128)}, u32[]{:S(2)}) copy-start(s32[1,64,1]{1,2,0:T(1,128)} %param.18) | copy-start | bytes 772
  28.7 11.0 %collective-permute-start.5 = (bf16[64,1280]{1,0:T(8,128)(2,1)}, bf16[64,1280]{1,0:T(8,128)(2,1)}, u32[]{:S(2)}, u32[]{:S(2)}) collective-permute-start(bf16[64,1280]{1,0:T(8,128)(2,1)} %collective-permute-done.2.refs_0_), channel_id=1, source_target_pairs={{0,4},{4,8},{8,12},{12,0},{1,5},{5,9},{9,13},{13,1},{2,6},{6,10},{... | collective-permute-start | bytes 491528 | tf_op jit(solution)/shard_map/ppermute | solution.py:215
  32.0 11.7 %collective-permute-start.8 = (bf16[64,1280]{1,0:T(8,128)(2,1)}, bf16[64,1280]{1,0:T(8,128)(2,1)}, u32[]{:S(2)}, u32[]{:S(2)}) collective-permute-start(bf16[64,1280]{1,0:T(8,128)(2,1)} %collective-permute-done.6.refs_1_), channel_id=1, source_target_pairs={{0,4},{4,8},{8,12},{12,0},{1,5},{5,9},{9,13},{13,1},{2,6},{6,10},{... | collective-permute-start | bytes 491528 | tf_op jit(solution)/shard_map/ppermute | solution.py:215
  32.0 3.5 %collective-permute-start.7 = (s32[1,64]{1,0:T(1,128)S(1)}, s32[1,64]{1,0:T(1,128)S(1)}, u32[]{:S(2)}, u32[]{:S(2)}) collective-permute-start(s32[1,64]{1,0:T(1,128)S(1)} %bitcast.21), channel_id=1, source_target_pairs={{0,2},{2,0},{1,3},{3,1},{4,6},{6,4},{5,7},{7,5},{8,10},{10,8},{9,1... | collective-permute-start | bytes 776 | tf_op jit(solution)/shard_map/ppermute | solution.py:215
  33.5 1.1 %copy-start.3 = (bf16[1,64,5120]{2,1,0:T(8,128)(2,1)S(1)}, bf16[1,64,5120]{2,1,0:T(8,128)(2,1)}, u32[]{:S(2)}) copy-start(bf16[1,64,5120]{2,1,0:T(8,128)(2,1)} %param.14) | copy-start | bytes 1966084
  34.6 9.1 %collective-permute-start.9 = (bf16[64,1280]{1,0:T(8,128)(2,1)S(1)}, bf16[64,1280]{1,0:T(8,128)(2,1)S(1)}, u32[]{:S(2)}, u32[]{:S(2)}) collective-permute-start(bf16[64,1280]{1,0:T(8,128)(2,1)S(1)} %shard_map.106.refs_0_), channel_id=1, source_target_pairs={{0,2},{2,0},{1,3},{3,1},{4,6},{6,4},{5,7},{7,5},{8,10},{10,8},{9,1... | collective-permute-start | bytes 491528 | tf_op jit(solution)/shard_map/ppermute | solution.py:215
  35.5 1.9 %copy-start.1 = (bf16[1280,1280]{1,0:T(8,128)(2,1)S(1)}, bf16[1280,1280]{1,0:T(8,128)(2,1)}, u32[]{:S(2)}) copy-start(bf16[1280,1280]{1,0:T(8,128)(2,1)} %refs_2_.7) | copy-start | bytes 9830404
  39.7 9.5 %copy-start.4 = (bf16[1,64,5120]{2,1,0:T(8,128)(2,1)S(1)}, bf16[1,64,5120]{2,1,0:T(8,128)(2,1)}, u32[]{:S(2)}) copy-start(bf16[1,64,5120]{2,1,0:T(8,128)(2,1)} %param.14) | copy-start | bytes 1966084
  39.7 16.1 %copy-start.2 = (bf16[1280,1280]{1,0:T(8,128)(2,1)S(1)}, bf16[1280,1280]{1,0:T(8,128)(2,1)}, u32[]{:S(2)}) copy-start(bf16[1280,1280]{1,0:T(8,128)(2,1)} %refs_2_.7) | copy-start | bytes 9830404
  39.7 9.2 %collective-permute-start.12 = (bf16[64,1280]{1,0:T(8,128)(2,1)}, bf16[64,1280]{1,0:T(8,128)(2,1)S(1)}, u32[]{:S(2)}, u32[]{:S(2)}) collective-permute-start(bf16[64,1280]{1,0:T(8,128)(2,1)} %collective-permute-done.5.refs_0_), channel_id=1, source_target_pairs={{0,4},{4,8},{8,12},{12,0},{1,5},{5,9},{9,13},{13,1},{2,6},{6,10},{... | collective-permute-start | bytes 491528 | tf_op jit(solution)/shard_map/ppermute | solution.py:215
  40.5 8.6 %collective-permute-start.15 = (bf16[64,1280]{1,0:T(8,128)(2,1)S(1)}, bf16[64,1280]{1,0:T(8,128)(2,1)S(1)}, u32[]{:S(2)}, u32[]{:S(2)}) collective-permute-start(bf16[64,1280]{1,0:T(8,128)(2,1)S(1)} %shard_map.105), channel_id=1, source_target_pairs={{0,12},{4,0},{8,4},{12,8},{1,13},{5,1},{9,5},{13,9},{2,14},{6,2},{... | collective-permute-start | bytes 491528 | tf_op jit(solution)/shard_map/ppermute | solution.py:215
  43.6 12.1 %collective-permute-start.13 = (bf16[64,1280]{1,0:T(8,128)(2,1)}, bf16[64,1280]{1,0:T(8,128)(2,1)S(1)}, u32[]{:S(2)}, u32[]{:S(2)}) collective-permute-start(bf16[64,1280]{1,0:T(8,128)(2,1)} %collective-permute-done.8.refs_1_), channel_id=1, source_target_pairs={{0,4},{4,8},{8,12},{12,0},{1,5},{5,9},{9,13},{13,1},{2,6},{6,10},{... | collective-permute-start | bytes 491528 | tf_op jit(solution)/shard_map/ppermute | solution.py:215
  45.9 18.6 %collective-permute-start.10 = (bf16[64,1280]{1,0:T(8,128)(2,1)S(1)}, bf16[64,1280]{1,0:T(8,128)(2,1)S(1)}, u32[]{:S(2)}, u32[]{:S(2)}) collective-permute-start(bf16[64,1280]{1,0:T(8,128)(2,1)S(1)} %shard_map.107), channel_id=1, source_target_pairs={{0,8},{4,12},{8,0},{12,4},{1,9},{5,13},{9,1},{13,5},{2,10},{6,14},... | collective-permute-start | bytes 491528 | tf_op jit(solution)/shard_map/ppermute | solution.py:215
  49.2 17.7 %copy-start.12 = (bf16[5120]{0:T(1024)(128)(2,1)S(1)}, bf16[5120]{0:T(1024)(128)(2,1)}, u32[]{:S(2)}) copy-start(bf16[5120]{0:T(1024)(128)(2,1)} %param.16) | copy-start | bytes 30724
  49.2 17.8 %copy-start.10 = (s32[64]{0:T(128)S(1)}, s32[64]{0:T(128)}, u32[]{:S(2)}) copy-start(s32[64]{0:T(128)} %param.19) | copy-start | bytes 772
  49.2 16.9 %collective-permute-start.16 = (bf16[64,1280]{1,0:T(8,128)(2,1)S(1)}, bf16[64,1280]{1,0:T(8,128)(2,1)S(1)}, u32[]{:S(2)}, u32[]{:S(2)}) collective-permute-start(bf16[64,1280]{1,0:T(8,128)(2,1)S(1)} %shard_map.110.refs_1_), channel_id=1, source_target_pairs={{0,2},{2,0},{1,3},{3,1},{4,6},{6,4},{5,7},{7,5},{8,10},{10,8},{9,1... | collective-permute-start | bytes 491528 | tf_op jit(solution)/shard_map/ppermute | solution.py:215
  57.0 9.2 %collective-permute-start.14 = (bf16[64,1280]{1,0:T(8,128)(2,1)S(1)}, bf16[64,1280]{1,0:T(8,128)(2,1)S(1)}, u32[]{:S(2)}, u32[]{:S(2)}) collective-permute-start(bf16[64,1280]{1,0:T(8,128)(2,1)S(1)} %shard_map.109), channel_id=1, source_target_pairs={{0,4},{4,8},{8,12},{12,0},{1,5},{5,9},{9,13},{13,1},{2,6},{6,10},{... | collective-permute-start | bytes 491528 | tf_op jit(solution)/shard_map/ppermute | solution.py:215
  64.6 5.8 %collective-permute-start.11 = (bf16[64,1280]{1,0:T(8,128)(2,1)S(1)}, bf16[64,1280]{1,0:T(8,128)(2,1)S(1)}, u32[]{:S(2)}, u32[]{:S(2)}) collective-permute-start(bf16[64,1280]{1,0:T(8,128)(2,1)S(1)} %shard_map.108.refs_0_), channel_id=1, source_target_pairs={{0,2},{2,0},{1,3},{3,1},{4,6},{6,4},{5,7},{7,5},{8,10},{10,8},{9,1... | collective-permute-start | bytes 491528 | tf_op jit(solution)/shard_map/ppermute | solution.py:215
  66.2 5.8 %collective-permute-start.17 = (bf16[64,1280]{1,0:T(8,128)(2,1)S(1)}, bf16[64,1280]{1,0:T(8,128)(2,1)S(1)}, u32[]{:S(2)}, u32[]{:S(2)}) collective-permute-start(bf16[64,1280]{1,0:T(8,128)(2,1)S(1)} %shard_map.112.refs_1_), channel_id=1, source_target_pairs={{0,2},{2,0},{1,3},{3,1},{4,6},{6,4},{5,7},{7,5},{8,10},{10,8},{9,1... | collective-permute-start | bytes 491528 | tf_op jit(solution)/shard_map/ppermute | solution.py:215
  67.0 1.0 %copy-start.7 = (bf16[5120,32]{0,1:T(8,128)(2,1)S(1)}, bf16[5120,32]{0,1:T(8,128)(2,1)}, u32[]{:S(2)}) copy-start(bf16[5120,32]{0,1:T(8,128)(2,1)} %param.17) | copy-start | bytes 983044

commit v3 on v1

--- a/solution.py
+++ b/solution.py
@@ -249,6 +249,7 @@
         compiler_params=much,
     )(own_queries, pack)
     all_ids = [ids] + [over(ids, "exp", back) for back in range(1, exp_count)]
+    staged_queries, all_ids = lax.optimization_barrier((staged_queries, all_ids))
     pieces = pl.pallas_call(
         functools.partial(attention_kernel, heads // groups, groups, pair),
         out_shape=[jax.ShapeDtypeStruct((part_rows, heads * head_size), bf16)] * pair,
@@ -308,23 +309,24 @@
     for step in range(ctx_count):
         last = step == ctx_count - 1
         following = None if last else [over(array, "ctx", 1) for array in block]
-        if step == 1:
-            block, all_ids = lax.optimization_barrier((block, all_ids))
         if step == 2:
-            block, chunks[1], flat[:1] = lax.optimization_barrier((block, chunks[1], flat[:1]))
+            block, chunks[1] = lax.optimization_barrier((block, chunks[1]))
+        if step == 3 and aligned:
+            block, flat[0] = lax.optimization_barrier((block, flat[0]))
         if last and aligned:
             hidden = collect(list(range(late_from)), ctx_count)
-            block, hidden = lax.optimization_barrier((block, hidden))
         total = project(*block, *weights)
         chunk = over(total, "ctx", ctx_count - step)
         if not last:
             block = [lax.optimization_barrier((array, total))[0] for array in following]
+        if last and aligned:
+            chunk, hidden = lax.optimization_barrier((chunk, hidden))
         chunks.append(chunk)
         if aligned:
-            if step == 2:
-                first, _ = lax.optimization_barrier((chunks[1], total))
-                flat[1] = forward(first, 1, ctx_count)
-            flat.append(forward(chunk, step, ctx_count) if step != 1 else None)
+            if step in (1, 2) and not last:
+                first, _ = lax.optimization_barrier((chunks[step - 1], [total] + following[:1]))
+                flat[step - 1] = forward(first, step - 1, ctx_count)
+            flat.append(forward(chunk, step, ctx_count) if step > 1 or last else None)
     if aligned:
         late_steps, spots = list(range(late_from, ctx_count)), ctx_count
     else:

time: 74.4 us -> 75.2 us (1.011)
  waiting for transfers between devices: 24.5 us -> 15.9 us
  local copies, waits for them, and re-layouts: 3.45 us -> 9.51 us
  starting transfers between devices: 28 us -> 30.1 us
  Pallas kernels: 17.9 us -> 19 us
    ppermute x16, waiting for transfers between devices: 23.1 us -> 15.9 us  [over(): lax.ppermute(array, axis, [(i, (i + step) % count) for i in range(count)])]
    unnamed x16 -> x26, local copies, waits for them, and re-layouts: 3.43 us -> 9.5 us
    ppermute x16, starting transfers between devices: 19 us -> 21.1 us  [over(): lax.ppermute(array, axis, [(i, (i + step) % count) for i in range(count)])]
    ppermute x2, waiting for transfers between devices: 1.35 us -> 0.01 us  [on_device(): lax.ppermute(pack, 'ctx', [(i, i + step) for i in range(ctx_count - step)])]
    pallas_call x4, Pallas kernels: 0.18 us -> 1.09 us  [forward(): pl.pallas_call(functools.partial(hidden_kernel, step, spots), out_shape=j...]
    pallas_call x4, Pallas kernels: 6.96 us -> 7.77 us  [on_device(): total = project(*block, *weights)]
  transfers between devices with their start and end apart: 18 -> 18, of which waited for: 11 -> 7; matrix products, arithmetic and copies ran while one was open for 0% -> 0% of each run, Pallas kernels for 18% -> 20%
where the time goes in v3:
time: 75.2 us; the launch traced here: 74.8 us
  starting transfers between devices  30.1 us (40%)
  Pallas kernels  19 us (25%)
  waiting for transfers between devices  15.9 us (21%)
  local copies, waits for them, and re-layouts  9.51 us (13%)
    ppermute x16, starting transfers between devices, over(): lax.ppermute(array, axis, [(i, (i + step) % count) for i in range(count)])  21.1 us
    ppermute x16, waiting for transfers between devices, over(): lax.ppermute(array, axis, [(i, (i + step) % count) for i in range(count)])  15.9 us
    unnamed x26, local copies, waits for them, and re-layouts  9.5 us
    ppermute x2, starting transfers between devices, on_device(): lax.ppermute(pack, 'ctx', [(i, i + step) for i in range(ctx_count - step)])  9 us
    pallas_call x4, Pallas kernels, on_device(): total = project(*block, *weights)  7.77 us
    pallas_call x2, Pallas kernels, on_device(): pl.pallas_call(functools.partial(finish_kernel, late_steps, spots, back,...  4.91 us
    pallas_call x1, Pallas kernels, on_device(): pl.pallas_call(functools.partial(attention_kernel, heads // groups, group...  2.73 us
    pallas_call x1, Pallas kernels, on_device(): pl.pallas_call(functools.partial(pack_kernel, groups), out_shape=jax.Shap...  1.77 us
  transfers between devices with their start and end apart: 18, of which 7 were waited for; matrix products, arithmetic and copies ran while one was open for 0% of the time, Pallas kernels for 20%

profile of v3, /device:TPU:0, one launch (start us, length us, event | category | flops | bytes accessed | tf_op | source)
XLA Modules:
  0.0 74.8 jit_solution(11103463093796612468)
XLA Ops:
  0.0 1.8 %shard_map.100.refs_1_ = bf16[528,128]{1,0:T(8,128)(2,1)} custom-call(bf16[256,128]{1,0:T(8,128)(2,1)} %bitcast.23, bf16[256,128]{1,0:T(8,128)(2,1)} %bitcast.24, s32[1,128]{1,0:T(1,128)} %doc_ref.1), custom_call_target="tpu_custom_call" | custom-call | tf_op jit(solution)/shard_map/pallas_call | solution.py:218
  2.3 4.5 %collective-permute-start.1 = (bf16[528,128]{1,0:T(8,128)(2,1)}, bf16[528,128]{1,0:T(8,128)(2,1)S(1)}, u32[]{:S(2)}, u32[]{:S(2)}) collective-permute-start(bf16[528,128]{1,0:T(8,128)(2,1)} %shard_map.100.refs_1_), channel_id=1, source_target_pairs={{0,4},{4,8},{8,12},{1,5},{5,9},{9,13},{2,6},{6,10},{10,14},{3,7},{... | collective-permute-start | bytes 405512 | tf_op jit(solution)/shard_map/ppermute | solution.py:232
  6.8 4.5 %collective-permute-start.2 = (bf16[528,128]{1,0:T(8,128)(2,1)}, bf16[528,128]{1,0:T(8,128)(2,1)S(1)}, u32[]{:S(2)}, u32[]{:S(2)}) collective-permute-start(bf16[528,128]{1,0:T(8,128)(2,1)} %shard_map.100.refs_1_), channel_id=1, source_target_pairs={{0,8},{4,12},{1,9},{5,13},{2,10},{6,14},{3,11},{7,15},{16,24},{20,... | collective-permute-start | bytes 405512 | tf_op jit(solution)/shard_map/ppermute | solution.py:232
  11.3 1.6 %collective-permute-start = (s32[1,64]{1,0:T(1,128)}, s32[1,64]{1,0:T(1,128)S(1)}, u32[]{:S(2)}, u32[]{:S(2)}) collective-permute-start(s32[1,64]{1,0:T(1,128)} %bitcast.21), channel_id=1, source_target_pairs={{0,2},{2,0},{1,3},{3,1},{4,6},{6,4},{5,7},{7,5},{8,10},{10,8},{9,1... | collective-permute-start | bytes 776 | tf_op jit(solution)/shard_map/ppermute | solution.py:213
  13.8 1.0 %copy-done.9 = bf16[1,128,10,128]{3,1,2,0:T(8,128)(2,1)S(1)} copy-done((bf16[1,128,10,128]{3,1,2,0:T(8,128)(2,1)S(1)}, bf16[1,128,10,128]{3,1,2,0:T(8,128)(2,1)}, u32[]{:S(2)}) %copy-start.9) | copy-done | bytes 327704
  15.1 2.7 %shard_map.102 = (bf16[64,1280]{1,0:T(8,128)(2,1)S(1)}, bf16[64,1280]{1,0:T(8,128)(2,1)S(1)}) custom-call(s32[1]{0:T(128)} %bitcast.3.place_ref, bf16[10,128,128]{2,1,0:T(8,128)(2,1)S(1)} %get-tuple-element.40.query_ref, bf16[528,128]{1,0:T(8,128)(2,1)S(1)} %get-tuple-element.41.refs_0_, bf16[528,128]{1,0:T(8,128)(2,1)S(1)} %collective-permute-done.1.refs_1_, ...), custom_call_target="tpu_custom_call" | custom-call | tf_op jit(solution)/shard_map/pallas_call | solution.py:253
  17.9 2.9 %collective-permute-start.3 = (bf16[64,1280]{1,0:T(8,128)(2,1)S(1)}, bf16[64,1280]{1,0:T(8,128)(2,1)}, u32[]{:S(2)}, u32[]{:S(2)}) collective-permute-start(bf16[64,1280]{1,0:T(8,128)(2,1)S(1)} %get-tuple-element.42.refs_0_), channel_id=1, source_target_pairs={{0,4},{4,8},{8,12},{12,0},{1,5},{5,9},{9,13},{13,1},{2,6},{6,10},{... | collective-permute-start | bytes 491528 | tf_op jit(solution)/shard_map/ppermute | solution.py:213
  20.8 1.7 %copy-done.5 = bf16[1280,1280]{1,0:T(8,128)(2,1)} copy-done((bf16[1280,1280]{1,0:T(8,128)(2,1)}, bf16[1280,1280]{1,0:T(8,128)(2,1)S(1)}, u32[]{:S(2)}) %copy-start.5) | copy-done | bytes 3276824
  22.5 1.3 %collective-permute-start.7 = (bf16[64,1280]{1,0:T(8,128)(2,1)S(1)}, bf16[64,1280]{1,0:T(8,128)(2,1)}, u32[]{:S(2)}, u32[]{:S(2)}) collective-permute-start(bf16[64,1280]{1,0:T(8,128)(2,1)S(1)} %collective-permute-done.4.refs_1_), channel_id=1, source_target_pairs={{0,4},{4,8},{8,12},{12,0},{1,5},{5,9},{9,13},{13,1},{2,6},{6,10},{... | collective-permute-start | bytes 491528 | tf_op jit(solution)/shard_map/ppermute | solution.py:213
  23.8 1.9 %copy-done.6 = bf16[1280,1280]{1,0:T(8,128)(2,1)S(1)} copy-done((bf16[1280,1280]{1,0:T(8,128)(2,1)S(1)}, bf16[1280,1280]{1,0:T(8,128)(2,1)}, u32[]{:S(2)}) %copy-start.6) | copy-done | bytes 3276824
  26.2 1.2 %shard_map.104.chunk_ref = bf16[64,1280]{1,0:T(8,128)(2,1)S(1)} custom-call(bf16[64,1280]{1,0:T(8,128)(2,1)S(1)} %get-tuple-element.42.refs_0_, bf16[64,1280]{1,0:T(8,128)(2,1)S(1)} %collective-permute-done.4.refs_1_, bf16[1280,1280]{1,0:T(8,128)(2,1)S(1)} %copy-done, bf16[1280,1280]{1,0:T(8,128)(2,1)S(1)} %shard_map.103.refs_3_), custom_call_target="tpu_custom_call" | custom-call | flops 419430400 | bytes 6553600 | tf_op jit(solution)/shard_map/pallas_call | solution.py:318
  27.4 1.3 %collective-permute-done.3.refs_0_ = bf16[64,1280]{1,0:T(8,128)(2,1)} collective-permute-done((bf16[64,1280]{1,0:T(8,128)(2,1)S(1)}, bf16[64,1280]{1,0:T(8,128)(2,1)}, u32[]{:S(2)}, u32[]{:S(2)}) %collective-permute-start.3) | collective-permute-done | bytes 163872 | tf_op jit(solution)/shard_map/ppermute | solution.py:213
  28.7 1.3 %collective-permute-start.6 = (bf16[64,1280]{1,0:T(8,128)(2,1)}, bf16[64,1280]{1,0:T(8,128)(2,1)}, u32[]{:S(2)}, u32[]{:S(2)}) collective-permute-start(bf16[64,1280]{1,0:T(8,128)(2,1)} %collective-permute-done.3.refs_0_), channel_id=1, source_target_pairs={{0,4},{4,8},{8,12},{12,0},{1,5},{5,9},{9,13},{13,1},{2,6},{6,10},{... | collective-permute-start | bytes 491528 | tf_op jit(solution)/shard_map/ppermute | solution.py:213
  30.0 2.0 %collective-permute-done.7.refs_1_ = bf16[64,1280]{1,0:T(8,128)(2,1)} collective-permute-done((bf16[64,1280]{1,0:T(8,128)(2,1)S(1)}, bf16[64,1280]{1,0:T(8,128)(2,1)}, u32[]{:S(2)}, u32[]{:S(2)}) %collective-permute-start.7) | collective-permute-done | bytes 163872 | tf_op jit(solution)/shard_map/ppermute | solution.py:213
  32.0 2.9 %shard_map.105 = bf16[64,1280]{1,0:T(8,128)(2,1)} custom-call(bf16[64,1280]{1,0:T(8,128)(2,1)} %collective-permute-done.3.refs_0_, bf16[64,1280]{1,0:T(8,128)(2,1)} %collective-permute-done.7.refs_1_, bf16[1280,1280]{1,0:T(8,128)(2,1)S(1)} %copy-done, bf16[1280,1280]{1,0:T(8,128)(2,1)S(1)} %shard_map.103.refs_3_), custom_call_target="tpu_custom_call" | custom-call | flops 419430400 | bytes 6553600 | tf_op jit(solution)/shard_map/pallas_call | solution.py:318
  34.9 3.8 %collective-permute-start.9 = (bf16[64,1280]{1,0:T(8,128)(2,1)}, bf16[64,1280]{1,0:T(8,128)(2,1)}, u32[]{:S(2)}, u32[]{:S(2)}) collective-permute-start(bf16[64,1280]{1,0:T(8,128)(2,1)} %shard_map.105), channel_id=1, source_target_pairs={{0,12},{4,0},{8,4},{12,8},{1,13},{5,1},{9,5},{13,9},{2,14},{6,2},{... | collective-permute-start | bytes 491528 | tf_op jit(solution)/shard_map/ppermute | solution.py:213
  38.7 1.9 %collective-permute-done.8.refs_1_ = bf16[64,1280]{1,0:T(8,128)(2,1)} collective-permute-done((bf16[64,1280]{1,0:T(8,128)(2,1)}, bf16[64,1280]{1,0:T(8,128)(2,1)}, u32[]{:S(2)}, u32[]{:S(2)}) %collective-permute-start.8) | collective-permute-done | bytes 163872 | tf_op jit(solution)/shard_map/ppermute | solution.py:213
  40.6 1.1 %copy-done.3 = bf16[1,64,5120]{2,1,0:T(8,128)(2,1)S(1)} copy-done((bf16[1,64,5120]{2,1,0:T(8,128)(2,1)S(1)}, bf16[1,64,5120]{2,1,0:T(8,128)(2,1)}, u32[]{:S(2)}) %copy-start.3) | copy-done | bytes 655384
  41.8 1.6 %collective-permute-start.14 = (bf16[64,1280]{1,0:T(8,128)(2,1)S(1)}, bf16[64,1280]{1,0:T(8,128)(2,1)S(1)}, u32[]{:S(2)}, u32[]{:S(2)}) collective-permute-start(bf16[64,1280]{1,0:T(8,128)(2,1)S(1)} %shard_map.108.refs_0_), channel_id=1, source_target_pairs={{0,2},{2,0},{1,3},{3,1},{4,6},{6,4},{5,7},{7,5},{8,10},{10,8},{9,1... | collective-permute-start | bytes 491528 | tf_op jit(solution)/shard_map/ppermute | solution.py:213
  43.3 1.0 %collective-permute-done.9.chunk_ref = bf16[64,1280]{1,0:T(8,128)(2,1)} collective-permute-done((bf16[64,1280]{1,0:T(8,128)(2,1)}, bf16[64,1280]{1,0:T(8,128)(2,1)}, u32[]{:S(2)}, u32[]{:S(2)}) %collective-permute-start.9) | collective-permute-done | bytes 163872 | tf_op jit(solution)/shard_map/ppermute | solution.py:213
  44.3 1.9 %copy-done.1 = bf16[1280,1280]{1,0:T(8,128)(2,1)S(1)} copy-done((bf16[1280,1280]{1,0:T(8,128)(2,1)S(1)}, bf16[1280,1280]{1,0:T(8,128)(2,1)}, u32[]{:S(2)}) %copy-start.1) | copy-done | bytes 3276824
  46.3 2.4 %shard_map.106 = bf16[64,1280]{1,0:T(8,128)(2,1)S(1)} custom-call(bf16[64,1280]{1,0:T(8,128)(2,1)} %collective-permute-done.6.refs_0_, bf16[64,1280]{1,0:T(8,128)(2,1)} %collective-permute-done.8.refs_1_, bf16[1280,1280]{1,0:T(8,128)(2,1)S(1)} %copy-done.1, bf16[1280,1280]{1,0:T(8,128)(2,1)S(1)} %shard_map.103.refs_3_), custom_call_target="tpu_custom_call" | custom-call | flops 419430400 | bytes 6553600 | tf_op jit(solution)/shard_map/pallas_call | solution.py:318
  48.6 1.5 %collective-permute-start.10 = (bf16[64,1280]{1,0:T(8,128)(2,1)S(1)}, bf16[64,1280]{1,0:T(8,128)(2,1)S(1)}, u32[]{:S(2)}, u32[]{:S(2)}) collective-permute-start(bf16[64,1280]{1,0:T(8,128)(2,1)S(1)} %shard_map.106), channel_id=1, source_target_pairs={{0,8},{4,12},{8,0},{12,4},{1,9},{5,13},{9,1},{13,5},{2,10},{6,14},... | collective-permute-start | bytes 491528 | tf_op jit(solution)/shard_map/ppermute | solution.py:213
  51.9 1.2 %shard_map.109 = bf16[64,1280]{1,0:T(8,128)(2,1)S(1)} custom-call(bf16[64,1280]{1,0:T(8,128)(2,1)S(1)} %collective-permute-done.12.refs_0_, bf16[64,1280]{1,0:T(8,128)(2,1)S(1)} %collective-permute-done.13.refs_1_, bf16[1280,1280]{1,0:T(8,128)(2,1)S(1)} %copy-done.2, bf16[1280,1280]{1,0:T(8,128)(2,1)S(1)} %shard_map.103.refs_3_), custom_call_target="tpu_custom_call" | custom-call | flops 419430400 | bytes 6553600 | tf_op jit(solution)/shard_map/pallas_call | solution.py:318
  53.1 3.7 %collective-permute-start.15 = (bf16[64,1280]{1,0:T(8,128)(2,1)S(1)}, bf16[64,1280]{1,0:T(8,128)(2,1)S(1)}, u32[]{:S(2)}, u32[]{:S(2)}) collective-permute-start(bf16[64,1280]{1,0:T(8,128)(2,1)S(1)} %shard_map.109), channel_id=1, source_target_pairs={{0,4},{4,8},{8,12},{12,0},{1,5},{5,9},{9,13},{13,1},{2,6},{6,10},{... | collective-permute-start | bytes 491528 | tf_op jit(solution)/shard_map/ppermute | solution.py:213
  56.8 5.8 %collective-permute-done.10.chunk_ref = bf16[64,1280]{1,0:T(8,128)(2,1)S(1)} collective-permute-done((bf16[64,1280]{1,0:T(8,128)(2,1)S(1)}, bf16[64,1280]{1,0:T(8,128)(2,1)S(1)}, u32[]{:S(2)}, u32[]{:S(2)}) %collective-permute-start.10) | collective-permute-done | bytes 163872 | tf_op jit(solution)/shard_map/ppermute | solution.py:213
  62.7 1.6 %collective-permute-start.11 = (bf16[64,1280]{1,0:T(8,128)(2,1)S(1)}, bf16[64,1280]{1,0:T(8,128)(2,1)S(1)}, u32[]{:S(2)}, u32[]{:S(2)}) collective-permute-start(bf16[64,1280]{1,0:T(8,128)(2,1)S(1)} %shard_map.107.refs_0_), channel_id=1, source_target_pairs={{0,2},{2,0},{1,3},{3,1},{4,6},{6,4},{5,7},{7,5},{8,10},{10,8},{9,1... | collective-permute-start | bytes 491528 | tf_op jit(solution)/shard_map/ppermute | solution.py:213
  65.1 1.0 %copy-done.7 = bf16[5120,32]{0,1:T(8,128)(2,1)S(1)} copy-done((bf16[5120,32]{0,1:T(8,128)(2,1)S(1)}, bf16[5120,32]{0,1:T(8,128)(2,1)}, u32[]{:S(2)}) %copy-start.7) | copy-done | bytes 327704
  66.0 2.5 %shard_map.113.refs_7_ = bf16[2,32,2,5120]{3,2,1,0:T(2,128)(2,1)} custom-call(s32[2]{0:T(128)S(1)} %pad_add_fusion.place_ref, bf16[64,1280]{1,0:T(8,128)(2,1)S(1)} %shard_map.107.refs_0_, bf16[64,1280]{1,0:T(8,128)(2,1)S(1)} %shard_map.112.refs_1_, bf16[64,5120]{1,0:T(8,128)(2,1)S(1)} %get-tuple-element.67.refs_2_, s32[1,64]{1,0:T(1,128)S(1)} %bitcast.22, ...), custom_call_target="tpu_custom_call" | custom-call | tf_op jit(solution)/shard_map/pallas_call | solution.py:348
  68.5 1.3 %collective-permute-done.11.refs_0_ = bf16[64,1280]{1,0:T(8,128)(2,1)S(1)} collective-permute-done((bf16[64,1280]{1,0:T(8,128)(2,1)S(1)}, bf16[64,1280]{1,0:T(8,128)(2,1)S(1)}, u32[]{:S(2)}, u32[]{:S(2)}) %collective-permute-start.11) | collective-permute-done | bytes 163872 | tf_op jit(solution)/shard_map/ppermute | solution.py:213
  69.8 2.5 %collective-permute-done.17.refs_1_ = bf16[64,1280]{1,0:T(8,128)(2,1)S(1)} collective-permute-done((bf16[64,1280]{1,0:T(8,128)(2,1)S(1)}, bf16[64,1280]{1,0:T(8,128)(2,1)S(1)}, u32[]{:S(2)}, u32[]{:S(2)}) %collective-permute-start.17) | collective-permute-done | bytes 163872 | tf_op jit(solution)/shard_map/ppermute | solution.py:213
  72.3 2.5 %shard_map.114 = bf16[2,32,2,5120]{3,2,1,0:T(2,128)(2,1)} custom-call(s32[2]{0:T(128)S(1)} %pad_add_fusion.place_ref, bf16[64,1280]{1,0:T(8,128)(2,1)S(1)} %collective-permute-done.11.refs_0_, bf16[64,1280]{1,0:T(8,128)(2,1)S(1)} %collective-permute-done.17.refs_1_, bf16[64,5120]{1,0:T(8,128)(2,1)S(1)} %get-tuple-element.65.refs_2_, ...), custom_call_target="tpu_custom_call", output_to_operand_aliasing={{}: (8, {})} | custom-call | tf_op jit(solution)/shard_map/pallas_call | solution.py:348
  (47 shorter events, 4.8 us)
Async XLA Ops:
  1.8 19.1 %collective-permute-start.5 = (bf16[1280,1280]{1,0:T(8,128)(2,1)}, bf16[1280,1280]{1,0:T(8,128)(2,1)S(1)}, u32[]{:S(2)}, u32[]{:S(2)}) collective-permute-start(bf16[1280,1280]{1,0:T(8,128)(2,1)} %refs_2_.7), channel_id=1, source_target_pairs={{0,1},{1,0},{2,3},{3,2},{4,5},{5,4},{6,7},{7,6},{8,9},{9,8},{10,11... | collective-permute-start | bytes 9830408 | tf_op jit(solution)/shard_map/ppermute | solution.py:213
  2.3 12.8 %collective-permute-start.1 = (bf16[528,128]{1,0:T(8,128)(2,1)}, bf16[528,128]{1,0:T(8,128)(2,1)S(1)}, u32[]{:S(2)}, u32[]{:S(2)}) collective-permute-start(bf16[528,128]{1,0:T(8,128)(2,1)} %shard_map.100.refs_1_), channel_id=1, source_target_pairs={{0,4},{4,8},{8,12},{1,5},{5,9},{9,13},{2,6},{6,10},{10,14},{3,7},{... | collective-permute-start | bytes 405512 | tf_op jit(solution)/shard_map/ppermute | solution.py:232
  6.8 8.3 %collective-permute-start.2 = (bf16[528,128]{1,0:T(8,128)(2,1)}, bf16[528,128]{1,0:T(8,128)(2,1)S(1)}, u32[]{:S(2)}, u32[]{:S(2)}) collective-permute-start(bf16[528,128]{1,0:T(8,128)(2,1)} %shard_map.100.refs_1_), channel_id=1, source_target_pairs={{0,8},{4,12},{1,9},{5,13},{2,10},{6,14},{3,11},{7,15},{16,24},{20,... | collective-permute-start | bytes 405512 | tf_op jit(solution)/shard_map/ppermute | solution.py:232
  11.3 3.7 %collective-permute-start = (s32[1,64]{1,0:T(1,128)}, s32[1,64]{1,0:T(1,128)S(1)}, u32[]{:S(2)}, u32[]{:S(2)}) collective-permute-start(s32[1,64]{1,0:T(1,128)} %bitcast.21), channel_id=1, source_target_pairs={{0,2},{2,0},{1,3},{3,1},{4,6},{6,4},{5,7},{7,5},{8,10},{10,8},{9,1... | collective-permute-start | bytes 776 | tf_op jit(solution)/shard_map/ppermute | solution.py:213
  12.9 0.9 %copy-start.8 = (bf16[528,128]{1,0:T(8,128)(2,1)S(1)}, bf16[528,128]{1,0:T(8,128)(2,1)}, u32[]{:S(2)}) copy-start(bf16[528,128]{1,0:T(8,128)(2,1)} %shard_map.100.refs_1_) | copy-start | bytes 405508
  13.8 1.0 %copy-start.9 = (bf16[1,128,10,128]{3,1,2,0:T(8,128)(2,1)S(1)}, bf16[1,128,10,128]{3,1,2,0:T(8,128)(2,1)}, u32[]{:S(2)}) copy-start(bf16[1,128,10,128]{3,1,2,0:T(8,128)(2,1)} %param.10) | copy-start | bytes 983044
  17.8 3.0 %collective-permute-start.4 = (bf16[64,1280]{1,0:T(8,128)(2,1)S(1)}, bf16[64,1280]{1,0:T(8,128)(2,1)S(1)}, u32[]{:S(2)}, u32[]{:S(2)}) collective-permute-start(bf16[64,1280]{1,0:T(8,128)(2,1)S(1)} %get-tuple-element.43), channel_id=1, source_target_pairs={{0,1},{1,0},{2,3},{3,2},{4,5},{5,4},{6,7},{7,6},{8,9},{9,8},{10,11... | collective-permute-start | bytes 491528 | tf_op jit(solution)/shard_map/ppermute | solution.py:213
  17.9 8.3 %copy-start = (bf16[1280,1280]{1,0:T(8,128)(2,1)S(1)}, bf16[1280,1280]{1,0:T(8,128)(2,1)}, u32[]{:S(2)}) copy-start(bf16[1280,1280]{1,0:T(8,128)(2,1)} %refs_2_.7) | copy-start | bytes 9830404
  17.9 10.8 %collective-permute-start.3 = (bf16[64,1280]{1,0:T(8,128)(2,1)S(1)}, bf16[64,1280]{1,0:T(8,128)(2,1)}, u32[]{:S(2)}, u32[]{:S(2)}) collective-permute-start(bf16[64,1280]{1,0:T(8,128)(2,1)S(1)} %get-tuple-element.42.refs_0_), channel_id=1, source_target_pairs={{0,4},{4,8},{8,12},{12,0},{1,5},{5,9},{9,13},{13,1},{2,6},{6,10},{... | collective-permute-start | bytes 491528 | tf_op jit(solution)/shard_map/ppermute | solution.py:213
  20.8 1.7 %copy-start.5 = (bf16[1280,1280]{1,0:T(8,128)(2,1)}, bf16[1280,1280]{1,0:T(8,128)(2,1)S(1)}, u32[]{:S(2)}) copy-start(bf16[1280,1280]{1,0:T(8,128)(2,1)S(1)} %collective-permute-done.5.refs_0_) | copy-start | bytes 9830404
  22.5 9.4 %collective-permute-start.7 = (bf16[64,1280]{1,0:T(8,128)(2,1)S(1)}, bf16[64,1280]{1,0:T(8,128)(2,1)}, u32[]{:S(2)}, u32[]{:S(2)}) collective-permute-start(bf16[64,1280]{1,0:T(8,128)(2,1)S(1)} %collective-permute-done.4.refs_1_), channel_id=1, source_target_pairs={{0,4},{4,8},{8,12},{12,0},{1,5},{5,9},{9,13},{13,1},{2,6},{6,10},{... | collective-permute-start | bytes 491528 | tf_op jit(solution)/shard_map/ppermute | solution.py:213
  23.8 1.9 %copy-start.6 = (bf16[1280,1280]{1,0:T(8,128)(2,1)S(1)}, bf16[1280,1280]{1,0:T(8,128)(2,1)}, u32[]{:S(2)}) copy-start(bf16[1280,1280]{1,0:T(8,128)(2,1)} %copy-done.5) | copy-start | bytes 9830404
  28.7 10.0 %collective-permute-start.6 = (bf16[64,1280]{1,0:T(8,128)(2,1)}, bf16[64,1280]{1,0:T(8,128)(2,1)}, u32[]{:S(2)}, u32[]{:S(2)}) collective-permute-start(bf16[64,1280]{1,0:T(8,128)(2,1)} %collective-permute-done.3.refs_0_), channel_id=1, source_target_pairs={{0,4},{4,8},{8,12},{12,0},{1,5},{5,9},{9,13},{13,1},{2,6},{6,10},{... | collective-permute-start | bytes 491528 | tf_op jit(solution)/shard_map/ppermute | solution.py:213
  32.0 8.7 %collective-permute-start.8 = (bf16[64,1280]{1,0:T(8,128)(2,1)}, bf16[64,1280]{1,0:T(8,128)(2,1)}, u32[]{:S(2)}, u32[]{:S(2)}) collective-permute-start(bf16[64,1280]{1,0:T(8,128)(2,1)} %collective-permute-done.7.refs_1_), channel_id=1, source_target_pairs={{0,4},{4,8},{8,12},{12,0},{1,5},{5,9},{9,13},{13,1},{2,6},{6,10},{... | collective-permute-start | bytes 491528 | tf_op jit(solution)/shard_map/ppermute | solution.py:213
  34.9 9.4 %collective-permute-start.9 = (bf16[64,1280]{1,0:T(8,128)(2,1)}, bf16[64,1280]{1,0:T(8,128)(2,1)}, u32[]{:S(2)}, u32[]{:S(2)}) collective-permute-start(bf16[64,1280]{1,0:T(8,128)(2,1)} %shard_map.105), channel_id=1, source_target_pairs={{0,12},{4,0},{8,4},{12,8},{1,13},{5,1},{9,5},{13,9},{2,14},{6,2},{... | collective-permute-start | bytes 491528 | tf_op jit(solution)/shard_map/ppermute | solution.py:213
  38.7 11.5 %collective-permute-start.12 = (bf16[64,1280]{1,0:T(8,128)(2,1)}, bf16[64,1280]{1,0:T(8,128)(2,1)S(1)}, u32[]{:S(2)}, u32[]{:S(2)}) collective-permute-start(bf16[64,1280]{1,0:T(8,128)(2,1)} %collective-permute-done.6.refs_0_), channel_id=1, source_target_pairs={{0,4},{4,8},{8,12},{12,0},{1,5},{5,9},{9,13},{13,1},{2,6},{6,10},{... | collective-permute-start | bytes 491528 | tf_op jit(solution)/shard_map/ppermute | solution.py:213
  40.6 11.3 %collective-permute-start.13 = (bf16[64,1280]{1,0:T(8,128)(2,1)}, bf16[64,1280]{1,0:T(8,128)(2,1)S(1)}, u32[]{:S(2)}, u32[]{:S(2)}) collective-permute-start(bf16[64,1280]{1,0:T(8,128)(2,1)} %collective-permute-done.8.refs_1_), channel_id=1, source_target_pairs={{0,4},{4,8},{8,12},{12,0},{1,5},{5,9},{9,13},{13,1},{2,6},{6,10},{... | collective-permute-start | bytes 491528 | tf_op jit(solution)/shard_map/ppermute | solution.py:213
  40.6 1.1 %copy-start.3 = (bf16[1,64,5120]{2,1,0:T(8,128)(2,1)S(1)}, bf16[1,64,5120]{2,1,0:T(8,128)(2,1)}, u32[]{:S(2)}) copy-start(bf16[1,64,5120]{2,1,0:T(8,128)(2,1)} %param.14) | copy-start | bytes 1966084
  41.7 8.5 %copy-start.4 = (bf16[1,64,5120]{2,1,0:T(8,128)(2,1)S(1)}, bf16[1,64,5120]{2,1,0:T(8,128)(2,1)}, u32[]{:S(2)}) copy-start(bf16[1,64,5120]{2,1,0:T(8,128)(2,1)} %param.14) | copy-start | bytes 1966084
  41.8 10.1 %collective-permute-start.14 = (bf16[64,1280]{1,0:T(8,128)(2,1)S(1)}, bf16[64,1280]{1,0:T(8,128)(2,1)S(1)}, u32[]{:S(2)}, u32[]{:S(2)}) collective-permute-start(bf16[64,1280]{1,0:T(8,128)(2,1)S(1)} %shard_map.108.refs_0_), channel_id=1, source_target_pairs={{0,2},{2,0},{1,3},{3,1},{4,6},{6,4},{5,7},{7,5},{8,10},{10,8},{9,1... | collective-permute-start | bytes 491528 | tf_op jit(solution)/shard_map/ppermute | solution.py:213
  44.3 1.9 %copy-start.1 = (bf16[1280,1280]{1,0:T(8,128)(2,1)S(1)}, bf16[1280,1280]{1,0:T(8,128)(2,1)}, u32[]{:S(2)}) copy-start(bf16[1280,1280]{1,0:T(8,128)(2,1)} %refs_2_.7) | copy-start | bytes 9830404
  46.2 5.6 %copy-start.2 = (bf16[1280,1280]{1,0:T(8,128)(2,1)S(1)}, bf16[1280,1280]{1,0:T(8,128)(2,1)}, u32[]{:S(2)}) copy-start(bf16[1280,1280]{1,0:T(8,128)(2,1)} %refs_2_.7) | copy-start | bytes 9830404
  48.6 14.0 %collective-permute-start.10 = (bf16[64,1280]{1,0:T(8,128)(2,1)S(1)}, bf16[64,1280]{1,0:T(8,128)(2,1)S(1)}, u32[]{:S(2)}, u32[]{:S(2)}) collective-permute-start(bf16[64,1280]{1,0:T(8,128)(2,1)S(1)} %shard_map.106), channel_id=1, source_target_pairs={{0,8},{4,12},{8,0},{12,4},{1,9},{5,13},{9,1},{13,5},{2,10},{6,14},... | collective-permute-start | bytes 491528 | tf_op jit(solution)/shard_map/ppermute | solution.py:213
  51.1 13.8 %copy-start.12 = (bf16[5120]{0:T(1024)(128)(2,1)S(1)}, bf16[5120]{0:T(1024)(128)(2,1)}, u32[]{:S(2)}) copy-start(bf16[5120]{0:T(1024)(128)(2,1)} %param.16) | copy-start | bytes 30724
  51.2 13.9 %copy-start.10 = (s32[64]{0:T(128)S(1)}, s32[64]{0:T(128)}, u32[]{:S(2)}) copy-start(s32[64]{0:T(128)} %param.19) | copy-start | bytes 772
  51.2 13.9 %copy-start.11 = (s32[1,64,1]{1,2,0:T(1,128)S(1)}, s32[1,64,1]{1,2,0:T(1,128)}, u32[]{:S(2)}) copy-start(s32[1,64,1]{1,2,0:T(1,128)} %param.18) | copy-start | bytes 772
  51.2 13.1 %collective-permute-start.16 = (bf16[64,1280]{1,0:T(8,128)(2,1)S(1)}, bf16[64,1280]{1,0:T(8,128)(2,1)S(1)}, u32[]{:S(2)}, u32[]{:S(2)}) collective-permute-start(bf16[64,1280]{1,0:T(8,128)(2,1)S(1)} %shard_map.110.refs_1_), channel_id=1, source_target_pairs={{0,2},{2,0},{1,3},{3,1},{4,6},{6,4},{5,7},{7,5},{8,10},{10,8},{9,1... | collective-permute-start | bytes 491528 | tf_op jit(solution)/shard_map/ppermute | solution.py:213
  53.1 11.1 %collective-permute-start.15 = (bf16[64,1280]{1,0:T(8,128)(2,1)S(1)}, bf16[64,1280]{1,0:T(8,128)(2,1)S(1)}, u32[]{:S(2)}, u32[]{:S(2)}) collective-permute-start(bf16[64,1280]{1,0:T(8,128)(2,1)S(1)} %shard_map.109), channel_id=1, source_target_pairs={{0,4},{4,8},{8,12},{12,0},{1,5},{5,9},{9,13},{13,1},{2,6},{6,10},{... | collective-permute-start | bytes 491528 | tf_op jit(solution)/shard_map/ppermute | solution.py:213
  62.7 7.1 %collective-permute-start.11 = (bf16[64,1280]{1,0:T(8,128)(2,1)S(1)}, bf16[64,1280]{1,0:T(8,128)(2,1)S(1)}, u32[]{:S(2)}, u32[]{:S(2)}) collective-permute-start(bf16[64,1280]{1,0:T(8,128)(2,1)S(1)} %shard_map.107.refs_0_), channel_id=1, source_target_pairs={{0,2},{2,0},{1,3},{3,1},{4,6},{6,4},{5,7},{7,5},{8,10},{10,8},{9,1... | collective-permute-start | bytes 491528 | tf_op jit(solution)/shard_map/ppermute | solution.py:213
  64.3 8.0 %collective-permute-start.17 = (bf16[64,1280]{1,0:T(8,128)(2,1)S(1)}, bf16[64,1280]{1,0:T(8,128)(2,1)S(1)}, u32[]{:S(2)}, u32[]{:S(2)}) collective-permute-start(bf16[64,1280]{1,0:T(8,128)(2,1)S(1)} %shard_map.112.refs_1_), channel_id=1, source_target_pairs={{0,2},{2,0},{1,3},{3,1},{4,6},{6,4},{5,7},{7,5},{8,10},{10,8},{9,1... | collective-permute-start | bytes 491528 | tf_op jit(solution)/shard_map/ppermute | solution.py:213
  65.0 1.0 %copy-start.7 = (bf16[5120,32]{0,1:T(8,128)(2,1)S(1)}, bf16[5120,32]{0,1:T(8,128)(2,1)}, u32[]{:S(2)}) copy-start(bf16[5120,32]{0,1:T(8,128)(2,1)} %param.17) | copy-start | bytes 983044

commit v4 on v3

--- a/solution.py
+++ b/solution.py
@@ -11,7 +11,7 @@
 CAP = 2
 EPSILON = 1e-05
 DOC_ROWS = 16
-VMEM_LIMIT = 12 * 1024 * 1024
+VMEM_LIMIT = 8 * 1024 * 1024
 VMEM_MOST = 61 * 1024 * 1024
 VMEM_MUCH = 52 * 1024 * 1024
 

time: 75.2 us -> 75.2 us (level)
  no operation moved by 1% of the time
where the time goes in v4:
time: 75.2 us; the launch traced here: 74.8 us
  starting transfers between devices  30.1 us (40%)
  Pallas kernels  19 us (25%)
  waiting for transfers between devices  15.9 us (21%)
  local copies, waits for them, and re-layouts  9.51 us (13%)
    ppermute x16, starting transfers between devices, over(): lax.ppermute(array, axis, [(i, (i + step) % count) for i in range(count)])  21.1 us
    ppermute x16, waiting for transfers between devices, over(): lax.ppermute(array, axis, [(i, (i + step) % count) for i in range(count)])  15.9 us
    unnamed x26, local copies, waits for them, and re-layouts  9.5 us
    ppermute x2, starting transfers between devices, on_device(): lax.ppermute(pack, 'ctx', [(i, i + step) for i in range(ctx_count - step)])  9 us
    pallas_call x4, Pallas kernels, on_device(): total = project(*block, *weights)  7.77 us
    pallas_call x2, Pallas kernels, on_device(): pl.pallas_call(functools.partial(finish_kernel, late_steps, spots, back,...  4.91 us
    pallas_call x1, Pallas kernels, on_device(): pl.pallas_call(functools.partial(attention_kernel, heads // groups, group...  2.73 us
    pallas_call x1, Pallas kernels, on_device(): pl.pallas_call(functools.partial(pack_kernel, groups), out_shape=jax.Shap...  1.77 us
  transfers between devices with their start and end apart: 18, of which 7 were waited for; matrix products, arithmetic and copies ran while one was open for 0% of the time, Pallas kernels for 20%

profile of v4, /device:TPU:0, one launch (start us, length us, event | category | flops | bytes accessed | tf_op | source)
XLA Modules:
  0.0 74.8 jit_solution(9292709477465073622)
XLA Ops:
  0.0 1.8 %shard_map.100.refs_1_ = bf16[528,128]{1,0:T(8,128)(2,1)} custom-call(bf16[256,128]{1,0:T(8,128)(2,1)} %bitcast.23, bf16[256,128]{1,0:T(8,128)(2,1)} %bitcast.24, s32[1,128]{1,0:T(1,128)} %doc_ref.1), custom_call_target="tpu_custom_call" | custom-call | tf_op jit(solution)/shard_map/pallas_call | solution.py:218
  2.3 4.5 %collective-permute-start.1 = (bf16[528,128]{1,0:T(8,128)(2,1)}, bf16[528,128]{1,0:T(8,128)(2,1)S(1)}, u32[]{:S(2)}, u32[]{:S(2)}) collective-permute-start(bf16[528,128]{1,0:T(8,128)(2,1)} %shard_map.100.refs_1_), channel_id=1, source_target_pairs={{0,4},{4,8},{8,12},{1,5},{5,9},{9,13},{2,6},{6,10},{10,14},{3,7},{... | collective-permute-start | bytes 405512 | tf_op jit(solution)/shard_map/ppermute | solution.py:232
  6.8 4.5 %collective-permute-start.2 = (bf16[528,128]{1,0:T(8,128)(2,1)}, bf16[528,128]{1,0:T(8,128)(2,1)S(1)}, u32[]{:S(2)}, u32[]{:S(2)}) collective-permute-start(bf16[528,128]{1,0:T(8,128)(2,1)} %shard_map.100.refs_1_), channel_id=1, source_target_pairs={{0,8},{4,12},{1,9},{5,13},{2,10},{6,14},{3,11},{7,15},{16,24},{20,... | collective-permute-start | bytes 405512 | tf_op jit(solution)/shard_map/ppermute | solution.py:232
  11.3 1.6 %collective-permute-start = (s32[1,64]{1,0:T(1,128)}, s32[1,64]{1,0:T(1,128)S(1)}, u32[]{:S(2)}, u32[]{:S(2)}) collective-permute-start(s32[1,64]{1,0:T(1,128)} %bitcast.21), channel_id=1, source_target_pairs={{0,2},{2,0},{1,3},{3,1},{4,6},{6,4},{5,7},{7,5},{8,10},{10,8},{9,1... | collective-permute-start | bytes 776 | tf_op jit(solution)/shard_map/ppermute | solution.py:213
  13.8 1.0 %copy-done.9 = bf16[1,128,10,128]{3,1,2,0:T(8,128)(2,1)S(1)} copy-done((bf16[1,128,10,128]{3,1,2,0:T(8,128)(2,1)S(1)}, bf16[1,128,10,128]{3,1,2,0:T(8,128)(2,1)}, u32[]{:S(2)}) %copy-start.9) | copy-done | bytes 327704
  15.1 2.7 %shard_map.102 = (bf16[64,1280]{1,0:T(8,128)(2,1)S(1)}, bf16[64,1280]{1,0:T(8,128)(2,1)S(1)}) custom-call(s32[1]{0:T(128)} %bitcast.3.place_ref, bf16[10,128,128]{2,1,0:T(8,128)(2,1)S(1)} %get-tuple-element.40.query_ref, bf16[528,128]{1,0:T(8,128)(2,1)S(1)} %get-tuple-element.41.refs_0_, bf16[528,128]{1,0:T(8,128)(2,1)S(1)} %collective-permute-done.1.refs_1_, ...), custom_call_target="tpu_custom_call" | custom-call | tf_op jit(solution)/shard_map/pallas_call | solution.py:253
  17.9 2.9 %collective-permute-start.3 = (bf16[64,1280]{1,0:T(8,128)(2,1)S(1)}, bf16[64,1280]{1,0:T(8,128)(2,1)}, u32[]{:S(2)}, u32[]{:S(2)}) collective-permute-start(bf16[64,1280]{1,0:T(8,128)(2,1)S(1)} %get-tuple-element.42.refs_0_), channel_id=1, source_target_pairs={{0,4},{4,8},{8,12},{12,0},{1,5},{5,9},{9,13},{13,1},{2,6},{6,10},{... | collective-permute-start | bytes 491528 | tf_op jit(solution)/shard_map/ppermute | solution.py:213
  20.8 1.7 %copy-done.5 = bf16[1280,1280]{1,0:T(8,128)(2,1)} copy-done((bf16[1280,1280]{1,0:T(8,128)(2,1)}, bf16[1280,1280]{1,0:T(8,128)(2,1)S(1)}, u32[]{:S(2)}) %copy-start.5) | copy-done | bytes 3276824
  22.5 1.3 %collective-permute-start.7 = (bf16[64,1280]{1,0:T(8,128)(2,1)S(1)}, bf16[64,1280]{1,0:T(8,128)(2,1)}, u32[]{:S(2)}, u32[]{:S(2)}) collective-permute-start(bf16[64,1280]{1,0:T(8,128)(2,1)S(1)} %collective-permute-done.4.refs_1_), channel_id=1, source_target_pairs={{0,4},{4,8},{8,12},{12,0},{1,5},{5,9},{9,13},{13,1},{2,6},{6,10},{... | collective-permute-start | bytes 491528 | tf_op jit(solution)/shard_map/ppermute | solution.py:213
  23.8 1.9 %copy-done.6 = bf16[1280,1280]{1,0:T(8,128)(2,1)S(1)} copy-done((bf16[1280,1280]{1,0:T(8,128)(2,1)S(1)}, bf16[1280,1280]{1,0:T(8,128)(2,1)}, u32[]{:S(2)}) %copy-start.6) | copy-done | bytes 3276824
  26.2 1.2 %shard_map.104.chunk_ref = bf16[64,1280]{1,0:T(8,128)(2,1)S(1)} custom-call(bf16[64,1280]{1,0:T(8,128)(2,1)S(1)} %get-tuple-element.42.refs_0_, bf16[64,1280]{1,0:T(8,128)(2,1)S(1)} %collective-permute-done.4.refs_1_, bf16[1280,1280]{1,0:T(8,128)(2,1)S(1)} %copy-done, bf16[1280,1280]{1,0:T(8,128)(2,1)S(1)} %shard_map.103.refs_3_), custom_call_target="tpu_custom_call" | custom-call | flops 419430400 | bytes 6553600 | tf_op jit(solution)/shard_map/pallas_call | solution.py:318
  27.4 1.3 %collective-permute-done.3.refs_0_ = bf16[64,1280]{1,0:T(8,128)(2,1)} collective-permute-done((bf16[64,1280]{1,0:T(8,128)(2,1)S(1)}, bf16[64,1280]{1,0:T(8,128)(2,1)}, u32[]{:S(2)}, u32[]{:S(2)}) %collective-permute-start.3) | collective-permute-done | bytes 163872 | tf_op jit(solution)/shard_map/ppermute | solution.py:213
  28.7 1.3 %collective-permute-start.6 = (bf16[64,1280]{1,0:T(8,128)(2,1)}, bf16[64,1280]{1,0:T(8,128)(2,1)}, u32[]{:S(2)}, u32[]{:S(2)}) collective-permute-start(bf16[64,1280]{1,0:T(8,128)(2,1)} %collective-permute-done.3.refs_0_), channel_id=1, source_target_pairs={{0,4},{4,8},{8,12},{12,0},{1,5},{5,9},{9,13},{13,1},{2,6},{6,10},{... | collective-permute-start | bytes 491528 | tf_op jit(solution)/shard_map/ppermute | solution.py:213
  30.0 2.0 %collective-permute-done.7.refs_1_ = bf16[64,1280]{1,0:T(8,128)(2,1)} collective-permute-done((bf16[64,1280]{1,0:T(8,128)(2,1)S(1)}, bf16[64,1280]{1,0:T(8,128)(2,1)}, u32[]{:S(2)}, u32[]{:S(2)}) %collective-permute-start.7) | collective-permute-done | bytes 163872 | tf_op jit(solution)/shard_map/ppermute | solution.py:213
  32.0 2.9 %shard_map.105 = bf16[64,1280]{1,0:T(8,128)(2,1)} custom-call(bf16[64,1280]{1,0:T(8,128)(2,1)} %collective-permute-done.3.refs_0_, bf16[64,1280]{1,0:T(8,128)(2,1)} %collective-permute-done.7.refs_1_, bf16[1280,1280]{1,0:T(8,128)(2,1)S(1)} %copy-done, bf16[1280,1280]{1,0:T(8,128)(2,1)S(1)} %shard_map.103.refs_3_), custom_call_target="tpu_custom_call" | custom-call | flops 419430400 | bytes 6553600 | tf_op jit(solution)/shard_map/pallas_call | solution.py:318
  34.9 3.8 %collective-permute-start.9 = (bf16[64,1280]{1,0:T(8,128)(2,1)}, bf16[64,1280]{1,0:T(8,128)(2,1)}, u32[]{:S(2)}, u32[]{:S(2)}) collective-permute-start(bf16[64,1280]{1,0:T(8,128)(2,1)} %shard_map.105), channel_id=1, source_target_pairs={{0,12},{4,0},{8,4},{12,8},{1,13},{5,1},{9,5},{13,9},{2,14},{6,2},{... | collective-permute-start | bytes 491528 | tf_op jit(solution)/shard_map/ppermute | solution.py:213
  38.7 1.9 %collective-permute-done.8.refs_1_ = bf16[64,1280]{1,0:T(8,128)(2,1)} collective-permute-done((bf16[64,1280]{1,0:T(8,128)(2,1)}, bf16[64,1280]{1,0:T(8,128)(2,1)}, u32[]{:S(2)}, u32[]{:S(2)}) %collective-permute-start.8) | collective-permute-done | bytes 163872 | tf_op jit(solution)/shard_map/ppermute | solution.py:213
  40.6 1.1 %copy-done.3 = bf16[1,64,5120]{2,1,0:T(8,128)(2,1)S(1)} copy-done((bf16[1,64,5120]{2,1,0:T(8,128)(2,1)S(1)}, bf16[1,64,5120]{2,1,0:T(8,128)(2,1)}, u32[]{:S(2)}) %copy-start.3) | copy-done | bytes 655384
  41.8 1.6 %collective-permute-start.14 = (bf16[64,1280]{1,0:T(8,128)(2,1)S(1)}, bf16[64,1280]{1,0:T(8,128)(2,1)S(1)}, u32[]{:S(2)}, u32[]{:S(2)}) collective-permute-start(bf16[64,1280]{1,0:T(8,128)(2,1)S(1)} %shard_map.108.refs_0_), channel_id=1, source_target_pairs={{0,2},{2,0},{1,3},{3,1},{4,6},{6,4},{5,7},{7,5},{8,10},{10,8},{9,1... | collective-permute-start | bytes 491528 | tf_op jit(solution)/shard_map/ppermute | solution.py:213
  43.3 1.0 %collective-permute-done.9.chunk_ref = bf16[64,1280]{1,0:T(8,128)(2,1)} collective-permute-done((bf16[64,1280]{1,0:T(8,128)(2,1)}, bf16[64,1280]{1,0:T(8,128)(2,1)}, u32[]{:S(2)}, u32[]{:S(2)}) %collective-permute-start.9) | collective-permute-done | bytes 163872 | tf_op jit(solution)/shard_map/ppermute | solution.py:213
  44.3 1.9 %copy-done.1 = bf16[1280,1280]{1,0:T(8,128)(2,1)S(1)} copy-done((bf16[1280,1280]{1,0:T(8,128)(2,1)S(1)}, bf16[1280,1280]{1,0:T(8,128)(2,1)}, u32[]{:S(2)}) %copy-start.1) | copy-done | bytes 3276824
  46.3 2.4 %shard_map.106 = bf16[64,1280]{1,0:T(8,128)(2,1)S(1)} custom-call(bf16[64,1280]{1,0:T(8,128)(2,1)} %collective-permute-done.6.refs_0_, bf16[64,1280]{1,0:T(8,128)(2,1)} %collective-permute-done.8.refs_1_, bf16[1280,1280]{1,0:T(8,128)(2,1)S(1)} %copy-done.1, bf16[1280,1280]{1,0:T(8,128)(2,1)S(1)} %shard_map.103.refs_3_), custom_call_target="tpu_custom_call" | custom-call | flops 419430400 | bytes 6553600 | tf_op jit(solution)/shard_map/pallas_call | solution.py:318
  48.6 1.5 %collective-permute-start.10 = (bf16[64,1280]{1,0:T(8,128)(2,1)S(1)}, bf16[64,1280]{1,0:T(8,128)(2,1)S(1)}, u32[]{:S(2)}, u32[]{:S(2)}) collective-permute-start(bf16[64,1280]{1,0:T(8,128)(2,1)S(1)} %shard_map.106), channel_id=1, source_target_pairs={{0,8},{4,12},{8,0},{12,4},{1,9},{5,13},{9,1},{13,5},{2,10},{6,14},... | collective-permute-start | bytes 491528 | tf_op jit(solution)/shard_map/ppermute | solution.py:213
  51.9 1.2 %shard_map.109 = bf16[64,1280]{1,0:T(8,128)(2,1)S(1)} custom-call(bf16[64,1280]{1,0:T(8,128)(2,1)S(1)} %collective-permute-done.12.refs_0_, bf16[64,1280]{1,0:T(8,128)(2,1)S(1)} %collective-permute-done.13.refs_1_, bf16[1280,1280]{1,0:T(8,128)(2,1)S(1)} %copy-done.2, bf16[1280,1280]{1,0:T(8,128)(2,1)S(1)} %shard_map.103.refs_3_), custom_call_target="tpu_custom_call" | custom-call | flops 419430400 | bytes 6553600 | tf_op jit(solution)/shard_map/pallas_call | solution.py:318
  53.1 3.7 %collective-permute-start.15 = (bf16[64,1280]{1,0:T(8,128)(2,1)S(1)}, bf16[64,1280]{1,0:T(8,128)(2,1)S(1)}, u32[]{:S(2)}, u32[]{:S(2)}) collective-permute-start(bf16[64,1280]{1,0:T(8,128)(2,1)S(1)} %shard_map.109), channel_id=1, source_target_pairs={{0,4},{4,8},{8,12},{12,0},{1,5},{5,9},{9,13},{13,1},{2,6},{6,10},{... | collective-permute-start | bytes 491528 | tf_op jit(solution)/shard_map/ppermute | solution.py:213
  56.8 5.8 %collective-permute-done.10.chunk_ref = bf16[64,1280]{1,0:T(8,128)(2,1)S(1)} collective-permute-done((bf16[64,1280]{1,0:T(8,128)(2,1)S(1)}, bf16[64,1280]{1,0:T(8,128)(2,1)S(1)}, u32[]{:S(2)}, u32[]{:S(2)}) %collective-permute-start.10) | collective-permute-done | bytes 163872 | tf_op jit(solution)/shard_map/ppermute | solution.py:213
  62.7 1.6 %collective-permute-start.11 = (bf16[64,1280]{1,0:T(8,128)(2,1)S(1)}, bf16[64,1280]{1,0:T(8,128)(2,1)S(1)}, u32[]{:S(2)}, u32[]{:S(2)}) collective-permute-start(bf16[64,1280]{1,0:T(8,128)(2,1)S(1)} %shard_map.107.refs_0_), channel_id=1, source_target_pairs={{0,2},{2,0},{1,3},{3,1},{4,6},{6,4},{5,7},{7,5},{8,10},{10,8},{9,1... | collective-permute-start | bytes 491528 | tf_op jit(solution)/shard_map/ppermute | solution.py:213
  65.1 1.0 %copy-done.7 = bf16[5120,32]{0,1:T(8,128)(2,1)S(1)} copy-done((bf16[5120,32]{0,1:T(8,128)(2,1)S(1)}, bf16[5120,32]{0,1:T(8,128)(2,1)}, u32[]{:S(2)}) %copy-start.7) | copy-done | bytes 327704
  66.0 2.5 %shard_map.113.refs_7_ = bf16[2,32,2,5120]{3,2,1,0:T(2,128)(2,1)} custom-call(s32[2]{0:T(128)S(1)} %pad_add_fusion.place_ref, bf16[64,1280]{1,0:T(8,128)(2,1)S(1)} %shard_map.107.refs_0_, bf16[64,1280]{1,0:T(8,128)(2,1)S(1)} %shard_map.112.refs_1_, bf16[64,5120]{1,0:T(8,128)(2,1)S(1)} %get-tuple-element.67.refs_2_, s32[1,64]{1,0:T(1,128)S(1)} %bitcast.22, ...), custom_call_target="tpu_custom_call" | custom-call | tf_op jit(solution)/shard_map/pallas_call | solution.py:348
  68.5 1.3 %collective-permute-done.11.refs_0_ = bf16[64,1280]{1,0:T(8,128)(2,1)S(1)} collective-permute-done((bf16[64,1280]{1,0:T(8,128)(2,1)S(1)}, bf16[64,1280]{1,0:T(8,128)(2,1)S(1)}, u32[]{:S(2)}, u32[]{:S(2)}) %collective-permute-start.11) | collective-permute-done | bytes 163872 | tf_op jit(solution)/shard_map/ppermute | solution.py:213
  69.8 2.5 %collective-permute-done.17.refs_1_ = bf16[64,1280]{1,0:T(8,128)(2,1)S(1)} collective-permute-done((bf16[64,1280]{1,0:T(8,128)(2,1)S(1)}, bf16[64,1280]{1,0:T(8,128)(2,1)S(1)}, u32[]{:S(2)}, u32[]{:S(2)}) %collective-permute-start.17) | collective-permute-done | bytes 163872 | tf_op jit(solution)/shard_map/ppermute | solution.py:213
  72.3 2.5 %shard_map.114 = bf16[2,32,2,5120]{3,2,1,0:T(2,128)(2,1)} custom-call(s32[2]{0:T(128)S(1)} %pad_add_fusion.place_ref, bf16[64,1280]{1,0:T(8,128)(2,1)S(1)} %collective-permute-done.11.refs_0_, bf16[64,1280]{1,0:T(8,128)(2,1)S(1)} %collective-permute-done.17.refs_1_, bf16[64,5120]{1,0:T(8,128)(2,1)S(1)} %get-tuple-element.65.refs_2_, ...), custom_call_target="tpu_custom_call", output_to_operand_aliasing={{}: (8, {})} | custom-call | tf_op jit(solution)/shard_map/pallas_call | solution.py:348
  (47 shorter events, 4.8 us)
Async XLA Ops:
  1.8 19.1 %collective-permute-start.5 = (bf16[1280,1280]{1,0:T(8,128)(2,1)}, bf16[1280,1280]{1,0:T(8,128)(2,1)S(1)}, u32[]{:S(2)}, u32[]{:S(2)}) collective-permute-start(bf16[1280,1280]{1,0:T(8,128)(2,1)} %refs_2_.7), channel_id=1, source_target_pairs={{0,1},{1,0},{2,3},{3,2},{4,5},{5,4},{6,7},{7,6},{8,9},{9,8},{10,11... | collective-permute-start | bytes 9830408 | tf_op jit(solution)/shard_map/ppermute | solution.py:213
  2.3 12.8 %collective-permute-start.1 = (bf16[528,128]{1,0:T(8,128)(2,1)}, bf16[528,128]{1,0:T(8,128)(2,1)S(1)}, u32[]{:S(2)}, u32[]{:S(2)}) collective-permute-start(bf16[528,128]{1,0:T(8,128)(2,1)} %shard_map.100.refs_1_), channel_id=1, source_target_pairs={{0,4},{4,8},{8,12},{1,5},{5,9},{9,13},{2,6},{6,10},{10,14},{3,7},{... | collective-permute-start | bytes 405512 | tf_op jit(solution)/shard_map/ppermute | solution.py:232
  6.8 8.3 %collective-permute-start.2 = (bf16[528,128]{1,0:T(8,128)(2,1)}, bf16[528,128]{1,0:T(8,128)(2,1)S(1)}, u32[]{:S(2)}, u32[]{:S(2)}) collective-permute-start(bf16[528,128]{1,0:T(8,128)(2,1)} %shard_map.100.refs_1_), channel_id=1, source_target_pairs={{0,8},{4,12},{1,9},{5,13},{2,10},{6,14},{3,11},{7,15},{16,24},{20,... | collective-permute-start | bytes 405512 | tf_op jit(solution)/shard_map/ppermute | solution.py:232
  11.3 3.7 %collective-permute-start = (s32[1,64]{1,0:T(1,128)}, s32[1,64]{1,0:T(1,128)S(1)}, u32[]{:S(2)}, u32[]{:S(2)}) collective-permute-start(s32[1,64]{1,0:T(1,128)} %bitcast.21), channel_id=1, source_target_pairs={{0,2},{2,0},{1,3},{3,1},{4,6},{6,4},{5,7},{7,5},{8,10},{10,8},{9,1... | collective-permute-start | bytes 776 | tf_op jit(solution)/shard_map/ppermute | solution.py:213
  12.9 0.9 %copy-start.8 = (bf16[528,128]{1,0:T(8,128)(2,1)S(1)}, bf16[528,128]{1,0:T(8,128)(2,1)}, u32[]{:S(2)}) copy-start(bf16[528,128]{1,0:T(8,128)(2,1)} %shard_map.100.refs_1_) | copy-start | bytes 405508
  13.8 1.0 %copy-start.9 = (bf16[1,128,10,128]{3,1,2,0:T(8,128)(2,1)S(1)}, bf16[1,128,10,128]{3,1,2,0:T(8,128)(2,1)}, u32[]{:S(2)}) copy-start(bf16[1,128,10,128]{3,1,2,0:T(8,128)(2,1)} %param.10) | copy-start | bytes 983044
  17.8 3.0 %collective-permute-start.4 = (bf16[64,1280]{1,0:T(8,128)(2,1)S(1)}, bf16[64,1280]{1,0:T(8,128)(2,1)S(1)}, u32[]{:S(2)}, u32[]{:S(2)}) collective-permute-start(bf16[64,1280]{1,0:T(8,128)(2,1)S(1)} %get-tuple-element.43), channel_id=1, source_target_pairs={{0,1},{1,0},{2,3},{3,2},{4,5},{5,4},{6,7},{7,6},{8,9},{9,8},{10,11... | collective-permute-start | bytes 491528 | tf_op jit(solution)/shard_map/ppermute | solution.py:213
  17.9 8.3 %copy-start = (bf16[1280,1280]{1,0:T(8,128)(2,1)S(1)}, bf16[1280,1280]{1,0:T(8,128)(2,1)}, u32[]{:S(2)}) copy-start(bf16[1280,1280]{1,0:T(8,128)(2,1)} %refs_2_.7) | copy-start | bytes 9830404
  17.9 10.8 %collective-permute-start.3 = (bf16[64,1280]{1,0:T(8,128)(2,1)S(1)}, bf16[64,1280]{1,0:T(8,128)(2,1)}, u32[]{:S(2)}, u32[]{:S(2)}) collective-permute-start(bf16[64,1280]{1,0:T(8,128)(2,1)S(1)} %get-tuple-element.42.refs_0_), channel_id=1, source_target_pairs={{0,4},{4,8},{8,12},{12,0},{1,5},{5,9},{9,13},{13,1},{2,6},{6,10},{... | collective-permute-start | bytes 491528 | tf_op jit(solution)/shard_map/ppermute | solution.py:213
  20.8 1.7 %copy-start.5 = (bf16[1280,1280]{1,0:T(8,128)(2,1)}, bf16[1280,1280]{1,0:T(8,128)(2,1)S(1)}, u32[]{:S(2)}) copy-start(bf16[1280,1280]{1,0:T(8,128)(2,1)S(1)} %collective-permute-done.5.refs_0_) | copy-start | bytes 9830404
  22.5 9.4 %collective-permute-start.7 = (bf16[64,1280]{1,0:T(8,128)(2,1)S(1)}, bf16[64,1280]{1,0:T(8,128)(2,1)}, u32[]{:S(2)}, u32[]{:S(2)}) collective-permute-start(bf16[64,1280]{1,0:T(8,128)(2,1)S(1)} %collective-permute-done.4.refs_1_), channel_id=1, source_target_pairs={{0,4},{4,8},{8,12},{12,0},{1,5},{5,9},{9,13},{13,1},{2,6},{6,10},{... | collective-permute-start | bytes 491528 | tf_op jit(solution)/shard_map/ppermute | solution.py:213
  23.8 1.9 %copy-start.6 = (bf16[1280,1280]{1,0:T(8,128)(2,1)S(1)}, bf16[1280,1280]{1,0:T(8,128)(2,1)}, u32[]{:S(2)}) copy-start(bf16[1280,1280]{1,0:T(8,128)(2,1)} %copy-done.5) | copy-start | bytes 9830404
  28.7 10.0 %collective-permute-start.6 = (bf16[64,1280]{1,0:T(8,128)(2,1)}, bf16[64,1280]{1,0:T(8,128)(2,1)}, u32[]{:S(2)}, u32[]{:S(2)}) collective-permute-start(bf16[64,1280]{1,0:T(8,128)(2,1)} %collective-permute-done.3.refs_0_), channel_id=1, source_target_pairs={{0,4},{4,8},{8,12},{12,0},{1,5},{5,9},{9,13},{13,1},{2,6},{6,10},{... | collective-permute-start | bytes 491528 | tf_op jit(solution)/shard_map/ppermute | solution.py:213
  32.0 8.7 %collective-permute-start.8 = (bf16[64,1280]{1,0:T(8,128)(2,1)}, bf16[64,1280]{1,0:T(8,128)(2,1)}, u32[]{:S(2)}, u32[]{:S(2)}) collective-permute-start(bf16[64,1280]{1,0:T(8,128)(2,1)} %collective-permute-done.7.refs_1_), channel_id=1, source_target_pairs={{0,4},{4,8},{8,12},{12,0},{1,5},{5,9},{9,13},{13,1},{2,6},{6,10},{... | collective-permute-start | bytes 491528 | tf_op jit(solution)/shard_map/ppermute | solution.py:213
  34.9 9.4 %collective-permute-start.9 = (bf16[64,1280]{1,0:T(8,128)(2,1)}, bf16[64,1280]{1,0:T(8,128)(2,1)}, u32[]{:S(2)}, u32[]{:S(2)}) collective-permute-start(bf16[64,1280]{1,0:T(8,128)(2,1)} %shard_map.105), channel_id=1, source_target_pairs={{0,12},{4,0},{8,4},{12,8},{1,13},{5,1},{9,5},{13,9},{2,14},{6,2},{... | collective-permute-start | bytes 491528 | tf_op jit(solution)/shard_map/ppermute | solution.py:213
  38.7 11.5 %collective-permute-start.12 = (bf16[64,1280]{1,0:T(8,128)(2,1)}, bf16[64,1280]{1,0:T(8,128)(2,1)S(1)}, u32[]{:S(2)}, u32[]{:S(2)}) collective-permute-start(bf16[64,1280]{1,0:T(8,128)(2,1)} %collective-permute-done.6.refs_0_), channel_id=1, source_target_pairs={{0,4},{4,8},{8,12},{12,0},{1,5},{5,9},{9,13},{13,1},{2,6},{6,10},{... | collective-permute-start | bytes 491528 | tf_op jit(solution)/shard_map/ppermute | solution.py:213
  40.6 11.3 %collective-permute-start.13 = (bf16[64,1280]{1,0:T(8,128)(2,1)}, bf16[64,1280]{1,0:T(8,128)(2,1)S(1)}, u32[]{:S(2)}, u32[]{:S(2)}) collective-permute-start(bf16[64,1280]{1,0:T(8,128)(2,1)} %collective-permute-done.8.refs_1_), channel_id=1, source_target_pairs={{0,4},{4,8},{8,12},{12,0},{1,5},{5,9},{9,13},{13,1},{2,6},{6,10},{... | collective-permute-start | bytes 491528 | tf_op jit(solution)/shard_map/ppermute | solution.py:213
  40.6 1.1 %copy-start.3 = (bf16[1,64,5120]{2,1,0:T(8,128)(2,1)S(1)}, bf16[1,64,5120]{2,1,0:T(8,128)(2,1)}, u32[]{:S(2)}) copy-start(bf16[1,64,5120]{2,1,0:T(8,128)(2,1)} %param.14) | copy-start | bytes 1966084
  41.7 8.5 %copy-start.4 = (bf16[1,64,5120]{2,1,0:T(8,128)(2,1)S(1)}, bf16[1,64,5120]{2,1,0:T(8,128)(2,1)}, u32[]{:S(2)}) copy-start(bf16[1,64,5120]{2,1,0:T(8,128)(2,1)} %param.14) | copy-start | bytes 1966084
  41.8 10.1 %collective-permute-start.14 = (bf16[64,1280]{1,0:T(8,128)(2,1)S(1)}, bf16[64,1280]{1,0:T(8,128)(2,1)S(1)}, u32[]{:S(2)}, u32[]{:S(2)}) collective-permute-start(bf16[64,1280]{1,0:T(8,128)(2,1)S(1)} %shard_map.108.refs_0_), channel_id=1, source_target_pairs={{0,2},{2,0},{1,3},{3,1},{4,6},{6,4},{5,7},{7,5},{8,10},{10,8},{9,1... | collective-permute-start | bytes 491528 | tf_op jit(solution)/shard_map/ppermute | solution.py:213
  44.3 1.9 %copy-start.1 = (bf16[1280,1280]{1,0:T(8,128)(2,1)S(1)}, bf16[1280,1280]{1,0:T(8,128)(2,1)}, u32[]{:S(2)}) copy-start(bf16[1280,1280]{1,0:T(8,128)(2,1)} %refs_2_.7) | copy-start | bytes 9830404
  46.2 5.6 %copy-start.2 = (bf16[1280,1280]{1,0:T(8,128)(2,1)S(1)}, bf16[1280,1280]{1,0:T(8,128)(2,1)}, u32[]{:S(2)}) copy-start(bf16[1280,1280]{1,0:T(8,128)(2,1)} %refs_2_.7) | copy-start | bytes 9830404
  48.6 14.0 %collective-permute-start.10 = (bf16[64,1280]{1,0:T(8,128)(2,1)S(1)}, bf16[64,1280]{1,0:T(8,128)(2,1)S(1)}, u32[]{:S(2)}, u32[]{:S(2)}) collective-permute-start(bf16[64,1280]{1,0:T(8,128)(2,1)S(1)} %shard_map.106), channel_id=1, source_target_pairs={{0,8},{4,12},{8,0},{12,4},{1,9},{5,13},{9,1},{13,5},{2,10},{6,14},... | collective-permute-start | bytes 491528 | tf_op jit(solution)/shard_map/ppermute | solution.py:213
  51.1 13.8 %copy-start.12 = (bf16[5120]{0:T(1024)(128)(2,1)S(1)}, bf16[5120]{0:T(1024)(128)(2,1)}, u32[]{:S(2)}) copy-start(bf16[5120]{0:T(1024)(128)(2,1)} %param.16) | copy-start | bytes 30724
  51.2 13.9 %copy-start.10 = (s32[64]{0:T(128)S(1)}, s32[64]{0:T(128)}, u32[]{:S(2)}) copy-start(s32[64]{0:T(128)} %param.19) | copy-start | bytes 772
  51.2 13.9 %copy-start.11 = (s32[1,64,1]{1,2,0:T(1,128)S(1)}, s32[1,64,1]{1,2,0:T(1,128)}, u32[]{:S(2)}) copy-start(s32[1,64,1]{1,2,0:T(1,128)} %param.18) | copy-start | bytes 772
  51.2 13.1 %collective-permute-start.16 = (bf16[64,1280]{1,0:T(8,128)(2,1)S(1)}, bf16[64,1280]{1,0:T(8,128)(2,1)S(1)}, u32[]{:S(2)}, u32[]{:S(2)}) collective-permute-start(bf16[64,1280]{1,0:T(8,128)(2,1)S(1)} %shard_map.110.refs_1_), channel_id=1, source_target_pairs={{0,2},{2,0},{1,3},{3,1},{4,6},{6,4},{5,7},{7,5},{8,10},{10,8},{9,1... | collective-permute-start | bytes 491528 | tf_op jit(solution)/shard_map/ppermute | solution.py:213
  53.1 11.1 %collective-permute-start.15 = (bf16[64,1280]{1,0:T(8,128)(2,1)S(1)}, bf16[64,1280]{1,0:T(8,128)(2,1)S(1)}, u32[]{:S(2)}, u32[]{:S(2)}) collective-permute-start(bf16[64,1280]{1,0:T(8,128)(2,1)S(1)} %shard_map.109), channel_id=1, source_target_pairs={{0,4},{4,8},{8,12},{12,0},{1,5},{5,9},{9,13},{13,1},{2,6},{6,10},{... | collective-permute-start | bytes 491528 | tf_op jit(solution)/shard_map/ppermute | solution.py:213
  62.7 7.1 %collective-permute-start.11 = (bf16[64,1280]{1,0:T(8,128)(2,1)S(1)}, bf16[64,1280]{1,0:T(8,128)(2,1)S(1)}, u32[]{:S(2)}, u32[]{:S(2)}) collective-permute-start(bf16[64,1280]{1,0:T(8,128)(2,1)S(1)} %shard_map.107.refs_0_), channel_id=1, source_target_pairs={{0,2},{2,0},{1,3},{3,1},{4,6},{6,4},{5,7},{7,5},{8,10},{10,8},{9,1... | collective-permute-start | bytes 491528 | tf_op jit(solution)/shard_map/ppermute | solution.py:213
  64.3 8.0 %collective-permute-start.17 = (bf16[64,1280]{1,0:T(8,128)(2,1)S(1)}, bf16[64,1280]{1,0:T(8,128)(2,1)S(1)}, u32[]{:S(2)}, u32[]{:S(2)}) collective-permute-start(bf16[64,1280]{1,0:T(8,128)(2,1)S(1)} %shard_map.112.refs_1_), channel_id=1, source_target_pairs={{0,2},{2,0},{1,3},{3,1},{4,6},{6,4},{5,7},{7,5},{8,10},{10,8},{9,1... | collective-permute-start | bytes 491528 | tf_op jit(solution)/shard_map/ppermute | solution.py:213
  65.0 1.0 %copy-start.7 = (bf16[5120,32]{0,1:T(8,128)(2,1)S(1)}, bf16[5120,32]{0,1:T(8,128)(2,1)}, u32[]{:S(2)}) copy-start(bf16[5120,32]{0,1:T(8,128)(2,1)} %param.17) | copy-start | bytes 983044

commit v5 on v3

--- a/solution.py
+++ b/solution.py
@@ -233,10 +233,8 @@
         for step in range(1, reach + 1)
     ]
     ids, own_residual = expert_ids[:, :, 0], residual[0]
-    pack, own_queries, early_weights = lax.optimization_barrier(
-        (pack, queries[0].transpose(1, 0, 2), out_proj)
-    )
-    weights = [out_proj] + [over(early_weights, "tp", turn) for turn in range(1, pair)]
+    weights = [over(out_proj, "tp", turn) for turn in range(pair)]
+    pack, own_queries = lax.optimization_barrier((pack, queries[0].transpose(1, 0, 2)))
     staged_queries, packs[0] = pl.pallas_call(
         functools.partial(stage_kernel, 2),
         out_shape=[
@@ -271,15 +269,15 @@
         ),
     )
     block = [over(pieces[turn], "tp", turn) for turn in range(pair)]
-    block[-1], swapped = lax.optimization_barrier((block[-1], weights[1:]))
-    weights = weights[:1] + [*pl.pallas_call(
-        functools.partial(stage_kernel, pair - 1),
-        out_shape=[jax.ShapeDtypeStruct(out_proj.shape, bf16)] * (pair - 1),
-        in_specs=[anywhere] * (pair - 1),
-        out_specs=[vmem] * (pair - 1),
-        scratch_shapes=[pltpu.SemaphoreType.DMA((pair - 1,))],
+    block[-1], weights = lax.optimization_barrier((block[-1], weights))
+    weights = pl.pallas_call(
+        functools.partial(stage_kernel, pair),
+        out_shape=[jax.ShapeDtypeStruct(out_proj.shape, bf16)] * pair,
+        in_specs=[anywhere] * pair,
+        out_specs=[vmem] * pair,
+        scratch_shapes=[pltpu.SemaphoreType.DMA((pair,))],
         compiler_params=params,
-    )(*swapped)]
+    )(*weights)
 
     aligned = columns % 128 == 0
     hidden = None

time: 75.2 us -> 75 us (level)
  Pallas kernels: 19 us -> 20.9 us
  local copies, waits for them, and re-layouts: 9.51 us -> 7.84 us
  waiting for transfers between devices: 15.9 us -> 14.9 us
    pallas_call x1, Pallas kernels: 0.39 us -> 2.32 us  [on_device(): pl.pallas_call(functools.partial(stage_kernel, pair), out_shape=[jax.Shap...]
    unnamed x26, local copies, waits for them, and re-layouts: 9.5 us -> 7.83 us
    ppermute x16, waiting for transfers between devices: 15.9 us -> 14.9 us  [over(): lax.ppermute(array, axis, [(i, (i + step) % count) for i in range(count)])]
  transfers between devices with their start and end apart: 18 -> 18, of which waited for: 7 -> 7; matrix products, arithmetic and copies ran while one was open for 0% -> 0% of each run, Pallas kernels for 20% -> 25%
where the time goes in v5:
time: 75 us; the launch traced here: 74.5 us
  starting transfers between devices  30.5 us (41%)
  Pallas kernels  20.9 us (28%)
  waiting for transfers between devices  14.9 us (20%)
  local copies, waits for them, and re-layouts  7.84 us (10%)
    ppermute x16, starting transfers between devices, over(): lax.ppermute(array, axis, [(i, (i + step) % count) for i in range(count)])  21.5 us
    ppermute x16, waiting for transfers between devices, over(): lax.ppermute(array, axis, [(i, (i + step) % count) for i in range(count)])  14.9 us
    ppermute x2, starting transfers between devices, on_device(): lax.ppermute(pack, 'ctx', [(i, i + step) for i in range(ctx_count - step)])  8.98 us
    unnamed x26, local copies, waits for them, and re-layouts  7.83 us
    pallas_call x4, Pallas kernels, on_device(): total = project(*block, *weights)  7.77 us
    pallas_call x2, Pallas kernels, on_device(): pl.pallas_call(functools.partial(finish_kernel, late_steps, spots, back,...  4.9 us
    pallas_call x1, Pallas kernels, on_device(): pl.pallas_call(functools.partial(attention_kernel, heads // groups, group...  2.74 us
    pallas_call x1, Pallas kernels, on_device(): pl.pallas_call(functools.partial(stage_kernel, pair), out_shape=[jax.Shap...  2.32 us
  transfers between devices with their start and end apart: 18, of which 7 were waited for; matrix products, arithmetic and copies ran while one was open for 0% of the time, Pallas kernels for 25%

profile of v5, /device:TPU:0, one launch (start us, length us, event | category | flops | bytes accessed | tf_op | source)
XLA Modules:
  0.0 74.5 jit_solution(10082542159746666512)
XLA Ops:
  0.5 1.8 %shard_map.100.refs_1_ = bf16[528,128]{1,0:T(8,128)(2,1)} custom-call(bf16[256,128]{1,0:T(8,128)(2,1)} %bitcast.23, bf16[256,128]{1,0:T(8,128)(2,1)} %bitcast.24, s32[1,128]{1,0:T(1,128)} %doc_ref.1), custom_call_target="tpu_custom_call" | custom-call | tf_op jit(solution)/shard_map/pallas_call | solution.py:218
  2.2 4.5 %collective-permute-start.1 = (bf16[528,128]{1,0:T(8,128)(2,1)}, bf16[528,128]{1,0:T(8,128)(2,1)S(1)}, u32[]{:S(2)}, u32[]{:S(2)}) collective-permute-start(bf16[528,128]{1,0:T(8,128)(2,1)} %shard_map.100.refs_1_), channel_id=1, source_target_pairs={{0,4},{4,8},{8,12},{1,5},{5,9},{9,13},{2,6},{6,10},{10,14},{3,7},{... | collective-permute-start | bytes 405512 | tf_op jit(solution)/shard_map/ppermute | solution.py:232
  6.7 4.5 %collective-permute-start.2 = (bf16[528,128]{1,0:T(8,128)(2,1)}, bf16[528,128]{1,0:T(8,128)(2,1)S(1)}, u32[]{:S(2)}, u32[]{:S(2)}) collective-permute-start(bf16[528,128]{1,0:T(8,128)(2,1)} %shard_map.100.refs_1_), channel_id=1, source_target_pairs={{0,8},{4,12},{1,9},{5,13},{2,10},{6,14},{3,11},{7,15},{16,24},{20,... | collective-permute-start | bytes 405512 | tf_op jit(solution)/shard_map/ppermute | solution.py:232
  11.2 1.6 %collective-permute-start = (s32[1,64]{1,0:T(1,128)}, s32[1,64]{1,0:T(1,128)S(1)}, u32[]{:S(2)}, u32[]{:S(2)}) collective-permute-start(s32[1,64]{1,0:T(1,128)} %bitcast.21), channel_id=1, source_target_pairs={{0,2},{2,0},{1,3},{3,1},{4,6},{6,4},{5,7},{7,5},{8,10},{10,8},{9,1... | collective-permute-start | bytes 776 | tf_op jit(solution)/shard_map/ppermute | solution.py:213
  13.7 1.0 %copy-done.9 = bf16[1,128,10,128]{3,1,2,0:T(8,128)(2,1)S(1)} copy-done((bf16[1,128,10,128]{3,1,2,0:T(8,128)(2,1)S(1)}, bf16[1,128,10,128]{3,1,2,0:T(8,128)(2,1)}, u32[]{:S(2)}) %copy-start.9) | copy-done | bytes 327704
  15.0 2.7 %shard_map.102 = (bf16[64,1280]{1,0:T(8,128)(2,1)S(1)}, bf16[64,1280]{1,0:T(8,128)(2,1)S(1)}) custom-call(s32[1]{0:T(128)} %bitcast.3.place_ref, bf16[10,128,128]{2,1,0:T(8,128)(2,1)S(1)} %get-tuple-element.42.query_ref, bf16[528,128]{1,0:T(8,128)(2,1)S(1)} %get-tuple-element.43.refs_0_, bf16[528,128]{1,0:T(8,128)(2,1)S(1)} %collective-permute-done.1.refs_1_, ...), custom_call_target="tpu_custom_call" | custom-call | tf_op jit(solution)/shard_map/pallas_call | solution.py:251
  17.8 2.9 %collective-permute-start.3 = (bf16[64,1280]{1,0:T(8,128)(2,1)S(1)}, bf16[64,1280]{1,0:T(8,128)(2,1)}, u32[]{:S(2)}, u32[]{:S(2)}) collective-permute-start(bf16[64,1280]{1,0:T(8,128)(2,1)S(1)} %get-tuple-element.44.refs_0_), channel_id=1, source_target_pairs={{0,4},{4,8},{8,12},{12,0},{1,5},{5,9},{9,13},{13,1},{2,6},{6,10},{... | collective-permute-start | bytes 491528 | tf_op jit(solution)/shard_map/ppermute | solution.py:213
  20.8 1.3 %collective-permute-start.7 = (bf16[64,1280]{1,0:T(8,128)(2,1)S(1)}, bf16[64,1280]{1,0:T(8,128)(2,1)}, u32[]{:S(2)}, u32[]{:S(2)}) collective-permute-start(bf16[64,1280]{1,0:T(8,128)(2,1)S(1)} %collective-permute-done.4.refs_1_), channel_id=1, source_target_pairs={{0,4},{4,8},{8,12},{12,0},{1,5},{5,9},{9,13},{13,1},{2,6},{6,10},{... | collective-permute-start | bytes 491528 | tf_op jit(solution)/shard_map/ppermute | solution.py:213
  22.1 1.9 %copy-done.5 = bf16[1280,1280]{1,0:T(8,128)(2,1)S(1)} copy-done((bf16[1280,1280]{1,0:T(8,128)(2,1)S(1)}, bf16[1280,1280]{1,0:T(8,128)(2,1)}, u32[]{:S(2)}) %copy-start.5) | copy-done | bytes 3276824
  24.0 2.3 %shard_map.103 = (bf16[1280,1280]{1,0:T(8,128)(2,1)S(1)}, bf16[1280,1280]{1,0:T(8,128)(2,1)S(1)}) custom-call(bf16[1280,1280]{1,0:T(8,128)(2,1)S(1)} %copy-done.5, bf16[1280,1280]{1,0:T(8,128)(2,1)} %collective-permute-done.5.refs_1_), custom_call_target="tpu_custom_call" | custom-call | tf_op jit(solution)/shard_map/pallas_call | solution.py:273
  26.4 1.2 %shard_map.104.chunk_ref = bf16[64,1280]{1,0:T(8,128)(2,1)S(1)} custom-call(bf16[64,1280]{1,0:T(8,128)(2,1)S(1)} %get-tuple-element.44.refs_0_, bf16[64,1280]{1,0:T(8,128)(2,1)S(1)} %collective-permute-done.4.refs_1_, bf16[1280,1280]{1,0:T(8,128)(2,1)S(1)} %get-tuple-element.49.refs_2_, bf16[1280,1280]{1,0:T(8,128)(2,1)S(1)} %get-tuple-element.50.refs_3_), custom_call_target="tpu_custom_call" | custom-call | flops 419430400 | bytes 6553600 | tf_op jit(solution)/shard_map/pallas_call | solution.py:316
  27.6 1.0 %collective-permute-done.3.refs_0_ = bf16[64,1280]{1,0:T(8,128)(2,1)} collective-permute-done((bf16[64,1280]{1,0:T(8,128)(2,1)S(1)}, bf16[64,1280]{1,0:T(8,128)(2,1)}, u32[]{:S(2)}, u32[]{:S(2)}) %collective-permute-start.3) | collective-permute-done | bytes 163872 | tf_op jit(solution)/shard_map/ppermute | solution.py:213
  28.6 1.6 %collective-permute-start.6 = (bf16[64,1280]{1,0:T(8,128)(2,1)}, bf16[64,1280]{1,0:T(8,128)(2,1)}, u32[]{:S(2)}, u32[]{:S(2)}) collective-permute-start(bf16[64,1280]{1,0:T(8,128)(2,1)} %collective-permute-done.3.refs_0_), channel_id=1, source_target_pairs={{0,4},{4,8},{8,12},{12,0},{1,5},{5,9},{9,13},{13,1},{2,6},{6,10},{... | collective-permute-start | bytes 491528 | tf_op jit(solution)/shard_map/ppermute | solution.py:213
  30.2 1.7 %collective-permute-done.7.refs_1_ = bf16[64,1280]{1,0:T(8,128)(2,1)} collective-permute-done((bf16[64,1280]{1,0:T(8,128)(2,1)S(1)}, bf16[64,1280]{1,0:T(8,128)(2,1)}, u32[]{:S(2)}, u32[]{:S(2)}) %collective-permute-start.7) | collective-permute-done | bytes 163872 | tf_op jit(solution)/shard_map/ppermute | solution.py:213
  31.9 2.9 %shard_map.105 = bf16[64,1280]{1,0:T(8,128)(2,1)} custom-call(bf16[64,1280]{1,0:T(8,128)(2,1)} %collective-permute-done.3.refs_0_, bf16[64,1280]{1,0:T(8,128)(2,1)} %collective-permute-done.7.refs_1_, bf16[1280,1280]{1,0:T(8,128)(2,1)S(1)} %get-tuple-element.49.refs_2_, bf16[1280,1280]{1,0:T(8,128)(2,1)S(1)} %get-tuple-element.50.refs_3_), custom_call_target="tpu_custom_call" | custom-call | flops 419430400 | bytes 6553600 | tf_op jit(solution)/shard_map/pallas_call | solution.py:316
  34.8 3.8 %collective-permute-start.9 = (bf16[64,1280]{1,0:T(8,128)(2,1)}, bf16[64,1280]{1,0:T(8,128)(2,1)}, u32[]{:S(2)}, u32[]{:S(2)}) collective-permute-start(bf16[64,1280]{1,0:T(8,128)(2,1)} %shard_map.105), channel_id=1, source_target_pairs={{0,12},{4,0},{8,4},{12,8},{1,13},{5,1},{9,5},{13,9},{2,14},{6,2},{... | collective-permute-start | bytes 491528 | tf_op jit(solution)/shard_map/ppermute | solution.py:213
  38.7 1.9 %collective-permute-done.8.refs_1_ = bf16[64,1280]{1,0:T(8,128)(2,1)} collective-permute-done((bf16[64,1280]{1,0:T(8,128)(2,1)}, bf16[64,1280]{1,0:T(8,128)(2,1)}, u32[]{:S(2)}, u32[]{:S(2)}) %collective-permute-start.8) | collective-permute-done | bytes 163872 | tf_op jit(solution)/shard_map/ppermute | solution.py:213
  40.6 1.1 %copy-done.3 = bf16[1,64,5120]{2,1,0:T(8,128)(2,1)S(1)} copy-done((bf16[1,64,5120]{2,1,0:T(8,128)(2,1)S(1)}, bf16[1,64,5120]{2,1,0:T(8,128)(2,1)}, u32[]{:S(2)}) %copy-start.3) | copy-done | bytes 655384
  41.7 1.6 %collective-permute-start.14 = (bf16[64,1280]{1,0:T(8,128)(2,1)S(1)}, bf16[64,1280]{1,0:T(8,128)(2,1)S(1)}, u32[]{:S(2)}, u32[]{:S(2)}) collective-permute-start(bf16[64,1280]{1,0:T(8,128)(2,1)S(1)} %shard_map.108.refs_0_), channel_id=1, source_target_pairs={{0,2},{2,0},{1,3},{3,1},{4,6},{6,4},{5,7},{7,5},{8,10},{10,8},{9,1... | collective-permute-start | bytes 491528 | tf_op jit(solution)/shard_map/ppermute | solution.py:213
  44.0 1.9 %copy-done.1 = bf16[1280,1280]{1,0:T(8,128)(2,1)S(1)} copy-done((bf16[1280,1280]{1,0:T(8,128)(2,1)S(1)}, bf16[1280,1280]{1,0:T(8,128)(2,1)}, u32[]{:S(2)}) %copy-start.1) | copy-done | bytes 3276824
  46.0 2.4 %shard_map.106 = bf16[64,1280]{1,0:T(8,128)(2,1)S(1)} custom-call(bf16[64,1280]{1,0:T(8,128)(2,1)} %collective-permute-done.6.refs_0_, bf16[64,1280]{1,0:T(8,128)(2,1)} %collective-permute-done.8.refs_1_, bf16[1280,1280]{1,0:T(8,128)(2,1)S(1)} %get-tuple-element.49.refs_2_, bf16[1280,1280]{1,0:T(8,128)(2,1)S(1)} %copy-done.1), custom_call_target="tpu_custom_call" | custom-call | flops 419430400 | bytes 6553600 | tf_op jit(solution)/shard_map/pallas_call | solution.py:316
  48.4 1.8 %collective-permute-start.10 = (bf16[64,1280]{1,0:T(8,128)(2,1)S(1)}, bf16[64,1280]{1,0:T(8,128)(2,1)S(1)}, u32[]{:S(2)}, u32[]{:S(2)}) collective-permute-start(bf16[64,1280]{1,0:T(8,128)(2,1)S(1)} %shard_map.106), channel_id=1, source_target_pairs={{0,8},{4,12},{8,0},{12,4},{1,9},{5,13},{9,1},{13,5},{2,10},{6,14},... | collective-permute-start | bytes 491528 | tf_op jit(solution)/shard_map/ppermute | solution.py:213
  50.1 1.0 %shard_map.110.refs_1_ = bf16[64,1280]{1,0:T(8,128)(2,1)S(1)} custom-call(s32[1]{0:T(128)} %bitcast.place_ref, bf16[64,5120]{1,0:T(8,128)(2,1)S(1)} %bitcast.13, bf16[64,1280]{1,0:T(8,128)(2,1)} %collective-permute-done.9.chunk_ref), custom_call_target="tpu_custom_call" | custom-call | tf_op jit(solution)/shard_map/pallas_call | solution.py:286
  51.7 1.2 %shard_map.109 = bf16[64,1280]{1,0:T(8,128)(2,1)S(1)} custom-call(bf16[64,1280]{1,0:T(8,128)(2,1)S(1)} %collective-permute-done.12.refs_0_, bf16[64,1280]{1,0:T(8,128)(2,1)S(1)} %collective-permute-done.13.refs_1_, bf16[1280,1280]{1,0:T(8,128)(2,1)S(1)} %get-tuple-element.49.refs_2_, bf16[1280,1280]{1,0:T(8,128)(2,1)S(1)} %copy-done.2), custom_call_target="tpu_custom_call" | custom-call | flops 419430400 | bytes 6553600 | tf_op jit(solution)/shard_map/pallas_call | solution.py:316
  53.0 3.7 %collective-permute-start.15 = (bf16[64,1280]{1,0:T(8,128)(2,1)S(1)}, bf16[64,1280]{1,0:T(8,128)(2,1)S(1)}, u32[]{:S(2)}, u32[]{:S(2)}) collective-permute-start(bf16[64,1280]{1,0:T(8,128)(2,1)S(1)} %shard_map.109), channel_id=1, source_target_pairs={{0,4},{4,8},{8,12},{12,0},{1,5},{5,9},{9,13},{13,1},{2,6},{6,10},{... | collective-permute-start | bytes 491528 | tf_op jit(solution)/shard_map/ppermute | solution.py:213
  56.7 5.6 %collective-permute-done.10.chunk_ref = bf16[64,1280]{1,0:T(8,128)(2,1)S(1)} collective-permute-done((bf16[64,1280]{1,0:T(8,128)(2,1)S(1)}, bf16[64,1280]{1,0:T(8,128)(2,1)S(1)}, u32[]{:S(2)}, u32[]{:S(2)}) %collective-permute-start.10) | collective-permute-done | bytes 163872 | tf_op jit(solution)/shard_map/ppermute | solution.py:213
  62.4 1.6 %collective-permute-start.11 = (bf16[64,1280]{1,0:T(8,128)(2,1)S(1)}, bf16[64,1280]{1,0:T(8,128)(2,1)S(1)}, u32[]{:S(2)}, u32[]{:S(2)}) collective-permute-start(bf16[64,1280]{1,0:T(8,128)(2,1)S(1)} %shard_map.107.refs_0_), channel_id=1, source_target_pairs={{0,2},{2,0},{1,3},{3,1},{4,6},{6,4},{5,7},{7,5},{8,10},{10,8},{9,1... | collective-permute-start | bytes 491528 | tf_op jit(solution)/shard_map/ppermute | solution.py:213
  64.8 1.0 %copy-done.6 = bf16[5120,32]{0,1:T(8,128)(2,1)S(1)} copy-done((bf16[5120,32]{0,1:T(8,128)(2,1)S(1)}, bf16[5120,32]{0,1:T(8,128)(2,1)}, u32[]{:S(2)}) %copy-start.6) | copy-done | bytes 327704
  65.7 2.5 %shard_map.113.refs_7_ = bf16[2,32,2,5120]{3,2,1,0:T(2,128)(2,1)} custom-call(s32[2]{0:T(128)S(1)} %pad_add_fusion.place_ref, bf16[64,1280]{1,0:T(8,128)(2,1)S(1)} %shard_map.107.refs_0_, bf16[64,1280]{1,0:T(8,128)(2,1)S(1)} %shard_map.112.refs_1_, bf16[64,5120]{1,0:T(8,128)(2,1)S(1)} %get-tuple-element.71.refs_2_, s32[1,64]{1,0:T(1,128)S(1)} %bitcast.22, ...), custom_call_target="tpu_custom_call" | custom-call | tf_op jit(solution)/shard_map/pallas_call | solution.py:346
  68.2 1.3 %collective-permute-done.11.refs_0_ = bf16[64,1280]{1,0:T(8,128)(2,1)S(1)} collective-permute-done((bf16[64,1280]{1,0:T(8,128)(2,1)S(1)}, bf16[64,1280]{1,0:T(8,128)(2,1)S(1)}, u32[]{:S(2)}, u32[]{:S(2)}) %collective-permute-start.11) | collective-permute-done | bytes 163872 | tf_op jit(solution)/shard_map/ppermute | solution.py:213
  69.5 2.5 %collective-permute-done.17.refs_1_ = bf16[64,1280]{1,0:T(8,128)(2,1)S(1)} collective-permute-done((bf16[64,1280]{1,0:T(8,128)(2,1)S(1)}, bf16[64,1280]{1,0:T(8,128)(2,1)S(1)}, u32[]{:S(2)}, u32[]{:S(2)}) %collective-permute-start.17) | collective-permute-done | bytes 163872 | tf_op jit(solution)/shard_map/ppermute | solution.py:213
  72.1 2.5 %shard_map.114 = bf16[2,32,2,5120]{3,2,1,0:T(2,128)(2,1)} custom-call(s32[2]{0:T(128)S(1)} %pad_add_fusion.place_ref, bf16[64,1280]{1,0:T(8,128)(2,1)S(1)} %collective-permute-done.11.refs_0_, bf16[64,1280]{1,0:T(8,128)(2,1)S(1)} %collective-permute-done.17.refs_1_, bf16[64,5120]{1,0:T(8,128)(2,1)S(1)} %get-tuple-element.69.refs_2_, ...), custom_call_target="tpu_custom_call", output_to_operand_aliasing={{}: (8, {})} | custom-call | tf_op jit(solution)/shard_map/pallas_call | solution.py:346
  (47 shorter events, 4.1 us)
Async XLA Ops:
  0.0 20.8 %collective-permute-start.5 = (bf16[1280,1280]{1,0:T(8,128)(2,1)}, bf16[1280,1280]{1,0:T(8,128)(2,1)}, u32[]{:S(2)}, u32[]{:S(2)}) collective-permute-start(bf16[1280,1280]{1,0:T(8,128)(2,1)} %refs_0_), channel_id=1, source_target_pairs={{0,1},{1,0},{2,3},{3,2},{4,5},{5,4},{6,7},{7,6},{8,9},{9,8},{10,11... | collective-permute-start | bytes 9830408 | tf_op jit(solution)/shard_map/ppermute | solution.py:213
  2.2 12.7 %collective-permute-start.1 = (bf16[528,128]{1,0:T(8,128)(2,1)}, bf16[528,128]{1,0:T(8,128)(2,1)S(1)}, u32[]{:S(2)}, u32[]{:S(2)}) collective-permute-start(bf16[528,128]{1,0:T(8,128)(2,1)} %shard_map.100.refs_1_), channel_id=1, source_target_pairs={{0,4},{4,8},{8,12},{1,5},{5,9},{9,13},{2,6},{6,10},{10,14},{3,7},{... | collective-permute-start | bytes 405512 | tf_op jit(solution)/shard_map/ppermute | solution.py:232
  6.7 8.3 %collective-permute-start.2 = (bf16[528,128]{1,0:T(8,128)(2,1)}, bf16[528,128]{1,0:T(8,128)(2,1)S(1)}, u32[]{:S(2)}, u32[]{:S(2)}) collective-permute-start(bf16[528,128]{1,0:T(8,128)(2,1)} %shard_map.100.refs_1_), channel_id=1, source_target_pairs={{0,8},{4,12},{1,9},{5,13},{2,10},{6,14},{3,11},{7,15},{16,24},{20,... | collective-permute-start | bytes 405512 | tf_op jit(solution)/shard_map/ppermute | solution.py:232
  11.2 3.7 %collective-permute-start = (s32[1,64]{1,0:T(1,128)}, s32[1,64]{1,0:T(1,128)S(1)}, u32[]{:S(2)}, u32[]{:S(2)}) collective-permute-start(s32[1,64]{1,0:T(1,128)} %bitcast.21), channel_id=1, source_target_pairs={{0,2},{2,0},{1,3},{3,1},{4,6},{6,4},{5,7},{7,5},{8,10},{10,8},{9,1... | collective-permute-start | bytes 776 | tf_op jit(solution)/shard_map/ppermute | solution.py:213
  12.8 0.9 %copy-start.8 = (bf16[528,128]{1,0:T(8,128)(2,1)S(1)}, bf16[528,128]{1,0:T(8,128)(2,1)}, u32[]{:S(2)}) copy-start(bf16[528,128]{1,0:T(8,128)(2,1)} %shard_map.100.refs_1_) | copy-start | bytes 405508
  13.7 1.0 %copy-start.9 = (bf16[1,128,10,128]{3,1,2,0:T(8,128)(2,1)S(1)}, bf16[1,128,10,128]{3,1,2,0:T(8,128)(2,1)}, u32[]{:S(2)}) copy-start(bf16[1,128,10,128]{3,1,2,0:T(8,128)(2,1)} %param.10) | copy-start | bytes 983044
  17.7 3.0 %collective-permute-start.4 = (bf16[64,1280]{1,0:T(8,128)(2,1)S(1)}, bf16[64,1280]{1,0:T(8,128)(2,1)S(1)}, u32[]{:S(2)}, u32[]{:S(2)}) collective-permute-start(bf16[64,1280]{1,0:T(8,128)(2,1)S(1)} %get-tuple-element.45), channel_id=1, source_target_pairs={{0,1},{1,0},{2,3},{3,2},{4,5},{5,4},{6,7},{7,6},{8,9},{9,8},{10,11... | collective-permute-start | bytes 491528 | tf_op jit(solution)/shard_map/ppermute | solution.py:213
  17.8 10.8 %collective-permute-start.3 = (bf16[64,1280]{1,0:T(8,128)(2,1)S(1)}, bf16[64,1280]{1,0:T(8,128)(2,1)}, u32[]{:S(2)}, u32[]{:S(2)}) collective-permute-start(bf16[64,1280]{1,0:T(8,128)(2,1)S(1)} %get-tuple-element.44.refs_0_), channel_id=1, source_target_pairs={{0,4},{4,8},{8,12},{12,0},{1,5},{5,9},{9,13},{13,1},{2,6},{6,10},{... | collective-permute-start | bytes 491528 | tf_op jit(solution)/shard_map/ppermute | solution.py:213
  20.8 11.1 %collective-permute-start.7 = (bf16[64,1280]{1,0:T(8,128)(2,1)S(1)}, bf16[64,1280]{1,0:T(8,128)(2,1)}, u32[]{:S(2)}, u32[]{:S(2)}) collective-permute-start(bf16[64,1280]{1,0:T(8,128)(2,1)S(1)} %collective-permute-done.4.refs_1_), channel_id=1, source_target_pairs={{0,4},{4,8},{8,12},{12,0},{1,5},{5,9},{9,13},{13,1},{2,6},{6,10},{... | collective-permute-start | bytes 491528 | tf_op jit(solution)/shard_map/ppermute | solution.py:213
  22.1 1.9 %copy-start.5 = (bf16[1280,1280]{1,0:T(8,128)(2,1)S(1)}, bf16[1280,1280]{1,0:T(8,128)(2,1)}, u32[]{:S(2)}) copy-start(bf16[1280,1280]{1,0:T(8,128)(2,1)} %refs_0_) | copy-start | bytes 9830404
  26.4 5.6 %copy-start = (bf16[1280,1280]{1,0:T(8,128)(2,1)}, bf16[1280,1280]{1,0:T(8,128)(2,1)S(1)}, u32[]{:S(2)}) copy-start(bf16[1280,1280]{1,0:T(8,128)(2,1)S(1)} %get-tuple-element.50.refs_3_) | copy-start | bytes 9830404
  28.6 10.0 %collective-permute-start.6 = (bf16[64,1280]{1,0:T(8,128)(2,1)}, bf16[64,1280]{1,0:T(8,128)(2,1)}, u32[]{:S(2)}, u32[]{:S(2)}) collective-permute-start(bf16[64,1280]{1,0:T(8,128)(2,1)} %collective-permute-done.3.refs_0_), channel_id=1, source_target_pairs={{0,4},{4,8},{8,12},{12,0},{1,5},{5,9},{9,13},{13,1},{2,6},{6,10},{... | collective-permute-start | bytes 491528 | tf_op jit(solution)/shard_map/ppermute | solution.py:213
  31.9 8.7 %collective-permute-start.8 = (bf16[64,1280]{1,0:T(8,128)(2,1)}, bf16[64,1280]{1,0:T(8,128)(2,1)}, u32[]{:S(2)}, u32[]{:S(2)}) collective-permute-start(bf16[64,1280]{1,0:T(8,128)(2,1)} %collective-permute-done.7.refs_1_), channel_id=1, source_target_pairs={{0,4},{4,8},{8,12},{12,0},{1,5},{5,9},{9,13},{13,1},{2,6},{6,10},{... | collective-permute-start | bytes 491528 | tf_op jit(solution)/shard_map/ppermute | solution.py:213
  34.8 9.2 %collective-permute-start.9 = (bf16[64,1280]{1,0:T(8,128)(2,1)}, bf16[64,1280]{1,0:T(8,128)(2,1)}, u32[]{:S(2)}, u32[]{:S(2)}) collective-permute-start(bf16[64,1280]{1,0:T(8,128)(2,1)} %shard_map.105), channel_id=1, source_target_pairs={{0,12},{4,0},{8,4},{12,8},{1,13},{5,1},{9,5},{13,9},{2,14},{6,2},{... | collective-permute-start | bytes 491528 | tf_op jit(solution)/shard_map/ppermute | solution.py:213
  38.7 11.5 %collective-permute-start.12 = (bf16[64,1280]{1,0:T(8,128)(2,1)}, bf16[64,1280]{1,0:T(8,128)(2,1)S(1)}, u32[]{:S(2)}, u32[]{:S(2)}) collective-permute-start(bf16[64,1280]{1,0:T(8,128)(2,1)} %collective-permute-done.6.refs_0_), channel_id=1, source_target_pairs={{0,4},{4,8},{8,12},{12,0},{1,5},{5,9},{9,13},{13,1},{2,6},{6,10},{... | collective-permute-start | bytes 491528 | tf_op jit(solution)/shard_map/ppermute | solution.py:213
  40.6 11.2 %collective-permute-start.13 = (bf16[64,1280]{1,0:T(8,128)(2,1)}, bf16[64,1280]{1,0:T(8,128)(2,1)S(1)}, u32[]{:S(2)}, u32[]{:S(2)}) collective-permute-start(bf16[64,1280]{1,0:T(8,128)(2,1)} %collective-permute-done.8.refs_1_), channel_id=1, source_target_pairs={{0,4},{4,8},{8,12},{12,0},{1,5},{5,9},{9,13},{13,1},{2,6},{6,10},{... | collective-permute-start | bytes 491528 | tf_op jit(solution)/shard_map/ppermute | solution.py:213
  40.6 1.1 %copy-start.3 = (bf16[1,64,5120]{2,1,0:T(8,128)(2,1)S(1)}, bf16[1,64,5120]{2,1,0:T(8,128)(2,1)}, u32[]{:S(2)}) copy-start(bf16[1,64,5120]{2,1,0:T(8,128)(2,1)} %param.14) | copy-start | bytes 1966084
  41.7 8.5 %copy-start.4 = (bf16[1,64,5120]{2,1,0:T(8,128)(2,1)S(1)}, bf16[1,64,5120]{2,1,0:T(8,128)(2,1)}, u32[]{:S(2)}) copy-start(bf16[1,64,5120]{2,1,0:T(8,128)(2,1)} %param.14) | copy-start | bytes 1966084
  41.7 10.0 %collective-permute-start.14 = (bf16[64,1280]{1,0:T(8,128)(2,1)S(1)}, bf16[64,1280]{1,0:T(8,128)(2,1)S(1)}, u32[]{:S(2)}, u32[]{:S(2)}) collective-permute-start(bf16[64,1280]{1,0:T(8,128)(2,1)S(1)} %shard_map.108.refs_0_), channel_id=1, source_target_pairs={{0,2},{2,0},{1,3},{3,1},{4,6},{6,4},{5,7},{7,5},{8,10},{10,8},{9,1... | collective-permute-start | bytes 491528 | tf_op jit(solution)/shard_map/ppermute | solution.py:213
  44.0 1.9 %copy-start.1 = (bf16[1280,1280]{1,0:T(8,128)(2,1)S(1)}, bf16[1280,1280]{1,0:T(8,128)(2,1)}, u32[]{:S(2)}) copy-start(bf16[1280,1280]{1,0:T(8,128)(2,1)} %copy-done) | copy-start | bytes 9830404
  46.0 5.8 %copy-start.2 = (bf16[1280,1280]{1,0:T(8,128)(2,1)S(1)}, bf16[1280,1280]{1,0:T(8,128)(2,1)}, u32[]{:S(2)}) copy-start(bf16[1280,1280]{1,0:T(8,128)(2,1)} %copy-done) | copy-start | bytes 9830404
  48.4 14.0 %collective-permute-start.10 = (bf16[64,1280]{1,0:T(8,128)(2,1)S(1)}, bf16[64,1280]{1,0:T(8,128)(2,1)S(1)}, u32[]{:S(2)}, u32[]{:S(2)}) collective-permute-start(bf16[64,1280]{1,0:T(8,128)(2,1)S(1)} %shard_map.106), channel_id=1, source_target_pairs={{0,8},{4,12},{8,0},{12,4},{1,9},{5,13},{9,1},{13,5},{2,10},{6,14},... | collective-permute-start | bytes 491528 | tf_op jit(solution)/shard_map/ppermute | solution.py:213
  51.1 13.6 %copy-start.12 = (bf16[5120]{0:T(1024)(128)(2,1)S(1)}, bf16[5120]{0:T(1024)(128)(2,1)}, u32[]{:S(2)}) copy-start(bf16[5120]{0:T(1024)(128)(2,1)} %param.16) | copy-start | bytes 30724
  51.1 13.7 %copy-start.10 = (s32[64]{0:T(128)S(1)}, s32[64]{0:T(128)}, u32[]{:S(2)}) copy-start(s32[64]{0:T(128)} %param.19) | copy-start | bytes 772
  51.1 13.6 %copy-start.11 = (s32[1,64,1]{1,2,0:T(1,128)S(1)}, s32[1,64,1]{1,2,0:T(1,128)}, u32[]{:S(2)}) copy-start(s32[1,64,1]{1,2,0:T(1,128)} %param.18) | copy-start | bytes 772
  51.1 12.8 %collective-permute-start.16 = (bf16[64,1280]{1,0:T(8,128)(2,1)S(1)}, bf16[64,1280]{1,0:T(8,128)(2,1)S(1)}, u32[]{:S(2)}, u32[]{:S(2)}) collective-permute-start(bf16[64,1280]{1,0:T(8,128)(2,1)S(1)} %shard_map.110.refs_1_), channel_id=1, source_target_pairs={{0,2},{2,0},{1,3},{3,1},{4,6},{6,4},{5,7},{7,5},{8,10},{10,8},{9,1... | collective-permute-start | bytes 491528 | tf_op jit(solution)/shard_map/ppermute | solution.py:213
  53.0 19.1 %copy-start.7 = (bf16[5120,32]{0,1:T(8,128)(2,1)S(1)}, bf16[5120,32]{0,1:T(8,128)(2,1)}, u32[]{:S(2)}) copy-start(bf16[5120,32]{0,1:T(8,128)(2,1)} %param.17) | copy-start | bytes 983044
  53.0 11.0 %collective-permute-start.15 = (bf16[64,1280]{1,0:T(8,128)(2,1)S(1)}, bf16[64,1280]{1,0:T(8,128)(2,1)S(1)}, u32[]{:S(2)}, u32[]{:S(2)}) collective-permute-start(bf16[64,1280]{1,0:T(8,128)(2,1)S(1)} %shard_map.109), channel_id=1, source_target_pairs={{0,4},{4,8},{8,12},{12,0},{1,5},{5,9},{9,13},{13,1},{2,6},{6,10},{... | collective-permute-start | bytes 491528 | tf_op jit(solution)/shard_map/ppermute | solution.py:213
  62.4 7.1 %collective-permute-start.11 = (bf16[64,1280]{1,0:T(8,128)(2,1)S(1)}, bf16[64,1280]{1,0:T(8,128)(2,1)S(1)}, u32[]{:S(2)}, u32[]{:S(2)}) collective-permute-start(bf16[64,1280]{1,0:T(8,128)(2,1)S(1)} %shard_map.107.refs_0_), channel_id=1, source_target_pairs={{0,2},{2,0},{1,3},{3,1},{4,6},{6,4},{5,7},{7,5},{8,10},{10,8},{9,1... | collective-permute-start | bytes 491528 | tf_op jit(solution)/shard_map/ppermute | solution.py:213
  64.1 8.0 %collective-permute-start.17 = (bf16[64,1280]{1,0:T(8,128)(2,1)S(1)}, bf16[64,1280]{1,0:T(8,128)(2,1)S(1)}, u32[]{:S(2)}, u32[]{:S(2)}) collective-permute-start(bf16[64,1280]{1,0:T(8,128)(2,1)S(1)} %shard_map.112.refs_1_), channel_id=1, source_target_pairs={{0,2},{2,0},{1,3},{3,1},{4,6},{6,4},{5,7},{7,5},{8,10},{10,8},{9,1... | collective-permute-start | bytes 491528 | tf_op jit(solution)/shard_map/ppermute | solution.py:213
  64.8 1.0 %copy-start.6 = (bf16[5120,32]{0,1:T(8,128)(2,1)S(1)}, bf16[5120,32]{0,1:T(8,128)(2,1)}, u32[]{:S(2)}) copy-start(bf16[5120,32]{0,1:T(8,128)(2,1)} %param.17) | copy-start | bytes 983044

commit v6 on v5

--- a/solution.py
+++ b/solution.py
@@ -56,14 +56,16 @@
     pack_refs, out_refs = refs[:-pair], refs[-pair:]
     heads, tokens, head_size = query_ref.shape
     scale = 1.0 / math.sqrt(head_size)
-    core = place_ref[0]
+    core, ctx_index = place_ref[0], place_ref[1]
     part_rows = tokens // pair
     held_rows = groups * tokens
     rows = lax.broadcasted_iota(jnp.int32, (tokens, tokens), 0)
     columns = lax.broadcasted_iota(jnp.int32, (tokens, tokens), 1)
     docs = [ref[2 * held_rows : 2 * held_rows + 1, :].astype(jnp.float32) for ref in pack_refs]
     own_doc = jnp.sum(jnp.where(rows == columns, docs[0], 0.0), axis=1, keepdims=True)
-    allowed = [(own_doc == docs[0]) & (columns <= rows)] + [own_doc == doc for doc in docs[1:]]
+    allowed = [(own_doc == docs[0]) & (columns <= rows)]
+    for step, doc in enumerate(docs[1:], 1):
+        allowed.append((own_doc == doc) & (ctx_index >= step))
     allowed = jnp.concatenate(allowed, axis=1)
     for group in range(groups):
         first = group * tokens
@@ -229,7 +231,14 @@
         doc_ids,
     )
     packs = [pack] + [
-        lax.ppermute(pack, "ctx", [(i, i + step) for i in range(ctx_count - step)])
+        lax.ppermute(
+            pack,
+            "ctx",
+            [
+                (i, (i + step) % ctx_count)
+                for i in range(ctx_count if step == 1 else ctx_count - step)
+            ],
+        )
         for step in range(1, reach + 1)
     ]
     ids, own_residual = expert_ids[:, :, 0], residual[0]
@@ -254,7 +263,7 @@
         in_specs=[smem] + [vmem] * (1 + len(packs)),
         out_specs=[vmem] * pair,
         compiler_params=params,
-    )(core.reshape(1), staged_queries, *packs)
+    )(jnp.stack([core, ctx_index]), staged_queries, *packs)
 
     project = pl.pallas_call(
         functools.partial(project_kernel, pair),

time: 75 us -> 71.9 us (0.959)
  local copies, waits for them, and re-layouts: 7.84 us -> 3.85 us
  waiting for transfers between devices: 14.9 us -> 18.5 us
  Pallas kernels: 20.9 us -> 17.7 us
    unnamed x26 -> x16, local copies, waits for them, and re-layouts: 7.83 us -> 3.83 us
    ppermute x16, waiting for transfers between devices: 14.9 us -> 18.5 us  [over(): lax.ppermute(array, axis, [(i, (i + step) % count) for i in range(count)])]
    pallas_call x4, Pallas kernels: 7.77 us -> 4.95 us  [on_device(): total = project(*block, *weights)]
    ppermute x16, starting transfers between devices: 21.5 us -> 24.1 us  [over(): lax.ppermute(array, axis, [(i, (i + step) % count) for i in range(count)])]
    ppermute x2, starting transfers between devices: 8.98 us -> 7.11 us  [on_device(): lax.ppermute(pack, 'ctx', [(i, (i + step) % ctx_count) for i in range(ctx...]
    pallas_call x4, Pallas kernels: 1.09 us -> 0.18 us  [forward(): pl.pallas_call(functools.partial(hidden_kernel, step, spots), out_shape=j...]
  transfers between devices with their start and end apart: 18 -> 18, of which waited for: 7 -> 7; matrix products, arithmetic and copies ran while one was open for 0% -> 0% of each run, Pallas kernels for 25% -> 21%
where the time goes in v6:
time: 71.9 us; the launch traced here: 71.6 us
  starting transfers between devices  31.2 us (43%)
  waiting for transfers between devices  18.5 us (26%)
  Pallas kernels  17.7 us (25%)
  local copies, waits for them, and re-layouts  3.85 us (5%)
    ppermute x16, starting transfers between devices, over(): lax.ppermute(array, axis, [(i, (i + step) % count) for i in range(count)])  24.1 us
    ppermute x16, waiting for transfers between devices, over(): lax.ppermute(array, axis, [(i, (i + step) % count) for i in range(count)])  18.5 us
    ppermute x2, starting transfers between devices, on_device(): lax.ppermute(pack, 'ctx', [(i, (i + step) % ctx_count) for i in range(ctx...  7.11 us
    pallas_call x4, Pallas kernels, on_device(): total = project(*block, *weights)  4.95 us
    pallas_call x2, Pallas kernels, on_device(): pl.pallas_call(functools.partial(finish_kernel, late_steps, spots, back,...  4.91 us
    unnamed x16, local copies, waits for them, and re-layouts  3.83 us
    pallas_call x1, Pallas kernels, on_device(): pl.pallas_call(functools.partial(attention_kernel, heads // groups, group...  3.26 us
    pallas_call x1, Pallas kernels, on_device(): pl.pallas_call(functools.partial(stage_kernel, pair), out_shape=[jax.Shap...  2.32 us
  transfers between devices with their start and end apart: 18, of which 7 were waited for; matrix products, arithmetic and copies ran while one was open for 0% of the time, Pallas kernels for 21%

profile of v6, /device:TPU:0, one launch (start us, length us, event | category | flops | bytes accessed | tf_op | source)
XLA Modules:
  0.0 71.6 jit_solution(13932387690155310800)
XLA Ops:
  0.5 1.8 %shard_map.100.refs_1_ = bf16[528,128]{1,0:T(8,128)(2,1)} custom-call(bf16[256,128]{1,0:T(8,128)(2,1)} %bitcast.23, bf16[256,128]{1,0:T(8,128)(2,1)} %bitcast.24, s32[1,128]{1,0:T(1,128)} %doc_ref.1), custom_call_target="tpu_custom_call" | custom-call | tf_op jit(solution)/shard_map/pallas_call | solution.py:220
  2.2 2.6 %collective-permute-start.1 = (bf16[528,128]{1,0:T(8,128)(2,1)}, bf16[528,128]{1,0:T(8,128)(2,1)S(1)}, u32[]{:S(2)}, u32[]{:S(2)}) collective-permute-start(bf16[528,128]{1,0:T(8,128)(2,1)} %shard_map.100.refs_1_), channel_id=1, source_target_pairs={{0,4},{4,8},{8,12},{12,0},{1,5},{5,9},{9,13},{13,1},{2,6},{6,10},{... | collective-permute-start | bytes 405512 | tf_op jit(solution)/shard_map/ppermute | solution.py:234
  4.9 4.5 %collective-permute-start.2 = (bf16[528,128]{1,0:T(8,128)(2,1)}, bf16[528,128]{1,0:T(8,128)(2,1)S(1)}, u32[]{:S(2)}, u32[]{:S(2)}) collective-permute-start(bf16[528,128]{1,0:T(8,128)(2,1)} %shard_map.100.refs_1_), channel_id=1, source_target_pairs={{0,8},{4,12},{1,9},{5,13},{2,10},{6,14},{3,11},{7,15},{16,24},{20,... | collective-permute-start | bytes 405512 | tf_op jit(solution)/shard_map/ppermute | solution.py:234
  9.4 1.6 %collective-permute-start = (s32[1,64]{1,0:T(1,128)}, s32[1,64]{1,0:T(1,128)S(1)}, u32[]{:S(2)}, u32[]{:S(2)}) collective-permute-start(s32[1,64]{1,0:T(1,128)} %bitcast.21), channel_id=1, source_target_pairs={{0,2},{2,0},{1,3},{3,1},{4,6},{6,4},{5,7},{7,5},{8,10},{10,8},{9,1... | collective-permute-start | bytes 776 | tf_op jit(solution)/shard_map/ppermute | solution.py:215
  11.0 0.9 %copy-done.3 = bf16[528,128]{1,0:T(8,128)(2,1)S(1)} copy-done((bf16[528,128]{1,0:T(8,128)(2,1)S(1)}, bf16[528,128]{1,0:T(8,128)(2,1)}, u32[]{:S(2)}) %copy-start.3) | copy-done | bytes 135192
  11.9 1.0 %copy-done.4 = bf16[1,128,10,128]{3,1,2,0:T(8,128)(2,1)S(1)} copy-done((bf16[1,128,10,128]{3,1,2,0:T(8,128)(2,1)S(1)}, bf16[1,128,10,128]{3,1,2,0:T(8,128)(2,1)}, u32[]{:S(2)}) %copy-start.4) | copy-done | bytes 327704
  13.2 3.3 %shard_map.102 = (bf16[64,1280]{1,0:T(8,128)(2,1)S(1)}, bf16[64,1280]{1,0:T(8,128)(2,1)S(1)}) custom-call(s32[2]{0:T(128)S(1)} %pad_add_fusion.1.place_ref, bf16[10,128,128]{2,1,0:T(8,128)(2,1)S(1)} %get-tuple-element.42.query_ref, bf16[528,128]{1,0:T(8,128)(2,1)S(1)} %get-tuple-element.43.refs_0_, bf16[528,128]{1,0:T(8,128)(2,1)S(1)} %collective-permute-done.1.refs_1_, ...), custom_call_target="tpu_custom_call" | custom-call | tf_op jit(solution)/shard_map/pallas_call | solution.py:260
  16.5 3.0 %collective-permute-start.3 = (bf16[64,1280]{1,0:T(8,128)(2,1)S(1)}, bf16[64,1280]{1,0:T(8,128)(2,1)S(1)}, u32[]{:S(2)}, u32[]{:S(2)}) collective-permute-start(bf16[64,1280]{1,0:T(8,128)(2,1)S(1)} %get-tuple-element.44.refs_0_), channel_id=1, source_target_pairs={{0,4},{4,8},{8,12},{12,0},{1,5},{5,9},{9,13},{13,1},{2,6},{6,10},{... | collective-permute-start | bytes 491528 | tf_op jit(solution)/shard_map/ppermute | solution.py:215
  19.5 1.3 %collective-permute-start.7 = (bf16[64,1280]{1,0:T(8,128)(2,1)S(1)}, bf16[64,1280]{1,0:T(8,128)(2,1)S(1)}, u32[]{:S(2)}, u32[]{:S(2)}) collective-permute-start(bf16[64,1280]{1,0:T(8,128)(2,1)S(1)} %collective-permute-done.4.refs_1_), channel_id=1, source_target_pairs={{0,4},{4,8},{8,12},{12,0},{1,5},{5,9},{9,13},{13,1},{2,6},{6,10},{... | collective-permute-start | bytes 491528 | tf_op jit(solution)/shard_map/ppermute | solution.py:215
  20.9 1.9 %copy-done.1 = bf16[1280,1280]{1,0:T(8,128)(2,1)S(1)} copy-done((bf16[1280,1280]{1,0:T(8,128)(2,1)S(1)}, bf16[1280,1280]{1,0:T(8,128)(2,1)}, u32[]{:S(2)}) %copy-start.1) | copy-done | bytes 3276824
  22.8 2.3 %shard_map.103 = (bf16[1280,1280]{1,0:T(8,128)(2,1)S(1)}, bf16[1280,1280]{1,0:T(8,128)(2,1)S(1)}) custom-call(bf16[1280,1280]{1,0:T(8,128)(2,1)S(1)} %copy-done.1, bf16[1280,1280]{1,0:T(8,128)(2,1)} %collective-permute-done.5.refs_1_), custom_call_target="tpu_custom_call" | custom-call | tf_op jit(solution)/shard_map/pallas_call | solution.py:282
  25.1 1.2 %shard_map.104.chunk_ref = bf16[64,1280]{1,0:T(8,128)(2,1)S(1)} custom-call(bf16[64,1280]{1,0:T(8,128)(2,1)S(1)} %get-tuple-element.44.refs_0_, bf16[64,1280]{1,0:T(8,128)(2,1)S(1)} %collective-permute-done.4.refs_1_, bf16[1280,1280]{1,0:T(8,128)(2,1)S(1)} %get-tuple-element.49.refs_2_, bf16[1280,1280]{1,0:T(8,128)(2,1)S(1)} %get-tuple-element.50.refs_3_), custom_call_target="tpu_custom_call" | custom-call | flops 419430400 | bytes 6553600 | tf_op jit(solution)/shard_map/pallas_call | solution.py:325
  26.4 0.9 %collective-permute-done.3.refs_0_ = bf16[64,1280]{1,0:T(8,128)(2,1)S(1)} collective-permute-done((bf16[64,1280]{1,0:T(8,128)(2,1)S(1)}, bf16[64,1280]{1,0:T(8,128)(2,1)S(1)}, u32[]{:S(2)}, u32[]{:S(2)}) %collective-permute-start.3) | collective-permute-done | bytes 163872 | tf_op jit(solution)/shard_map/ppermute | solution.py:215
  27.3 1.7 %collective-permute-start.6 = (bf16[64,1280]{1,0:T(8,128)(2,1)S(1)}, bf16[64,1280]{1,0:T(8,128)(2,1)S(1)}, u32[]{:S(2)}, u32[]{:S(2)}) collective-permute-start(bf16[64,1280]{1,0:T(8,128)(2,1)S(1)} %collective-permute-done.3.refs_0_), channel_id=1, source_target_pairs={{0,4},{4,8},{8,12},{12,0},{1,5},{5,9},{9,13},{13,1},{2,6},{6,10},{... | collective-permute-start | bytes 491528 | tf_op jit(solution)/shard_map/ppermute | solution.py:215
  28.9 1.6 %collective-permute-done.7.refs_1_ = bf16[64,1280]{1,0:T(8,128)(2,1)S(1)} collective-permute-done((bf16[64,1280]{1,0:T(8,128)(2,1)S(1)}, bf16[64,1280]{1,0:T(8,128)(2,1)S(1)}, u32[]{:S(2)}, u32[]{:S(2)}) %collective-permute-start.7) | collective-permute-done | bytes 163872 | tf_op jit(solution)/shard_map/ppermute | solution.py:215
  30.6 1.2 %shard_map.105 = bf16[64,1280]{1,0:T(8,128)(2,1)S(1)} custom-call(bf16[64,1280]{1,0:T(8,128)(2,1)S(1)} %collective-permute-done.3.refs_0_, bf16[64,1280]{1,0:T(8,128)(2,1)S(1)} %collective-permute-done.7.refs_1_, bf16[1280,1280]{1,0:T(8,128)(2,1)S(1)} %get-tuple-element.49.refs_2_, bf16[1280,1280]{1,0:T(8,128)(2,1)S(1)} %get-tuple-element.50.refs_3_), custom_call_target="tpu_custom_call" | custom-call | flops 419430400 | bytes 6553600 | tf_op jit(solution)/shard_map/pallas_call | solution.py:325
  31.8 3.9 %collective-permute-start.9 = (bf16[64,1280]{1,0:T(8,128)(2,1)S(1)}, bf16[64,1280]{1,0:T(8,128)(2,1)S(1)}, u32[]{:S(2)}, u32[]{:S(2)}) collective-permute-start(bf16[64,1280]{1,0:T(8,128)(2,1)S(1)} %shard_map.105), channel_id=1, source_target_pairs={{0,12},{4,0},{8,4},{12,8},{1,13},{5,1},{9,5},{13,9},{2,14},{6,2},{... | collective-permute-start | bytes 491528 | tf_op jit(solution)/shard_map/ppermute | solution.py:215
  36.0 3.4 %collective-permute-done.8.refs_1_ = bf16[64,1280]{1,0:T(8,128)(2,1)S(1)} collective-permute-done((bf16[64,1280]{1,0:T(8,128)(2,1)S(1)}, bf16[64,1280]{1,0:T(8,128)(2,1)S(1)}, u32[]{:S(2)}, u32[]{:S(2)}) %collective-permute-start.8) | collective-permute-done | bytes 163872 | tf_op jit(solution)/shard_map/ppermute | solution.py:215
  39.5 2.0 %collective-permute-start.13 = (bf16[64,1280]{1,0:T(8,128)(2,1)S(1)}, bf16[64,1280]{1,0:T(8,128)(2,1)S(1)}, u32[]{:S(2)}, u32[]{:S(2)}) collective-permute-start(bf16[64,1280]{1,0:T(8,128)(2,1)S(1)} %collective-permute-done.8.refs_1_), channel_id=1, source_target_pairs={{0,4},{4,8},{8,12},{12,0},{1,5},{5,9},{9,13},{13,1},{2,6},{6,10},{... | collective-permute-start | bytes 491528 | tf_op jit(solution)/shard_map/ppermute | solution.py:215
  41.5 1.5 %collective-permute-start.14 = (bf16[64,1280]{1,0:T(8,128)(2,1)S(1)}, bf16[64,1280]{1,0:T(8,128)(2,1)S(1)}, u32[]{:S(2)}, u32[]{:S(2)}) collective-permute-start(bf16[64,1280]{1,0:T(8,128)(2,1)S(1)} %shard_map.108.refs_0_), channel_id=1, source_target_pairs={{0,2},{2,0},{1,3},{3,1},{4,6},{6,4},{5,7},{7,5},{8,10},{10,8},{9,1... | collective-permute-start | bytes 491528 | tf_op jit(solution)/shard_map/ppermute | solution.py:215
  43.1 1.2 %shard_map.106 = bf16[64,1280]{1,0:T(8,128)(2,1)S(1)} custom-call(bf16[64,1280]{1,0:T(8,128)(2,1)S(1)} %collective-permute-done.6.refs_0_, bf16[64,1280]{1,0:T(8,128)(2,1)S(1)} %collective-permute-done.8.refs_1_, bf16[1280,1280]{1,0:T(8,128)(2,1)S(1)} %get-tuple-element.49.refs_2_, bf16[1280,1280]{1,0:T(8,128)(2,1)S(1)} %get-tuple-element.50.refs_3_), custom_call_target="tpu_custom_call" | custom-call | flops 419430400 | bytes 6553600 | tf_op jit(solution)/shard_map/pallas_call | solution.py:325
  44.3 2.4 %collective-permute-start.10 = (bf16[64,1280]{1,0:T(8,128)(2,1)S(1)}, bf16[64,1280]{1,0:T(8,128)(2,1)S(1)}, u32[]{:S(2)}, u32[]{:S(2)}) collective-permute-start(bf16[64,1280]{1,0:T(8,128)(2,1)S(1)} %shard_map.106), channel_id=1, source_target_pairs={{0,8},{4,12},{8,0},{12,4},{1,9},{5,13},{9,1},{13,5},{2,10},{6,14},... | collective-permute-start | bytes 491528 | tf_op jit(solution)/shard_map/ppermute | solution.py:215
  46.8 1.3 %collective-permute-start.16 = (bf16[64,1280]{1,0:T(8,128)(2,1)S(1)}, bf16[64,1280]{1,0:T(8,128)(2,1)S(1)}, u32[]{:S(2)}, u32[]{:S(2)}) collective-permute-start(bf16[64,1280]{1,0:T(8,128)(2,1)S(1)} %shard_map.110.refs_1_), channel_id=1, source_target_pairs={{0,2},{2,0},{1,3},{3,1},{4,6},{6,4},{5,7},{7,5},{8,10},{10,8},{9,1... | collective-permute-start | bytes 491528 | tf_op jit(solution)/shard_map/ppermute | solution.py:215
  48.1 2.0 %collective-permute-done.13.refs_1_ = bf16[64,1280]{1,0:T(8,128)(2,1)S(1)} collective-permute-done((bf16[64,1280]{1,0:T(8,128)(2,1)S(1)}, bf16[64,1280]{1,0:T(8,128)(2,1)S(1)}, u32[]{:S(2)}, u32[]{:S(2)}) %collective-permute-start.13) | collective-permute-done | bytes 163872 | tf_op jit(solution)/shard_map/ppermute | solution.py:215
  50.1 1.2 %shard_map.109 = bf16[64,1280]{1,0:T(8,128)(2,1)S(1)} custom-call(bf16[64,1280]{1,0:T(8,128)(2,1)S(1)} %collective-permute-done.12.refs_0_, bf16[64,1280]{1,0:T(8,128)(2,1)S(1)} %collective-permute-done.13.refs_1_, bf16[1280,1280]{1,0:T(8,128)(2,1)S(1)} %get-tuple-element.49.refs_2_, bf16[1280,1280]{1,0:T(8,128)(2,1)S(1)} %get-tuple-element.50.refs_3_), custom_call_target="tpu_custom_call" | custom-call | flops 419430400 | bytes 6553600 | tf_op jit(solution)/shard_map/pallas_call | solution.py:325
  51.3 2.4 %collective-permute-start.15 = (bf16[64,1280]{1,0:T(8,128)(2,1)S(1)}, bf16[64,1280]{1,0:T(8,128)(2,1)S(1)}, u32[]{:S(2)}, u32[]{:S(2)}) collective-permute-start(bf16[64,1280]{1,0:T(8,128)(2,1)S(1)} %shard_map.109), channel_id=1, source_target_pairs={{0,4},{4,8},{8,12},{12,0},{1,5},{5,9},{9,13},{13,1},{2,6},{6,10},{... | collective-permute-start | bytes 491528 | tf_op jit(solution)/shard_map/ppermute | solution.py:215
  53.7 5.7 %collective-permute-done.10.chunk_ref = bf16[64,1280]{1,0:T(8,128)(2,1)S(1)} collective-permute-done((bf16[64,1280]{1,0:T(8,128)(2,1)S(1)}, bf16[64,1280]{1,0:T(8,128)(2,1)S(1)}, u32[]{:S(2)}, u32[]{:S(2)}) %collective-permute-start.10) | collective-permute-done | bytes 163872 | tf_op jit(solution)/shard_map/ppermute | solution.py:215
  59.5 1.6 %collective-permute-start.11 = (bf16[64,1280]{1,0:T(8,128)(2,1)S(1)}, bf16[64,1280]{1,0:T(8,128)(2,1)S(1)}, u32[]{:S(2)}, u32[]{:S(2)}) collective-permute-start(bf16[64,1280]{1,0:T(8,128)(2,1)S(1)} %shard_map.107.refs_0_), channel_id=1, source_target_pairs={{0,2},{2,0},{1,3},{3,1},{4,6},{6,4},{5,7},{7,5},{8,10},{10,8},{9,1... | collective-permute-start | bytes 491528 | tf_op jit(solution)/shard_map/ppermute | solution.py:215
  61.9 2.5 %shard_map.113.refs_7_ = bf16[2,32,2,5120]{3,2,1,0:T(2,128)(2,1)} custom-call(s32[2]{0:T(128)S(1)} %pad_add_fusion.place_ref, bf16[64,1280]{1,0:T(8,128)(2,1)S(1)} %shard_map.107.refs_0_, bf16[64,1280]{1,0:T(8,128)(2,1)S(1)} %shard_map.112.refs_1_, bf16[64,5120]{1,0:T(8,128)(2,1)S(1)} %get-tuple-element.71.refs_2_, s32[1,64]{1,0:T(1,128)S(1)} %bitcast.22, ...), custom_call_target="tpu_custom_call" | custom-call | tf_op jit(solution)/shard_map/pallas_call | solution.py:355
  64.3 2.3 %collective-permute-done.11.refs_0_ = bf16[64,1280]{1,0:T(8,128)(2,1)S(1)} collective-permute-done((bf16[64,1280]{1,0:T(8,128)(2,1)S(1)}, bf16[64,1280]{1,0:T(8,128)(2,1)S(1)}, u32[]{:S(2)}, u32[]{:S(2)}) %collective-permute-start.11) | collective-permute-done | bytes 163872 | tf_op jit(solution)/shard_map/ppermute | solution.py:215
  66.6 2.6 %collective-permute-done.17.refs_1_ = bf16[64,1280]{1,0:T(8,128)(2,1)S(1)} collective-permute-done((bf16[64,1280]{1,0:T(8,128)(2,1)S(1)}, bf16[64,1280]{1,0:T(8,128)(2,1)S(1)}, u32[]{:S(2)}, u32[]{:S(2)}) %collective-permute-start.17) | collective-permute-done | bytes 163872 | tf_op jit(solution)/shard_map/ppermute | solution.py:215
  69.2 2.5 %shard_map.114 = bf16[2,32,2,5120]{3,2,1,0:T(2,128)(2,1)} custom-call(s32[2]{0:T(128)S(1)} %pad_add_fusion.place_ref, bf16[64,1280]{1,0:T(8,128)(2,1)S(1)} %collective-permute-done.11.refs_0_, bf16[64,1280]{1,0:T(8,128)(2,1)S(1)} %collective-permute-done.17.refs_1_, bf16[64,5120]{1,0:T(8,128)(2,1)S(1)} %get-tuple-element.69.refs_2_, ...), custom_call_target="tpu_custom_call", output_to_operand_aliasing={{}: (8, {})} | custom-call | tf_op jit(solution)/shard_map/pallas_call | solution.py:355
  (38 shorter events, 2.2 us)
Async XLA Ops:
  0.0 19.5 %collective-permute-start.5 = (bf16[1280,1280]{1,0:T(8,128)(2,1)}, bf16[1280,1280]{1,0:T(8,128)(2,1)}, u32[]{:S(2)}, u32[]{:S(2)}) collective-permute-start(bf16[1280,1280]{1,0:T(8,128)(2,1)} %refs_0_), channel_id=1, source_target_pairs={{0,1},{1,0},{2,3},{3,2},{4,5},{5,4},{6,7},{7,6},{8,9},{9,8},{10,11... | collective-permute-start | bytes 9830408 | tf_op jit(solution)/shard_map/ppermute | solution.py:215
  2.2 10.9 %collective-permute-start.1 = (bf16[528,128]{1,0:T(8,128)(2,1)}, bf16[528,128]{1,0:T(8,128)(2,1)S(1)}, u32[]{:S(2)}, u32[]{:S(2)}) collective-permute-start(bf16[528,128]{1,0:T(8,128)(2,1)} %shard_map.100.refs_1_), channel_id=1, source_target_pairs={{0,4},{4,8},{8,12},{12,0},{1,5},{5,9},{9,13},{13,1},{2,6},{6,10},{... | collective-permute-start | bytes 405512 | tf_op jit(solution)/shard_map/ppermute | solution.py:234
  4.9 8.3 %collective-permute-start.2 = (bf16[528,128]{1,0:T(8,128)(2,1)}, bf16[528,128]{1,0:T(8,128)(2,1)S(1)}, u32[]{:S(2)}, u32[]{:S(2)}) collective-permute-start(bf16[528,128]{1,0:T(8,128)(2,1)} %shard_map.100.refs_1_), channel_id=1, source_target_pairs={{0,8},{4,12},{1,9},{5,13},{2,10},{6,14},{3,11},{7,15},{16,24},{20,... | collective-permute-start | bytes 405512 | tf_op jit(solution)/shard_map/ppermute | solution.py:234
  9.4 3.8 %collective-permute-start = (s32[1,64]{1,0:T(1,128)}, s32[1,64]{1,0:T(1,128)S(1)}, u32[]{:S(2)}, u32[]{:S(2)}) collective-permute-start(s32[1,64]{1,0:T(1,128)} %bitcast.21), channel_id=1, source_target_pairs={{0,2},{2,0},{1,3},{3,1},{4,6},{6,4},{5,7},{7,5},{8,10},{10,8},{9,1... | collective-permute-start | bytes 776 | tf_op jit(solution)/shard_map/ppermute | solution.py:215
  11.0 0.9 %copy-start.3 = (bf16[528,128]{1,0:T(8,128)(2,1)S(1)}, bf16[528,128]{1,0:T(8,128)(2,1)}, u32[]{:S(2)}) copy-start(bf16[528,128]{1,0:T(8,128)(2,1)} %shard_map.100.refs_1_) | copy-start | bytes 405508
  11.9 1.0 %copy-start.4 = (bf16[1,128,10,128]{3,1,2,0:T(8,128)(2,1)S(1)}, bf16[1,128,10,128]{3,1,2,0:T(8,128)(2,1)}, u32[]{:S(2)}) copy-start(bf16[1,128,10,128]{3,1,2,0:T(8,128)(2,1)} %param.10) | copy-start | bytes 983044
  16.5 3.1 %collective-permute-start.4 = (bf16[64,1280]{1,0:T(8,128)(2,1)S(1)}, bf16[64,1280]{1,0:T(8,128)(2,1)S(1)}, u32[]{:S(2)}, u32[]{:S(2)}) collective-permute-start(bf16[64,1280]{1,0:T(8,128)(2,1)S(1)} %get-tuple-element.45), channel_id=1, source_target_pairs={{0,1},{1,0},{2,3},{3,2},{4,5},{5,4},{6,7},{7,6},{8,9},{9,8},{10,11... | collective-permute-start | bytes 491528 | tf_op jit(solution)/shard_map/ppermute | solution.py:215
  16.5 10.7 %collective-permute-start.3 = (bf16[64,1280]{1,0:T(8,128)(2,1)S(1)}, bf16[64,1280]{1,0:T(8,128)(2,1)S(1)}, u32[]{:S(2)}, u32[]{:S(2)}) collective-permute-start(bf16[64,1280]{1,0:T(8,128)(2,1)S(1)} %get-tuple-element.44.refs_0_), channel_id=1, source_target_pairs={{0,4},{4,8},{8,12},{12,0},{1,5},{5,9},{9,13},{13,1},{2,6},{6,10},{... | collective-permute-start | bytes 491528 | tf_op jit(solution)/shard_map/ppermute | solution.py:215
  19.5 11.0 %collective-permute-start.7 = (bf16[64,1280]{1,0:T(8,128)(2,1)S(1)}, bf16[64,1280]{1,0:T(8,128)(2,1)S(1)}, u32[]{:S(2)}, u32[]{:S(2)}) collective-permute-start(bf16[64,1280]{1,0:T(8,128)(2,1)S(1)} %collective-permute-done.4.refs_1_), channel_id=1, source_target_pairs={{0,4},{4,8},{8,12},{12,0},{1,5},{5,9},{9,13},{13,1},{2,6},{6,10},{... | collective-permute-start | bytes 491528 | tf_op jit(solution)/shard_map/ppermute | solution.py:215
  20.9 1.9 %copy-start.1 = (bf16[1280,1280]{1,0:T(8,128)(2,1)S(1)}, bf16[1280,1280]{1,0:T(8,128)(2,1)}, u32[]{:S(2)}) copy-start(bf16[1280,1280]{1,0:T(8,128)(2,1)} %refs_0_) | copy-start | bytes 9830404
  26.4 15.1 %copy-start = (bf16[1,64,5120]{2,1,0:T(8,128)(2,1)S(1)}, bf16[1,64,5120]{2,1,0:T(8,128)(2,1)}, u32[]{:S(2)}) copy-start(bf16[1,64,5120]{2,1,0:T(8,128)(2,1)} %param.14) | copy-start | bytes 1966084
  27.3 8.4 %collective-permute-start.6 = (bf16[64,1280]{1,0:T(8,128)(2,1)S(1)}, bf16[64,1280]{1,0:T(8,128)(2,1)S(1)}, u32[]{:S(2)}, u32[]{:S(2)}) collective-permute-start(bf16[64,1280]{1,0:T(8,128)(2,1)S(1)} %collective-permute-done.3.refs_0_), channel_id=1, source_target_pairs={{0,4},{4,8},{8,12},{12,0},{1,5},{5,9},{9,13},{13,1},{2,6},{6,10},{... | collective-permute-start | bytes 491528 | tf_op jit(solution)/shard_map/ppermute | solution.py:215
  30.5 8.9 %collective-permute-start.8 = (bf16[64,1280]{1,0:T(8,128)(2,1)S(1)}, bf16[64,1280]{1,0:T(8,128)(2,1)S(1)}, u32[]{:S(2)}, u32[]{:S(2)}) collective-permute-start(bf16[64,1280]{1,0:T(8,128)(2,1)S(1)} %collective-permute-done.7.refs_1_), channel_id=1, source_target_pairs={{0,4},{4,8},{8,12},{12,0},{1,5},{5,9},{9,13},{13,1},{2,6},{6,10},{... | collective-permute-start | bytes 491528 | tf_op jit(solution)/shard_map/ppermute | solution.py:215
  31.8 11.3 %collective-permute-start.9 = (bf16[64,1280]{1,0:T(8,128)(2,1)S(1)}, bf16[64,1280]{1,0:T(8,128)(2,1)S(1)}, u32[]{:S(2)}, u32[]{:S(2)}) collective-permute-start(bf16[64,1280]{1,0:T(8,128)(2,1)S(1)} %shard_map.105), channel_id=1, source_target_pairs={{0,12},{4,0},{8,4},{12,8},{1,13},{5,1},{9,5},{13,9},{2,14},{6,2},{... | collective-permute-start | bytes 491528 | tf_op jit(solution)/shard_map/ppermute | solution.py:215
  35.7 11.1 %collective-permute-start.12 = (bf16[64,1280]{1,0:T(8,128)(2,1)S(1)}, bf16[64,1280]{1,0:T(8,128)(2,1)S(1)}, u32[]{:S(2)}, u32[]{:S(2)}) collective-permute-start(bf16[64,1280]{1,0:T(8,128)(2,1)S(1)} %collective-permute-done.6.refs_0_), channel_id=1, source_target_pairs={{0,4},{4,8},{8,12},{12,0},{1,5},{5,9},{9,13},{13,1},{2,6},{6,10},{... | collective-permute-start | bytes 491528 | tf_op jit(solution)/shard_map/ppermute | solution.py:215
  39.5 10.6 %collective-permute-start.13 = (bf16[64,1280]{1,0:T(8,128)(2,1)S(1)}, bf16[64,1280]{1,0:T(8,128)(2,1)S(1)}, u32[]{:S(2)}, u32[]{:S(2)}) collective-permute-start(bf16[64,1280]{1,0:T(8,128)(2,1)S(1)} %collective-permute-done.8.refs_1_), channel_id=1, source_target_pairs={{0,4},{4,8},{8,12},{12,0},{1,5},{5,9},{9,13},{13,1},{2,6},{6,10},{... | collective-permute-start | bytes 491528 | tf_op jit(solution)/shard_map/ppermute | solution.py:215
  41.5 8.6 %collective-permute-start.14 = (bf16[64,1280]{1,0:T(8,128)(2,1)S(1)}, bf16[64,1280]{1,0:T(8,128)(2,1)S(1)}, u32[]{:S(2)}, u32[]{:S(2)}) collective-permute-start(bf16[64,1280]{1,0:T(8,128)(2,1)S(1)} %shard_map.108.refs_0_), channel_id=1, source_target_pairs={{0,2},{2,0},{1,3},{3,1},{4,6},{6,4},{5,7},{7,5},{8,10},{10,8},{9,1... | collective-permute-start | bytes 491528 | tf_op jit(solution)/shard_map/ppermute | solution.py:215
  44.3 15.1 %collective-permute-start.10 = (bf16[64,1280]{1,0:T(8,128)(2,1)S(1)}, bf16[64,1280]{1,0:T(8,128)(2,1)S(1)}, u32[]{:S(2)}, u32[]{:S(2)}) collective-permute-start(bf16[64,1280]{1,0:T(8,128)(2,1)S(1)} %shard_map.106), channel_id=1, source_target_pairs={{0,8},{4,12},{8,0},{12,4},{1,9},{5,13},{9,1},{13,5},{2,10},{6,14},... | collective-permute-start | bytes 491528 | tf_op jit(solution)/shard_map/ppermute | solution.py:215
  46.8 15.0 %copy-start.7 = (bf16[5120]{0:T(1024)(128)(2,1)S(1)}, bf16[5120]{0:T(1024)(128)(2,1)}, u32[]{:S(2)}) copy-start(bf16[5120]{0:T(1024)(128)(2,1)} %param.16) | copy-start | bytes 30724
  46.8 15.1 %copy-start.2 = (bf16[5120,32]{0,1:T(8,128)(2,1)S(1)}, bf16[5120,32]{0,1:T(8,128)(2,1)}, u32[]{:S(2)}) copy-start(bf16[5120,32]{0,1:T(8,128)(2,1)} %param.17) | copy-start | bytes 983044
  46.8 15.0 %copy-start.5 = (s32[64]{0:T(128)S(1)}, s32[64]{0:T(128)}, u32[]{:S(2)}) copy-start(s32[64]{0:T(128)} %param.19) | copy-start | bytes 772
  46.8 15.0 %copy-start.6 = (s32[1,64,1]{1,2,0:T(1,128)S(1)}, s32[1,64,1]{1,2,0:T(1,128)}, u32[]{:S(2)}) copy-start(s32[1,64,1]{1,2,0:T(1,128)} %param.18) | copy-start | bytes 772
  46.8 14.2 %collective-permute-start.16 = (bf16[64,1280]{1,0:T(8,128)(2,1)S(1)}, bf16[64,1280]{1,0:T(8,128)(2,1)S(1)}, u32[]{:S(2)}, u32[]{:S(2)}) collective-permute-start(bf16[64,1280]{1,0:T(8,128)(2,1)S(1)} %shard_map.110.refs_1_), channel_id=1, source_target_pairs={{0,2},{2,0},{1,3},{3,1},{4,6},{6,4},{5,7},{7,5},{8,10},{10,8},{9,1... | collective-permute-start | bytes 491528 | tf_op jit(solution)/shard_map/ppermute | solution.py:215
  51.3 9.7 %collective-permute-start.15 = (bf16[64,1280]{1,0:T(8,128)(2,1)S(1)}, bf16[64,1280]{1,0:T(8,128)(2,1)S(1)}, u32[]{:S(2)}, u32[]{:S(2)}) collective-permute-start(bf16[64,1280]{1,0:T(8,128)(2,1)S(1)} %shard_map.109), channel_id=1, source_target_pairs={{0,4},{4,8},{8,12},{12,0},{1,5},{5,9},{9,13},{13,1},{2,6},{6,10},{... | collective-permute-start | bytes 491528 | tf_op jit(solution)/shard_map/ppermute | solution.py:215
  59.5 7.1 %collective-permute-start.11 = (bf16[64,1280]{1,0:T(8,128)(2,1)S(1)}, bf16[64,1280]{1,0:T(8,128)(2,1)S(1)}, u32[]{:S(2)}, u32[]{:S(2)}) collective-permute-start(bf16[64,1280]{1,0:T(8,128)(2,1)S(1)} %shard_map.107.refs_0_), channel_id=1, source_target_pairs={{0,2},{2,0},{1,3},{3,1},{4,6},{6,4},{5,7},{7,5},{8,10},{10,8},{9,1... | collective-permute-start | bytes 491528 | tf_op jit(solution)/shard_map/ppermute | solution.py:215
  61.1 8.0 %collective-permute-start.17 = (bf16[64,1280]{1,0:T(8,128)(2,1)S(1)}, bf16[64,1280]{1,0:T(8,128)(2,1)S(1)}, u32[]{:S(2)}, u32[]{:S(2)}) collective-permute-start(bf16[64,1280]{1,0:T(8,128)(2,1)S(1)} %shard_map.112.refs_1_), channel_id=1, source_target_pairs={{0,2},{2,0},{1,3},{3,1},{4,6},{6,4},{5,7},{7,5},{8,10},{10,8},{9,1... | collective-permute-start | bytes 491528 | tf_op jit(solution)/shard_map/ppermute | solution.py:215

commit v7 on v6

--- a/solution.py
+++ b/solution.py
@@ -135,14 +135,21 @@
         lax.broadcasted_iota(jnp.int32, (rows, rows), 0)
         < lax.broadcasted_iota(jnp.int32, (rows, rows), 1)
     ).astype(jnp.bfloat16)
-    total_ref[...] = hidden_ref[...].astype(jnp.float32)
+    total_ref[...] = hidden_ref[...]
     for step, chunk_ref in zip(steps, chunk_refs):
-        part = columns_of(chunk_ref, step, spots, ctx_index)
-        total_ref[:, part] = chunk_ref[...].astype(jnp.float32)
-    hidden = total_ref[...]
-    power = jnp.sum(hidden * hidden, axis=1, keepdims=True)
+        total_ref[:, columns_of(chunk_ref, step, spots, ctx_index)] = chunk_ref[...]
+    pieces = out_sem.shape[0]
+    piece = width // pieces
+    parts = [slice(number * piece, (number + 1) * piece) for number in range(pieces)]
+    power = jnp.zeros((rows, 1), jnp.float32)
+    for part in parts:
+        hidden = total_ref[:, part].astype(jnp.float32)
+        power = power + jnp.sum(hidden * hidden, axis=1, keepdims=True)
     factor = lax.rsqrt(power / width + EPSILON)
-    normed_ref[...] = (hidden * factor * gain_ref[...].astype(jnp.float32)).astype(jnp.bfloat16)
+    for part in parts:
+        gain = gain_ref[:, part].astype(jnp.float32)
+        hidden = total_ref[:, part].astype(jnp.float32)
+        normed_ref[:, part] = (hidden * factor * gain).astype(jnp.bfloat16)
     ids = id_ref[...]
     onehot = (ids == lax.broadcasted_iota(jnp.int32, (experts, rows), 0)).astype(jnp.float32)
     earlier = jnp.dot(onehot.astype(jnp.bfloat16), upper, preferred_element_type=jnp.float32)
@@ -165,14 +172,21 @@
     target = jnp.where((ranking < limits) & (local >= 0) & (local < here), target, -1)
     table = lax.broadcasted_iota(jnp.int32, (here * CAP, rows), 0) == target
     slot_gates = jnp.sum(jnp.where(table, gates, 0.0), axis=1, keepdims=True)
-    slots = jnp.dot(
-        table.astype(jnp.bfloat16), normed_ref[...], preferred_element_type=jnp.float32
-    )
-    result_ref[...] = (slots * slot_gates).astype(jnp.bfloat16).reshape(result_ref.shape)
+    table = table.astype(jnp.bfloat16)
     source = lax.rem(exp_index - back + exp_count, exp_count)
-    copy = pltpu.make_async_copy(result_ref, out_ref.at[source], out_sem)
-    copy.start()
-    copy.wait()
+    copies = []
+    for number, part in enumerate(parts):
+        slots = jnp.dot(table, normed_ref[:, part], preferred_element_type=jnp.float32)
+        result_ref[:, :, part] = (
+            (slots * slot_gates).astype(jnp.bfloat16).reshape(here, CAP, piece)
+        )
+        copy = pltpu.make_async_copy(
+            result_ref.at[:, :, part], out_ref.at[source, :, :, part], out_sem.at[number]
+        )
+        copy.start()
+        copies.append(copy)
+    for copy in copies:
+        copy.wait()
 
 
 def on_device(
@@ -358,10 +372,10 @@
             in_specs=[smem] + [vmem] * (len(operands) - 1) + [anywhere] * len(kept),
             out_specs=anywhere,
             scratch_shapes=[
-                pltpu.VMEM((part_rows, width), f32),
+                pltpu.VMEM((part_rows, width), bf16),
                 pltpu.VMEM((part_rows, width), bf16),
                 pltpu.VMEM((experts_here, CAP, width), bf16),
-                pltpu.SemaphoreType.DMA,
+                pltpu.SemaphoreType.DMA((5 if width % (5 * 128) == 0 else 1,)),
             ],
             input_output_aliases={len(operands): 0} if kept else {},
             compiler_params=params,

time: 71.9 us -> 71.8 us (level)
  no operation moved by 1% of the time
where the time goes in v7:
time: 71.8 us; the launch traced here: 71.5 us
  starting transfers between devices  31.2 us (43%)
  waiting for transfers between devices  18.6 us (26%)
  Pallas kernels  17.6 us (25%)
  local copies, waits for them, and re-layouts  3.85 us (5%)
    ppermute x16, starting transfers between devices, over(): lax.ppermute(array, axis, [(i, (i + step) % count) for i in range(count)])  24.1 us
    ppermute x16, waiting for transfers between devices, over(): lax.ppermute(array, axis, [(i, (i + step) % count) for i in range(count)])  18.6 us
    ppermute x2, starting transfers between devices, on_device(): lax.ppermute(pack, 'ctx', [(i, (i + step) % ctx_count) for i in range(ctx...  7.11 us
    pallas_call x4, Pallas kernels, on_device(): total = project(*block, *weights)  4.95 us
    pallas_call x2, Pallas kernels, on_device(): pl.pallas_call(functools.partial(finish_kernel, late_steps, spots, back,...  4.75 us
    unnamed x16, local copies, waits for them, and re-layouts  3.83 us
    pallas_call x1, Pallas kernels, on_device(): pl.pallas_call(functools.partial(attention_kernel, heads // groups, group...  3.26 us
    pallas_call x1, Pallas kernels, on_device(): pl.pallas_call(functools.partial(stage_kernel, pair), out_shape=[jax.Shap...  2.32 us
  transfers between devices with their start and end apart: 18, of which 7 were waited for; matrix products, arithmetic and copies ran while one was open for 0% of the time, Pallas kernels for 21%

profile of v7, /device:TPU:0, one launch (start us, length us, event | category | flops | bytes accessed | tf_op | source)
XLA Modules:
  0.0 71.5 jit_solution(5818243814491375006)
XLA Ops:
  0.5 1.8 %shard_map.100.refs_1_ = bf16[528,128]{1,0:T(8,128)(2,1)} custom-call(bf16[256,128]{1,0:T(8,128)(2,1)} %bitcast.23, bf16[256,128]{1,0:T(8,128)(2,1)} %bitcast.24, s32[1,128]{1,0:T(1,128)} %doc_ref.1), custom_call_target="tpu_custom_call" | custom-call | tf_op jit(solution)/shard_map/pallas_call | solution.py:234
  2.2 2.6 %collective-permute-start.1 = (bf16[528,128]{1,0:T(8,128)(2,1)}, bf16[528,128]{1,0:T(8,128)(2,1)S(1)}, u32[]{:S(2)}, u32[]{:S(2)}) collective-permute-start(bf16[528,128]{1,0:T(8,128)(2,1)} %shard_map.100.refs_1_), channel_id=1, source_target_pairs={{0,4},{4,8},{8,12},{12,0},{1,5},{5,9},{9,13},{13,1},{2,6},{6,10},{... | collective-permute-start | bytes 405512 | tf_op jit(solution)/shard_map/ppermute | solution.py:248
  4.9 4.5 %collective-permute-start.2 = (bf16[528,128]{1,0:T(8,128)(2,1)}, bf16[528,128]{1,0:T(8,128)(2,1)S(1)}, u32[]{:S(2)}, u32[]{:S(2)}) collective-permute-start(bf16[528,128]{1,0:T(8,128)(2,1)} %shard_map.100.refs_1_), channel_id=1, source_target_pairs={{0,8},{4,12},{1,9},{5,13},{2,10},{6,14},{3,11},{7,15},{16,24},{20,... | collective-permute-start | bytes 405512 | tf_op jit(solution)/shard_map/ppermute | solution.py:248
  9.4 1.6 %collective-permute-start = (s32[1,64]{1,0:T(1,128)}, s32[1,64]{1,0:T(1,128)S(1)}, u32[]{:S(2)}, u32[]{:S(2)}) collective-permute-start(s32[1,64]{1,0:T(1,128)} %bitcast.21), channel_id=1, source_target_pairs={{0,2},{2,0},{1,3},{3,1},{4,6},{6,4},{5,7},{7,5},{8,10},{10,8},{9,1... | collective-permute-start | bytes 776 | tf_op jit(solution)/shard_map/ppermute | solution.py:229
  11.0 0.9 %copy-done.3 = bf16[528,128]{1,0:T(8,128)(2,1)S(1)} copy-done((bf16[528,128]{1,0:T(8,128)(2,1)S(1)}, bf16[528,128]{1,0:T(8,128)(2,1)}, u32[]{:S(2)}) %copy-start.3) | copy-done | bytes 135192
  11.9 1.0 %copy-done.4 = bf16[1,128,10,128]{3,1,2,0:T(8,128)(2,1)S(1)} copy-done((bf16[1,128,10,128]{3,1,2,0:T(8,128)(2,1)S(1)}, bf16[1,128,10,128]{3,1,2,0:T(8,128)(2,1)}, u32[]{:S(2)}) %copy-start.4) | copy-done | bytes 327704
  13.2 3.3 %shard_map.102 = (bf16[64,1280]{1,0:T(8,128)(2,1)S(1)}, bf16[64,1280]{1,0:T(8,128)(2,1)S(1)}) custom-call(s32[2]{0:T(128)S(1)} %pad_add_fusion.1.place_ref, bf16[10,128,128]{2,1,0:T(8,128)(2,1)S(1)} %get-tuple-element.42.query_ref, bf16[528,128]{1,0:T(8,128)(2,1)S(1)} %get-tuple-element.43.refs_0_, bf16[528,128]{1,0:T(8,128)(2,1)S(1)} %collective-permute-done.1.refs_1_, ...), custom_call_target="tpu_custom_call" | custom-call | tf_op jit(solution)/shard_map/pallas_call | solution.py:274
  16.5 3.0 %collective-permute-start.3 = (bf16[64,1280]{1,0:T(8,128)(2,1)S(1)}, bf16[64,1280]{1,0:T(8,128)(2,1)S(1)}, u32[]{:S(2)}, u32[]{:S(2)}) collective-permute-start(bf16[64,1280]{1,0:T(8,128)(2,1)S(1)} %get-tuple-element.44.refs_0_), channel_id=1, source_target_pairs={{0,4},{4,8},{8,12},{12,0},{1,5},{5,9},{9,13},{13,1},{2,6},{6,10},{... | collective-permute-start | bytes 491528 | tf_op jit(solution)/shard_map/ppermute | solution.py:229
  19.5 1.3 %collective-permute-start.7 = (bf16[64,1280]{1,0:T(8,128)(2,1)S(1)}, bf16[64,1280]{1,0:T(8,128)(2,1)S(1)}, u32[]{:S(2)}, u32[]{:S(2)}) collective-permute-start(bf16[64,1280]{1,0:T(8,128)(2,1)S(1)} %collective-permute-done.4.refs_1_), channel_id=1, source_target_pairs={{0,4},{4,8},{8,12},{12,0},{1,5},{5,9},{9,13},{13,1},{2,6},{6,10},{... | collective-permute-start | bytes 491528 | tf_op jit(solution)/shard_map/ppermute | solution.py:229
  20.9 1.9 %copy-done.1 = bf16[1280,1280]{1,0:T(8,128)(2,1)S(1)} copy-done((bf16[1280,1280]{1,0:T(8,128)(2,1)S(1)}, bf16[1280,1280]{1,0:T(8,128)(2,1)}, u32[]{:S(2)}) %copy-start.1) | copy-done | bytes 3276824
  22.8 2.3 %shard_map.103 = (bf16[1280,1280]{1,0:T(8,128)(2,1)S(1)}, bf16[1280,1280]{1,0:T(8,128)(2,1)S(1)}) custom-call(bf16[1280,1280]{1,0:T(8,128)(2,1)S(1)} %copy-done.1, bf16[1280,1280]{1,0:T(8,128)(2,1)} %collective-permute-done.5.refs_1_), custom_call_target="tpu_custom_call" | custom-call | tf_op jit(solution)/shard_map/pallas_call | solution.py:296
  25.1 1.2 %shard_map.104.chunk_ref = bf16[64,1280]{1,0:T(8,128)(2,1)S(1)} custom-call(bf16[64,1280]{1,0:T(8,128)(2,1)S(1)} %get-tuple-element.44.refs_0_, bf16[64,1280]{1,0:T(8,128)(2,1)S(1)} %collective-permute-done.4.refs_1_, bf16[1280,1280]{1,0:T(8,128)(2,1)S(1)} %get-tuple-element.49.refs_2_, bf16[1280,1280]{1,0:T(8,128)(2,1)S(1)} %get-tuple-element.50.refs_3_), custom_call_target="tpu_custom_call" | custom-call | flops 419430400 | bytes 6553600 | tf_op jit(solution)/shard_map/pallas_call | solution.py:339
  26.4 0.9 %collective-permute-done.3.refs_0_ = bf16[64,1280]{1,0:T(8,128)(2,1)S(1)} collective-permute-done((bf16[64,1280]{1,0:T(8,128)(2,1)S(1)}, bf16[64,1280]{1,0:T(8,128)(2,1)S(1)}, u32[]{:S(2)}, u32[]{:S(2)}) %collective-permute-start.3) | collective-permute-done | bytes 163872 | tf_op jit(solution)/shard_map/ppermute | solution.py:229
  27.3 1.7 %collective-permute-start.6 = (bf16[64,1280]{1,0:T(8,128)(2,1)S(1)}, bf16[64,1280]{1,0:T(8,128)(2,1)S(1)}, u32[]{:S(2)}, u32[]{:S(2)}) collective-permute-start(bf16[64,1280]{1,0:T(8,128)(2,1)S(1)} %collective-permute-done.3.refs_0_), channel_id=1, source_target_pairs={{0,4},{4,8},{8,12},{12,0},{1,5},{5,9},{9,13},{13,1},{2,6},{6,10},{... | collective-permute-start | bytes 491528 | tf_op jit(solution)/shard_map/ppermute | solution.py:229
  28.9 1.6 %collective-permute-done.7.refs_1_ = bf16[64,1280]{1,0:T(8,128)(2,1)S(1)} collective-permute-done((bf16[64,1280]{1,0:T(8,128)(2,1)S(1)}, bf16[64,1280]{1,0:T(8,128)(2,1)S(1)}, u32[]{:S(2)}, u32[]{:S(2)}) %collective-permute-start.7) | collective-permute-done | bytes 163872 | tf_op jit(solution)/shard_map/ppermute | solution.py:229
  30.6 1.2 %shard_map.105 = bf16[64,1280]{1,0:T(8,128)(2,1)S(1)} custom-call(bf16[64,1280]{1,0:T(8,128)(2,1)S(1)} %collective-permute-done.3.refs_0_, bf16[64,1280]{1,0:T(8,128)(2,1)S(1)} %collective-permute-done.7.refs_1_, bf16[1280,1280]{1,0:T(8,128)(2,1)S(1)} %get-tuple-element.49.refs_2_, bf16[1280,1280]{1,0:T(8,128)(2,1)S(1)} %get-tuple-element.50.refs_3_), custom_call_target="tpu_custom_call" | custom-call | flops 419430400 | bytes 6553600 | tf_op jit(solution)/shard_map/pallas_call | solution.py:339
  31.8 3.9 %collective-permute-start.9 = (bf16[64,1280]{1,0:T(8,128)(2,1)S(1)}, bf16[64,1280]{1,0:T(8,128)(2,1)S(1)}, u32[]{:S(2)}, u32[]{:S(2)}) collective-permute-start(bf16[64,1280]{1,0:T(8,128)(2,1)S(1)} %shard_map.105), channel_id=1, source_target_pairs={{0,12},{4,0},{8,4},{12,8},{1,13},{5,1},{9,5},{13,9},{2,14},{6,2},{... | collective-permute-start | bytes 491528 | tf_op jit(solution)/shard_map/ppermute | solution.py:229
  36.0 3.4 %collective-permute-done.8.refs_1_ = bf16[64,1280]{1,0:T(8,128)(2,1)S(1)} collective-permute-done((bf16[64,1280]{1,0:T(8,128)(2,1)S(1)}, bf16[64,1280]{1,0:T(8,128)(2,1)S(1)}, u32[]{:S(2)}, u32[]{:S(2)}) %collective-permute-start.8) | collective-permute-done | bytes 163872 | tf_op jit(solution)/shard_map/ppermute | solution.py:229
  39.5 2.0 %collective-permute-start.13 = (bf16[64,1280]{1,0:T(8,128)(2,1)S(1)}, bf16[64,1280]{1,0:T(8,128)(2,1)S(1)}, u32[]{:S(2)}, u32[]{:S(2)}) collective-permute-start(bf16[64,1280]{1,0:T(8,128)(2,1)S(1)} %collective-permute-done.8.refs_1_), channel_id=1, source_target_pairs={{0,4},{4,8},{8,12},{12,0},{1,5},{5,9},{9,13},{13,1},{2,6},{6,10},{... | collective-permute-start | bytes 491528 | tf_op jit(solution)/shard_map/ppermute | solution.py:229
  41.5 1.5 %collective-permute-start.14 = (bf16[64,1280]{1,0:T(8,128)(2,1)S(1)}, bf16[64,1280]{1,0:T(8,128)(2,1)S(1)}, u32[]{:S(2)}, u32[]{:S(2)}) collective-permute-start(bf16[64,1280]{1,0:T(8,128)(2,1)S(1)} %shard_map.108.refs_0_), channel_id=1, source_target_pairs={{0,2},{2,0},{1,3},{3,1},{4,6},{6,4},{5,7},{7,5},{8,10},{10,8},{9,1... | collective-permute-start | bytes 491528 | tf_op jit(solution)/shard_map/ppermute | solution.py:229
  43.1 1.2 %shard_map.106 = bf16[64,1280]{1,0:T(8,128)(2,1)S(1)} custom-call(bf16[64,1280]{1,0:T(8,128)(2,1)S(1)} %collective-permute-done.6.refs_0_, bf16[64,1280]{1,0:T(8,128)(2,1)S(1)} %collective-permute-done.8.refs_1_, bf16[1280,1280]{1,0:T(8,128)(2,1)S(1)} %get-tuple-element.49.refs_2_, bf16[1280,1280]{1,0:T(8,128)(2,1)S(1)} %get-tuple-element.50.refs_3_), custom_call_target="tpu_custom_call" | custom-call | flops 419430400 | bytes 6553600 | tf_op jit(solution)/shard_map/pallas_call | solution.py:339
  44.3 2.4 %collective-permute-start.10 = (bf16[64,1280]{1,0:T(8,128)(2,1)S(1)}, bf16[64,1280]{1,0:T(8,128)(2,1)S(1)}, u32[]{:S(2)}, u32[]{:S(2)}) collective-permute-start(bf16[64,1280]{1,0:T(8,128)(2,1)S(1)} %shard_map.106), channel_id=1, source_target_pairs={{0,8},{4,12},{8,0},{12,4},{1,9},{5,13},{9,1},{13,5},{2,10},{6,14},... | collective-permute-start | bytes 491528 | tf_op jit(solution)/shard_map/ppermute | solution.py:229
  46.8 1.3 %collective-permute-start.16 = (bf16[64,1280]{1,0:T(8,128)(2,1)S(1)}, bf16[64,1280]{1,0:T(8,128)(2,1)S(1)}, u32[]{:S(2)}, u32[]{:S(2)}) collective-permute-start(bf16[64,1280]{1,0:T(8,128)(2,1)S(1)} %shard_map.110.refs_1_), channel_id=1, source_target_pairs={{0,2},{2,0},{1,3},{3,1},{4,6},{6,4},{5,7},{7,5},{8,10},{10,8},{9,1... | collective-permute-start | bytes 491528 | tf_op jit(solution)/shard_map/ppermute | solution.py:229
  48.1 2.0 %collective-permute-done.13.refs_1_ = bf16[64,1280]{1,0:T(8,128)(2,1)S(1)} collective-permute-done((bf16[64,1280]{1,0:T(8,128)(2,1)S(1)}, bf16[64,1280]{1,0:T(8,128)(2,1)S(1)}, u32[]{:S(2)}, u32[]{:S(2)}) %collective-permute-start.13) | collective-permute-done | bytes 163872 | tf_op jit(solution)/shard_map/ppermute | solution.py:229
  50.1 1.2 %shard_map.109 = bf16[64,1280]{1,0:T(8,128)(2,1)S(1)} custom-call(bf16[64,1280]{1,0:T(8,128)(2,1)S(1)} %collective-permute-done.12.refs_0_, bf16[64,1280]{1,0:T(8,128)(2,1)S(1)} %collective-permute-done.13.refs_1_, bf16[1280,1280]{1,0:T(8,128)(2,1)S(1)} %get-tuple-element.49.refs_2_, bf16[1280,1280]{1,0:T(8,128)(2,1)S(1)} %get-tuple-element.50.refs_3_), custom_call_target="tpu_custom_call" | custom-call | flops 419430400 | bytes 6553600 | tf_op jit(solution)/shard_map/pallas_call | solution.py:339
  51.3 2.4 %collective-permute-start.15 = (bf16[64,1280]{1,0:T(8,128)(2,1)S(1)}, bf16[64,1280]{1,0:T(8,128)(2,1)S(1)}, u32[]{:S(2)}, u32[]{:S(2)}) collective-permute-start(bf16[64,1280]{1,0:T(8,128)(2,1)S(1)} %shard_map.109), channel_id=1, source_target_pairs={{0,4},{4,8},{8,12},{12,0},{1,5},{5,9},{9,13},{13,1},{2,6},{6,10},{... | collective-permute-start | bytes 491528 | tf_op jit(solution)/shard_map/ppermute | solution.py:229
  53.7 5.7 %collective-permute-done.10.chunk_ref = bf16[64,1280]{1,0:T(8,128)(2,1)S(1)} collective-permute-done((bf16[64,1280]{1,0:T(8,128)(2,1)S(1)}, bf16[64,1280]{1,0:T(8,128)(2,1)S(1)}, u32[]{:S(2)}, u32[]{:S(2)}) %collective-permute-start.10) | collective-permute-done | bytes 163872 | tf_op jit(solution)/shard_map/ppermute | solution.py:229
  59.5 1.6 %collective-permute-start.11 = (bf16[64,1280]{1,0:T(8,128)(2,1)S(1)}, bf16[64,1280]{1,0:T(8,128)(2,1)S(1)}, u32[]{:S(2)}, u32[]{:S(2)}) collective-permute-start(bf16[64,1280]{1,0:T(8,128)(2,1)S(1)} %shard_map.107.refs_0_), channel_id=1, source_target_pairs={{0,2},{2,0},{1,3},{3,1},{4,6},{6,4},{5,7},{7,5},{8,10},{10,8},{9,1... | collective-permute-start | bytes 491528 | tf_op jit(solution)/shard_map/ppermute | solution.py:229
  61.9 2.4 %shard_map.113.refs_7_ = bf16[2,32,2,5120]{3,2,1,0:T(2,128)(2,1)} custom-call(s32[2]{0:T(128)S(1)} %pad_add_fusion.place_ref, bf16[64,1280]{1,0:T(8,128)(2,1)S(1)} %shard_map.107.refs_0_, bf16[64,1280]{1,0:T(8,128)(2,1)S(1)} %shard_map.112.refs_1_, bf16[64,5120]{1,0:T(8,128)(2,1)S(1)} %get-tuple-element.71.refs_2_, s32[1,64]{1,0:T(1,128)S(1)} %bitcast.22, ...), custom_call_target="tpu_custom_call" | custom-call | tf_op jit(solution)/shard_map/pallas_call | solution.py:369
  64.2 2.4 %collective-permute-done.11.refs_0_ = bf16[64,1280]{1,0:T(8,128)(2,1)S(1)} collective-permute-done((bf16[64,1280]{1,0:T(8,128)(2,1)S(1)}, bf16[64,1280]{1,0:T(8,128)(2,1)S(1)}, u32[]{:S(2)}, u32[]{:S(2)}) %collective-permute-start.11) | collective-permute-done | bytes 163872 | tf_op jit(solution)/shard_map/ppermute | solution.py:229
  66.6 2.6 %collective-permute-done.17.refs_1_ = bf16[64,1280]{1,0:T(8,128)(2,1)S(1)} collective-permute-done((bf16[64,1280]{1,0:T(8,128)(2,1)S(1)}, bf16[64,1280]{1,0:T(8,128)(2,1)S(1)}, u32[]{:S(2)}, u32[]{:S(2)}) %collective-permute-start.17) | collective-permute-done | bytes 163872 | tf_op jit(solution)/shard_map/ppermute | solution.py:229
  69.2 2.4 %shard_map.114 = bf16[2,32,2,5120]{3,2,1,0:T(2,128)(2,1)} custom-call(s32[2]{0:T(128)S(1)} %pad_add_fusion.place_ref, bf16[64,1280]{1,0:T(8,128)(2,1)S(1)} %collective-permute-done.11.refs_0_, bf16[64,1280]{1,0:T(8,128)(2,1)S(1)} %collective-permute-done.17.refs_1_, bf16[64,5120]{1,0:T(8,128)(2,1)S(1)} %get-tuple-element.69.refs_2_, ...), custom_call_target="tpu_custom_call", output_to_operand_aliasing={{}: (8, {})} | custom-call | tf_op jit(solution)/shard_map/pallas_call | solution.py:369
  (38 shorter events, 2.2 us)
Async XLA Ops:
  0.0 19.5 %collective-permute-start.5 = (bf16[1280,1280]{1,0:T(8,128)(2,1)}, bf16[1280,1280]{1,0:T(8,128)(2,1)}, u32[]{:S(2)}, u32[]{:S(2)}) collective-permute-start(bf16[1280,1280]{1,0:T(8,128)(2,1)} %refs_0_), channel_id=1, source_target_pairs={{0,1},{1,0},{2,3},{3,2},{4,5},{5,4},{6,7},{7,6},{8,9},{9,8},{10,11... | collective-permute-start | bytes 9830408 | tf_op jit(solution)/shard_map/ppermute | solution.py:229
  2.2 10.9 %collective-permute-start.1 = (bf16[528,128]{1,0:T(8,128)(2,1)}, bf16[528,128]{1,0:T(8,128)(2,1)S(1)}, u32[]{:S(2)}, u32[]{:S(2)}) collective-permute-start(bf16[528,128]{1,0:T(8,128)(2,1)} %shard_map.100.refs_1_), channel_id=1, source_target_pairs={{0,4},{4,8},{8,12},{12,0},{1,5},{5,9},{9,13},{13,1},{2,6},{6,10},{... | collective-permute-start | bytes 405512 | tf_op jit(solution)/shard_map/ppermute | solution.py:248
  4.9 8.3 %collective-permute-start.2 = (bf16[528,128]{1,0:T(8,128)(2,1)}, bf16[528,128]{1,0:T(8,128)(2,1)S(1)}, u32[]{:S(2)}, u32[]{:S(2)}) collective-permute-start(bf16[528,128]{1,0:T(8,128)(2,1)} %shard_map.100.refs_1_), channel_id=1, source_target_pairs={{0,8},{4,12},{1,9},{5,13},{2,10},{6,14},{3,11},{7,15},{16,24},{20,... | collective-permute-start | bytes 405512 | tf_op jit(solution)/shard_map/ppermute | solution.py:248
  9.4 3.8 %collective-permute-start = (s32[1,64]{1,0:T(1,128)}, s32[1,64]{1,0:T(1,128)S(1)}, u32[]{:S(2)}, u32[]{:S(2)}) collective-permute-start(s32[1,64]{1,0:T(1,128)} %bitcast.21), channel_id=1, source_target_pairs={{0,2},{2,0},{1,3},{3,1},{4,6},{6,4},{5,7},{7,5},{8,10},{10,8},{9,1... | collective-permute-start | bytes 776 | tf_op jit(solution)/shard_map/ppermute | solution.py:229
  11.0 0.9 %copy-start.3 = (bf16[528,128]{1,0:T(8,128)(2,1)S(1)}, bf16[528,128]{1,0:T(8,128)(2,1)}, u32[]{:S(2)}) copy-start(bf16[528,128]{1,0:T(8,128)(2,1)} %shard_map.100.refs_1_) | copy-start | bytes 405508
  11.9 1.0 %copy-start.4 = (bf16[1,128,10,128]{3,1,2,0:T(8,128)(2,1)S(1)}, bf16[1,128,10,128]{3,1,2,0:T(8,128)(2,1)}, u32[]{:S(2)}) copy-start(bf16[1,128,10,128]{3,1,2,0:T(8,128)(2,1)} %param.10) | copy-start | bytes 983044
  16.5 3.1 %collective-permute-start.4 = (bf16[64,1280]{1,0:T(8,128)(2,1)S(1)}, bf16[64,1280]{1,0:T(8,128)(2,1)S(1)}, u32[]{:S(2)}, u32[]{:S(2)}) collective-permute-start(bf16[64,1280]{1,0:T(8,128)(2,1)S(1)} %get-tuple-element.45), channel_id=1, source_target_pairs={{0,1},{1,0},{2,3},{3,2},{4,5},{5,4},{6,7},{7,6},{8,9},{9,8},{10,11... | collective-permute-start | bytes 491528 | tf_op jit(solution)/shard_map/ppermute | solution.py:229
  16.5 10.7 %collective-permute-start.3 = (bf16[64,1280]{1,0:T(8,128)(2,1)S(1)}, bf16[64,1280]{1,0:T(8,128)(2,1)S(1)}, u32[]{:S(2)}, u32[]{:S(2)}) collective-permute-start(bf16[64,1280]{1,0:T(8,128)(2,1)S(1)} %get-tuple-element.44.refs_0_), channel_id=1, source_target_pairs={{0,4},{4,8},{8,12},{12,0},{1,5},{5,9},{9,13},{13,1},{2,6},{6,10},{... | collective-permute-start | bytes 491528 | tf_op jit(solution)/shard_map/ppermute | solution.py:229
  19.5 11.0 %collective-permute-start.7 = (bf16[64,1280]{1,0:T(8,128)(2,1)S(1)}, bf16[64,1280]{1,0:T(8,128)(2,1)S(1)}, u32[]{:S(2)}, u32[]{:S(2)}) collective-permute-start(bf16[64,1280]{1,0:T(8,128)(2,1)S(1)} %collective-permute-done.4.refs_1_), channel_id=1, source_target_pairs={{0,4},{4,8},{8,12},{12,0},{1,5},{5,9},{9,13},{13,1},{2,6},{6,10},{... | collective-permute-start | bytes 491528 | tf_op jit(solution)/shard_map/ppermute | solution.py:229
  20.9 1.9 %copy-start.1 = (bf16[1280,1280]{1,0:T(8,128)(2,1)S(1)}, bf16[1280,1280]{1,0:T(8,128)(2,1)}, u32[]{:S(2)}) copy-start(bf16[1280,1280]{1,0:T(8,128)(2,1)} %refs_0_) | copy-start | bytes 9830404
  26.4 15.1 %copy-start = (bf16[1,64,5120]{2,1,0:T(8,128)(2,1)S(1)}, bf16[1,64,5120]{2,1,0:T(8,128)(2,1)}, u32[]{:S(2)}) copy-start(bf16[1,64,5120]{2,1,0:T(8,128)(2,1)} %param.14) | copy-start | bytes 1966084
  27.3 8.4 %collective-permute-start.6 = (bf16[64,1280]{1,0:T(8,128)(2,1)S(1)}, bf16[64,1280]{1,0:T(8,128)(2,1)S(1)}, u32[]{:S(2)}, u32[]{:S(2)}) collective-permute-start(bf16[64,1280]{1,0:T(8,128)(2,1)S(1)} %collective-permute-done.3.refs_0_), channel_id=1, source_target_pairs={{0,4},{4,8},{8,12},{12,0},{1,5},{5,9},{9,13},{13,1},{2,6},{6,10},{... | collective-permute-start | bytes 491528 | tf_op jit(solution)/shard_map/ppermute | solution.py:229
  30.5 8.9 %collective-permute-start.8 = (bf16[64,1280]{1,0:T(8,128)(2,1)S(1)}, bf16[64,1280]{1,0:T(8,128)(2,1)S(1)}, u32[]{:S(2)}, u32[]{:S(2)}) collective-permute-start(bf16[64,1280]{1,0:T(8,128)(2,1)S(1)} %collective-permute-done.7.refs_1_), channel_id=1, source_target_pairs={{0,4},{4,8},{8,12},{12,0},{1,5},{5,9},{9,13},{13,1},{2,6},{6,10},{... | collective-permute-start | bytes 491528 | tf_op jit(solution)/shard_map/ppermute | solution.py:229
  31.8 11.3 %collective-permute-start.9 = (bf16[64,1280]{1,0:T(8,128)(2,1)S(1)}, bf16[64,1280]{1,0:T(8,128)(2,1)S(1)}, u32[]{:S(2)}, u32[]{:S(2)}) collective-permute-start(bf16[64,1280]{1,0:T(8,128)(2,1)S(1)} %shard_map.105), channel_id=1, source_target_pairs={{0,12},{4,0},{8,4},{12,8},{1,13},{5,1},{9,5},{13,9},{2,14},{6,2},{... | collective-permute-start | bytes 491528 | tf_op jit(solution)/shard_map/ppermute | solution.py:229
  35.7 11.1 %collective-permute-start.12 = (bf16[64,1280]{1,0:T(8,128)(2,1)S(1)}, bf16[64,1280]{1,0:T(8,128)(2,1)S(1)}, u32[]{:S(2)}, u32[]{:S(2)}) collective-permute-start(bf16[64,1280]{1,0:T(8,128)(2,1)S(1)} %collective-permute-done.6.refs_0_), channel_id=1, source_target_pairs={{0,4},{4,8},{8,12},{12,0},{1,5},{5,9},{9,13},{13,1},{2,6},{6,10},{... | collective-permute-start | bytes 491528 | tf_op jit(solution)/shard_map/ppermute | solution.py:229
  39.5 10.6 %collective-permute-start.13 = (bf16[64,1280]{1,0:T(8,128)(2,1)S(1)}, bf16[64,1280]{1,0:T(8,128)(2,1)S(1)}, u32[]{:S(2)}, u32[]{:S(2)}) collective-permute-start(bf16[64,1280]{1,0:T(8,128)(2,1)S(1)} %collective-permute-done.8.refs_1_), channel_id=1, source_target_pairs={{0,4},{4,8},{8,12},{12,0},{1,5},{5,9},{9,13},{13,1},{2,6},{6,10},{... | collective-permute-start | bytes 491528 | tf_op jit(solution)/shard_map/ppermute | solution.py:229
  41.5 8.6 %collective-permute-start.14 = (bf16[64,1280]{1,0:T(8,128)(2,1)S(1)}, bf16[64,1280]{1,0:T(8,128)(2,1)S(1)}, u32[]{:S(2)}, u32[]{:S(2)}) collective-permute-start(bf16[64,1280]{1,0:T(8,128)(2,1)S(1)} %shard_map.108.refs_0_), channel_id=1, source_target_pairs={{0,2},{2,0},{1,3},{3,1},{4,6},{6,4},{5,7},{7,5},{8,10},{10,8},{9,1... | collective-permute-start | bytes 491528 | tf_op jit(solution)/shard_map/ppermute | solution.py:229
  44.3 15.1 %collective-permute-start.10 = (bf16[64,1280]{1,0:T(8,128)(2,1)S(1)}, bf16[64,1280]{1,0:T(8,128)(2,1)S(1)}, u32[]{:S(2)}, u32[]{:S(2)}) collective-permute-start(bf16[64,1280]{1,0:T(8,128)(2,1)S(1)} %shard_map.106), channel_id=1, source_target_pairs={{0,8},{4,12},{8,0},{12,4},{1,9},{5,13},{9,1},{13,5},{2,10},{6,14},... | collective-permute-start | bytes 491528 | tf_op jit(solution)/shard_map/ppermute | solution.py:229
  46.8 15.0 %copy-start.7 = (bf16[5120]{0:T(1024)(128)(2,1)S(1)}, bf16[5120]{0:T(1024)(128)(2,1)}, u32[]{:S(2)}) copy-start(bf16[5120]{0:T(1024)(128)(2,1)} %param.16) | copy-start | bytes 30724
  46.8 15.1 %copy-start.2 = (bf16[5120,32]{0,1:T(8,128)(2,1)S(1)}, bf16[5120,32]{0,1:T(8,128)(2,1)}, u32[]{:S(2)}) copy-start(bf16[5120,32]{0,1:T(8,128)(2,1)} %param.17) | copy-start | bytes 983044
  46.8 15.0 %copy-start.5 = (s32[64]{0:T(128)S(1)}, s32[64]{0:T(128)}, u32[]{:S(2)}) copy-start(s32[64]{0:T(128)} %param.19) | copy-start | bytes 772
  46.8 15.0 %copy-start.6 = (s32[1,64,1]{1,2,0:T(1,128)S(1)}, s32[1,64,1]{1,2,0:T(1,128)}, u32[]{:S(2)}) copy-start(s32[1,64,1]{1,2,0:T(1,128)} %param.18) | copy-start | bytes 772
  46.8 14.2 %collective-permute-start.16 = (bf16[64,1280]{1,0:T(8,128)(2,1)S(1)}, bf16[64,1280]{1,0:T(8,128)(2,1)S(1)}, u32[]{:S(2)}, u32[]{:S(2)}) collective-permute-start(bf16[64,1280]{1,0:T(8,128)(2,1)S(1)} %shard_map.110.refs_1_), channel_id=1, source_target_pairs={{0,2},{2,0},{1,3},{3,1},{4,6},{6,4},{5,7},{7,5},{8,10},{10,8},{9,1... | collective-permute-start | bytes 491528 | tf_op jit(solution)/shard_map/ppermute | solution.py:229
  51.3 9.7 %collective-permute-start.15 = (bf16[64,1280]{1,0:T(8,128)(2,1)S(1)}, bf16[64,1280]{1,0:T(8,128)(2,1)S(1)}, u32[]{:S(2)}, u32[]{:S(2)}) collective-permute-start(bf16[64,1280]{1,0:T(8,128)(2,1)S(1)} %shard_map.109), channel_id=1, source_target_pairs={{0,4},{4,8},{8,12},{12,0},{1,5},{5,9},{9,13},{13,1},{2,6},{6,10},{... | collective-permute-start | bytes 491528 | tf_op jit(solution)/shard_map/ppermute | solution.py:229
  59.5 7.1 %collective-permute-start.11 = (bf16[64,1280]{1,0:T(8,128)(2,1)S(1)}, bf16[64,1280]{1,0:T(8,128)(2,1)S(1)}, u32[]{:S(2)}, u32[]{:S(2)}) collective-permute-start(bf16[64,1280]{1,0:T(8,128)(2,1)S(1)} %shard_map.107.refs_0_), channel_id=1, source_target_pairs={{0,2},{2,0},{1,3},{3,1},{4,6},{6,4},{5,7},{7,5},{8,10},{10,8},{9,1... | collective-permute-start | bytes 491528 | tf_op jit(solution)/shard_map/ppermute | solution.py:229
  61.1 8.0 %collective-permute-start.17 = (bf16[64,1280]{1,0:T(8,128)(2,1)S(1)}, bf16[64,1280]{1,0:T(8,128)(2,1)S(1)}, u32[]{:S(2)}, u32[]{:S(2)}) collective-permute-start(bf16[64,1280]{1,0:T(8,128)(2,1)S(1)} %shard_map.112.refs_1_), channel_id=1, source_target_pairs={{0,2},{2,0},{1,3},{3,1},{4,6},{6,4},{5,7},{7,5},{8,10},{10,8},{9,1... | collective-permute-start | bytes 491528 | tf_op jit(solution)/shard_map/ppermute | solution.py:229

commit v8 on v6

--- a/solution.py
+++ b/solution.py
@@ -12,6 +12,7 @@
 EPSILON = 1e-05
 DOC_ROWS = 16
 VMEM_LIMIT = 12 * 1024 * 1024
+VMEM_ATTENTION = 16 * 1024 * 1024
 VMEM_MOST = 61 * 1024 * 1024
 VMEM_MUCH = 52 * 1024 * 1024
 
@@ -262,7 +263,7 @@
         out_shape=[jax.ShapeDtypeStruct((part_rows, heads * head_size), bf16)] * pair,
         in_specs=[smem] + [vmem] * (1 + len(packs)),
         out_specs=[vmem] * pair,
-        compiler_params=params,
+        compiler_params=pltpu.CompilerParams(vmem_limit_bytes=VMEM_ATTENTION),
     )(jnp.stack([core, ctx_index]), staged_queries, *packs)
 
     project = pl.pallas_call(

time: 71.9 us -> 71.9 us (level)
  no operation moved by 1% of the time
where the time goes in v8:
time: 71.9 us; the launch traced here: 71.6 us
  starting transfers between devices  31.2 us (43%)
  waiting for transfers between devices  18.5 us (26%)
  Pallas kernels  17.7 us (25%)
  local copies, waits for them, and re-layouts  3.85 us (5%)
    ppermute x16, starting transfers between devices, over(): lax.ppermute(array, axis, [(i, (i + step) % count) for i in range(count)])  24.1 us
    ppermute x16, waiting for transfers between devices, over(): lax.ppermute(array, axis, [(i, (i + step) % count) for i in range(count)])  18.5 us
    ppermute x2, starting transfers between devices, on_device(): lax.ppermute(pack, 'ctx', [(i, (i + step) % ctx_count) for i in range(ctx...  7.11 us
    pallas_call x4, Pallas kernels, on_device(): total = project(*block, *weights)  4.95 us
    pallas_call x2, Pallas kernels, on_device(): pl.pallas_call(functools.partial(finish_kernel, late_steps, spots, back,...  4.91 us
    unnamed x16, local copies, waits for them, and re-layouts  3.83 us
    pallas_call x1, Pallas kernels, on_device(): pl.pallas_call(functools.partial(attention_kernel, heads // groups, group...  3.26 us
    pallas_call x1, Pallas kernels, on_device(): pl.pallas_call(functools.partial(stage_kernel, pair), out_shape=[jax.Shap...  2.32 us
  transfers between devices with their start and end apart: 18, of which 7 were waited for; matrix products, arithmetic and copies ran while one was open for 0% of the time, Pallas kernels for 21%

profile of v8, /device:TPU:0, one launch (start us, length us, event | category | flops | bytes accessed | tf_op | source)
XLA Modules:
  0.0 71.6 jit_solution(13932387690155310800)
XLA Ops:
  0.5 1.8 %shard_map.100.refs_1_ = bf16[528,128]{1,0:T(8,128)(2,1)} custom-call(bf16[256,128]{1,0:T(8,128)(2,1)} %bitcast.23, bf16[256,128]{1,0:T(8,128)(2,1)} %bitcast.24, s32[1,128]{1,0:T(1,128)} %doc_ref.1), custom_call_target="tpu_custom_call" | custom-call | tf_op jit(solution)/shard_map/pallas_call | solution.py:221
  2.2 2.6 %collective-permute-start.1 = (bf16[528,128]{1,0:T(8,128)(2,1)}, bf16[528,128]{1,0:T(8,128)(2,1)S(1)}, u32[]{:S(2)}, u32[]{:S(2)}) collective-permute-start(bf16[528,128]{1,0:T(8,128)(2,1)} %shard_map.100.refs_1_), channel_id=1, source_target_pairs={{0,4},{4,8},{8,12},{12,0},{1,5},{5,9},{9,13},{13,1},{2,6},{6,10},{... | collective-permute-start | bytes 405512 | tf_op jit(solution)/shard_map/ppermute | solution.py:235
  4.9 4.5 %collective-permute-start.2 = (bf16[528,128]{1,0:T(8,128)(2,1)}, bf16[528,128]{1,0:T(8,128)(2,1)S(1)}, u32[]{:S(2)}, u32[]{:S(2)}) collective-permute-start(bf16[528,128]{1,0:T(8,128)(2,1)} %shard_map.100.refs_1_), channel_id=1, source_target_pairs={{0,8},{4,12},{1,9},{5,13},{2,10},{6,14},{3,11},{7,15},{16,24},{20,... | collective-permute-start | bytes 405512 | tf_op jit(solution)/shard_map/ppermute | solution.py:235
  9.4 1.6 %collective-permute-start = (s32[1,64]{1,0:T(1,128)}, s32[1,64]{1,0:T(1,128)S(1)}, u32[]{:S(2)}, u32[]{:S(2)}) collective-permute-start(s32[1,64]{1,0:T(1,128)} %bitcast.21), channel_id=1, source_target_pairs={{0,2},{2,0},{1,3},{3,1},{4,6},{6,4},{5,7},{7,5},{8,10},{10,8},{9,1... | collective-permute-start | bytes 776 | tf_op jit(solution)/shard_map/ppermute | solution.py:216
  11.0 0.9 %copy-done.3 = bf16[528,128]{1,0:T(8,128)(2,1)S(1)} copy-done((bf16[528,128]{1,0:T(8,128)(2,1)S(1)}, bf16[528,128]{1,0:T(8,128)(2,1)}, u32[]{:S(2)}) %copy-start.3) | copy-done | bytes 135192
  11.9 1.0 %copy-done.4 = bf16[1,128,10,128]{3,1,2,0:T(8,128)(2,1)S(1)} copy-done((bf16[1,128,10,128]{3,1,2,0:T(8,128)(2,1)S(1)}, bf16[1,128,10,128]{3,1,2,0:T(8,128)(2,1)}, u32[]{:S(2)}) %copy-start.4) | copy-done | bytes 327704
  13.2 3.3 %shard_map.102 = (bf16[64,1280]{1,0:T(8,128)(2,1)S(1)}, bf16[64,1280]{1,0:T(8,128)(2,1)S(1)}) custom-call(s32[2]{0:T(128)S(1)} %pad_add_fusion.1.place_ref, bf16[10,128,128]{2,1,0:T(8,128)(2,1)S(1)} %get-tuple-element.42.query_ref, bf16[528,128]{1,0:T(8,128)(2,1)S(1)} %get-tuple-element.43.refs_0_, bf16[528,128]{1,0:T(8,128)(2,1)S(1)} %collective-permute-done.1.refs_1_, ...), custom_call_target="tpu_custom_call" | custom-call | tf_op jit(solution)/shard_map/pallas_call | solution.py:261
  16.5 3.0 %collective-permute-start.3 = (bf16[64,1280]{1,0:T(8,128)(2,1)S(1)}, bf16[64,1280]{1,0:T(8,128)(2,1)S(1)}, u32[]{:S(2)}, u32[]{:S(2)}) collective-permute-start(bf16[64,1280]{1,0:T(8,128)(2,1)S(1)} %get-tuple-element.44.refs_0_), channel_id=1, source_target_pairs={{0,4},{4,8},{8,12},{12,0},{1,5},{5,9},{9,13},{13,1},{2,6},{6,10},{... | collective-permute-start | bytes 491528 | tf_op jit(solution)/shard_map/ppermute | solution.py:216
  19.5 1.3 %collective-permute-start.7 = (bf16[64,1280]{1,0:T(8,128)(2,1)S(1)}, bf16[64,1280]{1,0:T(8,128)(2,1)S(1)}, u32[]{:S(2)}, u32[]{:S(2)}) collective-permute-start(bf16[64,1280]{1,0:T(8,128)(2,1)S(1)} %collective-permute-done.4.refs_1_), channel_id=1, source_target_pairs={{0,4},{4,8},{8,12},{12,0},{1,5},{5,9},{9,13},{13,1},{2,6},{6,10},{... | collective-permute-start | bytes 491528 | tf_op jit(solution)/shard_map/ppermute | solution.py:216
  20.9 1.9 %copy-done.1 = bf16[1280,1280]{1,0:T(8,128)(2,1)S(1)} copy-done((bf16[1280,1280]{1,0:T(8,128)(2,1)S(1)}, bf16[1280,1280]{1,0:T(8,128)(2,1)}, u32[]{:S(2)}) %copy-start.1) | copy-done | bytes 3276824
  22.8 2.3 %shard_map.103 = (bf16[1280,1280]{1,0:T(8,128)(2,1)S(1)}, bf16[1280,1280]{1,0:T(8,128)(2,1)S(1)}) custom-call(bf16[1280,1280]{1,0:T(8,128)(2,1)S(1)} %copy-done.1, bf16[1280,1280]{1,0:T(8,128)(2,1)} %collective-permute-done.5.refs_1_), custom_call_target="tpu_custom_call" | custom-call | tf_op jit(solution)/shard_map/pallas_call | solution.py:283
  25.1 1.2 %shard_map.104.chunk_ref = bf16[64,1280]{1,0:T(8,128)(2,1)S(1)} custom-call(bf16[64,1280]{1,0:T(8,128)(2,1)S(1)} %get-tuple-element.44.refs_0_, bf16[64,1280]{1,0:T(8,128)(2,1)S(1)} %collective-permute-done.4.refs_1_, bf16[1280,1280]{1,0:T(8,128)(2,1)S(1)} %get-tuple-element.49.refs_2_, bf16[1280,1280]{1,0:T(8,128)(2,1)S(1)} %get-tuple-element.50.refs_3_), custom_call_target="tpu_custom_call" | custom-call | flops 419430400 | bytes 6553600 | tf_op jit(solution)/shard_map/pallas_call | solution.py:326
  26.4 0.9 %collective-permute-done.3.refs_0_ = bf16[64,1280]{1,0:T(8,128)(2,1)S(1)} collective-permute-done((bf16[64,1280]{1,0:T(8,128)(2,1)S(1)}, bf16[64,1280]{1,0:T(8,128)(2,1)S(1)}, u32[]{:S(2)}, u32[]{:S(2)}) %collective-permute-start.3) | collective-permute-done | bytes 163872 | tf_op jit(solution)/shard_map/ppermute | solution.py:216
  27.3 1.7 %collective-permute-start.6 = (bf16[64,1280]{1,0:T(8,128)(2,1)S(1)}, bf16[64,1280]{1,0:T(8,128)(2,1)S(1)}, u32[]{:S(2)}, u32[]{:S(2)}) collective-permute-start(bf16[64,1280]{1,0:T(8,128)(2,1)S(1)} %collective-permute-done.3.refs_0_), channel_id=1, source_target_pairs={{0,4},{4,8},{8,12},{12,0},{1,5},{5,9},{9,13},{13,1},{2,6},{6,10},{... | collective-permute-start | bytes 491528 | tf_op jit(solution)/shard_map/ppermute | solution.py:216
  28.9 1.6 %collective-permute-done.7.refs_1_ = bf16[64,1280]{1,0:T(8,128)(2,1)S(1)} collective-permute-done((bf16[64,1280]{1,0:T(8,128)(2,1)S(1)}, bf16[64,1280]{1,0:T(8,128)(2,1)S(1)}, u32[]{:S(2)}, u32[]{:S(2)}) %collective-permute-start.7) | collective-permute-done | bytes 163872 | tf_op jit(solution)/shard_map/ppermute | solution.py:216
  30.6 1.2 %shard_map.105 = bf16[64,1280]{1,0:T(8,128)(2,1)S(1)} custom-call(bf16[64,1280]{1,0:T(8,128)(2,1)S(1)} %collective-permute-done.3.refs_0_, bf16[64,1280]{1,0:T(8,128)(2,1)S(1)} %collective-permute-done.7.refs_1_, bf16[1280,1280]{1,0:T(8,128)(2,1)S(1)} %get-tuple-element.49.refs_2_, bf16[1280,1280]{1,0:T(8,128)(2,1)S(1)} %get-tuple-element.50.refs_3_), custom_call_target="tpu_custom_call" | custom-call | flops 419430400 | bytes 6553600 | tf_op jit(solution)/shard_map/pallas_call | solution.py:326
  31.8 3.9 %collective-permute-start.9 = (bf16[64,1280]{1,0:T(8,128)(2,1)S(1)}, bf16[64,1280]{1,0:T(8,128)(2,1)S(1)}, u32[]{:S(2)}, u32[]{:S(2)}) collective-permute-start(bf16[64,1280]{1,0:T(8,128)(2,1)S(1)} %shard_map.105), channel_id=1, source_target_pairs={{0,12},{4,0},{8,4},{12,8},{1,13},{5,1},{9,5},{13,9},{2,14},{6,2},{... | collective-permute-start | bytes 491528 | tf_op jit(solution)/shard_map/ppermute | solution.py:216
  36.0 3.4 %collective-permute-done.8.refs_1_ = bf16[64,1280]{1,0:T(8,128)(2,1)S(1)} collective-permute-done((bf16[64,1280]{1,0:T(8,128)(2,1)S(1)}, bf16[64,1280]{1,0:T(8,128)(2,1)S(1)}, u32[]{:S(2)}, u32[]{:S(2)}) %collective-permute-start.8) | collective-permute-done | bytes 163872 | tf_op jit(solution)/shard_map/ppermute | solution.py:216
  39.5 2.0 %collective-permute-start.13 = (bf16[64,1280]{1,0:T(8,128)(2,1)S(1)}, bf16[64,1280]{1,0:T(8,128)(2,1)S(1)}, u32[]{:S(2)}, u32[]{:S(2)}) collective-permute-start(bf16[64,1280]{1,0:T(8,128)(2,1)S(1)} %collective-permute-done.8.refs_1_), channel_id=1, source_target_pairs={{0,4},{4,8},{8,12},{12,0},{1,5},{5,9},{9,13},{13,1},{2,6},{6,10},{... | collective-permute-start | bytes 491528 | tf_op jit(solution)/shard_map/ppermute | solution.py:216
  41.5 1.5 %collective-permute-start.14 = (bf16[64,1280]{1,0:T(8,128)(2,1)S(1)}, bf16[64,1280]{1,0:T(8,128)(2,1)S(1)}, u32[]{:S(2)}, u32[]{:S(2)}) collective-permute-start(bf16[64,1280]{1,0:T(8,128)(2,1)S(1)} %shard_map.108.refs_0_), channel_id=1, source_target_pairs={{0,2},{2,0},{1,3},{3,1},{4,6},{6,4},{5,7},{7,5},{8,10},{10,8},{9,1... | collective-permute-start | bytes 491528 | tf_op jit(solution)/shard_map/ppermute | solution.py:216
  43.1 1.2 %shard_map.106 = bf16[64,1280]{1,0:T(8,128)(2,1)S(1)} custom-call(bf16[64,1280]{1,0:T(8,128)(2,1)S(1)} %collective-permute-done.6.refs_0_, bf16[64,1280]{1,0:T(8,128)(2,1)S(1)} %collective-permute-done.8.refs_1_, bf16[1280,1280]{1,0:T(8,128)(2,1)S(1)} %get-tuple-element.49.refs_2_, bf16[1280,1280]{1,0:T(8,128)(2,1)S(1)} %get-tuple-element.50.refs_3_), custom_call_target="tpu_custom_call" | custom-call | flops 419430400 | bytes 6553600 | tf_op jit(solution)/shard_map/pallas_call | solution.py:326
  44.3 2.4 %collective-permute-start.10 = (bf16[64,1280]{1,0:T(8,128)(2,1)S(1)}, bf16[64,1280]{1,0:T(8,128)(2,1)S(1)}, u32[]{:S(2)}, u32[]{:S(2)}) collective-permute-start(bf16[64,1280]{1,0:T(8,128)(2,1)S(1)} %shard_map.106), channel_id=1, source_target_pairs={{0,8},{4,12},{8,0},{12,4},{1,9},{5,13},{9,1},{13,5},{2,10},{6,14},... | collective-permute-start | bytes 491528 | tf_op jit(solution)/shard_map/ppermute | solution.py:216
  46.8 1.3 %collective-permute-start.16 = (bf16[64,1280]{1,0:T(8,128)(2,1)S(1)}, bf16[64,1280]{1,0:T(8,128)(2,1)S(1)}, u32[]{:S(2)}, u32[]{:S(2)}) collective-permute-start(bf16[64,1280]{1,0:T(8,128)(2,1)S(1)} %shard_map.110.refs_1_), channel_id=1, source_target_pairs={{0,2},{2,0},{1,3},{3,1},{4,6},{6,4},{5,7},{7,5},{8,10},{10,8},{9,1... | collective-permute-start | bytes 491528 | tf_op jit(solution)/shard_map/ppermute | solution.py:216
  48.1 2.0 %collective-permute-done.13.refs_1_ = bf16[64,1280]{1,0:T(8,128)(2,1)S(1)} collective-permute-done((bf16[64,1280]{1,0:T(8,128)(2,1)S(1)}, bf16[64,1280]{1,0:T(8,128)(2,1)S(1)}, u32[]{:S(2)}, u32[]{:S(2)}) %collective-permute-start.13) | collective-permute-done | bytes 163872 | tf_op jit(solution)/shard_map/ppermute | solution.py:216
  50.1 1.2 %shard_map.109 = bf16[64,1280]{1,0:T(8,128)(2,1)S(1)} custom-call(bf16[64,1280]{1,0:T(8,128)(2,1)S(1)} %collective-permute-done.12.refs_0_, bf16[64,1280]{1,0:T(8,128)(2,1)S(1)} %collective-permute-done.13.refs_1_, bf16[1280,1280]{1,0:T(8,128)(2,1)S(1)} %get-tuple-element.49.refs_2_, bf16[1280,1280]{1,0:T(8,128)(2,1)S(1)} %get-tuple-element.50.refs_3_), custom_call_target="tpu_custom_call" | custom-call | flops 419430400 | bytes 6553600 | tf_op jit(solution)/shard_map/pallas_call | solution.py:326
  51.3 2.4 %collective-permute-start.15 = (bf16[64,1280]{1,0:T(8,128)(2,1)S(1)}, bf16[64,1280]{1,0:T(8,128)(2,1)S(1)}, u32[]{:S(2)}, u32[]{:S(2)}) collective-permute-start(bf16[64,1280]{1,0:T(8,128)(2,1)S(1)} %shard_map.109), channel_id=1, source_target_pairs={{0,4},{4,8},{8,12},{12,0},{1,5},{5,9},{9,13},{13,1},{2,6},{6,10},{... | collective-permute-start | bytes 491528 | tf_op jit(solution)/shard_map/ppermute | solution.py:216
  53.7 5.7 %collective-permute-done.10.chunk_ref = bf16[64,1280]{1,0:T(8,128)(2,1)S(1)} collective-permute-done((bf16[64,1280]{1,0:T(8,128)(2,1)S(1)}, bf16[64,1280]{1,0:T(8,128)(2,1)S(1)}, u32[]{:S(2)}, u32[]{:S(2)}) %collective-permute-start.10) | collective-permute-done | bytes 163872 | tf_op jit(solution)/shard_map/ppermute | solution.py:216
  59.5 1.6 %collective-permute-start.11 = (bf16[64,1280]{1,0:T(8,128)(2,1)S(1)}, bf16[64,1280]{1,0:T(8,128)(2,1)S(1)}, u32[]{:S(2)}, u32[]{:S(2)}) collective-permute-start(bf16[64,1280]{1,0:T(8,128)(2,1)S(1)} %shard_map.107.refs_0_), channel_id=1, source_target_pairs={{0,2},{2,0},{1,3},{3,1},{4,6},{6,4},{5,7},{7,5},{8,10},{10,8},{9,1... | collective-permute-start | bytes 491528 | tf_op jit(solution)/shard_map/ppermute | solution.py:216
  61.9 2.5 %shard_map.113.refs_7_ = bf16[2,32,2,5120]{3,2,1,0:T(2,128)(2,1)} custom-call(s32[2]{0:T(128)S(1)} %pad_add_fusion.place_ref, bf16[64,1280]{1,0:T(8,128)(2,1)S(1)} %shard_map.107.refs_0_, bf16[64,1280]{1,0:T(8,128)(2,1)S(1)} %shard_map.112.refs_1_, bf16[64,5120]{1,0:T(8,128)(2,1)S(1)} %get-tuple-element.71.refs_2_, s32[1,64]{1,0:T(1,128)S(1)} %bitcast.22, ...), custom_call_target="tpu_custom_call" | custom-call | tf_op jit(solution)/shard_map/pallas_call | solution.py:356
  64.3 2.3 %collective-permute-done.11.refs_0_ = bf16[64,1280]{1,0:T(8,128)(2,1)S(1)} collective-permute-done((bf16[64,1280]{1,0:T(8,128)(2,1)S(1)}, bf16[64,1280]{1,0:T(8,128)(2,1)S(1)}, u32[]{:S(2)}, u32[]{:S(2)}) %collective-permute-start.11) | collective-permute-done | bytes 163872 | tf_op jit(solution)/shard_map/ppermute | solution.py:216
  66.6 2.6 %collective-permute-done.17.refs_1_ = bf16[64,1280]{1,0:T(8,128)(2,1)S(1)} collective-permute-done((bf16[64,1280]{1,0:T(8,128)(2,1)S(1)}, bf16[64,1280]{1,0:T(8,128)(2,1)S(1)}, u32[]{:S(2)}, u32[]{:S(2)}) %collective-permute-start.17) | collective-permute-done | bytes 163872 | tf_op jit(solution)/shard_map/ppermute | solution.py:216
  69.2 2.5 %shard_map.114 = bf16[2,32,2,5120]{3,2,1,0:T(2,128)(2,1)} custom-call(s32[2]{0:T(128)S(1)} %pad_add_fusion.place_ref, bf16[64,1280]{1,0:T(8,128)(2,1)S(1)} %collective-permute-done.11.refs_0_, bf16[64,1280]{1,0:T(8,128)(2,1)S(1)} %collective-permute-done.17.refs_1_, bf16[64,5120]{1,0:T(8,128)(2,1)S(1)} %get-tuple-element.69.refs_2_, ...), custom_call_target="tpu_custom_call", output_to_operand_aliasing={{}: (8, {})} | custom-call | tf_op jit(solution)/shard_map/pallas_call | solution.py:356
  (38 shorter events, 2.2 us)
Async XLA Ops:
  0.0 19.5 %collective-permute-start.5 = (bf16[1280,1280]{1,0:T(8,128)(2,1)}, bf16[1280,1280]{1,0:T(8,128)(2,1)}, u32[]{:S(2)}, u32[]{:S(2)}) collective-permute-start(bf16[1280,1280]{1,0:T(8,128)(2,1)} %refs_0_), channel_id=1, source_target_pairs={{0,1},{1,0},{2,3},{3,2},{4,5},{5,4},{6,7},{7,6},{8,9},{9,8},{10,11... | collective-permute-start | bytes 9830408 | tf_op jit(solution)/shard_map/ppermute | solution.py:216
  2.2 10.9 %collective-permute-start.1 = (bf16[528,128]{1,0:T(8,128)(2,1)}, bf16[528,128]{1,0:T(8,128)(2,1)S(1)}, u32[]{:S(2)}, u32[]{:S(2)}) collective-permute-start(bf16[528,128]{1,0:T(8,128)(2,1)} %shard_map.100.refs_1_), channel_id=1, source_target_pairs={{0,4},{4,8},{8,12},{12,0},{1,5},{5,9},{9,13},{13,1},{2,6},{6,10},{... | collective-permute-start | bytes 405512 | tf_op jit(solution)/shard_map/ppermute | solution.py:235
  4.9 8.3 %collective-permute-start.2 = (bf16[528,128]{1,0:T(8,128)(2,1)}, bf16[528,128]{1,0:T(8,128)(2,1)S(1)}, u32[]{:S(2)}, u32[]{:S(2)}) collective-permute-start(bf16[528,128]{1,0:T(8,128)(2,1)} %shard_map.100.refs_1_), channel_id=1, source_target_pairs={{0,8},{4,12},{1,9},{5,13},{2,10},{6,14},{3,11},{7,15},{16,24},{20,... | collective-permute-start | bytes 405512 | tf_op jit(solution)/shard_map/ppermute | solution.py:235
  9.4 3.8 %collective-permute-start = (s32[1,64]{1,0:T(1,128)}, s32[1,64]{1,0:T(1,128)S(1)}, u32[]{:S(2)}, u32[]{:S(2)}) collective-permute-start(s32[1,64]{1,0:T(1,128)} %bitcast.21), channel_id=1, source_target_pairs={{0,2},{2,0},{1,3},{3,1},{4,6},{6,4},{5,7},{7,5},{8,10},{10,8},{9,1... | collective-permute-start | bytes 776 | tf_op jit(solution)/shard_map/ppermute | solution.py:216
  11.0 0.9 %copy-start.3 = (bf16[528,128]{1,0:T(8,128)(2,1)S(1)}, bf16[528,128]{1,0:T(8,128)(2,1)}, u32[]{:S(2)}) copy-start(bf16[528,128]{1,0:T(8,128)(2,1)} %shard_map.100.refs_1_) | copy-start | bytes 405508
  11.9 1.0 %copy-start.4 = (bf16[1,128,10,128]{3,1,2,0:T(8,128)(2,1)S(1)}, bf16[1,128,10,128]{3,1,2,0:T(8,128)(2,1)}, u32[]{:S(2)}) copy-start(bf16[1,128,10,128]{3,1,2,0:T(8,128)(2,1)} %param.10) | copy-start | bytes 983044
  16.5 3.1 %collective-permute-start.4 = (bf16[64,1280]{1,0:T(8,128)(2,1)S(1)}, bf16[64,1280]{1,0:T(8,128)(2,1)S(1)}, u32[]{:S(2)}, u32[]{:S(2)}) collective-permute-start(bf16[64,1280]{1,0:T(8,128)(2,1)S(1)} %get-tuple-element.45), channel_id=1, source_target_pairs={{0,1},{1,0},{2,3},{3,2},{4,5},{5,4},{6,7},{7,6},{8,9},{9,8},{10,11... | collective-permute-start | bytes 491528 | tf_op jit(solution)/shard_map/ppermute | solution.py:216
  16.5 10.7 %collective-permute-start.3 = (bf16[64,1280]{1,0:T(8,128)(2,1)S(1)}, bf16[64,1280]{1,0:T(8,128)(2,1)S(1)}, u32[]{:S(2)}, u32[]{:S(2)}) collective-permute-start(bf16[64,1280]{1,0:T(8,128)(2,1)S(1)} %get-tuple-element.44.refs_0_), channel_id=1, source_target_pairs={{0,4},{4,8},{8,12},{12,0},{1,5},{5,9},{9,13},{13,1},{2,6},{6,10},{... | collective-permute-start | bytes 491528 | tf_op jit(solution)/shard_map/ppermute | solution.py:216
  19.5 11.0 %collective-permute-start.7 = (bf16[64,1280]{1,0:T(8,128)(2,1)S(1)}, bf16[64,1280]{1,0:T(8,128)(2,1)S(1)}, u32[]{:S(2)}, u32[]{:S(2)}) collective-permute-start(bf16[64,1280]{1,0:T(8,128)(2,1)S(1)} %collective-permute-done.4.refs_1_), channel_id=1, source_target_pairs={{0,4},{4,8},{8,12},{12,0},{1,5},{5,9},{9,13},{13,1},{2,6},{6,10},{... | collective-permute-start | bytes 491528 | tf_op jit(solution)/shard_map/ppermute | solution.py:216
  20.9 1.9 %copy-start.1 = (bf16[1280,1280]{1,0:T(8,128)(2,1)S(1)}, bf16[1280,1280]{1,0:T(8,128)(2,1)}, u32[]{:S(2)}) copy-start(bf16[1280,1280]{1,0:T(8,128)(2,1)} %refs_0_) | copy-start | bytes 9830404
  26.4 15.1 %copy-start = (bf16[1,64,5120]{2,1,0:T(8,128)(2,1)S(1)}, bf16[1,64,5120]{2,1,0:T(8,128)(2,1)}, u32[]{:S(2)}) copy-start(bf16[1,64,5120]{2,1,0:T(8,128)(2,1)} %param.14) | copy-start | bytes 1966084
  27.3 8.4 %collective-permute-start.6 = (bf16[64,1280]{1,0:T(8,128)(2,1)S(1)}, bf16[64,1280]{1,0:T(8,128)(2,1)S(1)}, u32[]{:S(2)}, u32[]{:S(2)}) collective-permute-start(bf16[64,1280]{1,0:T(8,128)(2,1)S(1)} %collective-permute-done.3.refs_0_), channel_id=1, source_target_pairs={{0,4},{4,8},{8,12},{12,0},{1,5},{5,9},{9,13},{13,1},{2,6},{6,10},{... | collective-permute-start | bytes 491528 | tf_op jit(solution)/shard_map/ppermute | solution.py:216
  30.5 8.9 %collective-permute-start.8 = (bf16[64,1280]{1,0:T(8,128)(2,1)S(1)}, bf16[64,1280]{1,0:T(8,128)(2,1)S(1)}, u32[]{:S(2)}, u32[]{:S(2)}) collective-permute-start(bf16[64,1280]{1,0:T(8,128)(2,1)S(1)} %collective-permute-done.7.refs_1_), channel_id=1, source_target_pairs={{0,4},{4,8},{8,12},{12,0},{1,5},{5,9},{9,13},{13,1},{2,6},{6,10},{... | collective-permute-start | bytes 491528 | tf_op jit(solution)/shard_map/ppermute | solution.py:216
  31.8 11.3 %collective-permute-start.9 = (bf16[64,1280]{1,0:T(8,128)(2,1)S(1)}, bf16[64,1280]{1,0:T(8,128)(2,1)S(1)}, u32[]{:S(2)}, u32[]{:S(2)}) collective-permute-start(bf16[64,1280]{1,0:T(8,128)(2,1)S(1)} %shard_map.105), channel_id=1, source_target_pairs={{0,12},{4,0},{8,4},{12,8},{1,13},{5,1},{9,5},{13,9},{2,14},{6,2},{... | collective-permute-start | bytes 491528 | tf_op jit(solution)/shard_map/ppermute | solution.py:216
  35.7 11.1 %collective-permute-start.12 = (bf16[64,1280]{1,0:T(8,128)(2,1)S(1)}, bf16[64,1280]{1,0:T(8,128)(2,1)S(1)}, u32[]{:S(2)}, u32[]{:S(2)}) collective-permute-start(bf16[64,1280]{1,0:T(8,128)(2,1)S(1)} %collective-permute-done.6.refs_0_), channel_id=1, source_target_pairs={{0,4},{4,8},{8,12},{12,0},{1,5},{5,9},{9,13},{13,1},{2,6},{6,10},{... | collective-permute-start | bytes 491528 | tf_op jit(solution)/shard_map/ppermute | solution.py:216
  39.5 10.6 %collective-permute-start.13 = (bf16[64,1280]{1,0:T(8,128)(2,1)S(1)}, bf16[64,1280]{1,0:T(8,128)(2,1)S(1)}, u32[]{:S(2)}, u32[]{:S(2)}) collective-permute-start(bf16[64,1280]{1,0:T(8,128)(2,1)S(1)} %collective-permute-done.8.refs_1_), channel_id=1, source_target_pairs={{0,4},{4,8},{8,12},{12,0},{1,5},{5,9},{9,13},{13,1},{2,6},{6,10},{... | collective-permute-start | bytes 491528 | tf_op jit(solution)/shard_map/ppermute | solution.py:216
  41.5 8.6 %collective-permute-start.14 = (bf16[64,1280]{1,0:T(8,128)(2,1)S(1)}, bf16[64,1280]{1,0:T(8,128)(2,1)S(1)}, u32[]{:S(2)}, u32[]{:S(2)}) collective-permute-start(bf16[64,1280]{1,0:T(8,128)(2,1)S(1)} %shard_map.108.refs_0_), channel_id=1, source_target_pairs={{0,2},{2,0},{1,3},{3,1},{4,6},{6,4},{5,7},{7,5},{8,10},{10,8},{9,1... | collective-permute-start | bytes 491528 | tf_op jit(solution)/shard_map/ppermute | solution.py:216
  44.3 15.1 %collective-permute-start.10 = (bf16[64,1280]{1,0:T(8,128)(2,1)S(1)}, bf16[64,1280]{1,0:T(8,128)(2,1)S(1)}, u32[]{:S(2)}, u32[]{:S(2)}) collective-permute-start(bf16[64,1280]{1,0:T(8,128)(2,1)S(1)} %shard_map.106), channel_id=1, source_target_pairs={{0,8},{4,12},{8,0},{12,4},{1,9},{5,13},{9,1},{13,5},{2,10},{6,14},... | collective-permute-start | bytes 491528 | tf_op jit(solution)/shard_map/ppermute | solution.py:216
  46.8 15.0 %copy-start.7 = (bf16[5120]{0:T(1024)(128)(2,1)S(1)}, bf16[5120]{0:T(1024)(128)(2,1)}, u32[]{:S(2)}) copy-start(bf16[5120]{0:T(1024)(128)(2,1)} %param.16) | copy-start | bytes 30724
  46.8 15.1 %copy-start.2 = (bf16[5120,32]{0,1:T(8,128)(2,1)S(1)}, bf16[5120,32]{0,1:T(8,128)(2,1)}, u32[]{:S(2)}) copy-start(bf16[5120,32]{0,1:T(8,128)(2,1)} %param.17) | copy-start | bytes 983044
  46.8 15.0 %copy-start.5 = (s32[64]{0:T(128)S(1)}, s32[64]{0:T(128)}, u32[]{:S(2)}) copy-start(s32[64]{0:T(128)} %param.19) | copy-start | bytes 772
  46.8 15.0 %copy-start.6 = (s32[1,64,1]{1,2,0:T(1,128)S(1)}, s32[1,64,1]{1,2,0:T(1,128)}, u32[]{:S(2)}) copy-start(s32[1,64,1]{1,2,0:T(1,128)} %param.18) | copy-start | bytes 772
  46.8 14.2 %collective-permute-start.16 = (bf16[64,1280]{1,0:T(8,128)(2,1)S(1)}, bf16[64,1280]{1,0:T(8,128)(2,1)S(1)}, u32[]{:S(2)}, u32[]{:S(2)}) collective-permute-start(bf16[64,1280]{1,0:T(8,128)(2,1)S(1)} %shard_map.110.refs_1_), channel_id=1, source_target_pairs={{0,2},{2,0},{1,3},{3,1},{4,6},{6,4},{5,7},{7,5},{8,10},{10,8},{9,1... | collective-permute-start | bytes 491528 | tf_op jit(solution)/shard_map/ppermute | solution.py:216
  51.3 9.7 %collective-permute-start.15 = (bf16[64,1280]{1,0:T(8,128)(2,1)S(1)}, bf16[64,1280]{1,0:T(8,128)(2,1)S(1)}, u32[]{:S(2)}, u32[]{:S(2)}) collective-permute-start(bf16[64,1280]{1,0:T(8,128)(2,1)S(1)} %shard_map.109), channel_id=1, source_target_pairs={{0,4},{4,8},{8,12},{12,0},{1,5},{5,9},{9,13},{13,1},{2,6},{6,10},{... | collective-permute-start | bytes 491528 | tf_op jit(solution)/shard_map/ppermute | solution.py:216
  59.5 7.1 %collective-permute-start.11 = (bf16[64,1280]{1,0:T(8,128)(2,1)S(1)}, bf16[64,1280]{1,0:T(8,128)(2,1)S(1)}, u32[]{:S(2)}, u32[]{:S(2)}) collective-permute-start(bf16[64,1280]{1,0:T(8,128)(2,1)S(1)} %shard_map.107.refs_0_), channel_id=1, source_target_pairs={{0,2},{2,0},{1,3},{3,1},{4,6},{6,4},{5,7},{7,5},{8,10},{10,8},{9,1... | collective-permute-start | bytes 491528 | tf_op jit(solution)/shard_map/ppermute | solution.py:216
  61.1 8.0 %collective-permute-start.17 = (bf16[64,1280]{1,0:T(8,128)(2,1)S(1)}, bf16[64,1280]{1,0:T(8,128)(2,1)S(1)}, u32[]{:S(2)}, u32[]{:S(2)}) collective-permute-start(bf16[64,1280]{1,0:T(8,128)(2,1)S(1)} %shard_map.112.refs_1_), channel_id=1, source_target_pairs={{0,2},{2,0},{1,3},{3,1},{4,6},{6,4},{5,7},{7,5},{8,10},{10,8},{9,1... | collective-permute-start | bytes 491528 | tf_op jit(solution)/shard_map/ppermute | solution.py:216

commit v9 on v8

--- a/solution.py
+++ b/solution.py
@@ -103,7 +103,7 @@
 
 def columns_of(chunk_ref, step, spots, ctx_index):
     columns = chunk_ref.shape[1]
-    first = 0 if spots == 1 else lax.rem(ctx_index + step, spots) * columns
+    first = 0 if spots == 1 else lax.rem(ctx_index + spots - step, spots) * columns
     return pl.ds(pl.multiple_of(first, 128), columns)
 
 
@@ -316,7 +316,7 @@
     late_from = max(1, ctx_count - 2)
     for step in range(ctx_count):
         last = step == ctx_count - 1
-        following = None if last else [over(array, "ctx", 1) for array in block]
+        following = None if last else [over(array, "ctx", -1) for array in block]
         if step == 2:
             block, chunks[1] = lax.optimization_barrier((block, chunks[1]))
         if step == 3 and aligned:
@@ -324,7 +324,7 @@
         if last and aligned:
             hidden = collect(list(range(late_from)), ctx_count)
         total = project(*block, *weights)
-        chunk = over(total, "ctx", ctx_count - step)
+        chunk = over(total, "ctx", step)
         if not last:
             block = [lax.optimization_barrier((array, total))[0] for array in following]
         if last and aligned:
@@ -338,7 +338,7 @@
     if aligned:
         late_steps, spots = list(range(late_from, ctx_count)), ctx_count
     else:
-        whole = jnp.roll(jnp.stack(chunks), ctx_index, axis=0)
+        whole = jnp.roll(jnp.stack(chunks[:1] + chunks[:0:-1]), ctx_index, axis=0)
         whole = whole.transpose(1, 0, 2).reshape(part_rows, width)
         flat.append(forward(whole, 0, 1))
         hidden = collect([0], 1)

time: 71.9 us -> 70.2 us (0.976)
  the two profiles are of different devices: /device:TPU:0 before, /device:TPU:28 now
where the time goes in v9:
time: 70.2 us; the launch traced here: 69.9 us
  waiting for transfers between devices  32.6 us (46%)
  Pallas kernels  17.7 us (25%)
  starting transfers between devices  15.4 us (22%)
  local copies, waits for them, and re-layouts  3.85 us (5%)
    ppermute x16, waiting for transfers between devices, over(): lax.ppermute(array, axis, [(i, (i + step) % count) for i in range(count)])  26 us
    ppermute x16, starting transfers between devices, over(): lax.ppermute(array, axis, [(i, (i + step) % count) for i in range(count)])  13.9 us
    ppermute x2, waiting for transfers between devices, on_device(): lax.ppermute(pack, 'ctx', [(i, (i + step) % ctx_count) for i in range(ctx...  6.61 us
    pallas_call x4, Pallas kernels, on_device(): total = project(*block, *weights)  4.95 us
    pallas_call x2, Pallas kernels, on_device(): pl.pallas_call(functools.partial(finish_kernel, late_steps, spots, back,...  4.91 us
    unnamed x16, local copies, waits for them, and re-layouts  3.83 us
    pallas_call x1, Pallas kernels, on_device(): pl.pallas_call(functools.partial(attention_kernel, heads // groups, group...  3.26 us
    pallas_call x1, Pallas kernels, on_device(): pl.pallas_call(functools.partial(stage_kernel, pair), out_shape=[jax.Shap...  2.32 us
  transfers between devices with their start and end apart: 18, of which 12 were waited for; matrix products, arithmetic and copies ran while one was open for 0% of the time, Pallas kernels for 22%

profile of v9, /device:TPU:28, one launch (start us, length us, event | category | flops | bytes accessed | tf_op | source)
XLA Modules:
  0.0 69.9 jit_solution(3139182009831066118)
XLA Ops:
  0.0 1.8 %shard_map.100.refs_1_ = bf16[528,128]{1,0:T(8,128)(2,1)} custom-call(bf16[256,128]{1,0:T(8,128)(2,1)} %bitcast.23, bf16[256,128]{1,0:T(8,128)(2,1)} %bitcast.24, s32[1,128]{1,0:T(1,128)} %doc_ref.1), custom_call_target="tpu_custom_call" | custom-call | tf_op jit(solution)/shard_map/pallas_call | solution.py:221
  2.1 1.3 %collective-permute-start.2 = (bf16[528,128]{1,0:T(8,128)(2,1)}, bf16[528,128]{1,0:T(8,128)(2,1)S(1)}, u32[]{:S(2)}, u32[]{:S(2)}) collective-permute-start(bf16[528,128]{1,0:T(8,128)(2,1)} %shard_map.100.refs_1_), channel_id=1, source_target_pairs={{0,8},{4,12},{1,9},{5,13},{2,10},{6,14},{3,11},{7,15},{16,24},{20,... | collective-permute-start | bytes 405512 | tf_op jit(solution)/shard_map/ppermute | solution.py:235
  3.3 1.6 %collective-permute-start = (s32[1,64]{1,0:T(1,128)}, s32[1,64]{1,0:T(1,128)S(1)}, u32[]{:S(2)}, u32[]{:S(2)}) collective-permute-start(s32[1,64]{1,0:T(1,128)} %bitcast.21), channel_id=1, source_target_pairs={{0,2},{2,0},{1,3},{3,1},{4,6},{6,4},{5,7},{7,5},{8,10},{10,8},{9,1... | collective-permute-start | bytes 776 | tf_op jit(solution)/shard_map/ppermute | solution.py:216
  5.0 0.9 %copy-done.3 = bf16[528,128]{1,0:T(8,128)(2,1)S(1)} copy-done((bf16[528,128]{1,0:T(8,128)(2,1)S(1)}, bf16[528,128]{1,0:T(8,128)(2,1)}, u32[]{:S(2)}) %copy-start.3) | copy-done | bytes 135192
  5.9 1.0 %copy-done.4 = bf16[1,128,10,128]{3,1,2,0:T(8,128)(2,1)S(1)} copy-done((bf16[1,128,10,128]{3,1,2,0:T(8,128)(2,1)S(1)}, bf16[1,128,10,128]{3,1,2,0:T(8,128)(2,1)}, u32[]{:S(2)}) %copy-start.4) | copy-done | bytes 327704
  7.2 0.9 %collective-permute-done.1.refs_1_ = bf16[528,128]{1,0:T(8,128)(2,1)S(1)} collective-permute-done((bf16[528,128]{1,0:T(8,128)(2,1)}, bf16[528,128]{1,0:T(8,128)(2,1)S(1)}, u32[]{:S(2)}, u32[]{:S(2)}) %collective-permute-start.1) | collective-permute-done | bytes 135200 | tf_op jit(solution)/shard_map/ppermute | solution.py:235
  8.1 5.7 %collective-permute-done.2.refs_2_ = bf16[528,128]{1,0:T(8,128)(2,1)S(1)} collective-permute-done((bf16[528,128]{1,0:T(8,128)(2,1)}, bf16[528,128]{1,0:T(8,128)(2,1)S(1)}, u32[]{:S(2)}, u32[]{:S(2)}) %collective-permute-start.2) | collective-permute-done | bytes 135200 | tf_op jit(solution)/shard_map/ppermute | solution.py:235
  13.8 3.3 %shard_map.102 = (bf16[64,1280]{1,0:T(8,128)(2,1)S(1)}, bf16[64,1280]{1,0:T(8,128)(2,1)S(1)}) custom-call(s32[2]{0:T(128)S(1)} %pad_add_fusion.1.place_ref, bf16[10,128,128]{2,1,0:T(8,128)(2,1)S(1)} %get-tuple-element.42.query_ref, bf16[528,128]{1,0:T(8,128)(2,1)S(1)} %get-tuple-element.43.refs_0_, bf16[528,128]{1,0:T(8,128)(2,1)S(1)} %collective-permute-done.1.refs_1_, ...), custom_call_target="tpu_custom_call" | custom-call | tf_op jit(solution)/shard_map/pallas_call | solution.py:261
  17.2 1.3 %collective-permute-done.4.refs_1_ = bf16[64,1280]{1,0:T(8,128)(2,1)S(1)} collective-permute-done((bf16[64,1280]{1,0:T(8,128)(2,1)S(1)}, bf16[64,1280]{1,0:T(8,128)(2,1)S(1)}, u32[]{:S(2)}, u32[]{:S(2)}) %collective-permute-start.4) | collective-permute-done | bytes 163872 | tf_op jit(solution)/shard_map/ppermute | solution.py:216
  18.5 1.9 %copy-done.1 = bf16[1280,1280]{1,0:T(8,128)(2,1)S(1)} copy-done((bf16[1280,1280]{1,0:T(8,128)(2,1)S(1)}, bf16[1280,1280]{1,0:T(8,128)(2,1)}, u32[]{:S(2)}) %copy-start.1) | copy-done | bytes 3276824
  20.4 2.3 %shard_map.103 = (bf16[1280,1280]{1,0:T(8,128)(2,1)S(1)}, bf16[1280,1280]{1,0:T(8,128)(2,1)S(1)}) custom-call(bf16[1280,1280]{1,0:T(8,128)(2,1)S(1)} %copy-done.1, bf16[1280,1280]{1,0:T(8,128)(2,1)} %collective-permute-done.5.refs_1_), custom_call_target="tpu_custom_call" | custom-call | tf_op jit(solution)/shard_map/pallas_call | solution.py:283
  22.8 1.2 %shard_map.104.chunk_ref = bf16[64,1280]{1,0:T(8,128)(2,1)S(1)} custom-call(bf16[64,1280]{1,0:T(8,128)(2,1)S(1)} %get-tuple-element.44.refs_0_, bf16[64,1280]{1,0:T(8,128)(2,1)S(1)} %collective-permute-done.4.refs_1_, bf16[1280,1280]{1,0:T(8,128)(2,1)S(1)} %get-tuple-element.49.refs_2_, bf16[1280,1280]{1,0:T(8,128)(2,1)S(1)} %get-tuple-element.50.refs_3_), custom_call_target="tpu_custom_call" | custom-call | flops 419430400 | bytes 6553600 | tf_op jit(solution)/shard_map/pallas_call | solution.py:326
  24.0 1.9 %collective-permute-done.3.refs_0_ = bf16[64,1280]{1,0:T(8,128)(2,1)S(1)} collective-permute-done((bf16[64,1280]{1,0:T(8,128)(2,1)S(1)}, bf16[64,1280]{1,0:T(8,128)(2,1)S(1)}, u32[]{:S(2)}, u32[]{:S(2)}) %collective-permute-start.3) | collective-permute-done | bytes 163872 | tf_op jit(solution)/shard_map/ppermute | solution.py:216
  26.0 3.1 %collective-permute-done.7.refs_1_ = bf16[64,1280]{1,0:T(8,128)(2,1)S(1)} collective-permute-done((bf16[64,1280]{1,0:T(8,128)(2,1)S(1)}, bf16[64,1280]{1,0:T(8,128)(2,1)S(1)}, u32[]{:S(2)}, u32[]{:S(2)}) %collective-permute-start.7) | collective-permute-done | bytes 163872 | tf_op jit(solution)/shard_map/ppermute | solution.py:216
  29.0 1.2 %shard_map.105 = bf16[64,1280]{1,0:T(8,128)(2,1)S(1)} custom-call(bf16[64,1280]{1,0:T(8,128)(2,1)S(1)} %collective-permute-done.3.refs_0_, bf16[64,1280]{1,0:T(8,128)(2,1)S(1)} %collective-permute-done.7.refs_1_, bf16[1280,1280]{1,0:T(8,128)(2,1)S(1)} %get-tuple-element.49.refs_2_, bf16[1280,1280]{1,0:T(8,128)(2,1)S(1)} %get-tuple-element.50.refs_3_), custom_call_target="tpu_custom_call" | custom-call | flops 419430400 | bytes 6553600 | tf_op jit(solution)/shard_map/pallas_call | solution.py:326
  30.3 3.9 %collective-permute-start.9 = (bf16[64,1280]{1,0:T(8,128)(2,1)S(1)}, bf16[64,1280]{1,0:T(8,128)(2,1)S(1)}, u32[]{:S(2)}, u32[]{:S(2)}) collective-permute-start(bf16[64,1280]{1,0:T(8,128)(2,1)S(1)} %shard_map.105), channel_id=1, source_target_pairs={{0,4},{4,8},{8,12},{12,0},{1,5},{5,9},{9,13},{13,1},{2,6},{6,10},{... | collective-permute-start | bytes 491528 | tf_op jit(solution)/shard_map/ppermute | solution.py:216
  34.2 3.8 %collective-permute-done.8.refs_1_ = bf16[64,1280]{1,0:T(8,128)(2,1)S(1)} collective-permute-done((bf16[64,1280]{1,0:T(8,128)(2,1)S(1)}, bf16[64,1280]{1,0:T(8,128)(2,1)S(1)}, u32[]{:S(2)}, u32[]{:S(2)}) %collective-permute-start.8) | collective-permute-done | bytes 163872 | tf_op jit(solution)/shard_map/ppermute | solution.py:216
  38.0 1.6 %collective-permute-start.14 = (bf16[64,1280]{1,0:T(8,128)(2,1)S(1)}, bf16[64,1280]{1,0:T(8,128)(2,1)S(1)}, u32[]{:S(2)}, u32[]{:S(2)}) collective-permute-start(bf16[64,1280]{1,0:T(8,128)(2,1)S(1)} %shard_map.108.refs_0_), channel_id=1, source_target_pairs={{0,2},{2,0},{1,3},{3,1},{4,6},{6,4},{5,7},{7,5},{8,10},{10,8},{9,1... | collective-permute-start | bytes 491528 | tf_op jit(solution)/shard_map/ppermute | solution.py:216
  39.6 1.9 %collective-permute-done.9.chunk_ref = bf16[64,1280]{1,0:T(8,128)(2,1)S(1)} collective-permute-done((bf16[64,1280]{1,0:T(8,128)(2,1)S(1)}, bf16[64,1280]{1,0:T(8,128)(2,1)S(1)}, u32[]{:S(2)}, u32[]{:S(2)}) %collective-permute-start.9) | collective-permute-done | bytes 163872 | tf_op jit(solution)/shard_map/ppermute | solution.py:216
  41.5 1.2 %shard_map.106 = bf16[64,1280]{1,0:T(8,128)(2,1)S(1)} custom-call(bf16[64,1280]{1,0:T(8,128)(2,1)S(1)} %collective-permute-done.6.refs_0_, bf16[64,1280]{1,0:T(8,128)(2,1)S(1)} %collective-permute-done.8.refs_1_, bf16[1280,1280]{1,0:T(8,128)(2,1)S(1)} %get-tuple-element.49.refs_2_, bf16[1280,1280]{1,0:T(8,128)(2,1)S(1)} %get-tuple-element.50.refs_3_), custom_call_target="tpu_custom_call" | custom-call | flops 419430400 | bytes 6553600 | tf_op jit(solution)/shard_map/pallas_call | solution.py:326
  42.8 1.6 %collective-permute-start.10 = (bf16[64,1280]{1,0:T(8,128)(2,1)S(1)}, bf16[64,1280]{1,0:T(8,128)(2,1)S(1)}, u32[]{:S(2)}, u32[]{:S(2)}) collective-permute-start(bf16[64,1280]{1,0:T(8,128)(2,1)S(1)} %shard_map.106), channel_id=1, source_target_pairs={{0,8},{4,12},{8,0},{12,4},{1,9},{5,13},{9,1},{13,5},{2,10},{6,14},... | collective-permute-start | bytes 491528 | tf_op jit(solution)/shard_map/ppermute | solution.py:216
  44.4 0.6 collective-permute-done.12.refs_0_
  45.1 1.6 %collective-permute-start.16 = (bf16[64,1280]{1,0:T(8,128)(2,1)S(1)}, bf16[64,1280]{1,0:T(8,128)(2,1)S(1)}, u32[]{:S(2)}, u32[]{:S(2)}) collective-permute-start(bf16[64,1280]{1,0:T(8,128)(2,1)S(1)} %shard_map.110.refs_1_), channel_id=1, source_target_pairs={{0,2},{2,0},{1,3},{3,1},{4,6},{6,4},{5,7},{7,5},{8,10},{10,8},{9,1... | collective-permute-start | bytes 491528 | tf_op jit(solution)/shard_map/ppermute | solution.py:216
  46.7 1.7 %collective-permute-done.13.refs_1_ = bf16[64,1280]{1,0:T(8,128)(2,1)S(1)} collective-permute-done((bf16[64,1280]{1,0:T(8,128)(2,1)S(1)}, bf16[64,1280]{1,0:T(8,128)(2,1)S(1)}, u32[]{:S(2)}, u32[]{:S(2)}) %collective-permute-start.13) | collective-permute-done | bytes 163872 | tf_op jit(solution)/shard_map/ppermute | solution.py:216
  48.4 1.2 %shard_map.109 = bf16[64,1280]{1,0:T(8,128)(2,1)S(1)} custom-call(bf16[64,1280]{1,0:T(8,128)(2,1)S(1)} %collective-permute-done.12.refs_0_, bf16[64,1280]{1,0:T(8,128)(2,1)S(1)} %collective-permute-done.13.refs_1_, bf16[1280,1280]{1,0:T(8,128)(2,1)S(1)} %get-tuple-element.49.refs_2_, bf16[1280,1280]{1,0:T(8,128)(2,1)S(1)} %get-tuple-element.50.refs_3_), custom_call_target="tpu_custom_call" | custom-call | flops 419430400 | bytes 6553600 | tf_op jit(solution)/shard_map/pallas_call | solution.py:326
  49.6 1.4 %collective-permute-start.15 = (bf16[64,1280]{1,0:T(8,128)(2,1)S(1)}, bf16[64,1280]{1,0:T(8,128)(2,1)S(1)}, u32[]{:S(2)}, u32[]{:S(2)}) collective-permute-start(bf16[64,1280]{1,0:T(8,128)(2,1)S(1)} %shard_map.109), channel_id=1, source_target_pairs={{0,12},{4,0},{8,4},{12,8},{1,13},{5,1},{9,5},{13,9},{2,14},{6,2},{... | collective-permute-start | bytes 491528 | tf_op jit(solution)/shard_map/ppermute | solution.py:216
  51.0 6.7 %collective-permute-done.10.chunk_ref = bf16[64,1280]{1,0:T(8,128)(2,1)S(1)} collective-permute-done((bf16[64,1280]{1,0:T(8,128)(2,1)S(1)}, bf16[64,1280]{1,0:T(8,128)(2,1)S(1)}, u32[]{:S(2)}, u32[]{:S(2)}) %collective-permute-start.10) | collective-permute-done | bytes 163872 | tf_op jit(solution)/shard_map/ppermute | solution.py:216
  57.8 1.6 %collective-permute-start.11 = (bf16[64,1280]{1,0:T(8,128)(2,1)S(1)}, bf16[64,1280]{1,0:T(8,128)(2,1)S(1)}, u32[]{:S(2)}, u32[]{:S(2)}) collective-permute-start(bf16[64,1280]{1,0:T(8,128)(2,1)S(1)} %shard_map.107.refs_0_), channel_id=1, source_target_pairs={{0,2},{2,0},{1,3},{3,1},{4,6},{6,4},{5,7},{7,5},{8,10},{10,8},{9,1... | collective-permute-start | bytes 491528 | tf_op jit(solution)/shard_map/ppermute | solution.py:216
  60.2 2.5 %shard_map.113.refs_7_ = bf16[2,32,2,5120]{3,2,1,0:T(2,128)(2,1)} custom-call(s32[2]{0:T(128)S(1)} %pad_add_fusion.place_ref, bf16[64,1280]{1,0:T(8,128)(2,1)S(1)} %shard_map.107.refs_0_, bf16[64,1280]{1,0:T(8,128)(2,1)S(1)} %shard_map.112.refs_1_, bf16[64,5120]{1,0:T(8,128)(2,1)S(1)} %get-tuple-element.71.refs_2_, s32[1,64]{1,0:T(1,128)S(1)} %bitcast.22, ...), custom_call_target="tpu_custom_call" | custom-call | tf_op jit(solution)/shard_map/pallas_call | solution.py:356
  62.6 2.3 %collective-permute-done.11.refs_0_ = bf16[64,1280]{1,0:T(8,128)(2,1)S(1)} collective-permute-done((bf16[64,1280]{1,0:T(8,128)(2,1)S(1)}, bf16[64,1280]{1,0:T(8,128)(2,1)S(1)}, u32[]{:S(2)}, u32[]{:S(2)}) %collective-permute-start.11) | collective-permute-done | bytes 163872 | tf_op jit(solution)/shard_map/ppermute | solution.py:216
  64.9 2.6 %collective-permute-done.17.refs_1_ = bf16[64,1280]{1,0:T(8,128)(2,1)S(1)} collective-permute-done((bf16[64,1280]{1,0:T(8,128)(2,1)S(1)}, bf16[64,1280]{1,0:T(8,128)(2,1)S(1)}, u32[]{:S(2)}, u32[]{:S(2)}) %collective-permute-start.17) | collective-permute-done | bytes 163872 | tf_op jit(solution)/shard_map/ppermute | solution.py:216
  67.5 2.5 %shard_map.114 = bf16[2,32,2,5120]{3,2,1,0:T(2,128)(2,1)} custom-call(s32[2]{0:T(128)S(1)} %pad_add_fusion.place_ref, bf16[64,1280]{1,0:T(8,128)(2,1)S(1)} %collective-permute-done.11.refs_0_, bf16[64,1280]{1,0:T(8,128)(2,1)S(1)} %collective-permute-done.17.refs_1_, bf16[64,5120]{1,0:T(8,128)(2,1)S(1)} %get-tuple-element.69.refs_2_, ...), custom_call_target="tpu_custom_call", output_to_operand_aliasing={{}: (8, {})} | custom-call | tf_op jit(solution)/shard_map/pallas_call | solution.py:356
  (38 shorter events, 1.8 us)
Async XLA Ops:
  0.0 18.5 %collective-permute-start.5 = (bf16[1280,1280]{1,0:T(8,128)(2,1)}, bf16[1280,1280]{1,0:T(8,128)(2,1)}, u32[]{:S(2)}, u32[]{:S(2)}) collective-permute-start(bf16[1280,1280]{1,0:T(8,128)(2,1)} %refs_0_), channel_id=1, source_target_pairs={{0,1},{1,0},{2,3},{3,2},{4,5},{5,4},{6,7},{7,6},{8,9},{9,8},{10,11... | collective-permute-start | bytes 9830408 | tf_op jit(solution)/shard_map/ppermute | solution.py:216
  1.8 6.3 %collective-permute-start.1 = (bf16[528,128]{1,0:T(8,128)(2,1)}, bf16[528,128]{1,0:T(8,128)(2,1)S(1)}, u32[]{:S(2)}, u32[]{:S(2)}) collective-permute-start(bf16[528,128]{1,0:T(8,128)(2,1)} %shard_map.100.refs_1_), channel_id=1, source_target_pairs={{0,4},{4,8},{8,12},{12,0},{1,5},{5,9},{9,13},{13,1},{2,6},{6,10},{... | collective-permute-start | bytes 405512 | tf_op jit(solution)/shard_map/ppermute | solution.py:235
  2.1 11.7 %collective-permute-start.2 = (bf16[528,128]{1,0:T(8,128)(2,1)}, bf16[528,128]{1,0:T(8,128)(2,1)S(1)}, u32[]{:S(2)}, u32[]{:S(2)}) collective-permute-start(bf16[528,128]{1,0:T(8,128)(2,1)} %shard_map.100.refs_1_), channel_id=1, source_target_pairs={{0,8},{4,12},{1,9},{5,13},{2,10},{6,14},{3,11},{7,15},{16,24},{20,... | collective-permute-start | bytes 405512 | tf_op jit(solution)/shard_map/ppermute | solution.py:235
  3.3 3.8 %collective-permute-start = (s32[1,64]{1,0:T(1,128)}, s32[1,64]{1,0:T(1,128)S(1)}, u32[]{:S(2)}, u32[]{:S(2)}) collective-permute-start(s32[1,64]{1,0:T(1,128)} %bitcast.21), channel_id=1, source_target_pairs={{0,2},{2,0},{1,3},{3,1},{4,6},{6,4},{5,7},{7,5},{8,10},{10,8},{9,1... | collective-permute-start | bytes 776 | tf_op jit(solution)/shard_map/ppermute | solution.py:216
  5.0 0.9 %copy-start.3 = (bf16[528,128]{1,0:T(8,128)(2,1)S(1)}, bf16[528,128]{1,0:T(8,128)(2,1)}, u32[]{:S(2)}) copy-start(bf16[528,128]{1,0:T(8,128)(2,1)} %shard_map.100.refs_1_) | copy-start | bytes 405508
  5.9 1.0 %copy-start.4 = (bf16[1,128,10,128]{3,1,2,0:T(8,128)(2,1)S(1)}, bf16[1,128,10,128]{3,1,2,0:T(8,128)(2,1)}, u32[]{:S(2)}) copy-start(bf16[1,128,10,128]{3,1,2,0:T(8,128)(2,1)} %param.10) | copy-start | bytes 983044
  17.1 1.5 %collective-permute-start.4 = (bf16[64,1280]{1,0:T(8,128)(2,1)S(1)}, bf16[64,1280]{1,0:T(8,128)(2,1)S(1)}, u32[]{:S(2)}, u32[]{:S(2)}) collective-permute-start(bf16[64,1280]{1,0:T(8,128)(2,1)S(1)} %get-tuple-element.45), channel_id=1, source_target_pairs={{0,1},{1,0},{2,3},{3,2},{4,5},{5,4},{6,7},{7,6},{8,9},{9,8},{10,11... | collective-permute-start | bytes 491528 | tf_op jit(solution)/shard_map/ppermute | solution.py:216
  17.1 8.8 %collective-permute-start.3 = (bf16[64,1280]{1,0:T(8,128)(2,1)S(1)}, bf16[64,1280]{1,0:T(8,128)(2,1)S(1)}, u32[]{:S(2)}, u32[]{:S(2)}) collective-permute-start(bf16[64,1280]{1,0:T(8,128)(2,1)S(1)} %get-tuple-element.44.refs_0_), channel_id=1, source_target_pairs={{0,12},{4,0},{8,4},{12,8},{1,13},{5,1},{9,5},{13,9},{2,14},{6,2},{... | collective-permute-start | bytes 491528 | tf_op jit(solution)/shard_map/ppermute | solution.py:216
  18.5 10.5 %collective-permute-start.7 = (bf16[64,1280]{1,0:T(8,128)(2,1)S(1)}, bf16[64,1280]{1,0:T(8,128)(2,1)S(1)}, u32[]{:S(2)}, u32[]{:S(2)}) collective-permute-start(bf16[64,1280]{1,0:T(8,128)(2,1)S(1)} %collective-permute-done.4.refs_1_), channel_id=1, source_target_pairs={{0,12},{4,0},{8,4},{12,8},{1,13},{5,1},{9,5},{13,9},{2,14},{6,2},{... | collective-permute-start | bytes 491528 | tf_op jit(solution)/shard_map/ppermute | solution.py:216
  18.5 1.9 %copy-start.1 = (bf16[1280,1280]{1,0:T(8,128)(2,1)S(1)}, bf16[1280,1280]{1,0:T(8,128)(2,1)}, u32[]{:S(2)}) copy-start(bf16[1280,1280]{1,0:T(8,128)(2,1)} %refs_0_) | copy-start | bytes 9830404
  24.0 14.0 %copy-start = (bf16[1,64,5120]{2,1,0:T(8,128)(2,1)S(1)}, bf16[1,64,5120]{2,1,0:T(8,128)(2,1)}, u32[]{:S(2)}) copy-start(bf16[1,64,5120]{2,1,0:T(8,128)(2,1)} %param.14) | copy-start | bytes 1966084
  26.0 8.2 %collective-permute-start.6 = (bf16[64,1280]{1,0:T(8,128)(2,1)S(1)}, bf16[64,1280]{1,0:T(8,128)(2,1)S(1)}, u32[]{:S(2)}, u32[]{:S(2)}) collective-permute-start(bf16[64,1280]{1,0:T(8,128)(2,1)S(1)} %collective-permute-done.3.refs_0_), channel_id=1, source_target_pairs={{0,12},{4,0},{8,4},{12,8},{1,13},{5,1},{9,5},{13,9},{2,14},{6,2},{... | collective-permute-start | bytes 491528 | tf_op jit(solution)/shard_map/ppermute | solution.py:216
  29.0 8.9 %collective-permute-start.8 = (bf16[64,1280]{1,0:T(8,128)(2,1)S(1)}, bf16[64,1280]{1,0:T(8,128)(2,1)S(1)}, u32[]{:S(2)}, u32[]{:S(2)}) collective-permute-start(bf16[64,1280]{1,0:T(8,128)(2,1)S(1)} %collective-permute-done.7.refs_1_), channel_id=1, source_target_pairs={{0,12},{4,0},{8,4},{12,8},{1,13},{5,1},{9,5},{13,9},{2,14},{6,2},{... | collective-permute-start | bytes 491528 | tf_op jit(solution)/shard_map/ppermute | solution.py:216
  30.3 11.2 %collective-permute-start.9 = (bf16[64,1280]{1,0:T(8,128)(2,1)S(1)}, bf16[64,1280]{1,0:T(8,128)(2,1)S(1)}, u32[]{:S(2)}, u32[]{:S(2)}) collective-permute-start(bf16[64,1280]{1,0:T(8,128)(2,1)S(1)} %shard_map.105), channel_id=1, source_target_pairs={{0,4},{4,8},{8,12},{12,0},{1,5},{5,9},{9,13},{13,1},{2,6},{6,10},{... | collective-permute-start | bytes 491528 | tf_op jit(solution)/shard_map/ppermute | solution.py:216
  34.2 10.9 %collective-permute-start.12 = (bf16[64,1280]{1,0:T(8,128)(2,1)S(1)}, bf16[64,1280]{1,0:T(8,128)(2,1)S(1)}, u32[]{:S(2)}, u32[]{:S(2)}) collective-permute-start(bf16[64,1280]{1,0:T(8,128)(2,1)S(1)} %collective-permute-done.6.refs_0_), channel_id=1, source_target_pairs={{0,12},{4,0},{8,4},{12,8},{1,13},{5,1},{9,5},{13,9},{2,14},{6,2},{... | collective-permute-start | bytes 491528 | tf_op jit(solution)/shard_map/ppermute | solution.py:216
  38.0 10.4 %collective-permute-start.13 = (bf16[64,1280]{1,0:T(8,128)(2,1)S(1)}, bf16[64,1280]{1,0:T(8,128)(2,1)S(1)}, u32[]{:S(2)}, u32[]{:S(2)}) collective-permute-start(bf16[64,1280]{1,0:T(8,128)(2,1)S(1)} %collective-permute-done.8.refs_1_), channel_id=1, source_target_pairs={{0,12},{4,0},{8,4},{12,8},{1,13},{5,1},{9,5},{13,9},{2,14},{6,2},{... | collective-permute-start | bytes 491528 | tf_op jit(solution)/shard_map/ppermute | solution.py:216
  38.0 10.4 %collective-permute-start.14 = (bf16[64,1280]{1,0:T(8,128)(2,1)S(1)}, bf16[64,1280]{1,0:T(8,128)(2,1)S(1)}, u32[]{:S(2)}, u32[]{:S(2)}) collective-permute-start(bf16[64,1280]{1,0:T(8,128)(2,1)S(1)} %shard_map.108.refs_0_), channel_id=1, source_target_pairs={{0,2},{2,0},{1,3},{3,1},{4,6},{6,4},{5,7},{7,5},{8,10},{10,8},{9,1... | collective-permute-start | bytes 491528 | tf_op jit(solution)/shard_map/ppermute | solution.py:216
  42.8 15.0 %collective-permute-start.10 = (bf16[64,1280]{1,0:T(8,128)(2,1)S(1)}, bf16[64,1280]{1,0:T(8,128)(2,1)S(1)}, u32[]{:S(2)}, u32[]{:S(2)}) collective-permute-start(bf16[64,1280]{1,0:T(8,128)(2,1)S(1)} %shard_map.106), channel_id=1, source_target_pairs={{0,8},{4,12},{8,0},{12,4},{1,9},{5,13},{9,1},{13,5},{2,10},{6,14},... | collective-permute-start | bytes 491528 | tf_op jit(solution)/shard_map/ppermute | solution.py:216
  45.1 15.0 %copy-start.7 = (bf16[5120]{0:T(1024)(128)(2,1)S(1)}, bf16[5120]{0:T(1024)(128)(2,1)}, u32[]{:S(2)}) copy-start(bf16[5120]{0:T(1024)(128)(2,1)} %param.16) | copy-start | bytes 30724
  45.1 15.1 %copy-start.2 = (bf16[5120,32]{0,1:T(8,128)(2,1)S(1)}, bf16[5120,32]{0,1:T(8,128)(2,1)}, u32[]{:S(2)}) copy-start(bf16[5120,32]{0,1:T(8,128)(2,1)} %param.17) | copy-start | bytes 983044
  45.1 15.1 %copy-start.5 = (s32[64]{0:T(128)S(1)}, s32[64]{0:T(128)}, u32[]{:S(2)}) copy-start(s32[64]{0:T(128)} %param.19) | copy-start | bytes 772
  45.1 15.1 %copy-start.6 = (s32[1,64,1]{1,2,0:T(1,128)S(1)}, s32[1,64,1]{1,2,0:T(1,128)}, u32[]{:S(2)}) copy-start(s32[1,64,1]{1,2,0:T(1,128)} %param.18) | copy-start | bytes 772
  45.1 14.2 %collective-permute-start.16 = (bf16[64,1280]{1,0:T(8,128)(2,1)S(1)}, bf16[64,1280]{1,0:T(8,128)(2,1)S(1)}, u32[]{:S(2)}, u32[]{:S(2)}) collective-permute-start(bf16[64,1280]{1,0:T(8,128)(2,1)S(1)} %shard_map.110.refs_1_), channel_id=1, source_target_pairs={{0,2},{2,0},{1,3},{3,1},{4,6},{6,4},{5,7},{7,5},{8,10},{10,8},{9,1... | collective-permute-start | bytes 491528 | tf_op jit(solution)/shard_map/ppermute | solution.py:216
  49.6 9.8 %collective-permute-start.15 = (bf16[64,1280]{1,0:T(8,128)(2,1)S(1)}, bf16[64,1280]{1,0:T(8,128)(2,1)S(1)}, u32[]{:S(2)}, u32[]{:S(2)}) collective-permute-start(bf16[64,1280]{1,0:T(8,128)(2,1)S(1)} %shard_map.109), channel_id=1, source_target_pairs={{0,12},{4,0},{8,4},{12,8},{1,13},{5,1},{9,5},{13,9},{2,14},{6,2},{... | collective-permute-start | bytes 491528 | tf_op jit(solution)/shard_map/ppermute | solution.py:216
  57.8 7.1 %collective-permute-start.11 = (bf16[64,1280]{1,0:T(8,128)(2,1)S(1)}, bf16[64,1280]{1,0:T(8,128)(2,1)S(1)}, u32[]{:S(2)}, u32[]{:S(2)}) collective-permute-start(bf16[64,1280]{1,0:T(8,128)(2,1)S(1)} %shard_map.107.refs_0_), channel_id=1, source_target_pairs={{0,2},{2,0},{1,3},{3,1},{4,6},{6,4},{5,7},{7,5},{8,10},{10,8},{9,1... | collective-permute-start | bytes 491528 | tf_op jit(solution)/shard_map/ppermute | solution.py:216
  59.5 8.0 %collective-permute-start.17 = (bf16[64,1280]{1,0:T(8,128)(2,1)S(1)}, bf16[64,1280]{1,0:T(8,128)(2,1)S(1)}, u32[]{:S(2)}, u32[]{:S(2)}) collective-permute-start(bf16[64,1280]{1,0:T(8,128)(2,1)S(1)} %shard_map.112.refs_1_), channel_id=1, source_target_pairs={{0,2},{2,0},{1,3},{3,1},{4,6},{6,4},{5,7},{7,5},{8,10},{10,8},{9,1... | collective-permute-start | bytes 491528 | tf_op jit(solution)/shard_map/ppermute | solution.py:216

commit v10 on v7

--- a/solution.py
+++ b/solution.py
@@ -12,6 +12,7 @@
 EPSILON = 1e-05
 DOC_ROWS = 16
 VMEM_LIMIT = 12 * 1024 * 1024
+VMEM_ATTENTION = 16 * 1024 * 1024
 VMEM_MOST = 61 * 1024 * 1024
 VMEM_MUCH = 52 * 1024 * 1024
 
@@ -102,7 +103,7 @@
 
 def columns_of(chunk_ref, step, spots, ctx_index):
     columns = chunk_ref.shape[1]
-    first = 0 if spots == 1 else lax.rem(ctx_index + step, spots) * columns
+    first = 0 if spots == 1 else lax.rem(ctx_index + spots - step, spots) * columns
     return pl.ds(pl.multiple_of(first, 128), columns)
 
 
@@ -276,7 +277,7 @@
         out_shape=[jax.ShapeDtypeStruct((part_rows, heads * head_size), bf16)] * pair,
         in_specs=[smem] + [vmem] * (1 + len(packs)),
         out_specs=[vmem] * pair,
-        compiler_params=params,
+        compiler_params=pltpu.CompilerParams(vmem_limit_bytes=VMEM_ATTENTION),
     )(jnp.stack([core, ctx_index]), staged_queries, *packs)
 
     project = pl.pallas_call(
@@ -329,7 +330,7 @@
     late_from = max(1, ctx_count - 2)
     for step in range(ctx_count):
         last = step == ctx_count - 1
-        following = None if last else [over(array, "ctx", 1) for array in block]
+        following = None if last else [over(array, "ctx", -1) for array in block]
         if step == 2:
             block, chunks[1] = lax.optimization_barrier((block, chunks[1]))
         if step == 3 and aligned:
@@ -337,7 +338,7 @@
         if last and aligned:
             hidden = collect(list(range(late_from)), ctx_count)
         total = project(*block, *weights)
-        chunk = over(total, "ctx", ctx_count - step)
+        chunk = over(total, "ctx", step)
         if not last:
             block = [lax.optimization_barrier((array, total))[0] for array in following]
         if last and aligned:
@@ -351,7 +352,7 @@
     if aligned:
         late_steps, spots = list(range(late_from, ctx_count)), ctx_count
     else:
-        whole = jnp.roll(jnp.stack(chunks), ctx_index, axis=0)
+        whole = jnp.roll(jnp.stack(chunks[:1] + chunks[:0:-1]), ctx_index, axis=0)
         whole = whole.transpose(1, 0, 2).reshape(part_rows, width)
         flat.append(forward(whole, 0, 1))
         hidden = collect([0], 1)

time: 71.8 us -> 70.2 us (0.978)
  the two profiles are of different devices: /device:TPU:0 before, /device:TPU:28 now
where the time goes in v10:
time: 70.2 us; the launch traced here: 69.9 us
  waiting for transfers between devices  32.7 us (47%)
  Pallas kernels  17.6 us (25%)
  starting transfers between devices  15.4 us (22%)
  local copies, waits for them, and re-layouts  3.85 us (5%)
    ppermute x16, waiting for transfers between devices, over(): lax.ppermute(array, axis, [(i, (i + step) % count) for i in range(count)])  26 us
    ppermute x16, starting transfers between devices, over(): lax.ppermute(array, axis, [(i, (i + step) % count) for i in range(count)])  13.9 us
    ppermute x2, waiting for transfers between devices, on_device(): lax.ppermute(pack, 'ctx', [(i, (i + step) % ctx_count) for i in range(ctx...  6.61 us
    pallas_call x4, Pallas kernels, on_device(): total = project(*block, *weights)  4.95 us
    pallas_call x2, Pallas kernels, on_device(): pl.pallas_call(functools.partial(finish_kernel, late_steps, spots, back,...  4.75 us
    unnamed x16, local copies, waits for them, and re-layouts  3.83 us
    pallas_call x1, Pallas kernels, on_device(): pl.pallas_call(functools.partial(attention_kernel, heads // groups, group...  3.26 us
    pallas_call x1, Pallas kernels, on_device(): pl.pallas_call(functools.partial(stage_kernel, pair), out_shape=[jax.Shap...  2.32 us
  transfers between devices with their start and end apart: 18, of which 12 were waited for; matrix products, arithmetic and copies ran while one was open for 0% of the time, Pallas kernels for 22%

profile of v10, /device:TPU:28, one launch (start us, length us, event | category | flops | bytes accessed | tf_op | source)
XLA Modules:
  0.0 69.9 jit_solution(16846087353206124638)
XLA Ops:
  0.0 1.8 %shard_map.100.refs_1_ = bf16[528,128]{1,0:T(8,128)(2,1)} custom-call(bf16[256,128]{1,0:T(8,128)(2,1)} %bitcast.23, bf16[256,128]{1,0:T(8,128)(2,1)} %bitcast.24, s32[1,128]{1,0:T(1,128)} %doc_ref.1), custom_call_target="tpu_custom_call" | custom-call | tf_op jit(solution)/shard_map/pallas_call | solution.py:235
  2.1 1.3 %collective-permute-start.2 = (bf16[528,128]{1,0:T(8,128)(2,1)}, bf16[528,128]{1,0:T(8,128)(2,1)S(1)}, u32[]{:S(2)}, u32[]{:S(2)}) collective-permute-start(bf16[528,128]{1,0:T(8,128)(2,1)} %shard_map.100.refs_1_), channel_id=1, source_target_pairs={{0,8},{4,12},{1,9},{5,13},{2,10},{6,14},{3,11},{7,15},{16,24},{20,... | collective-permute-start | bytes 405512 | tf_op jit(solution)/shard_map/ppermute | solution.py:249
  3.3 1.6 %collective-permute-start = (s32[1,64]{1,0:T(1,128)}, s32[1,64]{1,0:T(1,128)S(1)}, u32[]{:S(2)}, u32[]{:S(2)}) collective-permute-start(s32[1,64]{1,0:T(1,128)} %bitcast.21), channel_id=1, source_target_pairs={{0,2},{2,0},{1,3},{3,1},{4,6},{6,4},{5,7},{7,5},{8,10},{10,8},{9,1... | collective-permute-start | bytes 776 | tf_op jit(solution)/shard_map/ppermute | solution.py:230
  5.0 0.9 %copy-done.3 = bf16[528,128]{1,0:T(8,128)(2,1)S(1)} copy-done((bf16[528,128]{1,0:T(8,128)(2,1)S(1)}, bf16[528,128]{1,0:T(8,128)(2,1)}, u32[]{:S(2)}) %copy-start.3) | copy-done | bytes 135192
  5.9 1.0 %copy-done.4 = bf16[1,128,10,128]{3,1,2,0:T(8,128)(2,1)S(1)} copy-done((bf16[1,128,10,128]{3,1,2,0:T(8,128)(2,1)S(1)}, bf16[1,128,10,128]{3,1,2,0:T(8,128)(2,1)}, u32[]{:S(2)}) %copy-start.4) | copy-done | bytes 327704
  7.2 0.9 %collective-permute-done.1.refs_1_ = bf16[528,128]{1,0:T(8,128)(2,1)S(1)} collective-permute-done((bf16[528,128]{1,0:T(8,128)(2,1)}, bf16[528,128]{1,0:T(8,128)(2,1)S(1)}, u32[]{:S(2)}, u32[]{:S(2)}) %collective-permute-start.1) | collective-permute-done | bytes 135200 | tf_op jit(solution)/shard_map/ppermute | solution.py:249
  8.1 5.7 %collective-permute-done.2.refs_2_ = bf16[528,128]{1,0:T(8,128)(2,1)S(1)} collective-permute-done((bf16[528,128]{1,0:T(8,128)(2,1)}, bf16[528,128]{1,0:T(8,128)(2,1)S(1)}, u32[]{:S(2)}, u32[]{:S(2)}) %collective-permute-start.2) | collective-permute-done | bytes 135200 | tf_op jit(solution)/shard_map/ppermute | solution.py:249
  13.8 3.3 %shard_map.102 = (bf16[64,1280]{1,0:T(8,128)(2,1)S(1)}, bf16[64,1280]{1,0:T(8,128)(2,1)S(1)}) custom-call(s32[2]{0:T(128)S(1)} %pad_add_fusion.1.place_ref, bf16[10,128,128]{2,1,0:T(8,128)(2,1)S(1)} %get-tuple-element.42.query_ref, bf16[528,128]{1,0:T(8,128)(2,1)S(1)} %get-tuple-element.43.refs_0_, bf16[528,128]{1,0:T(8,128)(2,1)S(1)} %collective-permute-done.1.refs_1_, ...), custom_call_target="tpu_custom_call" | custom-call | tf_op jit(solution)/shard_map/pallas_call | solution.py:275
  17.2 1.3 %collective-permute-done.4.refs_1_ = bf16[64,1280]{1,0:T(8,128)(2,1)S(1)} collective-permute-done((bf16[64,1280]{1,0:T(8,128)(2,1)S(1)}, bf16[64,1280]{1,0:T(8,128)(2,1)S(1)}, u32[]{:S(2)}, u32[]{:S(2)}) %collective-permute-start.4) | collective-permute-done | bytes 163872 | tf_op jit(solution)/shard_map/ppermute | solution.py:230
  18.5 1.9 %copy-done.1 = bf16[1280,1280]{1,0:T(8,128)(2,1)S(1)} copy-done((bf16[1280,1280]{1,0:T(8,128)(2,1)S(1)}, bf16[1280,1280]{1,0:T(8,128)(2,1)}, u32[]{:S(2)}) %copy-start.1) | copy-done | bytes 3276824
  20.4 2.3 %shard_map.103 = (bf16[1280,1280]{1,0:T(8,128)(2,1)S(1)}, bf16[1280,1280]{1,0:T(8,128)(2,1)S(1)}) custom-call(bf16[1280,1280]{1,0:T(8,128)(2,1)S(1)} %copy-done.1, bf16[1280,1280]{1,0:T(8,128)(2,1)} %collective-permute-done.5.refs_1_), custom_call_target="tpu_custom_call" | custom-call | tf_op jit(solution)/shard_map/pallas_call | solution.py:297
  22.8 1.2 %shard_map.104.chunk_ref = bf16[64,1280]{1,0:T(8,128)(2,1)S(1)} custom-call(bf16[64,1280]{1,0:T(8,128)(2,1)S(1)} %get-tuple-element.44.refs_0_, bf16[64,1280]{1,0:T(8,128)(2,1)S(1)} %collective-permute-done.4.refs_1_, bf16[1280,1280]{1,0:T(8,128)(2,1)S(1)} %get-tuple-element.49.refs_2_, bf16[1280,1280]{1,0:T(8,128)(2,1)S(1)} %get-tuple-element.50.refs_3_), custom_call_target="tpu_custom_call" | custom-call | flops 419430400 | bytes 6553600 | tf_op jit(solution)/shard_map/pallas_call | solution.py:340
  24.0 1.9 %collective-permute-done.3.refs_0_ = bf16[64,1280]{1,0:T(8,128)(2,1)S(1)} collective-permute-done((bf16[64,1280]{1,0:T(8,128)(2,1)S(1)}, bf16[64,1280]{1,0:T(8,128)(2,1)S(1)}, u32[]{:S(2)}, u32[]{:S(2)}) %collective-permute-start.3) | collective-permute-done | bytes 163872 | tf_op jit(solution)/shard_map/ppermute | solution.py:230
  26.0 3.1 %collective-permute-done.7.refs_1_ = bf16[64,1280]{1,0:T(8,128)(2,1)S(1)} collective-permute-done((bf16[64,1280]{1,0:T(8,128)(2,1)S(1)}, bf16[64,1280]{1,0:T(8,128)(2,1)S(1)}, u32[]{:S(2)}, u32[]{:S(2)}) %collective-permute-start.7) | collective-permute-done | bytes 163872 | tf_op jit(solution)/shard_map/ppermute | solution.py:230
  29.0 1.2 %shard_map.105 = bf16[64,1280]{1,0:T(8,128)(2,1)S(1)} custom-call(bf16[64,1280]{1,0:T(8,128)(2,1)S(1)} %collective-permute-done.3.refs_0_, bf16[64,1280]{1,0:T(8,128)(2,1)S(1)} %collective-permute-done.7.refs_1_, bf16[1280,1280]{1,0:T(8,128)(2,1)S(1)} %get-tuple-element.49.refs_2_, bf16[1280,1280]{1,0:T(8,128)(2,1)S(1)} %get-tuple-element.50.refs_3_), custom_call_target="tpu_custom_call" | custom-call | flops 419430400 | bytes 6553600 | tf_op jit(solution)/shard_map/pallas_call | solution.py:340
  30.3 3.9 %collective-permute-start.9 = (bf16[64,1280]{1,0:T(8,128)(2,1)S(1)}, bf16[64,1280]{1,0:T(8,128)(2,1)S(1)}, u32[]{:S(2)}, u32[]{:S(2)}) collective-permute-start(bf16[64,1280]{1,0:T(8,128)(2,1)S(1)} %shard_map.105), channel_id=1, source_target_pairs={{0,4},{4,8},{8,12},{12,0},{1,5},{5,9},{9,13},{13,1},{2,6},{6,10},{... | collective-permute-start | bytes 491528 | tf_op jit(solution)/shard_map/ppermute | solution.py:230
  34.2 3.8 %collective-permute-done.8.refs_1_ = bf16[64,1280]{1,0:T(8,128)(2,1)S(1)} collective-permute-done((bf16[64,1280]{1,0:T(8,128)(2,1)S(1)}, bf16[64,1280]{1,0:T(8,128)(2,1)S(1)}, u32[]{:S(2)}, u32[]{:S(2)}) %collective-permute-start.8) | collective-permute-done | bytes 163872 | tf_op jit(solution)/shard_map/ppermute | solution.py:230
  38.0 1.6 %collective-permute-start.14 = (bf16[64,1280]{1,0:T(8,128)(2,1)S(1)}, bf16[64,1280]{1,0:T(8,128)(2,1)S(1)}, u32[]{:S(2)}, u32[]{:S(2)}) collective-permute-start(bf16[64,1280]{1,0:T(8,128)(2,1)S(1)} %shard_map.108.refs_0_), channel_id=1, source_target_pairs={{0,2},{2,0},{1,3},{3,1},{4,6},{6,4},{5,7},{7,5},{8,10},{10,8},{9,1... | collective-permute-start | bytes 491528 | tf_op jit(solution)/shard_map/ppermute | solution.py:230
  39.6 1.9 %collective-permute-done.9.chunk_ref = bf16[64,1280]{1,0:T(8,128)(2,1)S(1)} collective-permute-done((bf16[64,1280]{1,0:T(8,128)(2,1)S(1)}, bf16[64,1280]{1,0:T(8,128)(2,1)S(1)}, u32[]{:S(2)}, u32[]{:S(2)}) %collective-permute-start.9) | collective-permute-done | bytes 163872 | tf_op jit(solution)/shard_map/ppermute | solution.py:230
  41.5 1.2 %shard_map.106 = bf16[64,1280]{1,0:T(8,128)(2,1)S(1)} custom-call(bf16[64,1280]{1,0:T(8,128)(2,1)S(1)} %collective-permute-done.6.refs_0_, bf16[64,1280]{1,0:T(8,128)(2,1)S(1)} %collective-permute-done.8.refs_1_, bf16[1280,1280]{1,0:T(8,128)(2,1)S(1)} %get-tuple-element.49.refs_2_, bf16[1280,1280]{1,0:T(8,128)(2,1)S(1)} %get-tuple-element.50.refs_3_), custom_call_target="tpu_custom_call" | custom-call | flops 419430400 | bytes 6553600 | tf_op jit(solution)/shard_map/pallas_call | solution.py:340
  42.8 1.6 %collective-permute-start.10 = (bf16[64,1280]{1,0:T(8,128)(2,1)S(1)}, bf16[64,1280]{1,0:T(8,128)(2,1)S(1)}, u32[]{:S(2)}, u32[]{:S(2)}) collective-permute-start(bf16[64,1280]{1,0:T(8,128)(2,1)S(1)} %shard_map.106), channel_id=1, source_target_pairs={{0,8},{4,12},{8,0},{12,4},{1,9},{5,13},{9,1},{13,5},{2,10},{6,14},... | collective-permute-start | bytes 491528 | tf_op jit(solution)/shard_map/ppermute | solution.py:230
  44.4 0.6 collective-permute-done.12.refs_0_
  45.1 1.6 %collective-permute-start.16 = (bf16[64,1280]{1,0:T(8,128)(2,1)S(1)}, bf16[64,1280]{1,0:T(8,128)(2,1)S(1)}, u32[]{:S(2)}, u32[]{:S(2)}) collective-permute-start(bf16[64,1280]{1,0:T(8,128)(2,1)S(1)} %shard_map.110.refs_1_), channel_id=1, source_target_pairs={{0,2},{2,0},{1,3},{3,1},{4,6},{6,4},{5,7},{7,5},{8,10},{10,8},{9,1... | collective-permute-start | bytes 491528 | tf_op jit(solution)/shard_map/ppermute | solution.py:230
  46.7 1.7 %collective-permute-done.13.refs_1_ = bf16[64,1280]{1,0:T(8,128)(2,1)S(1)} collective-permute-done((bf16[64,1280]{1,0:T(8,128)(2,1)S(1)}, bf16[64,1280]{1,0:T(8,128)(2,1)S(1)}, u32[]{:S(2)}, u32[]{:S(2)}) %collective-permute-start.13) | collective-permute-done | bytes 163872 | tf_op jit(solution)/shard_map/ppermute | solution.py:230
  48.4 1.2 %shard_map.109 = bf16[64,1280]{1,0:T(8,128)(2,1)S(1)} custom-call(bf16[64,1280]{1,0:T(8,128)(2,1)S(1)} %collective-permute-done.12.refs_0_, bf16[64,1280]{1,0:T(8,128)(2,1)S(1)} %collective-permute-done.13.refs_1_, bf16[1280,1280]{1,0:T(8,128)(2,1)S(1)} %get-tuple-element.49.refs_2_, bf16[1280,1280]{1,0:T(8,128)(2,1)S(1)} %get-tuple-element.50.refs_3_), custom_call_target="tpu_custom_call" | custom-call | flops 419430400 | bytes 6553600 | tf_op jit(solution)/shard_map/pallas_call | solution.py:340
  49.6 1.4 %collective-permute-start.15 = (bf16[64,1280]{1,0:T(8,128)(2,1)S(1)}, bf16[64,1280]{1,0:T(8,128)(2,1)S(1)}, u32[]{:S(2)}, u32[]{:S(2)}) collective-permute-start(bf16[64,1280]{1,0:T(8,128)(2,1)S(1)} %shard_map.109), channel_id=1, source_target_pairs={{0,12},{4,0},{8,4},{12,8},{1,13},{5,1},{9,5},{13,9},{2,14},{6,2},{... | collective-permute-start | bytes 491528 | tf_op jit(solution)/shard_map/ppermute | solution.py:230
  51.0 6.7 %collective-permute-done.10.chunk_ref = bf16[64,1280]{1,0:T(8,128)(2,1)S(1)} collective-permute-done((bf16[64,1280]{1,0:T(8,128)(2,1)S(1)}, bf16[64,1280]{1,0:T(8,128)(2,1)S(1)}, u32[]{:S(2)}, u32[]{:S(2)}) %collective-permute-start.10) | collective-permute-done | bytes 163872 | tf_op jit(solution)/shard_map/ppermute | solution.py:230
  57.8 1.6 %collective-permute-start.11 = (bf16[64,1280]{1,0:T(8,128)(2,1)S(1)}, bf16[64,1280]{1,0:T(8,128)(2,1)S(1)}, u32[]{:S(2)}, u32[]{:S(2)}) collective-permute-start(bf16[64,1280]{1,0:T(8,128)(2,1)S(1)} %shard_map.107.refs_0_), channel_id=1, source_target_pairs={{0,2},{2,0},{1,3},{3,1},{4,6},{6,4},{5,7},{7,5},{8,10},{10,8},{9,1... | collective-permute-start | bytes 491528 | tf_op jit(solution)/shard_map/ppermute | solution.py:230
  60.2 2.4 %shard_map.113.refs_7_ = bf16[2,32,2,5120]{3,2,1,0:T(2,128)(2,1)} custom-call(s32[2]{0:T(128)S(1)} %pad_add_fusion.place_ref, bf16[64,1280]{1,0:T(8,128)(2,1)S(1)} %shard_map.107.refs_0_, bf16[64,1280]{1,0:T(8,128)(2,1)S(1)} %shard_map.112.refs_1_, bf16[64,5120]{1,0:T(8,128)(2,1)S(1)} %get-tuple-element.71.refs_2_, s32[1,64]{1,0:T(1,128)S(1)} %bitcast.22, ...), custom_call_target="tpu_custom_call" | custom-call | tf_op jit(solution)/shard_map/pallas_call | solution.py:370
  62.6 2.4 %collective-permute-done.11.refs_0_ = bf16[64,1280]{1,0:T(8,128)(2,1)S(1)} collective-permute-done((bf16[64,1280]{1,0:T(8,128)(2,1)S(1)}, bf16[64,1280]{1,0:T(8,128)(2,1)S(1)}, u32[]{:S(2)}, u32[]{:S(2)}) %collective-permute-start.11) | collective-permute-done | bytes 163872 | tf_op jit(solution)/shard_map/ppermute | solution.py:230
  64.9 2.6 %collective-permute-done.17.refs_1_ = bf16[64,1280]{1,0:T(8,128)(2,1)S(1)} collective-permute-done((bf16[64,1280]{1,0:T(8,128)(2,1)S(1)}, bf16[64,1280]{1,0:T(8,128)(2,1)S(1)}, u32[]{:S(2)}, u32[]{:S(2)}) %collective-permute-start.17) | collective-permute-done | bytes 163872 | tf_op jit(solution)/shard_map/ppermute | solution.py:230
  67.5 2.4 %shard_map.114 = bf16[2,32,2,5120]{3,2,1,0:T(2,128)(2,1)} custom-call(s32[2]{0:T(128)S(1)} %pad_add_fusion.place_ref, bf16[64,1280]{1,0:T(8,128)(2,1)S(1)} %collective-permute-done.11.refs_0_, bf16[64,1280]{1,0:T(8,128)(2,1)S(1)} %collective-permute-done.17.refs_1_, bf16[64,5120]{1,0:T(8,128)(2,1)S(1)} %get-tuple-element.69.refs_2_, ...), custom_call_target="tpu_custom_call", output_to_operand_aliasing={{}: (8, {})} | custom-call | tf_op jit(solution)/shard_map/pallas_call | solution.py:370
  (38 shorter events, 1.8 us)
Async XLA Ops:
  0.0 18.5 %collective-permute-start.5 = (bf16[1280,1280]{1,0:T(8,128)(2,1)}, bf16[1280,1280]{1,0:T(8,128)(2,1)}, u32[]{:S(2)}, u32[]{:S(2)}) collective-permute-start(bf16[1280,1280]{1,0:T(8,128)(2,1)} %refs_0_), channel_id=1, source_target_pairs={{0,1},{1,0},{2,3},{3,2},{4,5},{5,4},{6,7},{7,6},{8,9},{9,8},{10,11... | collective-permute-start | bytes 9830408 | tf_op jit(solution)/shard_map/ppermute | solution.py:230
  1.8 6.3 %collective-permute-start.1 = (bf16[528,128]{1,0:T(8,128)(2,1)}, bf16[528,128]{1,0:T(8,128)(2,1)S(1)}, u32[]{:S(2)}, u32[]{:S(2)}) collective-permute-start(bf16[528,128]{1,0:T(8,128)(2,1)} %shard_map.100.refs_1_), channel_id=1, source_target_pairs={{0,4},{4,8},{8,12},{12,0},{1,5},{5,9},{9,13},{13,1},{2,6},{6,10},{... | collective-permute-start | bytes 405512 | tf_op jit(solution)/shard_map/ppermute | solution.py:249
  2.1 11.7 %collective-permute-start.2 = (bf16[528,128]{1,0:T(8,128)(2,1)}, bf16[528,128]{1,0:T(8,128)(2,1)S(1)}, u32[]{:S(2)}, u32[]{:S(2)}) collective-permute-start(bf16[528,128]{1,0:T(8,128)(2,1)} %shard_map.100.refs_1_), channel_id=1, source_target_pairs={{0,8},{4,12},{1,9},{5,13},{2,10},{6,14},{3,11},{7,15},{16,24},{20,... | collective-permute-start | bytes 405512 | tf_op jit(solution)/shard_map/ppermute | solution.py:249
  3.3 3.8 %collective-permute-start = (s32[1,64]{1,0:T(1,128)}, s32[1,64]{1,0:T(1,128)S(1)}, u32[]{:S(2)}, u32[]{:S(2)}) collective-permute-start(s32[1,64]{1,0:T(1,128)} %bitcast.21), channel_id=1, source_target_pairs={{0,2},{2,0},{1,3},{3,1},{4,6},{6,4},{5,7},{7,5},{8,10},{10,8},{9,1... | collective-permute-start | bytes 776 | tf_op jit(solution)/shard_map/ppermute | solution.py:230
  5.0 0.9 %copy-start.3 = (bf16[528,128]{1,0:T(8,128)(2,1)S(1)}, bf16[528,128]{1,0:T(8,128)(2,1)}, u32[]{:S(2)}) copy-start(bf16[528,128]{1,0:T(8,128)(2,1)} %shard_map.100.refs_1_) | copy-start | bytes 405508
  5.9 1.0 %copy-start.4 = (bf16[1,128,10,128]{3,1,2,0:T(8,128)(2,1)S(1)}, bf16[1,128,10,128]{3,1,2,0:T(8,128)(2,1)}, u32[]{:S(2)}) copy-start(bf16[1,128,10,128]{3,1,2,0:T(8,128)(2,1)} %param.10) | copy-start | bytes 983044
  17.1 1.5 %collective-permute-start.4 = (bf16[64,1280]{1,0:T(8,128)(2,1)S(1)}, bf16[64,1280]{1,0:T(8,128)(2,1)S(1)}, u32[]{:S(2)}, u32[]{:S(2)}) collective-permute-start(bf16[64,1280]{1,0:T(8,128)(2,1)S(1)} %get-tuple-element.45), channel_id=1, source_target_pairs={{0,1},{1,0},{2,3},{3,2},{4,5},{5,4},{6,7},{7,6},{8,9},{9,8},{10,11... | collective-permute-start | bytes 491528 | tf_op jit(solution)/shard_map/ppermute | solution.py:230
  17.1 8.8 %collective-permute-start.3 = (bf16[64,1280]{1,0:T(8,128)(2,1)S(1)}, bf16[64,1280]{1,0:T(8,128)(2,1)S(1)}, u32[]{:S(2)}, u32[]{:S(2)}) collective-permute-start(bf16[64,1280]{1,0:T(8,128)(2,1)S(1)} %get-tuple-element.44.refs_0_), channel_id=1, source_target_pairs={{0,12},{4,0},{8,4},{12,8},{1,13},{5,1},{9,5},{13,9},{2,14},{6,2},{... | collective-permute-start | bytes 491528 | tf_op jit(solution)/shard_map/ppermute | solution.py:230
  18.5 10.5 %collective-permute-start.7 = (bf16[64,1280]{1,0:T(8,128)(2,1)S(1)}, bf16[64,1280]{1,0:T(8,128)(2,1)S(1)}, u32[]{:S(2)}, u32[]{:S(2)}) collective-permute-start(bf16[64,1280]{1,0:T(8,128)(2,1)S(1)} %collective-permute-done.4.refs_1_), channel_id=1, source_target_pairs={{0,12},{4,0},{8,4},{12,8},{1,13},{5,1},{9,5},{13,9},{2,14},{6,2},{... | collective-permute-start | bytes 491528 | tf_op jit(solution)/shard_map/ppermute | solution.py:230
  18.5 1.9 %copy-start.1 = (bf16[1280,1280]{1,0:T(8,128)(2,1)S(1)}, bf16[1280,1280]{1,0:T(8,128)(2,1)}, u32[]{:S(2)}) copy-start(bf16[1280,1280]{1,0:T(8,128)(2,1)} %refs_0_) | copy-start | bytes 9830404
  24.0 14.0 %copy-start = (bf16[1,64,5120]{2,1,0:T(8,128)(2,1)S(1)}, bf16[1,64,5120]{2,1,0:T(8,128)(2,1)}, u32[]{:S(2)}) copy-start(bf16[1,64,5120]{2,1,0:T(8,128)(2,1)} %param.14) | copy-start | bytes 1966084
  26.0 8.2 %collective-permute-start.6 = (bf16[64,1280]{1,0:T(8,128)(2,1)S(1)}, bf16[64,1280]{1,0:T(8,128)(2,1)S(1)}, u32[]{:S(2)}, u32[]{:S(2)}) collective-permute-start(bf16[64,1280]{1,0:T(8,128)(2,1)S(1)} %collective-permute-done.3.refs_0_), channel_id=1, source_target_pairs={{0,12},{4,0},{8,4},{12,8},{1,13},{5,1},{9,5},{13,9},{2,14},{6,2},{... | collective-permute-start | bytes 491528 | tf_op jit(solution)/shard_map/ppermute | solution.py:230
  29.0 8.9 %collective-permute-start.8 = (bf16[64,1280]{1,0:T(8,128)(2,1)S(1)}, bf16[64,1280]{1,0:T(8,128)(2,1)S(1)}, u32[]{:S(2)}, u32[]{:S(2)}) collective-permute-start(bf16[64,1280]{1,0:T(8,128)(2,1)S(1)} %collective-permute-done.7.refs_1_), channel_id=1, source_target_pairs={{0,12},{4,0},{8,4},{12,8},{1,13},{5,1},{9,5},{13,9},{2,14},{6,2},{... | collective-permute-start | bytes 491528 | tf_op jit(solution)/shard_map/ppermute | solution.py:230
  30.3 11.2 %collective-permute-start.9 = (bf16[64,1280]{1,0:T(8,128)(2,1)S(1)}, bf16[64,1280]{1,0:T(8,128)(2,1)S(1)}, u32[]{:S(2)}, u32[]{:S(2)}) collective-permute-start(bf16[64,1280]{1,0:T(8,128)(2,1)S(1)} %shard_map.105), channel_id=1, source_target_pairs={{0,4},{4,8},{8,12},{12,0},{1,5},{5,9},{9,13},{13,1},{2,6},{6,10},{... | collective-permute-start | bytes 491528 | tf_op jit(solution)/shard_map/ppermute | solution.py:230
  34.2 10.9 %collective-permute-start.12 = (bf16[64,1280]{1,0:T(8,128)(2,1)S(1)}, bf16[64,1280]{1,0:T(8,128)(2,1)S(1)}, u32[]{:S(2)}, u32[]{:S(2)}) collective-permute-start(bf16[64,1280]{1,0:T(8,128)(2,1)S(1)} %collective-permute-done.6.refs_0_), channel_id=1, source_target_pairs={{0,12},{4,0},{8,4},{12,8},{1,13},{5,1},{9,5},{13,9},{2,14},{6,2},{... | collective-permute-start | bytes 491528 | tf_op jit(solution)/shard_map/ppermute | solution.py:230
  38.0 10.4 %collective-permute-start.13 = (bf16[64,1280]{1,0:T(8,128)(2,1)S(1)}, bf16[64,1280]{1,0:T(8,128)(2,1)S(1)}, u32[]{:S(2)}, u32[]{:S(2)}) collective-permute-start(bf16[64,1280]{1,0:T(8,128)(2,1)S(1)} %collective-permute-done.8.refs_1_), channel_id=1, source_target_pairs={{0,12},{4,0},{8,4},{12,8},{1,13},{5,1},{9,5},{13,9},{2,14},{6,2},{... | collective-permute-start | bytes 491528 | tf_op jit(solution)/shard_map/ppermute | solution.py:230
  38.0 10.4 %collective-permute-start.14 = (bf16[64,1280]{1,0:T(8,128)(2,1)S(1)}, bf16[64,1280]{1,0:T(8,128)(2,1)S(1)}, u32[]{:S(2)}, u32[]{:S(2)}) collective-permute-start(bf16[64,1280]{1,0:T(8,128)(2,1)S(1)} %shard_map.108.refs_0_), channel_id=1, source_target_pairs={{0,2},{2,0},{1,3},{3,1},{4,6},{6,4},{5,7},{7,5},{8,10},{10,8},{9,1... | collective-permute-start | bytes 491528 | tf_op jit(solution)/shard_map/ppermute | solution.py:230
  42.8 15.0 %collective-permute-start.10 = (bf16[64,1280]{1,0:T(8,128)(2,1)S(1)}, bf16[64,1280]{1,0:T(8,128)(2,1)S(1)}, u32[]{:S(2)}, u32[]{:S(2)}) collective-permute-start(bf16[64,1280]{1,0:T(8,128)(2,1)S(1)} %shard_map.106), channel_id=1, source_target_pairs={{0,8},{4,12},{8,0},{12,4},{1,9},{5,13},{9,1},{13,5},{2,10},{6,14},... | collective-permute-start | bytes 491528 | tf_op jit(solution)/shard_map/ppermute | solution.py:230
  45.1 15.0 %copy-start.7 = (bf16[5120]{0:T(1024)(128)(2,1)S(1)}, bf16[5120]{0:T(1024)(128)(2,1)}, u32[]{:S(2)}) copy-start(bf16[5120]{0:T(1024)(128)(2,1)} %param.16) | copy-start | bytes 30724
  45.1 15.1 %copy-start.2 = (bf16[5120,32]{0,1:T(8,128)(2,1)S(1)}, bf16[5120,32]{0,1:T(8,128)(2,1)}, u32[]{:S(2)}) copy-start(bf16[5120,32]{0,1:T(8,128)(2,1)} %param.17) | copy-start | bytes 983044
  45.1 15.1 %copy-start.5 = (s32[64]{0:T(128)S(1)}, s32[64]{0:T(128)}, u32[]{:S(2)}) copy-start(s32[64]{0:T(128)} %param.19) | copy-start | bytes 772
  45.1 15.1 %copy-start.6 = (s32[1,64,1]{1,2,0:T(1,128)S(1)}, s32[1,64,1]{1,2,0:T(1,128)}, u32[]{:S(2)}) copy-start(s32[1,64,1]{1,2,0:T(1,128)} %param.18) | copy-start | bytes 772
  45.1 14.2 %collective-permute-start.16 = (bf16[64,1280]{1,0:T(8,128)(2,1)S(1)}, bf16[64,1280]{1,0:T(8,128)(2,1)S(1)}, u32[]{:S(2)}, u32[]{:S(2)}) collective-permute-start(bf16[64,1280]{1,0:T(8,128)(2,1)S(1)} %shard_map.110.refs_1_), channel_id=1, source_target_pairs={{0,2},{2,0},{1,3},{3,1},{4,6},{6,4},{5,7},{7,5},{8,10},{10,8},{9,1... | collective-permute-start | bytes 491528 | tf_op jit(solution)/shard_map/ppermute | solution.py:230
  49.6 9.8 %collective-permute-start.15 = (bf16[64,1280]{1,0:T(8,128)(2,1)S(1)}, bf16[64,1280]{1,0:T(8,128)(2,1)S(1)}, u32[]{:S(2)}, u32[]{:S(2)}) collective-permute-start(bf16[64,1280]{1,0:T(8,128)(2,1)S(1)} %shard_map.109), channel_id=1, source_target_pairs={{0,12},{4,0},{8,4},{12,8},{1,13},{5,1},{9,5},{13,9},{2,14},{6,2},{... | collective-permute-start | bytes 491528 | tf_op jit(solution)/shard_map/ppermute | solution.py:230
  57.8 7.1 %collective-permute-start.11 = (bf16[64,1280]{1,0:T(8,128)(2,1)S(1)}, bf16[64,1280]{1,0:T(8,128)(2,1)S(1)}, u32[]{:S(2)}, u32[]{:S(2)}) collective-permute-start(bf16[64,1280]{1,0:T(8,128)(2,1)S(1)} %shard_map.107.refs_0_), channel_id=1, source_target_pairs={{0,2},{2,0},{1,3},{3,1},{4,6},{6,4},{5,7},{7,5},{8,10},{10,8},{9,1... | collective-permute-start | bytes 491528 | tf_op jit(solution)/shard_map/ppermute | solution.py:230
  59.5 8.0 %collective-permute-start.17 = (bf16[64,1280]{1,0:T(8,128)(2,1)S(1)}, bf16[64,1280]{1,0:T(8,128)(2,1)S(1)}, u32[]{:S(2)}, u32[]{:S(2)}) collective-permute-start(bf16[64,1280]{1,0:T(8,128)(2,1)S(1)} %shard_map.112.refs_1_), channel_id=1, source_target_pairs={{0,2},{2,0},{1,3},{3,1},{4,6},{6,4},{5,7},{7,5},{8,10},{10,8},{9,1... | collective-permute-start | bytes 491528 | tf_op jit(solution)/shard_map/ppermute | solution.py:230
